TPU v7x, 32 devices: a whole 2x2x4 slice. The times are simulated.
32 devices in a mesh: seq: 8 (over y, x, core), shard: 4 (over z).
Axes of the slice: x: 2, y: 2, z: 4, core: 2. Of those that a mesh axis runs over, the one named last changes fastest.
Arguments:
- tokens: bfloat16 [4, 1536, 1536], P('shard', 'seq'), may hold values from -6 to 6
- out_grad: bfloat16 [4, 1536, 1536], P('shard', 'seq'), may hold values from -6 to 6
- deal_order: int32 [4, 1536], P('shard'), may hold values from 0 to 1535, each once within a row
- lengths: int32 [4, 4], P('shard'), may hold values from 1 to 1024, 1536 in all within a row
- routes: int32 [4, 1536, 6], P('shard', 'seq'), may hold values from 0 to 63, all different within a row; in each aligned block of 192 rows (0 to 191, 192 to 383, ..., all dimensions but the last counted through in order) at most 30 rows name the same one
- norm_in: bfloat16 [1536], P('shard'), may hold values from 0.5 to 1.5
- w_in: bfloat16 [1536, 6400], P('shard'), may hold values from -0.15625 to 0.15625
- w_dt: bfloat16 [1536, 48], P('shard'), may hold values from -0.15625 to 0.15625
- conv_w: bfloat16 [3328, 4], P('shard'), may hold values from -0.5 to 0.5
- conv_b: bfloat16 [3328], P('shard'), may hold values from -0.5 to 0.5
- dt_bias: bfloat16 [48], P('shard'), may hold values from -6.5 to -2.5
- a_log: bfloat16 [48], P('shard'), may hold values from 0 to 2.765625
- d_skip: bfloat16 [48], P('shard'), may hold values from 0.5 to 1.5
- norm_gate: bfloat16 [3072], P('shard'), may hold values from 0.5 to 1.5
- w_out: bfloat16 [3072, 1536], P('shard'), may hold values from -0.109375 to 0.109375
- norm_moe: bfloat16 [1536], P('shard'), may hold values from 0.5 to 1.5
- w_router: bfloat16 [1536, 64], P('shard'), may hold values from -0.078125 to 0.078125
- w_shared: bfloat16 [1536, 2048], P('shard'), may hold values from -0.15625 to 0.15625
- w_shared_down: bfloat16 [1024, 1536], P('shard'), may hold values from -0.375 to 0.375
- w_experts: bfloat16 [64, 1536, 1024], P('seq', 'shard'), may hold values from -0.15625 to 0.15625
- w_experts_down: bfloat16 [64, 512, 1536], P('seq', 'shard'), may hold values from -1 to 1
Outputs:
- layer_out: bfloat16 [4, 1536, 1536], P('shard', 'seq')
- tokens_grad: bfloat16 [4, 1536, 1536], P('shard', 'seq')
- norm_in_grad: float32 [1536], P('shard')
- w_in_grad: float32 [1536, 6400], P('shard')
- w_dt_grad: float32 [1536, 48], P('shard')
- conv_w_grad: float32 [3328, 4], P('shard')
- conv_b_grad: float32 [3328], P('shard')
- dt_bias_grad: float32 [48], P('shard')
- a_log_grad: float32 [48], P('shard')
- d_skip_grad: float32 [48], P('shard')
- norm_gate_grad: float32 [3072], P('shard')
- w_out_grad: float32 [3072, 1536], P('shard')
- norm_moe_grad: float32 [1536], P('shard')
- w_router_grad: float32 [1536, 64], P('shard')
- w_shared_grad: float32 [1536, 2048], P('shard')
- w_shared_down_grad: float32 [1024, 1536], P('shard')
- w_experts_grad: float32 [64, 1536, 1024], P('seq', 'shard')
- w_experts_down_grad: float32 [64, 512, 1536], P('seq', 'shard')
Inputs may be any that keep to these rules, and one draw needn't show every extreme that they name: Each group's row holds every token number of the group once: dealt position i holds the group's token deal_order[i] in sequence order. A group's 4 lengths sum to 1536; its longest is exactly 1024. `routes`: A token names 6 different experts; among the tokens of one device no expert is named more than 30 times, a bound that some block reaches.
All inputs are finite; a program needn't handle non-finite values.
Results may differ from a plain program's by a relative error of at most 0.02.
Values may be sent and summed in bfloat16 or wider, within the bound.
A program may use at most 320 MiB of HBM per device.

v0:
```python
import jax
import jax.numpy as jnp
from jax import lax
from jax.sharding import PartitionSpec as P

STRETCH = 256


EPSILON = 1e-05
HIGHEST = lax.Precision.HIGHEST


def matmul(left_side, right_side):
    return jnp.dot(left_side, right_side, preferred_element_type=jnp.float32)


def left_contract(left_side, right_side):
    return lax.dot_general(
        left_side, right_side, (((0,), (0,)), ((), ())), preferred_element_type=jnp.float32
    )


def right_contract(left_side, right_side):
    return lax.dot_general(
        left_side, right_side, (((1,), (1,)), ((), ())), preferred_element_type=jnp.float32
    )


def to_low(values):
    return values.astype(jnp.bfloat16)


def rms_norm(values, gain_vec):
    scale = lax.rsqrt(jnp.mean(values * values, axis=-1, keepdims=True) + EPSILON)
    return values * scale * gain_vec


def swiglu(joined):
    half_width = joined.shape[-1] // 2
    return jax.nn.silu(joined[..., :half_width]) * joined[..., half_width:]


def gated_norm(values, gates_in, gain_vec):
    return rms_norm(values * jax.nn.silu(gates_in), gain_vec)


def sequence_ids(seq_lengths, row_count):
    seq_ends = jnp.cumsum(seq_lengths)
    places = jnp.arange(row_count, dtype=jnp.int32)
    return jnp.sum((places[:, None] >= seq_ends[None, :]).astype(jnp.int32), axis=1)


def causal_conv(inputs, weight_rows, bias_rows, seq_index):
    tap_count = weight_rows.shape[1]
    result = inputs * weight_rows[:, tap_count - 1] + bias_rows
    for offset in range(1, tap_count):
        shifted = jnp.concatenate(
            [jnp.zeros((offset, inputs.shape[1]), inputs.dtype), inputs[:-offset]], axis=0
        )
        before = jnp.concatenate([jnp.full((offset,), -1, jnp.int32), seq_index[:-offset]], axis=0)
        result = (
            result
            + jnp.where((before == seq_index)[:, None], shifted, 0.0)
            * weight_rows[:, tap_count - 1 - offset]
        )
    return result


def stretch_step(carried_in, block_data):
    state_now, last_id = carried_in
    xblock, dtblock, logblock, bblock, cblock, idblock = block_data
    block_len = idblock.shape[0]
    cumulative = jnp.cumsum(logblock, axis=0)
    places = jnp.arange(block_len, dtype=jnp.int32)
    causal = (idblock[:, None] == idblock[None, :]) & (places[:, None] >= places[None, :])
    spread = cumulative[:, None, :] - cumulative[None, :, :]
    decays = jnp.exp(jnp.minimum(spread, 0.0)) * causal[:, :, None].astype(jnp.float32)
    scores = jnp.dot(cblock, bblock.T, precision=HIGHEST, preferred_element_type=jnp.float32)
    weights = decays * scores[:, :, None] * dtblock[None, :, :]
    within = jnp.einsum("ijh,jhp->ihp", weights, xblock, precision=HIGHEST)
    carried = (idblock == last_id).astype(jnp.float32)[:, None] * jnp.exp(cumulative)
    earlier = jnp.einsum("in,hpn->ihp", cblock, state_now, precision=HIGHEST) * carried[:, :, None]
    end_id = idblock[block_len - 1]
    tail_weight = (
        (idblock == end_id).astype(jnp.float32)[:, None]
        * jnp.exp(cumulative[block_len - 1][None, :] - cumulative)
        * dtblock
    )
    keeping = (last_id == end_id).astype(jnp.float32) * jnp.exp(cumulative[block_len - 1])
    added_state = jnp.einsum("jh,jhp,jn->hpn", tail_weight, xblock, bblock, precision=HIGHEST)
    return ((keeping[:, None, None] * state_now + added_state, end_id), within + earlier)


def state_scan(xheads, step_sizes, decay_rate, bvalues, cvalues, seq_index, skip_gain):
    row_count, head_count, head_size = xheads.shape
    block_count = row_count // STRETCH
    log_decay = step_sizes * decay_rate
    inputs = (
        xheads.reshape(block_count, STRETCH, head_count, head_size),
        step_sizes.reshape(block_count, STRETCH, head_count),
        log_decay.reshape(block_count, STRETCH, head_count),
        bvalues.reshape(block_count, STRETCH, -1),
        cvalues.reshape(block_count, STRETCH, -1),
        seq_index.reshape(block_count, STRETCH),
    )
    start_state = (
        jnp.zeros((head_count, head_size, bvalues.shape[1]), xheads.dtype),
        jnp.array(-1, jnp.int32),
    )
    final_state, outputs = lax.scan(jax.checkpoint(stretch_step), start_state, inputs)
    return outputs.reshape(row_count, head_count, head_size) + skip_gain[None, :, None] * xheads


def head_side(
    xs_seq, bc_seq, dtr_seq, conv_part, conv_bias_part, step_part, decay_part, skip_part, seq_index
):
    channels = xs_seq.shape[1]
    head_count = dtr_seq.shape[1]
    state_size = bc_seq.shape[1] // 2
    joined = jnp.concatenate([xs_seq, bc_seq], axis=1)
    activated = jax.nn.silu(causal_conv(joined, conv_part, conv_bias_part, seq_index))
    xheads = activated[:, :channels].reshape(-1, head_count, channels // head_count)
    bvalues = activated[:, channels : channels + state_size]
    cvalues = activated[:, channels + state_size :]
    step_sizes = jax.nn.softplus(dtr_seq + step_part)
    outputs = state_scan(
        xheads, step_sizes, -jnp.exp(decay_part), bvalues, cvalues, seq_index, skip_part
    )
    return outputs.reshape(-1, channels)


def fetch_weights(
    norm_in,
    w_in,
    w_dt,
    conv_w,
    conv_b,
    dt_bias,
    a_log,
    d_skip,
    norm_gate,
    w_out,
    norm_moe,
    w_router,
    w_shared,
    w_shared_down,
    w_experts,
    w_experts_down,
):
    return (
        lax.all_gather(norm_in, "shard", axis=0, tiled=True),
        lax.all_gather(w_in, "shard", axis=0, tiled=True),
        lax.all_gather(w_dt, "shard", axis=0, tiled=True),
        lax.all_gather(conv_w, "shard", axis=0, tiled=True),
        lax.all_gather(conv_b, "shard", axis=0, tiled=True),
        lax.all_gather(dt_bias, "shard", axis=0, tiled=True),
        lax.all_gather(a_log, "shard", axis=0, tiled=True),
        lax.all_gather(d_skip, "shard", axis=0, tiled=True),
        lax.all_gather(norm_gate, "shard", axis=0, tiled=True),
        lax.all_gather(w_out, "shard", axis=0, tiled=True),
        lax.all_gather(norm_moe, "shard", axis=0, tiled=True),
        lax.all_gather(w_router, "shard", axis=0, tiled=True),
        lax.all_gather(w_shared, "shard", axis=0, tiled=True),
        lax.all_gather(w_shared_down, "shard", axis=0, tiled=True),
        lax.all_gather(w_experts, "shard", axis=1, tiled=True),
        lax.all_gather(w_experts_down, "shard", axis=1, tiled=True),
    )


def local(
    tokens,
    out_grad,
    deal_order,
    lengths,
    routes,
    norm_in,
    w_in,
    w_dt,
    conv_w,
    conv_b,
    dt_bias,
    a_log,
    d_skip,
    norm_gate,
    w_out,
    norm_moe,
    w_router,
    w_shared,
    w_shared_down,
    w_experts,
    w_experts_down,
):
    shards = (
        norm_in,
        w_in,
        w_dt,
        conv_w,
        conv_b,
        dt_bias,
        a_log,
        d_skip,
        norm_gate,
        w_out,
        norm_moe,
        w_router,
        w_shared,
        w_shared_down,
        w_experts,
        w_experts_down,
    )
    gathered = fetch_weights(*shards)
    (
        gain_in,
        proj_in,
        proj_dt,
        conv_weight,
        conv_bias,
        step_bias,
        decay_log,
        skip_gain,
        gain_gate,
        proj_out,
        gain_moe,
        router,
        shared_up,
        shared_down,
        expert_up,
        expert_down,
    ) = gathered
    residual = tokens[0].astype(jnp.float32)
    tok_rows, model_width = residual.shape
    seq_devices = lax.axis_size("seq")
    head_group = lax.axis_index("seq")
    inner_width = proj_out.shape[0]
    head_total = proj_dt.shape[1]
    group_heads = head_total // seq_devices
    group_width = inner_width // seq_devices
    normed_in, norm_in_pull = jax.vjp(rms_norm, residual, gain_in.astype(jnp.float32))
    hidden = to_low(normed_in)
    projected = matmul(hidden, proj_in)
    gate_in = projected[:, :inner_width]
    xs_low = to_low(projected[:, inner_width : 2 * inner_width])
    bc_low = to_low(projected[:, 2 * inner_width :])
    dtr_low = to_low(matmul(hidden, proj_dt))
    xs_heads, dtr_heads = (
        lax.all_to_all(xs_low, "seq", split_axis=1, concat_axis=0, tiled=True),
        lax.all_to_all(dtr_low, "seq", split_axis=1, concat_axis=0, tiled=True),
    )
    bc_group = lax.all_gather(bc_low, "seq", axis=0, tiled=True)
    group_rows = bc_group.shape[0]
    deal_rows = deal_order[0]
    inverse = (
        jnp.zeros((group_rows,), jnp.int32)
        .at[deal_rows]
        .set(jnp.arange(group_rows, dtype=jnp.int32))
    )
    seq_index = sequence_ids(lengths[0], group_rows)
    conv_rows = jnp.concatenate(
        [
            lax.dynamic_slice_in_dim(conv_weight, head_group * group_width, group_width, 0),
            conv_weight[inner_width:],
        ],
        axis=0,
    ).astype(jnp.float32)
    bias_rows = jnp.concatenate(
        [
            lax.dynamic_slice_in_dim(conv_bias, head_group * group_width, group_width, 0),
            conv_bias[inner_width:],
        ],
        axis=0,
    ).astype(jnp.float32)
    step_part = lax.dynamic_slice_in_dim(
        step_bias, head_group * group_heads, group_heads, 0
    ).astype(jnp.float32)
    decay_part = lax.dynamic_slice_in_dim(
        decay_log, head_group * group_heads, group_heads, 0
    ).astype(jnp.float32)
    skip_part = lax.dynamic_slice_in_dim(
        skip_gain, head_group * group_heads, group_heads, 0
    ).astype(jnp.float32)

    def heads_forward(
        xs_seq, bc_seq, dtr_seq, conv_part, conv_bias_part, step_piece, decay_piece, skip_piece
    ):
        return head_side(
            xs_seq,
            bc_seq,
            dtr_seq,
            conv_part,
            conv_bias_part,
            step_piece,
            decay_piece,
            skip_piece,
            seq_index,
        )

    head_out, heads_pull = jax.vjp(
        heads_forward,
        xs_heads[inverse].astype(jnp.float32),
        bc_group[inverse].astype(jnp.float32),
        dtr_heads[inverse].astype(jnp.float32),
        conv_rows,
        bias_rows,
        step_part,
        decay_part,
        skip_part,
    )
    mixed_back = lax.all_to_all(
        to_low(head_out[deal_rows]), "seq", split_axis=0, concat_axis=1, tiled=True
    )
    normed_full, gated_pull = jax.vjp(
        gated_norm, mixed_back.astype(jnp.float32), gate_in, gain_gate.astype(jnp.float32)
    )
    normed = to_low(normed_full)
    after_mix = residual + matmul(normed, proj_out)
    moe_full, moe_norm_pull = jax.vjp(rms_norm, after_mix, gain_moe.astype(jnp.float32))
    moe_in = to_low(moe_full)
    logits = matmul(moe_in, router)
    route_ids = routes[0]
    expert_total = router.shape[1]
    top_count = route_ids.shape[1]
    chosen = route_ids[:, :, None] == jnp.arange(expert_total, dtype=jnp.int32)[None, None, :]

    def gate_softmax(logit_rows):
        picked_logits = jnp.sum(jnp.where(chosen, logit_rows[:, None, :], 0.0), axis=2)
        return jax.nn.softmax(picked_logits, axis=1)

    gate_values, gates_pull = jax.vjp(gate_softmax, logits)
    shared_gu = matmul(moe_in, shared_up)
    shared_full, shared_pull = jax.vjp(swiglu, shared_gu)
    shared_act = to_low(shared_full)
    shared_res = matmul(shared_act, shared_down)
    flat_routes = route_ids.reshape(-1)
    assigned = tok_rows * top_count
    capacity = min(tok_rows, max(2, assigned * 5 // (expert_total * 3)))
    onehot = (flat_routes[:, None] == jnp.arange(expert_total, dtype=jnp.int32)[None, :]).astype(
        jnp.int32
    )
    slot_ranks = jnp.sum((jnp.cumsum(onehot, axis=0) - onehot) * onehot, axis=1)
    slot_index = flat_routes * capacity + slot_ranks
    sources = (
        jnp.full((expert_total * capacity,), assigned, jnp.int32)
        .at[slot_index]
        .set(jnp.arange(assigned, dtype=jnp.int32))
    )
    padded = jnp.concatenate([moe_in, jnp.zeros((1, model_width), jnp.bfloat16)], axis=0)
    local_experts = expert_up.shape[0]
    outgoing = padded[sources // top_count].reshape(
        seq_devices, local_experts, capacity, model_width
    )
    incoming = lax.all_to_all(outgoing, "seq", split_axis=0, concat_axis=0, tiled=True)
    expert_gu = jnp.einsum(
        "secd,edf->secf", incoming, expert_up, preferred_element_type=jnp.float32
    )
    expert_full, expert_pull = jax.vjp(swiglu, expert_gu)
    expert_act = to_low(expert_full)
    expert_res = to_low(
        jnp.einsum("secf,efd->secd", expert_act, expert_down, preferred_element_type=jnp.float32)
    )
    returned = lax.all_to_all(expert_res, "seq", split_axis=0, concat_axis=0, tiled=True).reshape(
        expert_total * capacity, model_width
    )
    picked = returned[slot_index].reshape(tok_rows, top_count, model_width)
    routed = jnp.sum(gate_values[:, :, None] * picked, axis=1)
    layer_out = after_mix + routed + shared_res
    gathered_back = fetch_weights(*shards)
    back_proj_in = gathered_back[1]
    back_proj_dt = gathered_back[2]
    back_proj_out = gathered_back[9]
    back_router = gathered_back[11]
    back_shared_up = gathered_back[12]
    back_shared_down = gathered_back[13]
    back_expert_up = gathered_back[14]
    back_expert_down = gathered_back[15]
    cotangent = out_grad[0]
    grad_out = cotangent.astype(jnp.float32)
    weighted = to_low(gate_values[:, :, None] * grad_out[:, None, :]).reshape(assigned, model_width)
    gate_grad = jnp.sum(picked * grad_out[:, None, :], axis=2)
    weighted_pad = jnp.concatenate([weighted, jnp.zeros((1, model_width), jnp.bfloat16)], axis=0)
    grad_send = weighted_pad[sources].reshape(seq_devices, local_experts, capacity, model_width)
    grad_in = lax.all_to_all(grad_send, "seq", split_axis=0, concat_axis=0, tiled=True)
    act_grad = jnp.einsum(
        "secd,efd->secf", grad_in, back_expert_down, preferred_element_type=jnp.float32
    )
    down_grad = jnp.einsum(
        "secf,secd->efd", expert_act, grad_in, preferred_element_type=jnp.float32
    )
    gu_grad = to_low(expert_pull(act_grad)[0])
    up_grad = jnp.einsum("secd,secf->edf", incoming, gu_grad, preferred_element_type=jnp.float32)
    rows_grad = to_low(
        jnp.einsum("secf,edf->secd", gu_grad, back_expert_up, preferred_element_type=jnp.float32)
    )
    rows_back = lax.all_to_all(rows_grad, "seq", split_axis=0, concat_axis=0, tiled=True).reshape(
        expert_total * capacity, model_width
    )
    up_part, down_part = (
        lax.psum_scatter(
            up_grad.astype(jnp.bfloat16), "shard", scatter_dimension=1, tiled=True
        ).astype(jnp.float32),
        lax.psum_scatter(
            down_grad.astype(jnp.bfloat16), "shard", scatter_dimension=1, tiled=True
        ).astype(jnp.float32),
    )
    moe_grad = jnp.sum(
        rows_back[slot_index].reshape(tok_rows, top_count, model_width), axis=1, dtype=jnp.float32
    )
    logit_grad = to_low(gates_pull(gate_grad)[0])
    router_grad = left_contract(moe_in, logit_grad)
    shared_down_grad = left_contract(shared_act, cotangent)
    shared_act_grad = right_contract(cotangent, back_shared_down)
    shared_gu_grad = to_low(shared_pull(shared_act_grad)[0])
    shared_up_grad = left_contract(moe_in, shared_gu_grad)
    moe_grad = (
        moe_grad
        + right_contract(logit_grad, back_router)
        + right_contract(shared_gu_grad, back_shared_up)
    )
    mix_norm_grad, gain_moe_grad = moe_norm_pull(moe_grad)
    mix_grad = grad_out + mix_norm_grad
    mix_low = to_low(mix_grad)
    proj_out_grad = left_contract(normed, mix_low)
    normed_grad = right_contract(mix_low, back_proj_out)
    mixed_grad, gate_in_grad, gain_gate_grad = gated_pull(normed_grad)
    heads_grad = lax.all_to_all(to_low(mixed_grad), "seq", split_axis=1, concat_axis=0, tiled=True)
    (
        xs_seq_grad,
        bc_seq_grad,
        dtr_seq_grad,
        conv_rows_grad,
        bias_rows_grad,
        step_part_grad,
        decay_part_grad,
        skip_part_grad,
    ) = heads_pull(heads_grad[inverse].astype(jnp.float32))
    xs_tok_grad, dtr_tok_grad = (
        lax.all_to_all(
            to_low(xs_seq_grad[deal_rows]), "seq", split_axis=0, concat_axis=1, tiled=True
        ),
        lax.all_to_all(
            to_low(dtr_seq_grad[deal_rows]), "seq", split_axis=0, concat_axis=1, tiled=True
        ),
    )
    bc_tok_grad = to_low(
        lax.psum_scatter(
            to_low(bc_seq_grad[deal_rows]).astype(jnp.float32).astype(jnp.bfloat16),
            "seq",
            scatter_dimension=0,
            tiled=True,
        ).astype(jnp.float32)
    )
    proj_grad = jnp.concatenate([to_low(gate_in_grad), xs_tok_grad, bc_tok_grad], axis=1)
    proj_in_grad = left_contract(hidden, proj_grad)
    proj_dt_grad = left_contract(hidden, dtr_tok_grad)
    hidden_grad = right_contract(proj_grad, back_proj_in) + right_contract(
        dtr_tok_grad, back_proj_dt
    )
    residual_grad, gain_in_grad = norm_in_pull(hidden_grad)
    tokens_grad = to_low(mix_grad + residual_grad)
    tap_count = conv_rows.shape[1]
    conv_full = jnp.concatenate(
        [
            lax.dynamic_update_slice_in_dim(
                jnp.zeros((inner_width, tap_count), jnp.float32),
                conv_rows_grad[:group_width],
                head_group * group_width,
                0,
            ),
            conv_rows_grad[group_width:],
        ],
        axis=0,
    )
    bias_full = jnp.concatenate(
        [
            lax.dynamic_update_slice_in_dim(
                jnp.zeros((inner_width,), jnp.float32),
                bias_rows_grad[:group_width],
                head_group * group_width,
                0,
            ),
            bias_rows_grad[group_width:],
        ],
        axis=0,
    )
    step_full = lax.dynamic_update_slice_in_dim(
        jnp.zeros((head_total,), jnp.float32), step_part_grad, head_group * group_heads, 0
    )
    decay_full = lax.dynamic_update_slice_in_dim(
        jnp.zeros((head_total,), jnp.float32), decay_part_grad, head_group * group_heads, 0
    )
    skip_full = lax.dynamic_update_slice_in_dim(
        jnp.zeros((head_total,), jnp.float32), skip_part_grad, head_group * group_heads, 0
    )
    (
        part_gain_in,
        part_proj_in,
        part_proj_dt,
        part_conv,
        part_bias,
        part_step,
        part_decay,
        part_skip,
        part_gate,
        part_proj_out,
        part_gain_moe,
        part_router,
        part_shared_up,
        part_shared_down,
    ) = (
        lax.psum_scatter(
            gain_in_grad.astype(jnp.bfloat16), "shard", scatter_dimension=0, tiled=True
        ).astype(jnp.float32),
        lax.psum_scatter(
            proj_in_grad.astype(jnp.bfloat16), "shard", scatter_dimension=0, tiled=True
        ).astype(jnp.float32),
        lax.psum_scatter(
            proj_dt_grad.astype(jnp.bfloat16), "shard", scatter_dimension=0, tiled=True
        ).astype(jnp.float32),
        lax.psum_scatter(
            conv_full.astype(jnp.bfloat16), "shard", scatter_dimension=0, tiled=True
        ).astype(jnp.float32),
        lax.psum_scatter(
            bias_full.astype(jnp.bfloat16), "shard", scatter_dimension=0, tiled=True
        ).astype(jnp.float32),
        lax.psum_scatter(
            step_full.astype(jnp.bfloat16), "shard", scatter_dimension=0, tiled=True
        ).astype(jnp.float32),
        lax.psum_scatter(
            decay_full.astype(jnp.bfloat16), "shard", scatter_dimension=0, tiled=True
        ).astype(jnp.float32),
        lax.psum_scatter(
            skip_full.astype(jnp.bfloat16), "shard", scatter_dimension=0, tiled=True
        ).astype(jnp.float32),
        lax.psum_scatter(
            gain_gate_grad.astype(jnp.bfloat16), "shard", scatter_dimension=0, tiled=True
        ).astype(jnp.float32),
        lax.psum_scatter(
            proj_out_grad.astype(jnp.bfloat16), "shard", scatter_dimension=0, tiled=True
        ).astype(jnp.float32),
        lax.psum_scatter(
            gain_moe_grad.astype(jnp.bfloat16), "shard", scatter_dimension=0, tiled=True
        ).astype(jnp.float32),
        lax.psum_scatter(
            router_grad.astype(jnp.bfloat16), "shard", scatter_dimension=0, tiled=True
        ).astype(jnp.float32),
        lax.psum_scatter(
            shared_up_grad.astype(jnp.bfloat16), "shard", scatter_dimension=0, tiled=True
        ).astype(jnp.float32),
        lax.psum_scatter(
            shared_down_grad.astype(jnp.bfloat16), "shard", scatter_dimension=0, tiled=True
        ).astype(jnp.float32),
    )
    summed = (
        lax.psum(part_gain_in.astype(jnp.bfloat16), "seq").astype(jnp.float32),
        lax.psum(part_proj_in.astype(jnp.bfloat16), "seq").astype(jnp.float32),
        lax.psum(part_proj_dt.astype(jnp.bfloat16), "seq").astype(jnp.float32),
        lax.psum(part_conv.astype(jnp.bfloat16), "seq").astype(jnp.float32),
        lax.psum(part_bias.astype(jnp.bfloat16), "seq").astype(jnp.float32),
        lax.psum(part_step.astype(jnp.bfloat16), "seq").astype(jnp.float32),
        lax.psum(part_decay.astype(jnp.bfloat16), "seq").astype(jnp.float32),
        lax.psum(part_skip.astype(jnp.bfloat16), "seq").astype(jnp.float32),
        lax.psum(part_gate.astype(jnp.bfloat16), "seq").astype(jnp.float32),
        lax.psum(part_proj_out.astype(jnp.bfloat16), "seq").astype(jnp.float32),
        lax.psum(part_gain_moe.astype(jnp.bfloat16), "seq").astype(jnp.float32),
        lax.psum(part_router.astype(jnp.bfloat16), "seq").astype(jnp.float32),
        lax.psum(part_shared_up.astype(jnp.bfloat16), "seq").astype(jnp.float32),
        lax.psum(part_shared_down.astype(jnp.bfloat16), "seq").astype(jnp.float32),
    )
    return (
        to_low(layer_out)[None],
        tokens_grad[None],
        summed[0],
        summed[1],
        summed[2],
        summed[3],
        summed[4],
        summed[5],
        summed[6],
        summed[7],
        summed[8],
        summed[9],
        summed[10],
        summed[11],
        summed[12],
        summed[13],
        up_part,
        down_part,
    )


def solution(mesh):
    placed = (
        P("shard", "seq", None),
        P("shard", "seq", None),
        P("shard", None),
        P("shard", None),
        P("shard", "seq", None),
        P("shard"),
        P("shard", None),
        P("shard", None),
        P("shard", None),
        P("shard"),
        P("shard"),
        P("shard"),
        P("shard"),
        P("shard"),
        P("shard", None),
        P("shard"),
        P("shard", None),
        P("shard", None),
        P("shard", None),
        P("seq", "shard", None),
        P("seq", "shard", None),
    )
    return jax.shard_map(
        local,
        mesh=mesh,
        in_specs=placed,
        out_specs=(
            P("shard", "seq", None),
            P("shard", "seq", None),
            P("shard"),
            P("shard", None),
            P("shard", None),
            P("shard", None),
            P("shard"),
            P("shard"),
            P("shard"),
            P("shard"),
            P("shard"),
            P("shard", None),
            P("shard"),
            P("shard", None),
            P("shard", None),
            P("shard", None),
            P("seq", "shard", None),
            P("seq", "shard", None),
        ),
        check_vma=False,
    )
```

profile of v0, /device:TPU:0, one launch (start us, length us, event | category | flops | bytes accessed | tf_op | source)
XLA Modules:
  0.0 3392.0 jit_solution(13053334283351141452)
XLA Ops:
  45.1 32.4 all-gather.1
  96.9 42.3 %all-gather.2 = bf16[4,1,768]{2,1,0:T(2,128)(2,1)S(1)} all-gather(bf16[1,1,768]{2,1,0:T(2,128)(2,1)S(1)} %reshape.873), channel_id=1, replica_groups=mesh['seq'=8,'shard'=4] {'shard'}, dimensions={0}, use_global_device_ids=true | all-gather | bytes 7680 | tf_op jit(solution)/shard_map/all_gather | solution.py:159
  139.2 25.1 all-gather.3
  164.7 185.5 %all-gather.11.cloned.1.call-done = bf16[1536,6400]{1,0:T(8,128)(2,1)} async-done(((bf16[384,6400]{1,0:T(8,128)(2,1)}), bf16[1536,6400]{1,0:T(8,128)(2,1)}) %all-gather.11.cloned.1.call-update) | async-done | bytes 19660816 | tf_op jit(solution)/shard_map/all_gather | solution.py:152
  422.7 100.9 %while.44 = (s32[]{:T(128)}, f32[6,64,128]{2,1,0:T(8,128)S(1)}, s32[]{:T(128)}, f32[6,256,6,64]{1,3,2,0:T(8,128)}, f32[6,6,64,128]{3,2,1,0:T(8,128)}, /*index=5*...) while((s32[]{:T(128)}, f32[6,64,128]{2,1,0:T(8,128)S(1)}, ...), condition=%wide.region_7.8_spmd.clone, body=%wide.region_4.7_spmd.clone.sunk | while | flops 707615744 | bytes 4666793 | solution.py:110
  548.7 18.1 reduce-window.73
  630.1 17.5 all_gather.71
  692.7 252.5 %all-gather.15.cloned.1.call-done = bf16[8,1536,1024]{2,1,0:T(8,128)(2,1)} async-done(((bf16[8,384,1024]{2,1,0:T(8,128)(2,1)}), bf16[8,1536,1024]{2,1,0:T(8,128)(2,1)}) %all-gather.15.cloned.1.call-update) | async-done | bytes 25165840 | tf_op jit(solution)/shard_map/all_gather | solution.py:165
  945.1 23.0 fusion.125
  968.1 194.9 %all-gather.17.cloned.1.call-done = bf16[8,512,1536]{2,1,0:T(8,128)(2,1)} async-done(((bf16[8,128,1536]{2,1,0:T(8,128)(2,1)}), bf16[8,512,1536]{2,1,0:T(8,128)(2,1)}) %all-gather.17.cloned.1.call-update) | async-done | bytes 12582928 | tf_op jit(solution)/shard_map/all_gather | solution.py:166
  1225.5 40.8 %all-to-all-done.4 = bf16[8,8,30,1536]{3,1,2,0:T(8,128)(2,1)} async-done(((bf16[8,8,30,1536]{3,1,2,0:T(8,128)(2,1)}), bf16[8,8,30,1536]{3,1,2,0:T(8,128)(2,1)}, u32[]{:S(2)}, u32[]{:S(2)}) %all-to-all-start.4) | async-done | bytes 5898272 | tf_op jit(solution)/shard_map/all_to_all | solution.py:360
  1283.3 57.9 %all-gather.21.cloned.1.call-done = bf16[1024,1536]{1,0:T(8,128)(2,1)} async-done(((bf16[256,1536]{1,0:T(8,128)(2,1)}), bf16[1024,1536]{1,0:T(8,128)(2,1)}) %all-gather.21.cloned.1.call-update) | async-done | bytes 3145744 | tf_op jit(solution)/shard_map/all_gather | solution.py:164
  1493.1 228.7 %while.45 = (s32[]{:T(128)}, f32[6,64,128]{2,1,0:T(8,128)}, f32[6,256,6,64]{1,3,2,0:T(8,128)}, f32[6,256,6]{1,2,0:T(8,128)}, f32[6,256,6]{1,2,0:T(8,128)}, /*ind...) while((s32[]{:T(128)}, f32[6,64,128]{2,1,0:T(8,128)}, ...), condition=%wide.region_36.37_spmd.clone, body=%wide.region_24.36_spmd.clone.sunk | while | flops 1672199168 | bytes 15275845 | solution.py:110
  1802.4 20.4 all_to_all.119
  1841.6 17.7 reduce-scatter.31.cloned.1.call-done
  1873.4 17.4 all-reduce.36
  1908.5 19.0 bitcast_convert_fusion
  1927.8 107.7 %reduce-scatter.23.cloned.1.call-done = bf16[384,2048]{1,0:T(8,128)(2,1)} async-done(((bf16[1536,2048]{1,0:T(8,128)(2,1)}), bf16[384,2048]{1,0:T(8,128)(2,1)}) %reduce-scatter.23.cloned.1.call-update) | async-done | bytes 1572880 | tf_op jit(solution)/shard_map/reduce_scatter | solution.py:545
  2035.5 164.9 %reduce-scatter.21.cloned.1.call-done = bf16[768,1536]{1,0:T(8,128)(2,1)} async-done(((bf16[3072,1536]{1,0:T(8,128)(2,1)}), bf16[768,1536]{1,0:T(8,128)(2,1)}) %reduce-scatter.21.cloned.1.call-update) | async-done | bytes 2359312 | tf_op jit(solution)/shard_map/reduce_scatter | solution.py:536
  2200.4 329.5 %reduce-scatter.19.cloned.1.call-done = bf16[384,6400]{1,0:T(8,128)(2,1)} async-done(((bf16[1536,6400]{1,0:T(8,128)(2,1)}), bf16[384,6400]{1,0:T(8,128)(2,1)}) %reduce-scatter.19.cloned.1.call-update) | async-done | bytes 4915216 | tf_op jit(solution)/shard_map/reduce_scatter | solution.py:512
  2536.4 54.8 %all-reduce.41.cloned.1.call-done = (bf16[384]{0:T(512)(128)(2,1)}, bf16[384,48]{0,1:T(8,128)(2,1)}, bf16[832,4]{0,1:T(4,128)(2,1)}, bf16[832]{0:T(1024)(128)(2,...) async-done(((bf16[384]{0:T(512)(128)(2,1)}, ...) | async-done | bytes 97496 | tf_op jit(solution)/shard_map/psum | solution.py:553
  2603.8 202.7 %reduce-scatter.29.cloned.1.call-done = bf16[8,128,1536]{2,1,0:T(8,128)(2,1)} async-done(((bf16[8,512,1536]{2,1,0:T(8,128)(2,1)}), bf16[8,128,1536]{2,1,0:T(8,128)(2,1)}) %reduce-scatter.29.cloned.1.call-update) | async-done | bytes 3145744 | tf_op jit(solution)/shard_map/reduce_scatter | solution.py:400
  2812.0 412.4 %reduce-scatter.27.cloned.1.call-done = bf16[8,384,1024]{2,1,0:T(8,128)(2,1)} async-done(((bf16[8,1536,1024]{2,1,0:T(8,128)(2,1)}), bf16[8,384,1024]{2,1,0:T(8,128)(2,1)}) %reduce-scatter.27.cloned.1.call-update) | async-done | bytes 6291472 | tf_op jit(solution)/shard_map/reduce_scatter | solution.py:397
  3233.5 138.2 %all-reduce.43.cloned.1.call-done = (bf16[384,6400]{1,0:T(8,128)(2,1)}, bf16[768,1536]{1,0:T(8,128)(2,1)}, bf16[384,2048]{1,0:T(8,128)(2,1)}, bf16[256,1536]{1,0:T(8,128)(2,1)}) async-done(((bf16[384,6400]{1,0:T(8,128)(2,1)}, bf16[768,1536]{1,0:T(8,128)(2,1)}, bf16[384,2048]{1,0:T(8,128)(2,1)}, bf16[256,1536]{1,0:T(8,128)(2,1)}), (bf16[384,6400]{1,0:T(8,128)(2,1)}, bf16[768,1536]{1,0:T(8,128)(2,1)}, ...) | async-done | bytes 9633808 | tf_op jit(solution)/shard_map/psum | solution.py:554
  (995 shorter events, 980.3 us)
Async XLA Ops:
  7.2 343.0 %all-gather.11.cloned.1.call-start = ((), (), s32[]{:S(2)}) async-start(), calls=%async_computation.20 | async-start | bytes 24576000 | tf_op jit(solution)/shard_map/all_gather | solution.py:152
  7.9 570.3 %all-gather.13.cloned.1.call-start = ((), (), s32[]{:S(2)}) async-start(), calls=%async_computation.21 | async-start | bytes 11796480 | tf_op jit(solution)/shard_map/all_gather | solution.py:160
  8.7 936.4 %all-gather.15.cloned.1.call-start = ((), (), s32[]{:S(2)}) async-start(), calls=%async_computation.22 | async-start | bytes 31457280 | tf_op jit(solution)/shard_map/all_gather | solution.py:165
  38.7 327.1 %all-to-all-start = ((bf16[192,8,6]{0,2,1:T(8,128)(2,1)}), bf16[192,8,6]{0,2,1:T(8,128)(2,1)S(1)}, u32[]{:S(2)}, u32[]{:S(2)}) async-start(bf16[192,8,6]{0,2,1:T(8,128)(2,1)} %all_to_all.86), calls=%async_computation | async-start | bytes 65536 | tf_op jit(solution)/shard_map/all_to_all | solution.py:247
  42.5 1120.5 %all-gather.17.cloned.1.call-start = ((), (), s32[]{:S(2)}) async-start(), calls=%async_computation.23 | async-start | bytes 15728640 | tf_op jit(solution)/shard_map/all_gather | solution.py:166
  365.9 31.5 all-to-all-start.1
  610.8 75.9 %all-to-all-start.3 = ((bf16[8,8,30,1536]{3,1,2,0:T(8,128)(2,1)}), bf16[8,8,30,1536]{3,1,2,0:T(8,128)(2,1)}, u32[]{:S(2)}, u32[]{:S(2)}) async-start(bf16[8,8,30,1536]{3,1,2,0:T(8,128)(2,1)} %copy.403), calls=%async_computation.3 | async-start | bytes 11796480 | tf_op jit(solution)/shard_map/all_to_all | solution.py:351
  686.6 476.3 %all-to-all-start.5 = ((bf16[8,8,30,1536]{3,1,2,0:T(8,128)(2,1)}), bf16[8,8,30,1536]{3,1,2,0:T(8,128)(2,1)}, u32[]{:S(2)}, u32[]{:S(2)}) async-start(bf16[8,8,30,1536]{3,1,2,0:T(8,128)(2,1)} %copy.408), calls=%async_computation.5 | async-start | bytes 11796480 | tf_op jit(solution)/shard_map/all_to_all | solution.py:381
  692.1 585.9 %all-gather.19.cloned.1.call-start = ((), (), s32[]{:S(2)}) async-start(), calls=%async_computation.24 | async-start | bytes 7864320 | tf_op jit(solution)/shard_map/all_gather | solution.py:163
  1194.2 72.1 %all-to-all-start.4 = ((bf16[8,8,30,1536]{3,1,2,0:T(8,128)(2,1)}), bf16[8,8,30,1536]{3,1,2,0:T(8,128)(2,1)}, u32[]{:S(2)}, u32[]{:S(2)}) async-start(bf16[8,8,30,1536]{3,1,2,0:T(8,128)(2,1)} %copy.405), calls=%async_computation.4 | async-start | bytes 11796480 | tf_op jit(solution)/shard_map/all_to_all | solution.py:360
  1198.9 142.2 %all-gather.21.cloned.1.call-start = ((), (), s32[]{:S(2)}) async-start(), calls=%async_computation.25 | async-start | bytes 3932160 | tf_op jit(solution)/shard_map/all_gather | solution.py:164
  1266.3 126.8 %all-to-all-start.6 = ((bf16[8,8,30,1536]{3,1,2,0:T(8,128)(2,1)}), bf16[8,8,30,1536]{3,1,2,0:T(8,128)(2,1)}, u32[]{:S(2)}, u32[]{:S(2)}) async-start(bf16[8,8,30,1536]{3,1,2,0:T(8,128)(2,1)} %copy.410), calls=%async_computation.6 | async-start | bytes 11796480 | tf_op jit(solution)/shard_map/all_to_all | solution.py:393
  1455.6 367.3 %reduce-scatter.17.cloned.1.call-start = ((), (), s32[]{:S(2)}) async-start(), calls=%async_computation.26 | async-start | bytes 884736 | tf_op jit(solution)/shard_map/reduce_scatter | solution.py:444
  1757.0 79.8 %reduce-scatter.35.cloned.1.call-start = ((), (), s32[]{:S(2)}) async-start(), calls=%async_computation.35 | async-start | bytes 491520
  1771.1 68.8 %reduce-scatter.33.cloned.1.call-start = ((), (), s32[]{:S(2)}) async-start(), calls=%async_computation.34 | async-start | bytes 1064960
  1772.6 86.7 %reduce-scatter.31.cloned.1.call-start = ((), (), s32[]{:S(2)}) async-start(), calls=%async_computation.33 | async-start | bytes 491520
  1778.8 148.9 %reduce-scatter.25.cloned.1.call-start = ((), (), s32[]{:S(2)}) async-start(), calls=%async_computation.30 | async-start | bytes 3932160 | tf_op jit(solution)/shard_map/reduce_scatter | solution.py:548
  1781.6 253.9 %reduce-scatter.23.cloned.1.call-start = ((), (), s32[]{:S(2)}) async-start(), calls=%async_computation.29 | async-start | bytes 7864320 | tf_op jit(solution)/shard_map/reduce_scatter | solution.py:545
  1787.5 412.9 %reduce-scatter.21.cloned.1.call-start = ((), (), s32[]{:S(2)}) async-start(), calls=%async_computation.28 | async-start | bytes 11796480 | tf_op jit(solution)/shard_map/reduce_scatter | solution.py:536
  1795.2 734.8 %reduce-scatter.19.cloned.1.call-start = ((), (), s32[]{:S(2)}) async-start(), calls=%async_computation.27 | async-start | bytes 24576000 | tf_op jit(solution)/shard_map/reduce_scatter | solution.py:512
  1834.0 757.2 %all-reduce.41.cloned.1.call-start = ((), (), s32[]{:S(2)}) async-start(), calls=%async_computation.36 | async-start | bytes 201728 | tf_op jit(solution)/shard_map/psum | solution.py:553
  1895.1 911.4 %reduce-scatter.29.cloned.1.call-start = ((), (), s32[]{:S(2)}) async-start(), calls=%async_computation.32 | async-start | bytes 15728640 | tf_op jit(solution)/shard_map/reduce_scatter | solution.py:400
  1908.4 1315.9 %reduce-scatter.27.cloned.1.call-start = ((), (), s32[]{:S(2)}) async-start(), calls=%async_computation.31 | async-start | bytes 31457280 | tf_op jit(solution)/shard_map/reduce_scatter | solution.py:397
  1927.5 1444.1 %all-reduce.43.cloned.1.call-start = ((), (), s32[]{:S(2)}) async-start(), calls=%async_computation.37 | async-start | bytes 19267584 | tf_op jit(solution)/shard_map/psum | solution.py:554
  (140 other events, 4683.1 us)
Sparse Core Ops, SparseCore 0:
  9.6 340.5 all-gather.10
  351.8 165.4 all-gather.12
  518.9 426.2 all-gather.14
  946.5 216.3 all-gather.16
  1164.4 113.5 all-gather.18
  1279.4 61.7 all-gather.20
  1757.1 31.8 reduce-scatter.16
  1791.3 20.6 reduce-scatter.34
  1814.4 22.3 reduce-scatter.32
  1839.5 19.7 reduce-scatter.30
  1862.3 59.5 reduce-scatter.24
  1924.7 110.7 reduce-scatter.22
  2038.6 161.7 reduce-scatter.20
  2202.8 327.1 reduce-scatter.18
  2535.3 55.8 all-reduce.40
  2594.2 212.3 reduce-scatter.28
  2808.9 415.4 reduce-scatter.26
  3228.2 143.3 all-reduce.42
where the time goes:
time: 3410 us; the launch traced here: 3390 us
  waiting for transfers between devices  2190 us (64%)
  local copies, waits for them, and re-layouts  377 us (11%)
  matrix products  308 us (9%)
  other arithmetic  233 us (7%)
  blocking collectives  210 us (6%)
  starting transfers between devices  39.7 us (1%)
    reduce_scatter x1, waiting for transfers between devices, local(): lax.psum_scatter(up_grad.astype(jnp.bfloat16), 'shard', scatter_dimension...  412 us
    reduce_scatter x1, waiting for transfers between devices, local(): lax.psum_scatter(proj_in_grad.astype(jnp.bfloat16), 'shard', scatter_dime...  330 us
    all_gather x1, waiting for transfers between devices, fetch_weights(): lax.all_gather(w_experts, 'shard', axis=1, tiled=True)  252 us
    reduce_scatter x1, waiting for transfers between devices, local(): lax.psum_scatter(down_grad.astype(jnp.bfloat16), 'shard', scatter_dimensi...  203 us
    all_gather x1, waiting for transfers between devices, fetch_weights(): lax.all_gather(w_experts_down, 'shard', axis=1, tiled=True)  195 us
    all_gather x1, waiting for transfers between devices, fetch_weights(): lax.all_gather(w_in, 'shard', axis=0, tiled=True)  185 us
    reduce_scatter x1, waiting for transfers between devices, local(): lax.psum_scatter(proj_out_grad.astype(jnp.bfloat16), 'shard', scatter_dim...  165 us
    psum x1, waiting for transfers between devices, local(): lax.psum(part_proj_in.astype(jnp.bfloat16), 'seq').astype(jnp.float32)  138 us
  transfers between devices with their start and end apart: 27, of which 16 were waited for; matrix products, arithmetic and copies ran while one was open for 16% of the time, Pallas kernels for 0%

commit v1 on v0

v1 whole, which is shorter than its diff:
```python
import functools

import jax
import jax.numpy as jnp
from jax import lax
from jax.experimental import pallas as pl
from jax.experimental.pallas import tpu as pltpu
from jax.sharding import PartitionSpec as P

STRETCH = 256
INNER = 4
EPSILON = 1e-05
HIGHEST = lax.Precision.HIGHEST


def matmul(left_side, right_side):
    return jnp.dot(left_side, right_side, preferred_element_type=jnp.float32)


def left_contract(left_side, right_side):
    return lax.dot_general(
        left_side, right_side, (((0,), (0,)), ((), ())), preferred_element_type=jnp.float32
    )


def right_contract(left_side, right_side):
    return lax.dot_general(
        left_side, right_side, (((1,), (1,)), ((), ())), preferred_element_type=jnp.float32
    )


def to_low(values):
    return values.astype(jnp.bfloat16)


def to_full(values):
    return values.astype(jnp.float32)


def norm_scale(values):
    return lax.rsqrt(jnp.mean(values * values, axis=-1, keepdims=True) + EPSILON)


LANES = 128
VMEM_BYTES = 56 * 1024 * 1024


def dot_rows(left_side, right_side, precision=None):
    return lax.dot_general(
        left_side,
        right_side,
        (((0,), (0,)), ((), ())),
        precision=precision,
        preferred_element_type=jnp.float32,
    )


def dot_lanes(left_side, right_side, precision=None):
    return lax.dot_general(
        left_side,
        right_side,
        (((1,), (1,)), ((), ())),
        precision=precision,
        preferred_element_type=jnp.float32,
    )


def dot_full(left_side, right_side, precision=None):
    return jnp.dot(
        left_side, right_side, precision=precision, preferred_element_type=jnp.float32
    )


def iota_of(shape, axis):
    return lax.broadcasted_iota(jnp.int32, shape, axis)


def ids_at(places, ends_ref):
    total = jnp.zeros(places.shape, jnp.int32)
    for seq in range(ends_ref.shape[0]):
        total = total + (places >= ends_ref[seq]).astype(jnp.int32)
    return total


def id_at(place, ends_ref):
    total = jnp.int32(0)
    for seq in range(ends_ref.shape[0]):
        total = total + (place >= ends_ref[seq]).astype(jnp.int32)
    return total


class Stretch:
    def __init__(self, start, rows, before, conv_ref, head_ref, ends_ref, channels):
        length = rows.shape[0]
        self.channels = channels
        self.heads = channels // 64
        width = conv_ref.shape[1]
        state = (width - channels) // 2
        places = start + iota_of((length, 1), 0)
        self.ids = ids_at(places, ends_ref)
        self.ids_row = ids_at(start + iota_of((1, length), 1), ends_ref)
        inputs = rows[:, :width]
        joined = jnp.concatenate([before[:, :width], inputs], axis=0)
        self.shifted = [inputs]
        value = conv_ref[4:5, :] + inputs * conv_ref[3:4, :]
        for offset in range(1, 4):
            same = (ids_at(places - offset, ends_ref) == self.ids) & (places >= offset)
            moved = pltpu.roll(joined, offset, 0)[8:, :]
            moved = jnp.where(same, moved, 0.0)
            self.shifted.append(moved)
            value = value + moved * conv_ref[3 - offset : 4 - offset, :]
        self.value = value
        self.sig = jax.nn.sigmoid(value)
        act = value * self.sig
        self.x = act[:, :channels]
        self.b = act[:, channels : channels + state]
        self.c = act[:, channels + state :]
        self.b_low = to_low(self.b)
        self.c_low = to_low(self.c)
        self.dt_in = rows[:, width:] + head_ref[0:1, :]
        self.dt = jnp.maximum(self.dt_in, 0.0) + jnp.log1p(jnp.exp(-jnp.abs(self.dt_in)))
        self.rate = head_ref[1:2, :]
        rows_at = iota_of((length, length), 0)
        columns_at = iota_of((length, length), 1)
        lower = (rows_at >= columns_at).astype(jnp.float32)
        self.cum = dot_full(lower, self.dt * self.rate, HIGHEST)
        self.cum_rows = self.cum.T[:8, :]
        self.dt_rows = self.dt.T[:8, :]
        self.causal = (self.ids == self.ids_row) & (rows_at >= columns_at)
        self.scores = dot_lanes(self.c_low, self.b_low)
        last_id = jnp.where(start > 0, id_at(start - 1, ends_ref), -1)
        end_id = id_at(start + length - 1, ends_ref)
        self.enter = jnp.where(self.ids == last_id, jnp.exp(self.cum), 0.0)
        end_cum = self.cum[length - 1 : length, :]
        self.tail = jnp.where(self.ids == end_id, jnp.exp(end_cum - self.cum), 0.0)
        self.tail_weight = self.tail * self.dt
        self.keep = jnp.where(last_id == end_id, jnp.exp(end_cum), 0.0)

    def decay(self, head):
        spread = self.cum[:, head : head + 1] - self.cum_rows[head : head + 1, :]
        return jnp.where(self.causal, jnp.exp(jnp.minimum(spread, 0.0)), 0.0)

    def per_channel(self, by_head):
        return jnp.concatenate(
            [
                jnp.broadcast_to(by_head[:, head : head + 1], (by_head.shape[0], 64))
                for head in range(self.heads)
            ],
            axis=1,
        )

    def state_keep(self):
        return jnp.concatenate(
            [
                jnp.broadcast_to(self.keep[:, head : head + 1], (64, LANES))
                for head in range(self.heads)
            ],
            axis=0,
        )


def head_lanes(channels):
    return (iota_of((channels, LANES), 0) // 64 == iota_of((channels, LANES), 1)).astype(
        jnp.float32
    )


def pick_rows(deal_ref, start, length):
    places = start + iota_of((length, 1), 0)
    return jnp.where(deal_ref[...] == places, 1.0, 0.0).astype(jnp.bfloat16)


def scan_forward_kernel(
    ends_ref, deal_ref, rows_ref, conv_ref, head_ref, y_ref, seq_ref, states_ref, before, state, total
):
    step = pl.program_id(0)
    length = seq_ref.shape[0]
    channels = y_ref.shape[1]
    start = step * length

    @pl.when(step == 0)
    def _():
        before[...] = jnp.zeros_like(before)
        state[...] = jnp.zeros_like(state)
        total[...] = jnp.zeros_like(total)

    picks = pick_rows(deal_ref, start, length)
    rows = dot_full(picks, rows_ref[...])
    seq_ref[...] = to_low(rows)
    part = Stretch(start, rows, before[...], conv_ref, head_ref, ends_ref, channels)
    before[...] = rows[length - 8 :, :]
    state_now = state[...]
    states_ref[0] = state_now
    x_low = to_low(part.x)
    outs = []
    lane = iota_of((length, LANES), 1)
    for pair in range(channels // LANES):
        x_pair = x_low[:, pair * LANES : (pair + 1) * LANES]
        halves = []
        for head in (2 * pair, 2 * pair + 1):
            weights = part.decay(head) * part.scores * part.dt_rows[head : head + 1, :]
            halves.append(dot_full(to_low(weights), x_pair))
        outs.append(jnp.where(lane < 64, halves[0], halves[1]))
    earlier = dot_lanes(part.c_low, to_low(state_now))
    skip = part.per_channel(head_ref[2:3, :])
    y = jnp.concatenate(outs, axis=1) + part.per_channel(part.enter) * earlier + skip * part.x
    state[...] = part.state_keep() * state_now + dot_rows(
        to_low(part.per_channel(part.tail_weight) * part.x), part.b_low
    )
    total[...] += dot_rows(picks, to_low(y))

    @pl.when(step == pl.num_programs(0) - 1)
    def _():
        y_ref[...] = to_low(total[...])


def scan_forward(ends, deal_row, rows, conv_table, head_table, channels):
    group_rows, width = rows.shape
    steps = group_rows // STRETCH
    state_rows = (channels, LANES)
    whole = lambda shape: pl.BlockSpec(shape, lambda step: (0,) * len(shape))
    return pl.pallas_call(
        scan_forward_kernel,
        grid=(steps,),
        in_specs=[
            pl.BlockSpec(memory_space=pltpu.SMEM),
            whole(deal_row.shape),
            whole(rows.shape),
            whole(conv_table.shape),
            whole(head_table.shape),
        ],
        out_specs=[
            whole((group_rows, channels)),
            pl.BlockSpec((STRETCH, width), lambda step: (step, 0)),
            pl.BlockSpec((1,) + state_rows, lambda step: (step, 0, 0)),
        ],
        out_shape=[
            jax.ShapeDtypeStruct((group_rows, channels), jnp.bfloat16),
            jax.ShapeDtypeStruct((group_rows, width), jnp.bfloat16),
            jax.ShapeDtypeStruct((steps,) + state_rows, jnp.float32),
        ],
        scratch_shapes=[
            pltpu.VMEM((8, width), jnp.float32),
            pltpu.VMEM(state_rows, jnp.float32),
            pltpu.VMEM((group_rows, channels), jnp.float32),
        ],
        compiler_params=pltpu.CompilerParams(vmem_limit_bytes=VMEM_BYTES),
        name="scan_forward",
    )(ends, deal_row, rows, conv_table, head_table)


def scan_backward_kernel(
    ends_ref,
    deal_ref,
    seq_ref,
    states_ref,
    dy_ref,
    conv_ref,
    head_ref,
    drows_ref,
    conv_grad_ref,
    head_grad_ref,
    after,
    state_grad,
    total,
):
    order = pl.program_id(0)
    steps = pl.num_programs(0)
    step = steps - 1 - order
    length = STRETCH
    channels = dy_ref.shape[1]
    width = conv_ref.shape[1]
    state_width = (width - channels) // 2
    start = pl.multiple_of(step * length, length)

    @pl.when(order == 0)
    def _():
        after[...] = jnp.zeros_like(after)
        state_grad[...] = jnp.zeros_like(state_grad)
        total[...] = jnp.zeros_like(total)
        conv_grad_ref[...] = jnp.zeros_like(conv_grad_ref)
        head_grad_ref[...] = jnp.zeros_like(head_grad_ref)

    picks = pick_rows(deal_ref, start, length)
    dy = dot_full(picks, dy_ref[...])
    rows = seq_ref[pl.ds(start, length), :].astype(jnp.float32)
    place = pl.multiple_of(jnp.maximum(start - 16, 0), 16)
    before = seq_ref[pl.ds(place, 16), :].astype(jnp.float32)[8:, :]
    part = Stretch(start, rows, before, conv_ref, head_ref, ends_ref, channels)
    state_now = states_ref[0]
    state_low = to_low(state_now)
    next_grad = state_grad[...]
    next_low = to_low(next_grad)
    lanes_of = head_lanes(channels)
    x_low = to_low(part.x)
    dy_low = to_low(dy)
    lane = iota_of((length, LANES), 1)

    enter = part.per_channel(part.enter)
    tail_weight = part.per_channel(part.tail_weight)
    earlier = dot_lanes(part.c_low, state_low)
    enter_grad = dot_full(dy * earlier, lanes_of, HIGHEST)
    entered = to_low(enter * dy)
    c_grad = dot_full(entered, state_low)
    state_grad[...] = part.state_keep() * next_grad + dot_rows(entered, part.c_low)
    onward = dot_lanes(part.b_low, next_low)
    x_grad = part.per_channel(head_ref[2:3, :]) * dy + tail_weight * onward
    tail_grad = dot_full(part.x * onward, lanes_of, HIGHEST)
    b_grad = dot_full(to_low(tail_weight * part.x), next_low)
    tail_part = tail_grad * part.tail_weight
    cum_grad = enter_grad * part.enter - tail_part
    dt_grad = tail_grad * part.tail
    kept = dot_lanes(jnp.ones((8, LANES), jnp.float32), next_grad * state_now, HIGHEST)
    keep_grad = dot_full(kept, lanes_of, HIGHEST)[:1, :]
    end_grad = jnp.sum(tail_part, axis=0, keepdims=True) + keep_grad * part.keep

    score_grad = jnp.zeros((length, length), jnp.float32)
    cum_columns, cum_rows, dt_rows, outs = [], [], [], []
    for pair in range(channels // LANES):
        x_pair = x_low[:, pair * LANES : (pair + 1) * LANES]
        dy_pair = dy_low[:, pair * LANES : (pair + 1) * LANES]
        halves = []
        for half, head in enumerate((2 * pair, 2 * pair + 1)):
            mine = (lane < 64) if half == 0 else (lane >= 64)
            weight_grad = dot_lanes(jnp.where(mine, dy_pair, jnp.zeros_like(dy_pair)), x_pair)
            decay = part.decay(head)
            dt_row = part.dt_rows[head : head + 1, :]
            by_decay = weight_grad * decay
            by_dt = by_decay * part.scores
            by_spread = by_dt * dt_row
            dt_rows.append(jnp.sum(by_dt, axis=0, keepdims=True))
            cum_rows.append(jnp.sum(by_spread, axis=0, keepdims=True))
            cum_columns.append(jnp.sum(by_spread, axis=1, keepdims=True))
            score_grad = score_grad + by_decay * dt_row
            halves.append(dot_rows(to_low(decay * part.scores * dt_row), dy_pair))
        outs.append(jnp.where(lane < 64, halves[0], halves[1]))
    x_grad = x_grad + jnp.concatenate(outs, axis=1)
    score_low = to_low(score_grad)
    c_grad = c_grad + dot_full(score_low, part.b_low)
    b_grad = b_grad + dot_rows(score_low, part.c_low)

    heads = len(dt_rows)
    blank = jnp.zeros((LANES - heads, length), jnp.float32)
    dt_grad = dt_grad + jnp.concatenate(dt_rows + [blank], axis=0).T
    cum_grad = cum_grad - jnp.concatenate(cum_rows + [blank], axis=0).T
    for head in range(heads):
        cum_grad = cum_grad + jnp.where(lane == head, cum_columns[head], 0.0)
    at_end = iota_of((length, 1), 0) == length - 1
    cum_grad = cum_grad + jnp.where(at_end, end_grad, 0.0)
    upper = (iota_of((length, length), 1) >= iota_of((length, length), 0)).astype(jnp.float32)
    log_grad = dot_full(upper, cum_grad, HIGHEST)
    dt_grad = dt_grad + log_grad * part.rate
    dt_in_grad = dt_grad * jax.nn.sigmoid(part.dt_in)
    dt_in_grad = jnp.where(lane < heads, dt_in_grad, 0.0)
    head_grad_ref[0:1, :] += jnp.sum(dt_in_grad, axis=0, keepdims=True)
    head_grad_ref[1:2, :] += jnp.sum(log_grad * part.dt, axis=0, keepdims=True) * part.rate
    skip_sum = jnp.broadcast_to(jnp.sum(dy * part.x, axis=0, keepdims=True), (8, channels))
    head_grad_ref[2:3, :] += dot_full(skip_sum, lanes_of, HIGHEST)[:1, :]

    act_grad = jnp.concatenate([x_grad, b_grad, c_grad], axis=1)
    value_grad = act_grad * part.sig * (1.0 + part.value * (1.0 - part.sig))
    conv_grad_ref[4:5, :] += jnp.sum(value_grad, axis=0, keepdims=True)
    for offset in range(4):
        conv_grad_ref[3 - offset : 4 - offset, :] += jnp.sum(
            value_grad * part.shifted[offset], axis=0, keepdims=True
        )
    joined = jnp.concatenate([value_grad, after[...]], axis=0)
    places = start + iota_of((length, 1), 0)
    rows_grad = value_grad * conv_ref[3:4, :]
    for offset in range(1, 4):
        moved = pltpu.roll(joined, length + 8 - offset, 0)[:length, :]
        same = (ids_at(places + offset, ends_ref) == part.ids) & (
            places + offset < steps * length
        )
        rows_grad = rows_grad + jnp.where(same, moved, 0.0) * conv_ref[3 - offset : 4 - offset, :]
    after[...] = value_grad[:8, :]
    total[...] += dot_rows(picks, to_low(jnp.concatenate([rows_grad, dt_in_grad], axis=1)))

    @pl.when(order == steps - 1)
    def _():
        drows_ref[...] = to_low(total[...])


def scan_backward(ends, deal_row, seq_rows, states, dy, conv_table, head_table):
    group_rows, width = seq_rows.shape
    channels = dy.shape[1]
    steps = group_rows // STRETCH
    whole = lambda shape: pl.BlockSpec(shape, lambda step: (0,) * len(shape))
    return pl.pallas_call(
        scan_backward_kernel,
        grid=(steps,),
        in_specs=[
            pl.BlockSpec(memory_space=pltpu.SMEM),
            whole(deal_row.shape),
            whole(seq_rows.shape),
            pl.BlockSpec((1, channels, LANES), lambda step: (steps - 1 - step, 0, 0)),
            whole(dy.shape),
            whole(conv_table.shape),
            whole(head_table.shape),
        ],
        out_specs=[
            whole((group_rows, width)),
            whole(conv_table.shape),
            whole(head_table.shape),
        ],
        out_shape=[
            jax.ShapeDtypeStruct((group_rows, width), jnp.bfloat16),
            jax.ShapeDtypeStruct(conv_table.shape, jnp.float32),
            jax.ShapeDtypeStruct(head_table.shape, jnp.float32),
        ],
        scratch_shapes=[
            pltpu.VMEM((8, conv_table.shape[1]), jnp.float32),
            pltpu.VMEM((channels, LANES), jnp.float32),
            pltpu.VMEM((group_rows, width), jnp.float32),
        ],
        compiler_params=pltpu.CompilerParams(vmem_limit_bytes=VMEM_BYTES),
        name="scan_backward",
    )(ends, deal_row, seq_rows, states, dy, conv_table, head_table)


MESH = pl.DeviceIdType.MESH
FLIPS = (1, 2, 4)


def flipped(place, flip):
    result = place
    for bit in FLIPS:
        if flip & bit:
            result = result + bit - 2 * bit * lax.rem(lax.div(place, bit), 2)
    return result


def own_shard_group(inner):
    shard = lax.axis_index("shard")
    place = lax.rem(shard, inner)
    return place, shard - place


def peers_in_order(place, inner):
    if inner == 1:
        return []
    if inner == 4:
        half = lax.div(place, 2)
        return [flipped(place, 1), 2 - half, 3 - 3 * half]
    return [lax.rem(place + shift, inner) for shift in range(1, inner)]


def greet(inner):
    barrier = pltpu.get_barrier_semaphore()
    part = lax.axis_index("seq")
    place, first = own_shard_group(inner)
    for flip in FLIPS:
        pl.semaphore_signal(
            barrier, inc=1, device_id={"seq": flipped(part, flip)}, device_id_type=MESH
        )
    for peer in peers_in_order(place, inner):
        pl.semaphore_signal(
            barrier, inc=1, device_id={"shard": first + peer}, device_id_type=MESH
        )
    pl.semaphore_wait(barrier, len(FLIPS) + inner - 1)


def gather_kernel(inner, x_ref, out_ref, own_sem, zsend, zrecv, send, recv):
    part = lax.axis_index("seq")
    place, first = own_shard_group(inner)
    rows = x_ref.shape[0]
    half = rows // 2
    spans = [pl.ds(0, half), pl.ds(half, half)]
    others = peers_in_order(place, inner)
    sources = [place] + others
    greet(inner)
    own = pltpu.make_async_copy(x_ref, out_ref.at[place, part], own_sem)
    own.start()
    across = []
    for order, peer in enumerate(others):
        copy = pltpu.make_async_remote_copy(
            src_ref=x_ref,
            dst_ref=out_ref.at[place, part],
            send_sem=zsend.at[order],
            recv_sem=zrecv.at[place],
            device_id={"shard": first + peer},
            device_id_type=MESH,
        )
        copy.start()
        across.append(copy)

    def copy_of(order, kind, block, span, flip, from_input=False):
        whole = out_ref.at[sources[order], block, spans[span]]
        return pltpu.make_async_remote_copy(
            src_ref=x_ref.at[spans[span]] if from_input else whole,
            dst_ref=whole,
            send_sem=send.at[order, kind],
            recv_sem=recv.at[order, kind],
            device_id={"seq": flipped(part, flip)},
            device_id_type=MESH,
        )

    started = []

    def push(order, kind, block, span, flip, from_input=False):
        copy = copy_of(order, kind, block, span, flip, from_input)
        copy.start()
        started.append(copy)

    def arrived(order, kind, block, span, flip):
        copy_of(order, kind, block, span, flip).wait_recv()

    def stage_a(order):
        if order:
            arrive = pltpu.make_async_remote_copy(
                src_ref=x_ref,
                dst_ref=out_ref.at[sources[order], part],
                send_sem=zsend.at[order - 1],
                recv_sem=zrecv.at[sources[order]],
                device_id={"shard": first + sources[order]},
                device_id_type=MESH,
            )
            arrive.wait_recv()
        direct = order == 0
        push(order, 3, part, 1, 2, direct)
        push(order, 4, part, 0, 4, direct)
        push(order, 2, part, 0, 2, direct)
        push(order, 5, part, 1, 4, direct)
        push(order, 0, part, 0, 1, direct)
        push(order, 1, part, 1, 1, direct)

    def stage_b(order):
        side, over = flipped(part, 2), flipped(part, 4)
        arrived(order, 3, side, 1, 2)
        push(order, 6, side, 1, 4)
        arrived(order, 4, over, 0, 4)
        push(order, 7, over, 0, 2)
        push(order, 9, side, 1, 1)
        push(order, 10, over, 0, 1)
        arrived(order, 2, side, 0, 2)
        push(order, 8, side, 0, 1)
        arrived(order, 5, over, 1, 4)
        push(order, 11, over, 1, 1)

    def stage_c(order):
        far = flipped(part, 6)
        arrived(order, 6, far, 1, 4)
        push(order, 13, far, 1, 1)
        arrived(order, 7, far, 0, 2)
        push(order, 12, far, 0, 1)

    def stage_d(order):
        for kind, flip, span in (
            (0, 1, 0),
            (1, 1, 1),
            (9, 3, 1),
            (10, 5, 0),
            (8, 3, 0),
            (11, 5, 1),
            (13, 7, 1),
            (12, 7, 0),
        ):
            arrived(order, kind, flipped(part, flip), span, 1)

    count = len(sources)
    stage_a(0)
    stage_b(0)
    for order in range(1, count):
        stage_a(order)
        stage_c(order - 1)
        stage_b(order)
    stage_c(count - 1)
    for order in range(count):
        stage_d(order)
    for copy in started:
        copy.wait_send()
    for copy in across:
        copy.wait_send()
    own.wait()


def gather_rows(x, inner, collective):
    rows, width = x.shape
    seq_devices = lax.axis_size("seq")
    return pl.pallas_call(
        functools.partial(gather_kernel, inner),
        in_specs=[pl.BlockSpec(memory_space=pl.ANY)],
        out_specs=pl.BlockSpec(memory_space=pl.ANY),
        out_shape=jax.ShapeDtypeStruct((inner, seq_devices, rows, width), x.dtype),
        scratch_shapes=[
            pltpu.SemaphoreType.DMA(()),
            pltpu.SemaphoreType.DMA((max(1, inner - 1),)),
            pltpu.SemaphoreType.DMA((inner,)),
            pltpu.SemaphoreType.DMA((inner, 14)),
            pltpu.SemaphoreType.DMA((inner, 14)),
        ],
        compiler_params=pltpu.CompilerParams(collective_id=collective, has_side_effects=True),
        name="gather_rows",
    )(x)


def reduce_kernel(
    inner,
    p_ref,
    out_ref,
    held,
    paired,
    turned,
    crossed,
    sums,
    summed,
    load,
    core_send,
    core_recv,
    turn_send,
    turn_recv,
    cross_send,
    cross_recv,
    zsend,
    zrecv,
):
    part = lax.axis_index("seq")
    place, first = own_shard_group(inner)
    rows = out_ref.shape[0]
    half = rows // 2
    spans = [pl.ds(0, half), pl.ds(half, half)]
    targets = list(reversed(peers_in_order(place, inner))) + [place]
    evens = (6, 2, 4, 0)
    greet(inner)
    loads, cores = {}, {}
    for order, target in enumerate(targets):
        for slot, flip in enumerate(evens):
            copy = pltpu.make_async_remote_copy(
                src_ref=p_ref.at[target, flipped(part, flip + 1)],
                dst_ref=paired.at[order, slot],
                send_sem=core_send.at[order, slot],
                recv_sem=core_recv.at[order, slot],
                device_id={"seq": flipped(part, 1)},
                device_id_type=MESH,
            )
            copy.start()
            cores[order, slot] = copy
            copy = pltpu.make_async_copy(
                p_ref.at[target, flipped(part, flip)], held.at[order, slot], load.at[order, slot]
            )
            copy.start()
            loads[order, slot] = copy

    def total_of(order, slot):
        loads[order, slot].wait()
        cores[order, slot].wait_recv()
        return to_full(held[order, slot]) + to_full(paired[order, slot])

    sends = []

    def push(source, target, send_sem, recv_sem, flip):
        copy = pltpu.make_async_remote_copy(
            src_ref=source,
            dst_ref=target,
            send_sem=send_sem,
            recv_sem=recv_sem,
            device_id={"seq": flipped(part, flip)},
            device_id_type=MESH,
        )
        copy.start()
        sends.append(copy)
        return copy

    turns, crosses, across = {}, {}, []

    def stage_a(order):
        held[order, 0] = to_low(total_of(order, 0))
        for span, flip in ((0, 2), (1, 4)):
            turns[order, span] = push(
                held.at[order, 0, spans[span]],
                turned.at[order, span],
                turn_send.at[order, span],
                turn_recv.at[order, span],
                flip,
            )
        held[order, 1] = to_low(total_of(order, 1))
        held[order, 2] = to_low(total_of(order, 2))
        for kind, slot, flip, span in ((0, 1, 2, 0), (1, 2, 4, 1)):
            crosses[order, kind] = push(
                held.at[order, slot, spans[span]],
                crossed.at[order, kind],
                cross_send.at[order, kind],
                cross_recv.at[order, kind],
                flip,
            )

    def stage_b(order):
        for kind, slot, flip, span in ((2, 2, 4, 0), (3, 1, 2, 1)):
            turns[order, span].wait_recv()
            held[order, slot, spans[span]] = to_low(
                to_full(held[order, slot, spans[span]]) + to_full(turned[order, span])
            )
            crosses[order, kind] = push(
                held.at[order, slot, spans[span]],
                crossed.at[order, kind],
                cross_send.at[order, kind],
                cross_recv.at[order, kind],
                flip,
            )

    def stage_c(order):
        total = total_of(order, 3)
        for kind in range(4):
            crosses[order, kind].wait_recv()
        low_part = to_full(crossed[order, 0]) + to_full(crossed[order, 2])
        high_part = to_full(crossed[order, 1]) + to_full(crossed[order, 3])
        total = total + jnp.concatenate([low_part, high_part], axis=0)
        if order == inner - 1:
            return total
        sums[order] = to_low(total)
        copy = pltpu.make_async_remote_copy(
            src_ref=sums.at[order],
            dst_ref=summed.at[place],
            send_sem=zsend.at[order],
            recv_sem=zrecv.at[place],
            device_id={"shard": first + targets[order]},
            device_id_type=MESH,
        )
        copy.start()
        across.append(copy)
        return None

    stage_a(0)
    for order in range(1, inner):
        stage_a(order)
        stage_b(order - 1)
        if order > 1:
            stage_c(order - 2)
    stage_b(inner - 1)
    if inner > 1:
        stage_c(inner - 2)
    total = stage_c(inner - 1)
    for peer in peers_in_order(place, inner):
        arrive = pltpu.make_async_remote_copy(
            src_ref=sums.at[0],
            dst_ref=summed.at[peer],
            send_sem=zsend.at[0],
            recv_sem=zrecv.at[peer],
            device_id={"shard": first + peer},
            device_id_type=MESH,
        )
        arrive.wait_recv()
        total = total + to_full(summed[peer])
    out_ref[...] = total
    for copy in sends:
        copy.wait_send()
    for copy in cores.values():
        copy.wait_send()
    for copy in across:
        copy.wait_send()


def reduce_rows(partial, collective):
    inner, seq_devices, rows, width = partial.shape
    low = jnp.bfloat16
    sems = lambda *shape: pltpu.SemaphoreType.DMA(shape)
    return pl.pallas_call(
        functools.partial(reduce_kernel, inner),
        in_specs=[pl.BlockSpec(memory_space=pl.ANY)],
        out_specs=pl.BlockSpec(memory_space=pltpu.VMEM),
        out_shape=jax.ShapeDtypeStruct((rows, width), jnp.float32),
        scratch_shapes=[
            pltpu.VMEM((inner, 4, rows, width), low),
            pltpu.VMEM((inner, 4, rows, width), low),
            pltpu.VMEM((inner, 2, rows // 2, width), low),
            pltpu.VMEM((inner, 4, rows // 2, width), low),
            pltpu.VMEM((max(1, inner - 1), rows, width), low),
            pltpu.VMEM((inner, rows, width), low),
            sems(inner, 4),
            sems(inner, 4),
            sems(inner, 4),
            sems(inner, 2),
            sems(inner, 2),
            sems(inner, 4),
            sems(inner, 4),
            sems(max(1, inner - 1)),
            sems(inner),
        ],
        compiler_params=pltpu.CompilerParams(
            collective_id=collective, has_side_effects=True, vmem_limit_bytes=VMEM_BYTES
        ),
        name="reduce_rows",
    )(partial)


def whole(shape):
    return pl.BlockSpec(shape, lambda *steps: (0,) * len(shape))


def params_of(limit=VMEM_BYTES):
    return pltpu.CompilerParams(vmem_limit_bytes=limit)


def project_kernel(x_ref, gain_ref, w_ref, hidden_ref, gate_ref, rows_ref):
    x = to_full(x_ref[...])
    hidden = to_low(x * norm_scale(x) * gain_ref[...])
    hidden_ref[...] = hidden
    projected = dot_full(hidden, w_ref[...])
    gate_width = gate_ref.shape[1]
    gate_ref[...] = projected[:, :gate_width]
    rows_ref[...] = to_low(projected[:, gate_width:])


def project(x, gain, weights, gate_width):
    rows, width = x.shape
    columns = weights.shape[1]
    tile = 256
    block = lambda extent: pl.BlockSpec((tile, extent), lambda step: (step, 0))
    return pl.pallas_call(
        project_kernel,
        grid=(rows // tile,),
        in_specs=[block(width), whole(gain.shape), whole(weights.shape)],
        out_specs=[block(width), block(gate_width), block(columns - gate_width)],
        out_shape=[
            jax.ShapeDtypeStruct((rows, width), jnp.bfloat16),
            jax.ShapeDtypeStruct((rows, gate_width), jnp.float32),
            jax.ShapeDtypeStruct((rows, columns - gate_width), jnp.bfloat16),
        ],
        compiler_params=params_of(),
        name="project",
    )(x, gain, weights)


def put_split(columns, rows):
    lane = iota_of((rows, LANES), 1)
    result = jnp.zeros((rows, LANES), jnp.float32)
    for place, column in enumerate(columns):
        high = to_full(to_low(column))
        result = jnp.where(lane == 2 * place, high, result)
        result = jnp.where(lane == 2 * place + 1, column - high, result)
    return to_low(result)


def mix_out_kernel(y_ref, gate_ref, gain_ref, w_ref, part_ref):
    width = w_ref.shape[1]
    gated = to_full(y_ref[...]) * jax.nn.silu(gate_ref[...])
    part_ref[0, :, :width] = to_low(dot_full(to_low(gated * gain_ref[...]), w_ref[...]))
    squares = jnp.sum(gated * gated, axis=1, keepdims=True)
    part_ref[0, :, width:] = put_split([squares], y_ref.shape[0])


def mix_out(y, gate, gain, weights, blocks):
    rows, channels = y.shape
    width = weights.shape[1]
    tile = rows // blocks
    block = pl.BlockSpec((tile, channels), lambda step: (step, 0))
    return pl.pallas_call(
        mix_out_kernel,
        grid=(blocks,),
        in_specs=[block, block, whole(gain.shape), whole(weights.shape)],
        out_specs=pl.BlockSpec((1, tile, width + LANES), lambda step: (step, 0, 0)),
        out_shape=jax.ShapeDtypeStruct((blocks, tile, width + LANES), jnp.bfloat16),
        compiler_params=params_of(),
        name="mix_out",
    )(y, gate, gain, weights)


def mix_back_kernel(
    mix_ref, y_ref, gate_ref, gain_ref, w_ref, dy_ref, dgate_ref, w_grad_ref, gain_grad_ref, total
):
    step = pl.program_id(0)
    width = w_ref.shape[1]

    @pl.when(step == 0)
    def _():
        total[...] = jnp.zeros_like(total)
        gain_grad_ref[...] = jnp.zeros_like(gain_grad_ref)

    mix = mix_ref[0, :, :width]
    extra = to_full(mix_ref[0, :, width:])
    share = extra[:, 0:1] + extra[:, 1:2]
    scale = extra[:, 2:3] + extra[:, 3:4]
    normed_grad = dot_lanes(mix, w_ref[...])
    y = to_full(y_ref[...])
    gate = gate_ref[...]
    sig = jax.nn.sigmoid(gate)
    act = gate * sig
    unit = y * act * scale
    gain = gain_ref[...]
    gain_grad_ref[0:1, :] += jnp.sum(normed_grad * unit, axis=0, keepdims=True)
    gated_grad = scale * (normed_grad * gain - unit * share)
    dy_ref[...] = to_low(gated_grad * act)
    dgate_ref[...] = to_low(gated_grad * y * sig * (1.0 + gate * (1.0 - sig)))
    total[...] += dot_rows(to_low(unit * gain), mix)

    @pl.when(step == pl.num_programs(0) - 1)
    def _():
        w_grad_ref[...] = to_low(total[...])


def mix_back(mix, y, gate, gain, weights):
    blocks, tile, wide = mix.shape
    rows, channels = y.shape
    block = pl.BlockSpec((tile, channels), lambda step: (step, 0))
    return pl.pallas_call(
        mix_back_kernel,
        grid=(blocks,),
        in_specs=[
            pl.BlockSpec((1, tile, wide), lambda step: (step, 0, 0)),
            block,
            block,
            whole(gain.shape),
            whole(weights.shape),
        ],
        out_specs=[block, block, whole(weights.shape), whole((8, channels))],
        out_shape=[
            jax.ShapeDtypeStruct((rows, channels), jnp.bfloat16),
            jax.ShapeDtypeStruct((rows, channels), jnp.bfloat16),
            jax.ShapeDtypeStruct(weights.shape, jnp.bfloat16),
            jax.ShapeDtypeStruct((8, channels), jnp.float32),
        ],
        scratch_shapes=[pltpu.VMEM(weights.shape, jnp.float32)],
        compiler_params=params_of(),
        name="mix_back",
    )(mix, y, gate, gain, weights)


def project_back_kernel(dgate_ref, drows_ref, hidden_ref, w_ref, part_ref, w_grad_ref, total):
    step = pl.program_id(0)

    @pl.when(step == 0)
    def _():
        total[...] = jnp.zeros_like(total)

    grads = jnp.concatenate([dgate_ref[...], drows_ref[...]], axis=1)
    part_ref[0] = to_low(dot_lanes(grads, w_ref[...]))
    total[...] += dot_rows(hidden_ref[...], grads)

    @pl.when(step == pl.num_programs(0) - 1)
    def _():
        w_grad_ref[...] = to_low(total[...])


def project_back(dgate, drows, hidden, weights, blocks):
    rows, width = hidden.shape
    tile = rows // blocks
    block = lambda extent: pl.BlockSpec((tile, extent), lambda step: (step, 0))
    return pl.pallas_call(
        project_back_kernel,
        grid=(blocks,),
        in_specs=[
            block(dgate.shape[1]),
            block(drows.shape[1]),
            block(width),
            whole(weights.shape),
        ],
        out_specs=[
            pl.BlockSpec((1, tile, width), lambda step: (step, 0, 0)),
            whole(weights.shape),
        ],
        out_shape=[
            jax.ShapeDtypeStruct((blocks, tile, width), jnp.bfloat16),
            jax.ShapeDtypeStruct(weights.shape, jnp.bfloat16),
        ],
        scratch_shapes=[pltpu.VMEM(weights.shape, jnp.float32)],
        compiler_params=params_of(),
        name="project_back",
    )(dgate, drows, hidden, weights)


def shared_kernel(
    rows_ref, grad_ref, up_ref, down_ref, res_ref, back_ref, up_grad_ref, down_grad_ref, up_sum, down_sum
):
    step = pl.program_id(0)

    @pl.when(step == 0)
    def _():
        up_sum[...] = jnp.zeros_like(up_sum)
        down_sum[...] = jnp.zeros_like(down_sum)

    width = grad_ref.shape[2]
    hidden = down_ref.shape[0]
    rows = rows_ref[0, :, :width]
    grad = grad_ref[0]
    joined = dot_full(rows, up_ref[...])
    gate, up = joined[:, :hidden], joined[:, hidden:]
    sig = jax.nn.sigmoid(gate)
    act = gate * sig
    acted = to_low(act * up)
    res_ref[0] = to_low(dot_full(acted, down_ref[...]))
    down_sum[...] += dot_rows(acted, grad)
    act_grad = dot_lanes(grad, down_ref[...])
    joined_grad = to_low(
        jnp.concatenate(
            [act_grad * up * sig * (1.0 + gate * (1.0 - sig)), act_grad * act], axis=1
        )
    )
    up_sum[...] += dot_rows(rows, joined_grad)
    back_ref[0] = to_low(dot_lanes(joined_grad, up_ref[...]))

    @pl.when(step == pl.num_programs(0) - 1)
    def _():
        up_grad_ref[...] = to_low(up_sum[...])
        down_grad_ref[...] = to_low(down_sum[...])


def shared_expert(rows, grad, up, down):
    blocks, tile, wide = rows.shape
    width = grad.shape[2]
    block = lambda extent: pl.BlockSpec((1, tile, extent), lambda step: (step, 0, 0))
    return pl.pallas_call(
        shared_kernel,
        grid=(blocks,),
        in_specs=[block(wide), block(width), whole(up.shape), whole(down.shape)],
        out_specs=[block(width), block(width), whole(up.shape), whole(down.shape)],
        out_shape=[
            jax.ShapeDtypeStruct((blocks, tile, width), jnp.bfloat16),
            jax.ShapeDtypeStruct((blocks, tile, width), jnp.bfloat16),
            jax.ShapeDtypeStruct(up.shape, jnp.bfloat16),
            jax.ShapeDtypeStruct(down.shape, jnp.bfloat16),
        ],
        scratch_shapes=[
            pltpu.VMEM(up.shape, jnp.float32),
            pltpu.VMEM(down.shape, jnp.float32),
        ],
        compiler_params=params_of(),
        name="shared_expert",
    )(rows, grad, up, down)


def dispatch_kernel(
    first_ref, rows_ref, grad_ref, x_ref, g_ref, picks_ref, *, top_count, slots
):
    per_device = x_ref.shape[0]
    tok_rows = rows_ref.shape[1]
    width = grad_ref.shape[2]
    block = rows_ref[0]
    extra = to_full(block[:, width:])
    lane = iota_of((tok_rows, LANES), 1)
    named = (lane >= 2 * top_count) & (lane < 3 * top_count)
    member = jnp.zeros((tok_rows, LANES), jnp.float32)
    for expert in range(per_device):
        own = to_full(first_ref[0] + expert)
        hit = jnp.sum(jnp.where(named & (extra == own), 1.0, 0.0), axis=1, keepdims=True)
        member = jnp.where(lane // slots == expert, hit, member)
    before = iota_of((tok_rows, tok_rows), 0) > iota_of((tok_rows, tok_rows), 1)
    ranks = dot_full(to_low(jnp.where(before, 1.0, 0.0)), to_low(member))
    picks = jnp.where(
        (ranks == to_full(lane % slots)) & (member > 0.0), 1.0, 0.0
    ).astype(jnp.bfloat16)
    picks_ref[0] = picks
    rows = to_low(dot_rows(picks, block))
    grads = to_low(dot_rows(picks, grad_ref[0]))
    for expert in range(per_device):
        x_ref[expert] = rows[expert * slots : (expert + 1) * slots]
        g_ref[expert] = grads[expert * slots : (expert + 1) * slots]


def dispatch(first, rows, grad, per_device, top_count, slots):
    blocks, tok_rows, wide = rows.shape
    width = grad.shape[2]
    block = lambda extent: pl.BlockSpec((1, tok_rows, extent), lambda step: (step, 0, 0))
    taken = lambda extent: pl.BlockSpec((per_device, slots, extent), lambda step: (0, step, 0))
    return pl.pallas_call(
        functools.partial(dispatch_kernel, top_count=top_count, slots=slots),
        grid=(blocks,),
        in_specs=[pl.BlockSpec(memory_space=pltpu.SMEM), block(wide), block(width)],
        out_specs=[taken(wide), taken(width), block(LANES)],
        out_shape=[
            jax.ShapeDtypeStruct((per_device, blocks * slots, wide), jnp.bfloat16),
            jax.ShapeDtypeStruct((per_device, blocks * slots, width), jnp.bfloat16),
            jax.ShapeDtypeStruct((blocks, tok_rows, LANES), jnp.bfloat16),
        ],
        compiler_params=params_of(),
        name="dispatch",
    )(first, rows, grad)


def experts_kernel(first_ref, place_ref, *refs, count, top_count):
    x_ref, g_ref = refs[:2]
    ups, downs = refs[2 : 2 + count], refs[2 + count : 2 + 2 * count]
    refs = refs[2 + 2 * count :]
    res_ref, dx_ref = refs[:2]
    up_outs, down_outs = refs[2 : 2 + count], refs[2 + count : 2 + 2 * count]
    up_held, down_held, up_sum, down_sum, up_low, down_low, up_sems, down_sems = refs[
        2 + 2 * count :
    ]
    expert, step = pl.program_id(0), pl.program_id(1)
    experts, steps = pl.num_programs(0), pl.num_programs(1)
    slot = lax.rem(expert, 2)
    width, double = up_held.shape[1:]
    hidden = double // 2
    tile = x_ref.shape[1]

    def spans(extent):
        piece = extent // count
        return [
            pl.ds(
                pl.multiple_of(lax.rem(place_ref[0] + count - shift, count) * piece, piece), piece
            )
            for shift in range(count)
        ]

    def fetch(which, into):
        copies = []
        for shift, span in enumerate(spans(width)):
            copies.append(
                pltpu.make_async_copy(
                    ups[shift].at[which], up_held.at[into, span], up_sems.at[into, shift]
                )
            )
        for shift, span in enumerate(spans(hidden)):
            copies.append(
                pltpu.make_async_copy(
                    downs[shift].at[which], down_held.at[into, span], down_sems.at[into, shift]
                )
            )
        return copies

    @pl.when(step == 0)
    def _():
        @pl.when(expert == 0)
        def _():
            for copy in fetch(expert, slot):
                copy.start()

        for copy in fetch(expert, slot):
            copy.wait()

        @pl.when(expert + 1 < experts)
        def _():
            for copy in fetch(expert + 1, 1 - slot):
                copy.start()

        up_sum[...] = jnp.zeros_like(up_sum)
        down_sum[...] = jnp.zeros_like(down_sum)

    up, down = up_held.at[slot], down_held.at[slot]
    rows = x_ref[0, :, :width]
    extra = to_full(x_ref[0, :, width:])
    lane = iota_of((tile, LANES), 1)
    own = first_ref[0] + expert
    hits = jnp.where((lane < 3 * top_count) & (extra == to_full(own)), 1.0, 0.0)
    gate_slot = jnp.zeros((tile, 1), jnp.float32)
    for route in range(top_count):
        place = 2 * top_count + route
        value = extra[:, 2 * route : 2 * route + 1] + extra[:, 2 * route + 1 : 2 * route + 2]
        gate_slot = gate_slot + hits[:, place : place + 1] * value
    joined = dot_full(rows, up[...])
    gate, lift = joined[:, :hidden], joined[:, hidden:]
    sig = jax.nn.sigmoid(gate)
    act = gate * sig
    acted = to_low(act * lift)
    res = to_low(dot_full(acted, down[...]))
    grads = g_ref[0]
    wide_grads = to_full(grads)
    wide_res = to_full(res)
    gate_grad = jnp.sum(wide_res * wide_grads, axis=1, keepdims=True)
    res_ref[0] = to_low(wide_res * gate_slot)
    weighted = to_low(wide_grads * gate_slot)
    act_grad = dot_lanes(weighted, down[...])
    down_sum[...] += dot_rows(acted, weighted)
    joined_grad = to_low(
        jnp.concatenate(
            [act_grad * lift * sig * (1.0 + gate * (1.0 - sig)), act_grad * act], axis=1
        )
    )
    dx_ref[0, :, :width] = to_low(dot_lanes(joined_grad, up[...]))
    high = to_full(to_low(gate_grad))
    half = LANES // 2
    dx_ref[0, :, width:] = to_low(
        jnp.where(lane == own, high, 0.0) + jnp.where(lane == own + half, gate_grad - high, 0.0)
    )
    up_sum[...] += dot_rows(rows, joined_grad)

    @pl.when(step == steps - 1)
    def _():
        up_low[...] = to_low(up_sum[...])
        down_low[...] = to_low(down_sum[...])
        copies = []
        for shift, span in enumerate(spans(width)):
            copies.append(
                pltpu.make_async_copy(
                    up_low.at[span], up_outs[shift].at[expert], up_sems.at[2, shift]
                )
            )
        for shift, span in enumerate(spans(hidden)):
            copies.append(
                pltpu.make_async_copy(
                    down_low.at[span], down_outs[shift].at[expert], down_sems.at[2, shift]
                )
            )
        for copy in copies:
            copy.start()
        for copy in copies:
            copy.wait()


def experts(first, place, x, g, ups, downs, top_count):
    per_device, rows, wide = x.shape
    width = g.shape[2]
    count = len(ups)
    double = ups[0].shape[2]
    hidden = double // 2
    tile = min(rows, 256)
    block = lambda extent: pl.BlockSpec((1, tile, extent), lambda e, step: (e, step, 0))
    anywhere = pl.BlockSpec(memory_space=pl.ANY)
    scalars = pl.BlockSpec(memory_space=pltpu.SMEM)
    low = jnp.bfloat16
    outs = pl.pallas_call(
        functools.partial(experts_kernel, count=count, top_count=top_count),
        grid=(per_device, rows // tile),
        in_specs=[scalars, scalars, block(wide), block(width)] + [anywhere] * (2 * count),
        out_specs=[block(width), block(wide)] + [anywhere] * (2 * count),
        out_shape=[
            jax.ShapeDtypeStruct((per_device, rows, width), low),
            jax.ShapeDtypeStruct((per_device, rows, wide), low),
        ]
        + [jax.ShapeDtypeStruct(piece.shape, low) for piece in list(ups) + list(downs)],
        scratch_shapes=[
            pltpu.VMEM((2, width, double), low),
            pltpu.VMEM((2, hidden, width), low),
            pltpu.VMEM((width, double), jnp.float32),
            pltpu.VMEM((hidden, width), jnp.float32),
            pltpu.VMEM((width, double), low),
            pltpu.VMEM((hidden, width), low),
            pltpu.SemaphoreType.DMA((3, count)),
            pltpu.SemaphoreType.DMA((3, count)),
        ],
        compiler_params=params_of(),
        name="experts",
    )(first, place, x, g, *ups, *downs)
    return outs[0], outs[1], outs[2 : 2 + count], outs[2 + count :]


def combine_kernel(place_ref, picks_ref, res_ref, dx_ref, sres_ref, sback_ref, out_ref, back_ref):
    step = pl.program_id(0)
    width = out_ref.shape[2]
    per_device, slots = res_ref.shape[:2]
    taken = per_device * slots
    picks = picks_ref[0, :, :taken]
    out = dot_full(picks, res_ref[...].reshape(taken, width))
    back = dot_full(picks, dx_ref[...].reshape(taken, width + LANES))
    out_ref[0] = to_low(out)
    back_ref[0] = to_low(back)

    @pl.when(lax.div(step, sres_ref.shape[0]) == place_ref[0])
    def _():
        block = lax.rem(step, sres_ref.shape[0])
        out_ref[0] = to_low(out + to_full(sres_ref[block]))
        back_ref[0, :, :width] = to_low(back[:, :width] + to_full(sback_ref[block]))


def combine(place, picks, res, dx, shared_res, shared_back):
    blocks, tok_rows, _ = picks.shape
    per_device, rows, width = res.shape
    slots = rows // blocks
    block = lambda extent: pl.BlockSpec((1, tok_rows, extent), lambda step: (step, 0, 0))
    taken = lambda extent: pl.BlockSpec((per_device, slots, extent), lambda step: (0, step, 0))
    return pl.pallas_call(
        combine_kernel,
        grid=(blocks,),
        in_specs=[
            pl.BlockSpec(memory_space=pltpu.SMEM),
            block(LANES),
            taken(width),
            taken(width + LANES),
            whole(shared_res.shape),
            whole(shared_back.shape),
        ],
        out_specs=[block(width), block(width + LANES)],
        out_shape=[
            jax.ShapeDtypeStruct((blocks, tok_rows, width), jnp.bfloat16),
            jax.ShapeDtypeStruct((blocks, tok_rows, width + LANES), jnp.bfloat16),
        ],
        compiler_params=params_of(),
        name="combine",
    )(place, picks, res, dx, shared_res, shared_back)


def gather_small(arrays):
    flat = jnp.concatenate([piece.reshape(-1) for piece in arrays])
    joined = lax.all_gather(flat, "shard")
    results, start = [], 0
    for piece in arrays:
        part = joined[:, start : start + piece.size]
        results.append(part.reshape((-1,) + piece.shape[1:]))
        start += piece.size
    return results


def rows_to_owner(shard_rows, part):
    seq_devices = lax.axis_size("seq")
    shard_devices = lax.axis_size("shard")
    rows, width = shard_rows.shape
    own_rows = rows * shard_devices // seq_devices
    halves = max(1, rows // own_rows)
    fine = rows // halves // seq_devices
    mine = lax.dynamic_index_in_dim(
        shard_rows.reshape(halves, seq_devices, fine, width), part, 1, keepdims=False
    )
    spread = lax.all_gather(mine, "shard").reshape(seq_devices, -1, width)
    return (
        lax.all_to_all(spread, "seq", split_axis=0, concat_axis=0, tiled=True)
        .reshape(seq_devices, own_rows // fine // seq_devices, fine, width)
        .transpose(1, 0, 2, 3)
        .reshape(own_rows, width)
    )


def rows_from_owner(own, part_rows):
    seq_devices = lax.axis_size("seq")
    shard_devices = lax.axis_size("shard")
    own_rows, width = own.shape
    halves = max(1, part_rows // own_rows)
    fine = part_rows // halves // seq_devices
    pieces = own.reshape(own_rows // fine // seq_devices, seq_devices, fine, width)
    pieces = pieces.transpose(1, 0, 2, 3).reshape(seq_devices, -1, width)
    spread = lax.all_to_all(pieces, "seq", split_axis=0, concat_axis=0, tiled=True)
    mine = lax.psum_scatter(
        spread.reshape(shard_devices, halves * fine, width), "shard", tiled=True
    )
    joined = lax.all_gather(mine.reshape(halves, fine, width), "seq", axis=1)
    return joined.reshape(part_rows, width)


def inner_groups(inner):
    count = lax.axis_size("shard")
    return [list(range(start, start + inner)) for start in range(0, count, inner)]


def outer_groups(inner):
    count = lax.axis_size("shard")
    return [list(range(start, count, inner)) for start in range(inner)]


def exchange(pieces, inner):
    received = [pieces[0]]
    for shift in range(1, inner):
        pairs = [
            (group[place], group[(place + shift) % inner])
            for group in inner_groups(inner)
            for place in range(inner)
        ]
        received.append(lax.ppermute(pieces[shift], "shard", pairs))
    return received


def by_place(received, place, inner):
    return jnp.stack(received)[lax.rem(place + inner - jnp.arange(inner), inner)]


def local(
    tokens,
    out_grad,
    deal_order,
    lengths,
    routes,
    norm_in,
    w_in,
    w_dt,
    conv_w,
    conv_b,
    dt_bias,
    a_log,
    d_skip,
    norm_gate,
    w_out,
    norm_moe,
    w_router,
    w_shared,
    w_shared_down,
    w_experts,
    w_experts_down,
):
    seq_devices = lax.axis_size("seq")
    shard_devices = lax.axis_size("shard")
    part = lax.axis_index("seq")
    shard = lax.axis_index("shard")
    inner = min(shard_devices, INNER)
    outer = shard_devices // inner
    place = lax.rem(shard, inner)
    residual = to_full(tokens[0])
    tok_rows, width = residual.shape
    group_rows = tok_rows * seq_devices
    inner_width = w_out.shape[0] * shard_devices
    channels = inner_width // seq_devices
    head_total = w_dt.shape[1]
    heads = head_total // seq_devices
    shared_width = w_shared_down.shape[0] * shard_devices
    shared_part = shared_width // seq_devices
    depth_rows = w_in.shape[0]
    expert_total = w_router.shape[1]
    local_experts, _, double = w_experts.shape
    hidden = double // 2
    hidden_rows = w_experts_down.shape[1]
    top_count = routes.shape[2]
    per_device = local_experts // inner
    blocks = inner * seq_devices

    def own_columns(array, start, extent):
        return lax.dynamic_slice_in_dim(array, start + part * extent, extent, 1)

    def own_rows(array, extent):
        return lax.dynamic_slice_in_dim(array, part * extent, extent, 0)

    x_group = gather_rows(tokens[0], 1, 1).reshape(group_rows, width)
    (
        gain_in,
        conv_weight,
        conv_bias,
        step_bias,
        decay_log,
        skip_gain,
        gain_gate,
        gain_moe,
        router,
    ) = gather_small(
        [norm_in, conv_w, conv_b, dt_bias, a_log, d_skip, norm_gate, norm_moe, w_router]
    )
    in_columns = jnp.concatenate(
        [
            own_columns(w_in, 0, channels),
            own_columns(w_in, inner_width, channels),
            w_in[:, 2 * inner_width :],
            own_columns(w_dt, 0, heads),
            jnp.zeros((depth_rows, LANES - heads), jnp.bfloat16),
        ],
        axis=1,
    )
    proj_in = lax.all_gather(in_columns, "shard", tiled=True)
    out_rows = rows_to_owner(w_out, part)
    shared_up = lax.all_gather(
        jnp.concatenate(
            [
                own_columns(w_shared, 0, shared_part),
                own_columns(w_shared, shared_width, shared_part),
            ],
            axis=1,
        ),
        "shard",
        tiled=True,
    )
    shared_down = rows_to_owner(w_shared_down, part)
    if outer == 1:
        grad_all = lax.all_gather(out_grad[0], ("shard", "seq"))
    else:
        grad_all = lax.all_gather(
            lax.all_gather(out_grad[0], "shard", axis_index_groups=inner_groups(inner)),
            "seq",
            axis=1,
        )
    grad_all = grad_all.reshape(blocks, tok_rows, width)

    def experts_of(array, shift):
        start = lax.rem(place + shift, inner) * per_device
        return lax.dynamic_slice_in_dim(array, start, per_device, 0)

    up_pieces = exchange([experts_of(w_experts, shift) for shift in range(inner)], inner)
    down_pieces = exchange([experts_of(w_experts_down, shift) for shift in range(inner)], inner)
    if outer > 1:

        def assembled(pieces):
            joined = lax.all_gather(
                by_place(pieces, place, inner), "shard", axis_index_groups=outer_groups(inner)
            )
            return [
                joined.transpose(2, 0, 1, 3, 4).reshape(per_device, -1, joined.shape[-1])
            ]

        up_pieces, down_pieces = assembled(up_pieces), assembled(down_pieces)

    gain_row = to_full(gain_in)[None]
    hidden_in, gate_in, rows_in = project(x_group, gain_row, proj_in, channels)
    ends = jnp.cumsum(lengths[0]).astype(jnp.int32)
    conv_part = jnp.concatenate(
        [own_rows(conv_weight, channels), conv_weight[inner_width:]], axis=0
    )
    bias_part = jnp.concatenate([own_rows(conv_bias, channels), conv_bias[inner_width:]], axis=0)
    conv_table = to_full(
        jnp.pad(jnp.concatenate([conv_part.T, bias_part[None]], axis=0), ((0, 3), (0, 0)))
    )
    head_table = jnp.pad(
        jnp.stack(
            [
                to_full(own_rows(step_bias, heads)),
                -jnp.exp(to_full(own_rows(decay_log, heads))),
                to_full(own_rows(skip_gain, heads)),
            ]
        ),
        ((0, 5), (0, LANES - heads)),
    )
    y, seq_rows, states = scan_forward(
        ends, deal_order, rows_in, conv_table, head_table, channels
    )
    gate_gain = to_full(own_rows(gain_gate, channels))[None]
    mixed = reduce_rows(mix_out(y, gate_in, gate_gain, out_rows, seq_devices)[None], 2)
    gate_scale = lax.rsqrt(
        (mixed[:, width : width + 1] + mixed[:, width + 1 : width + 2]) / inner_width + EPSILON
    )
    mix_sum = mixed[:, :width] * gate_scale
    after_mix = residual + mix_sum

    gain_moe = to_full(gain_moe)
    moe_scale = norm_scale(after_mix)
    moe_unit = after_mix * moe_scale
    moe_in = to_low(moe_unit * gain_moe)
    logits = matmul(moe_in, router)
    route_ids = routes[0]
    chosen = to_full(
        route_ids[:, :, None] == jnp.arange(expert_total, dtype=jnp.int32)[None, None, :]
    )
    gate_values = jax.nn.softmax(jnp.sum(chosen * logits[:, None, :], axis=2), axis=1)
    gate_high = to_low(gate_values)
    gate_rest = to_low(gate_values - to_full(gate_high))
    extra = jnp.concatenate(
        [
            jnp.stack([gate_high, gate_rest], axis=2).reshape(tok_rows, 2 * top_count),
            route_ids.astype(jnp.bfloat16),
            jnp.zeros((tok_rows, LANES - 3 * top_count), jnp.bfloat16),
        ],
        axis=1,
    )
    moe_all = gather_rows(jnp.concatenate([moe_in, extra], axis=1), inner, 3)
    moe_all = moe_all.reshape(blocks, tok_rows, width + LANES)
    moe_group = lax.dynamic_slice_in_dim(moe_all, place * seq_devices, seq_devices, 0)
    grad_group = lax.dynamic_slice_in_dim(grad_all, place * seq_devices, seq_devices, 0)
    shared_res, shared_back, shared_up_grad, shared_down_grad = shared_expert(
        moe_group, grad_group, shared_up, shared_down
    )
    capacity = min(tok_rows, max(2, tok_rows * top_count * 5 // (expert_total * 3)))
    slots = -(-capacity // 16) * 16
    first = (part * local_experts + place * per_device).astype(jnp.int32)[None]
    place_row = place.astype(jnp.int32)[None]
    expert_rows, grad_rows, picks = dispatch(
        first, moe_all, grad_all, per_device, top_count, slots
    )
    expert_res, expert_back, up_grads, down_grads = experts(
        first, place_row, expert_rows, grad_rows, up_pieces, down_pieces, top_count
    )
    out_part, back_part = combine(
        place_row, picks, expert_res, expert_back, shared_res, shared_back
    )
    back = reduce_rows(back_part.reshape(inner, seq_devices, tok_rows, -1), 4)
    if outer == 1:
        out_sum = lax.psum_scatter(
            out_part.reshape(blocks * tok_rows, width), ("shard", "seq"), tiled=True
        )
    else:
        out_sum = lax.psum_scatter(
            lax.psum_scatter(
                out_part.reshape(inner, seq_devices, tok_rows, width),
                "seq",
                scatter_dimension=1,
            ),
            "shard",
            axis_index_groups=inner_groups(inner),
        )
    layer_out = to_low(after_mix + to_full(out_sum))

    if outer > 1:

        def scattered(grads):
            full = grads[0]
            piece = full.shape[1] // shard_devices
            split = full.reshape(per_device, outer, inner, piece, full.shape[2])
            own = lax.psum_scatter(
                split.transpose(1, 2, 0, 3, 4),
                "shard",
                axis_index_groups=outer_groups(inner),
            )
            return [
                lax.dynamic_index_in_dim(own, lax.rem(place + shift, inner), 0, keepdims=False)
                for shift in range(inner)
            ]

        up_back, down_back = scattered(up_grads), scattered(down_grads)
    else:
        turned = lambda pieces: [pieces[(inner - shift) % inner] for shift in range(inner)]
        up_back, down_back = turned(up_grads), turned(down_grads)

    def whole_shard(pieces):
        received = by_place(exchange(pieces, inner), place, inner)
        return to_full(received.reshape((local_experts,) + received.shape[2:]))

    experts_grad = whole_shard(up_back)
    experts_down_grad = whole_shard(down_back)

    half = LANES // 2
    gate_grad_all = (
        back[:, width : width + expert_total]
        + back[:, width + half : width + half + expert_total]
    )
    gate_grad = jnp.sum(chosen * gate_grad_all[:, None, :], axis=2)
    mixed_gate = jnp.sum(gate_values * gate_grad, axis=1, keepdims=True)
    logit_grad = to_low(
        jnp.sum(chosen * (gate_values * (gate_grad - mixed_gate))[:, :, None], axis=1)
    )
    router_grad = left_contract(moe_in, logit_grad)
    moe_grad = back[:, :width] + right_contract(logit_grad, router)
    gain_moe_grad = jnp.sum(moe_grad * moe_unit, axis=0)
    moe_scaled = moe_grad * gain_moe
    mix_grad = to_full(out_grad[0]) + moe_scale * (
        moe_scaled - moe_unit * jnp.mean(moe_scaled * moe_unit, axis=1, keepdims=True)
    )
    mix_low = to_low(mix_grad)
    share = jnp.sum(to_full(mix_low) * mix_sum, axis=1, keepdims=True) / inner_width
    carried = put_split([share, gate_scale], tok_rows)

    mix_group = gather_rows(jnp.concatenate([mix_low, carried], axis=1), 1, 5)[0]
    dy, gate_in_grad, proj_out_grad, gain_gate_grad = mix_back(
        mix_group, y, gate_in, gate_gain, out_rows
    )
    rows_grad, conv_grad, head_grad = scan_backward(
        ends, deal_order, seq_rows, states, dy, conv_table, head_table
    )
    hidden_part, proj_in_grad = project_back(
        gate_in_grad, rows_grad, hidden_in, proj_in, seq_devices
    )
    hidden_grad = reduce_rows(hidden_part[None], 6)
    own_scale = norm_scale(residual)
    own_unit = residual * own_scale
    gain_in_grad = jnp.sum(hidden_grad * own_unit, axis=0)
    hidden_scaled = hidden_grad * gain_row
    tokens_grad = to_low(
        mix_grad
        + own_scale
        * (hidden_scaled - own_unit * jnp.mean(hidden_scaled * own_unit, axis=1, keepdims=True))
    )

    own_in_grad = lax.all_gather(
        lax.psum_scatter(proj_in_grad[:, : 2 * channels], "shard", tiled=True), "seq"
    )
    w_in_main = (
        own_in_grad.reshape(seq_devices, depth_rows, 2, channels)
        .transpose(1, 2, 0, 3)
        .reshape(depth_rows, 2 * inner_width)
    )
    own_shared_grad = lax.all_gather(
        lax.psum_scatter(shared_up_grad, "shard", tiled=True), "seq"
    )
    w_shared_grad = to_full(
        own_shared_grad.reshape(seq_devices, depth_rows, 2, shared_part)
        .transpose(1, 2, 0, 3)
        .reshape(depth_rows, 2 * shared_width)
    )
    w_out_grad = to_full(rows_from_owner(proj_out_grad, w_out.shape[0]))
    w_shared_down_grad = to_full(rows_from_owner(shared_down_grad, w_shared_down.shape[0]))

    def spread(values, length, axis=0):
        shape = values.shape[:axis] + (length,) + values.shape[axis + 1 :]
        return lax.dynamic_update_slice_in_dim(
            jnp.zeros(shape, values.dtype), values, part * values.shape[axis], axis
        )

    conv_rows_grad = conv_grad[:5].T
    conv_full = jnp.concatenate(
        [spread(conv_rows_grad[:channels], inner_width), conv_rows_grad[channels:]], axis=0
    )
    small = [
        gain_in_grad,
        spread(proj_in_grad[:, -LANES:][:, :heads], head_total, 1),
        conv_full[:, :4],
        conv_full[:, 4],
        spread(head_grad[0, :heads], head_total),
        spread(head_grad[1, :heads], head_total),
        spread(head_grad[2, :heads], head_total),
        spread(gain_gate_grad[0], inner_width),
        gain_moe_grad,
        router_grad,
        proj_in_grad[:, 2 * channels : -LANES],
    ]
    shapes = [(piece.shape[0] // shard_devices,) + piece.shape[1:] for piece in small]
    packed = jnp.concatenate(
        [to_low(piece).reshape(shard_devices, -1) for piece in small], axis=1
    )
    summed = lax.psum(lax.psum_scatter(packed, "shard", tiled=True), "seq").reshape(-1)
    results, start = [], 0
    for shape in shapes:
        size = 1
        for extent in shape:
            size *= extent
        results.append(to_full(summed[start : start + size]).reshape(shape))
        start += size
    w_in_grad = jnp.concatenate([to_full(w_in_main), results[10]], axis=1)
    return (
        layer_out[None],
        tokens_grad[None],
        results[0],
        w_in_grad,
        results[1],
        results[2],
        results[3],
        results[4],
        results[5],
        results[6],
        results[7],
        w_out_grad,
        results[8],
        results[9],
        w_shared_grad,
        w_shared_down_grad,
        experts_grad,
        experts_down_grad,
    )


def solution(mesh):
    placed = (
        P("shard", "seq", None),
        P("shard", "seq", None),
        P("shard", None),
        P("shard", None),
        P("shard", "seq", None),
        P("shard"),
        P("shard", None),
        P("shard", None),
        P("shard", None),
        P("shard"),
        P("shard"),
        P("shard"),
        P("shard"),
        P("shard"),
        P("shard", None),
        P("shard"),
        P("shard", None),
        P("shard", None),
        P("shard", None),
        P("seq", "shard", None),
        P("seq", "shard", None),
    )
    return jax.shard_map(
        local,
        mesh=mesh,
        in_specs=placed,
        out_specs=(
            P("shard", "seq", None),
            P("shard", "seq", None),
            P("shard"),
            P("shard", None),
            P("shard", None),
            P("shard", None),
            P("shard"),
            P("shard"),
            P("shard"),
            P("shard"),
            P("shard"),
            P("shard", None),
            P("shard"),
            P("shard", None),
            P("shard", None),
            P("shard", None),
            P("seq", "shard", None),
            P("seq", "shard", None),
        ),
        check_vma=False,
    )
```

time: 3410 us -> 1660 us (0.49)
  waiting for transfers between devices: 2190 us -> 477 us
  Pallas kernels: 0 us -> 617 us
  matrix products: 308 us -> 3.12 us
  local copies, waits for them, and re-layouts: 377 us -> 133 us
  other arithmetic: 233 us -> 61.6 us
  blocking collectives: 210 us -> 312 us
    reduce_scatter x7 -> x5, waiting for transfers between devices: 1220 us -> 292 us  [the longest x1 190 us: local(): lax.psum_scatter(out_part.reshape(blocks * tok_rows, width), ('shard', 's...]
    all_gather x6, waiting for transfers between devices: 697 us -> 4.71 us  [the longest x1 4.7 us: local(): lax.all_gather(lax.psum_scatter(proj_in_grad[:, :2 * channels], 'shard',...]
    pallas_call x0 -> x16, Pallas kernels: none -> 617 us  [the longest x3 181 us: gather_rows(): pl.pallas_call(functools.partial(gather_kernel, inner), in_specs=[pl.Bloc...]
    dot_general x90 -> x0, matrix products: 223 us -> none  [the longest x18 52.4 us: stretch_step(): within = jnp.einsum('ijh,jhp->ihp', weights, xblock, precision=HIGHEST)]
    psum x2 -> x1, waiting for transfers between devices: 193 us -> 51.3 us  [local(): lax.psum(lax.psum_scatter(packed, 'shard', tiled=True), 'seq').reshape(-1)]
    all_gather x7 -> x3, blocking collectives: 162 us -> 280 us  [the longest x1 244 us: rows_to_owner(): spread = lax.all_gather(mine, 'shard').reshape(seq_devices, -1, width)]
    ppermute x0 -> x12, waiting for transfers between devices: none -> 108 us  [exchange(): received.append(lax.ppermute(pieces[shift], 'shard', pairs))]
    another operation x54 -> x8, other arithmetic: 95.9 us -> 10.1 us  [the longest x2 8.64 us: by_place(): jnp.stack(received)[lax.rem(place + inner - jnp.arange(inner), inner)]]
  transfers between devices with their start and end apart: 27 -> 28, of which waited for: 16 -> 10; matrix products, arithmetic and copies ran while one was open for 16% -> 8% of each run, Pallas kernels for 0% -> 19%
where the time goes in v1:
time: 1660 us; the launch traced here: 1650 us
  Pallas kernels  617 us (37%)
  waiting for transfers between devices  477 us (29%)
  blocking collectives  312 us (19%)
  local copies, waits for them, and re-layouts  133 us (8%)
  other arithmetic  61.6 us (4%)
  starting transfers between devices  32.3 us (2%)
    all_gather x1, blocking collectives, rows_to_owner(): spread = lax.all_gather(mine, 'shard').reshape(seq_devices, -1, width)  244 us
    reduce_scatter x1, waiting for transfers between devices, local(): lax.psum_scatter(out_part.reshape(blocks * tok_rows, width), ('shard', 's...  190 us
    pallas_call x3, Pallas kernels, gather_rows(): pl.pallas_call(functools.partial(gather_kernel, inner), in_specs=[pl.Bloc...  181 us
    pallas_call x3, Pallas kernels, reduce_rows(): pl.pallas_call(functools.partial(reduce_kernel, inner), in_specs=[pl.Bloc...  176 us
    ppermute x12, waiting for transfers between devices, exchange(): received.append(lax.ppermute(pieces[shift], 'shard', pairs))  108 us
    psum x1, waiting for transfers between devices, local(): lax.psum(lax.psum_scatter(packed, 'shard', tiled=True), 'seq').reshape(-1)  51.3 us
    reduce_scatter x1, waiting for transfers between devices, local(): lax.psum_scatter(proj_in_grad[:, :2 * channels], 'shard', tiled=True)  49.7 us
    pallas_call x1, Pallas kernels, experts(): pl.pallas_call(functools.partial(experts_kernel, count=count, top_count=t...  44.6 us
  transfers between devices with their start and end apart: 28, of which 10 were waited for; matrix products, arithmetic and copies ran while one was open for 8% of the time, Pallas kernels for 19%

profile of v1, /device:TPU:0, one launch (start us, length us, event | category | flops | bytes accessed | tf_op | source)
XLA Modules:
  0.0 1651.5 jit_solution(10354434951439418260)
XLA Ops:
  39.4 24.4 %gather_rows.3 = bf16[1,8,192,1536]{3,2,1,0:T(8,128)(2,1)} custom-call(bf16[192,1536]{1,0:T(8,128)(2,1)} %bitcast.153), custom_call_target="tpu_custom_call" | custom-call | tf_op jit(solution)/shard_map/gather_rows/pallas_call | solution.py:580
  66.8 243.8 %all-gather.2 = bf16[8,1,16,1536]{3,2,1,0:T(8,128)(2,1)} all-gather(bf16[2,1,16,1536]{3,2,1,0:T(8,128)(2,1)S(1)} %constant_dynamic-slice_fusion), channel_id=4, replica_groups=mesh['seq'=8,'shard'=4] {'shard'}, dimensions={0}, use_global_device_ids=true | all-gather | bytes 491520 | tf_op jit(solution)/shard_map/all_gather | solution.py:1292
  311.3 24.8 %all_gather.51.up_ref = bf16[1536,256]{1,0:T(8,128)(2,1)} all-gather(bf16[384,256]{1,0:T(8,128)(2,1)S(1)} %pad_maximum_fusion.3), channel_id=1, replica_groups=mesh['seq'=8,'shard'=4] {'shard'}, dimensions={0}, use_global_device_ids=true | all-gather | bytes 983040 | tf_op jit(solution)/shard_map/all_gather | solution.py:1423
  359.1 24.8 %scan_forward.1 = (bf16[1536,384]{1,0:T(8,128)(2,1)}, bf16[1536,768]{1,0:T(8,128)(2,1)}, f32[6,384,128]{2,1,0:T(8,128)}) custom-call(s32[4]{0:T(128)} %bitcast.172, s32[1,1536]{1,0:T(1,128)} %deal_ref.3, bf16[1536,768]{1,0:T(8,128)(2,1)} %get-tuple-element.52.rows_ref, f32[8,640]{1,0:T(8,128)} %fusion.21.conv_ref, f32[8,128]{1,0:T(8,128)} %select_maximum_fusion.head_ref), custom_call_target="tpu_custom_call" | custom-call | tf_op jit(solution)/shard_map/scan_forward/pallas_call | solution.py:222
  397.5 49.3 %reduce_rows.3 = f32[192,1664]{1,0:T(8,128)} custom-call(bf16[1,8,192,1664]{3,2,1,0:T(8,128)(2,1)} %bitcast.141), custom_call_target="tpu_custom_call" | custom-call | tf_op jit(solution)/shard_map/reduce_rows/pallas_call | solution.py:757
  456.7 131.4 %gather_rows.4 = bf16[4,8,192,1664]{3,2,1,0:T(8,128)(2,1)} custom-call(bf16[192,1664]{1,0:T(8,128)(2,1)} %concatenate.41.x_ref), custom_call_target="tpu_custom_call" | custom-call | tf_op jit(solution)/shard_map/gather_rows/pallas_call | solution.py:580
  598.1 18.8 %shared_expert.1 = (bf16[8,192,1536]{2,1,0:T(8,128)(2,1)}, bf16[8,192,1536]{2,1,0:T(8,128)(2,1)}, bf16[1536,256]{1,0:T(8,128)(2,1)}, bf16[128,1536]{1,0:T(8,128)(2,1)}) custom-call(bf16[8,192,1664]{2,1,0:T(8,128)(2,1)} %constant_dynamic-slice_fusion.4.rows_ref, bf16[8,192,1536]{2,1,0:T(8,128)(2,1)} %constant_dynamic-slice_fusion.3.grad_ref, ...), custom_call_target="tpu_custom_call" | custom-call | tf_op jit(solution)/shard_map/shared_expert/pallas_call | solution.py:1001
  616.9 37.5 %dispatch.1 = (bf16[2,1024,1664]{2,1,0:T(8,128)(2,1)}, bf16[2,1024,1536]{2,1,0:T(8,128)(2,1)}, bf16[32,192,128]{2,1,0:T(8,128)(2,1)}) custom-call(s32[1]{0:T(128)} %bitcast.14.first_ref, bf16[32,192,1664]{2,1,0:T(8,128)(2,1)} %bitcast.140, bf16[32,192,1536]{2,1,0:T(8,128)(2,1)} %all-gather.14.cloned.1.call-done.grad_ref), custom_call_target="tpu_custom_call" | custom-call | tf_op jit(solution)/shard_map/dispatch/pallas_call | solution.py:1054
  655.3 44.6 %experts.1 = (bf16[2,1024,1536]{2,1,0:T(8,128)(2,1)}, bf16[2,1024,1664]{2,1,0:T(8,128)(2,1)}, bf16[2,384,1024]{2,1,0:T(8,128)(2,1)}, bf16[2,384,1024]{2,1,0:T(8,...) custom-call(s32[1]{0:T(128)} %bitcast.14.first_ref, ...), custom_call_target="tpu_custom_call" | custom-call | tf_op jit(solution)/shard_map/experts/pallas_call | solution.py:1200
  699.9 37.4 %combine.1 = (bf16[32,192,1536]{2,1,0:T(8,128)(2,1)}, bf16[32,192,1664]{2,1,0:T(8,128)(2,1)}) custom-call(s32[1]{0:T(128)} %bitcast.13.place_ref, bf16[32,192,128]{2,1,0:T(8,128)(2,1)} %get-tuple-element.55.picks_ref, bf16[2,1024,1536]{2,1,0:T(8,128)(2,1)} %get-tuple-element.58.res_ref, bf16[2,1024,1664]{2,1,0:T(8,128)(2,1)} %get-tuple-element.59.dx_ref, ...), custom_call_target="tpu_custom_call" | custom-call | tf_op jit(solution)/shard_map/combine/pallas_call | solution.py:1250
  737.3 100.6 %reduce_rows.4 = f32[192,1664]{1,0:T(8,128)} custom-call(bf16[4,8,192,1664]{3,2,1,0:T(8,128)(2,1)} %bitcast.142), custom_call_target="tpu_custom_call" | custom-call | tf_op jit(solution)/shard_map/reduce_rows/pallas_call | solution.py:757
  844.0 25.6 %gather_rows.5 = bf16[1,8,192,1664]{3,2,1,0:T(8,128)(2,1)} custom-call(bf16[192,1664]{1,0:T(8,128)(2,1)} %pad_maximum_fusion.2.x_ref), custom_call_target="tpu_custom_call" | custom-call | tf_op jit(solution)/shard_map/gather_rows/pallas_call | solution.py:580
  881.8 39.4 %scan_backward.1 = (bf16[1536,768]{1,0:T(8,128)(2,1)}, f32[8,640]{1,0:T(8,128)}, f32[8,128]{1,0:T(8,128)}) custom-call(s32[4]{0:T(128)} %bitcast.173, s32[1,1536]{1,0:T(1,128)} %deal_ref.3, bf16[1536,768]{1,0:T(8,128)(2,1)} %get-tuple-element.65.seq_ref, f32[6,384,128]{2,1,0:T(8,128)} %get-tuple-element.66.states_ref, ...), custom_call_target="tpu_custom_call" | custom-call | tf_op jit(solution)/shard_map/scan_backward/pallas_call | solution.py:389
  922.2 24.6 %project_back.1 = (bf16[8,192,1536]{2,1,0:T(8,128)(2,1)}, bf16[1536,1152]{1,0:T(8,128)(2,1)}) custom-call(bf16[1536,384]{1,0:T(8,128)(2,1)} %get-tuple-element.64.dgate_ref, bf16[1536,768]{1,0:T(8,128)(2,1)} %get-tuple-element.68.drows_ref, bf16[1536,1536]{1,0:T(8,128)(2,1)} %get-tuple-element.69.hidden_ref, ...), custom_call_target="tpu_custom_call" | custom-call | tf_op jit(solution)/shard_map/project_back/pallas_call | solution.py:938
  949.0 25.7 %reduce_rows.5 = f32[192,1536]{1,0:T(8,128)} custom-call(bf16[1,8,192,1536]{3,2,1,0:T(8,128)(2,1)} %bitcast.154), custom_call_target="tpu_custom_call" | custom-call | tf_op jit(solution)/shard_map/reduce_rows/pallas_call | solution.py:757
  1010.8 20.6 %all_to_all.20 = bf16[8,48,1536]{2,1,0:T(8,128)(2,1)} all-to-all(bf16[8,48,1536]{2,1,0:T(8,128)(2,1)S(1)} %bitcast.160), channel_id=1, replica_groups=mesh['seq'=8,'shard'=4] {'seq'}, dimensions={0} | all-to-all | bytes 2359296 | tf_op jit(solution)/shard_map/all_to_all | solution.py:1309
  1047.2 19.3 %all-reduce.12.cloned.1.call-done = bf16[4,147044]{1,0:T(4,128)(2,1)} async-done(((bf16[4,147044]{1,0:T(4,128)(2,1)}), bf16[4,147044]{1,0:T(4,128)(2,1)}) %all-reduce.12.cloned.1.call-update) | async-done | bytes 1176368
  1069.6 22.0 %reduce-scatter.12.cloned.1.call-done = bf16[384,256]{1,0:T(8,128)(2,1)} async-done(((bf16[1536,256]{1,0:T(8,128)(2,1)}), bf16[384,256]{1,0:T(8,128)(2,1)}) %reduce-scatter.12.cloned.1.call-update) | async-done | bytes 196624 | tf_op jit(solution)/shard_map/reduce_scatter | solution.py:1630
  1091.7 30.8 %reduce-scatter.10.cloned.1.call-done = bf16[1,96,1536]{2,1,0:T(8,128)(2,1)} async-done(((bf16[4,96,1536]{2,1,0:T(8,128)(2,1)}), bf16[1,96,1536]{2,1,0:T(8,128)(2,1)}) %reduce-scatter.10.cloned.1.call-update) | async-done | bytes 294928 | tf_op jit(solution)/shard_map/reduce_scatter | solution.py:1310
  1122.6 49.7 %reduce-scatter.8.cloned.1.call-done = bf16[384,768]{1,0:T(8,128)(2,1)} async-done(((bf16[1536,768]{1,0:T(8,128)(2,1)}), bf16[384,768]{1,0:T(8,128)(2,1)}) %reduce-scatter.8.cloned.1.call-update) | async-done | bytes 589840 | tf_op jit(solution)/shard_map/reduce_scatter | solution.py:1622
  1203.5 46.8 %collective-permute-done.10 = bf16[2,128,1536]{2,1,0:T(8,128)(2,1)S(1)} collective-permute-done((bf16[2,128,1536]{2,1,0:T(8,128)(2,1)}, bf16[2,128,1536]{2,1,0:T(8,128)(2,1)S(1)}, u32[]{:S(2)}, u32[]{:S(2)}) %collective-permute-start.10) | collective-permute-done | bytes 786464 | tf_op jit(solution)/shard_map/ppermute | solution.py:1335
  1275.4 51.3 %all-reduce.8.cloned.1.call-done = bf16[1,147044]{1,0:T(2,128)(2,1)} async-done(((bf16[1,147044]{1,0:T(2,128)(2,1)}), bf16[1,147044]{1,0:T(2,128)(2,1)}) %all-reduce.8.cloned.1.call-update) | async-done | bytes 294104 | tf_op jit(solution)/shard_map/psum | solution.py:1667
  1340.2 44.3 %collective-permute-done.7 = bf16[2,384,1024]{2,1,0:T(8,128)(2,1)} collective-permute-done((bf16[2,384,1024]{2,1,0:T(8,128)(2,1)}, bf16[2,384,1024]{2,1,0:T(8,128)(2,1)}, u32[]{:S(2)}, u32[]{:S(2)}) %collective-permute-start.7) | collective-permute-done | bytes 1572896 | tf_op jit(solution)/shard_map/ppermute | solution.py:1335
  1450.7 189.9 %reduce-scatter.6.cloned.1.call-done = bf16[192,1536]{1,0:T(8,128)(2,1)} async-done(((bf16[6144,1536]{1,0:T(8,128)(2,1)}), bf16[192,1536]{1,0:T(8,128)(2,1)}) %reduce-scatter.6.cloned.1.call-update) | async-done | bytes 589840 | tf_op jit(solution)/shard_map/reduce_scatter | solution.py:1536
  (306 shorter events, 308.0 us)
Async XLA Ops:
  7.2 328.9 %all-reduce.10.cloned.1.call-start = ((), (), s32[]{:S(2)}) async-start(), calls=%async_computation.21 | async-start | bytes 487424
  17.9 319.8 %all-gather.18.cloned.1.call-start = ((), (), s32[]{:S(2)}) async-start(), calls=%async_computation.18 | async-start | bytes 1474560 | tf_op jit(solution)/shard_map/all_gather | solution.py:1292
  18.7 329.1 %all-gather.12.cloned.1.call-start = ((), (), s32[]{:S(2)}) async-start(), calls=%async_computation.9 | async-start | bytes 4423680 | tf_op jit(solution)/shard_map/all_gather | solution.py:1421
  22.0 571.3 %all-gather.14.cloned.1.call-start = ((), (), s32[]{:S(2)}) async-start(), calls=%async_computation.10 | async-start | bytes 19464192 | tf_op jit(solution)/shard_map/all_gather | solution.py:1436
  28.8 625.6 %collective-permute-start = (bf16[2,384,1024]{2,1,0:T(8,128)(2,1)}, bf16[2,384,1024]{2,1,0:T(8,128)(2,1)}, u32[]{:S(2)}, u32[]{:S(2)}) collective-permute-start(bf16[2,384,1024]{2,1,0:T(8,128)(2,1)} %get-tuple-element.172), channel_id=1, source_target_pairs={{0,1},{1,2},{2,3},{3,0},{4,5},{5,6},{6,7},{7,4},{8,9},{9,10},{10,1... | collective-permute-start | bytes 4718600 | tf_op jit(solution)/shard_map/ppermute | solution.py:1335
  31.9 622.5 %collective-permute-start.1 = (bf16[2,384,1024]{2,1,0:T(8,128)(2,1)}, bf16[2,384,1024]{2,1,0:T(8,128)(2,1)}, u32[]{:S(2)}, u32[]{:S(2)}) collective-permute-start(bf16[2,384,1024]{2,1,0:T(8,128)(2,1)} %get-tuple-element.174), channel_id=1, source_target_pairs={{0,2},{1,3},{2,0},{3,1},{4,6},{5,7},{6,4},{7,5},{8,10},{9,11},{10,... | collective-permute-start | bytes 4718600 | tf_op jit(solution)/shard_map/ppermute | solution.py:1335
  34.5 619.9 %collective-permute-start.2 = (bf16[2,384,1024]{2,1,0:T(8,128)(2,1)}, bf16[2,384,1024]{2,1,0:T(8,128)(2,1)}, u32[]{:S(2)}, u32[]{:S(2)}) collective-permute-start(bf16[2,384,1024]{2,1,0:T(8,128)(2,1)} %get-tuple-element.171), channel_id=1, source_target_pairs={{0,3},{1,0},{2,1},{3,2},{4,7},{5,4},{6,5},{7,6},{8,11},{9,8},{10,9... | collective-permute-start | bytes 4718600 | tf_op jit(solution)/shard_map/ppermute | solution.py:1335
  37.6 414.4 %collective-permute-start.3 = (bf16[2,128,1536]{2,1,0:T(8,128)(2,1)}, bf16[2,128,1536]{2,1,0:T(8,128)(2,1)}, u32[]{:S(2)}, u32[]{:S(2)}) collective-permute-start(bf16[2,128,1536]{2,1,0:T(8,128)(2,1)} %get-tuple-element.178), channel_id=1, source_target_pairs={{0,1},{1,2},{2,3},{3,0},{4,5},{5,6},{6,7},{7,4},{8,9},{9,10},{10,1... | collective-permute-start | bytes 2359304 | tf_op jit(solution)/shard_map/ppermute | solution.py:1335
  38.3 616.1 %collective-permute-start.4 = (bf16[2,128,1536]{2,1,0:T(8,128)(2,1)}, bf16[2,128,1536]{2,1,0:T(8,128)(2,1)}, u32[]{:S(2)}, u32[]{:S(2)}) collective-permute-start(bf16[2,128,1536]{2,1,0:T(8,128)(2,1)} %get-tuple-element.180), channel_id=1, source_target_pairs={{0,2},{1,3},{2,0},{3,1},{4,6},{5,7},{6,4},{7,5},{8,10},{9,11},{10,... | collective-permute-start | bytes 2359304 | tf_op jit(solution)/shard_map/ppermute | solution.py:1335
  383.9 214.2 %all-to-all-start.1 = ((bf16[8,16,1536]{2,1,0:T(8,128)(2,1)}), bf16[8,16,1536]{2,1,0:T(8,128)(2,1)}, u32[]{:S(2)}, u32[]{:S(2)}) async-start(bf16[8,16,1536]{2,1,0:T(8,128)(2,1)} %bitcast.20), calls=%async_computation.1 | async-start | bytes 786432 | tf_op jit(solution)/shard_map/all_to_all | solution.py:1294
  388.1 678.4 %all-reduce.12.cloned.1.call-start = ((), (), s32[]{:S(2)}) async-start(), calls=%async_computation.22 | async-start | bytes 2353152
  452.0 202.4 %collective-permute-start.5 = (bf16[2,128,1536]{2,1,0:T(8,128)(2,1)}, bf16[2,128,1536]{2,1,0:T(8,128)(2,1)S(1)}, u32[]{:S(2)}, u32[]{:S(2)}) collective-permute-start(bf16[2,128,1536]{2,1,0:T(8,128)(2,1)} %get-tuple-element.177), channel_id=1, source_target_pairs={{0,3},{1,0},{2,1},{3,2},{4,7},{5,4},{6,5},{7,6},{8,11},{9,8},{10,9... | collective-permute-start | bytes 2359304 | tf_op jit(solution)/shard_map/ppermute | solution.py:1335
  1010.2 81.4 %reduce-scatter.12.cloned.1.call-start = ((), (), s32[]{:S(2)}) async-start(), calls=%async_computation.16 | async-start | bytes 983040 | tf_op jit(solution)/shard_map/reduce_scatter | solution.py:1630
  1010.7 111.8 %reduce-scatter.10.cloned.1.call-start = ((), (), s32[]{:S(2)}) async-start(), calls=%async_computation.14 | async-start | bytes 1474560 | tf_op jit(solution)/shard_map/reduce_scatter | solution.py:1310
  1031.5 140.8 %reduce-scatter.8.cloned.1.call-start = ((), (), s32[]{:S(2)}) async-start(), calls=%async_computation.13 | async-start | bytes 2949120 | tf_op jit(solution)/shard_map/reduce_scatter | solution.py:1622
  1034.8 228.3 %reduce-scatter.14.cloned.1.call-start = ((), (), s32[]{:S(2)}) async-start(), calls=%async_computation.17 | async-start | bytes 491520 | tf_op jit(solution)/shard_map/reduce_scatter | solution.py:1310
  1047.2 279.5 %all-reduce.8.cloned.1.call-start = ((), (), s32[]{:S(2)}) async-start(), calls=%async_computation.12 | async-start | bytes 1176576 | tf_op jit(solution)/shard_map/psum | solution.py:1667
  1069.6 336.4 %all-gather.22.cloned.1.call-start = ((), (), s32[]{:S(2)}) async-start(), calls=%async_computation.20 | async-start | bytes 1769472 | tf_op jit(solution)/shard_map/all_gather | solution.py:1629
  1091.6 325.5 %all-gather.16.cloned.1.call-start = ((), (), s32[]{:S(2)}) async-start(), calls=%async_computation.15 | async-start | bytes 2654208 | tf_op jit(solution)/shard_map/all_gather | solution.py:1313
  1122.5 303.8 %all-gather.20.cloned.1.call-start = ((), (), s32[]{:S(2)}) async-start(), calls=%async_computation.19 | async-start | bytes 5308416 | tf_op jit(solution)/shard_map/all_gather | solution.py:1621
  1172.3 468.3 %reduce-scatter.6.cloned.1.call-start = ((), (), s32[]{:S(2)}) async-start(), calls=%async_computation.11 | async-start | bytes 19464192 | tf_op jit(solution)/shard_map/reduce_scatter | solution.py:1536
  1177.5 162.7 %collective-permute-start.8 = (bf16[2,384,1024]{2,1,0:T(8,128)(2,1)}, bf16[2,384,1024]{2,1,0:T(8,128)(2,1)}, u32[]{:S(2)}, u32[]{:S(2)}) collective-permute-start(bf16[2,384,1024]{2,1,0:T(8,128)(2,1)} %get-tuple-element.81), channel_id=1, source_target_pairs={{0,3},{1,0},{2,1},{3,2},{4,7},{5,4},{6,5},{7,6},{8,11},{9,8},{10,9... | collective-permute-start | bytes 4718600 | tf_op jit(solution)/shard_map/ppermute | solution.py:1335
  1179.4 205.1 %collective-permute-start.7 = (bf16[2,384,1024]{2,1,0:T(8,128)(2,1)}, bf16[2,384,1024]{2,1,0:T(8,128)(2,1)}, u32[]{:S(2)}, u32[]{:S(2)}) collective-permute-start(bf16[2,384,1024]{2,1,0:T(8,128)(2,1)} %get-tuple-element.80), channel_id=1, source_target_pairs={{0,2},{1,3},{2,0},{3,1},{4,6},{5,7},{6,4},{7,5},{8,10},{9,11},{10,... | collective-permute-start | bytes 4718600 | tf_op jit(solution)/shard_map/ppermute | solution.py:1335
  1198.0 186.5 %collective-permute-start.6 = (bf16[2,384,1024]{2,1,0:T(8,128)(2,1)}, bf16[2,384,1024]{2,1,0:T(8,128)(2,1)}, u32[]{:S(2)}, u32[]{:S(2)}) collective-permute-start(bf16[2,384,1024]{2,1,0:T(8,128)(2,1)} %get-tuple-element.79), channel_id=1, source_target_pairs={{0,1},{1,2},{2,3},{3,0},{4,5},{5,6},{6,7},{7,4},{8,9},{9,10},{10,1... | collective-permute-start | bytes 4718600 | tf_op jit(solution)/shard_map/ppermute | solution.py:1335
  (37 other events, 629.9 us)
Sparse Core Ops, SparseCore 0:
  18.0 140.8 all-reduce.9
  161.2 44.7 all-gather.17
  208.2 96.9 all-gather.11
  308.4 171.5 all-gather.13
  1010.3 56.1 all-reduce.11
  1068.7 22.8 reduce-scatter.11
  1094.0 28.4 reduce-scatter.9
  1125.5 46.7 reduce-scatter.7
  1174.7 61.9 reduce-scatter.13
  1240.2 86.4 all-reduce.7
  1328.7 25.6 all-gather.21
  1356.3 29.0 all-gather.15
  1387.4 38.9 all-gather.19
  1433.8 206.7 reduce-scatter.5

commit v2 on v1

--- a/solution.py
+++ b/solution.py
@@ -43,6 +43,10 @@
 
 LANES = 128
 VMEM_BYTES = 56 * 1024 * 1024
+
+
+def cost_of(micros):
+    return pl.CostEstimate(flops=0, transcendentals=0, bytes_accessed=int(micros * 3.6e6))
 
 
 def dot_rows(left_side, right_side, precision=None):
@@ -214,13 +218,13 @@
         y_ref[...] = to_low(total[...])
 
 
-def scan_forward(ends, deal_row, rows, conv_table, head_table, channels):
+def scan_forward(ends, deal_row, rows, conv_table, head_table, channels, freight):
     group_rows, width = rows.shape
     steps = group_rows // STRETCH
     state_rows = (channels, LANES)
-    whole = lambda shape: pl.BlockSpec(shape, lambda step: (0,) * len(shape))
-    return pl.pallas_call(
+    return run(
         scan_forward_kernel,
+        (ends, deal_row, rows, conv_table, head_table),
         grid=(steps,),
         in_specs=[
             pl.BlockSpec(memory_space=pltpu.SMEM),
@@ -239,14 +243,15 @@
             jax.ShapeDtypeStruct((group_rows, width), jnp.bfloat16),
             jax.ShapeDtypeStruct((steps,) + state_rows, jnp.float32),
         ],
-        scratch_shapes=[
+        scratch=[
             pltpu.VMEM((8, width), jnp.float32),
             pltpu.VMEM(state_rows, jnp.float32),
             pltpu.VMEM((group_rows, channels), jnp.float32),
         ],
-        compiler_params=pltpu.CompilerParams(vmem_limit_bytes=VMEM_BYTES),
+        freight=freight,
+        micros=25,
         name="scan_forward",
-    )(ends, deal_row, rows, conv_table, head_table)
+    )
 
 
 def scan_backward_kernel(
@@ -381,13 +386,13 @@
         drows_ref[...] = to_low(total[...])
 
 
-def scan_backward(ends, deal_row, seq_rows, states, dy, conv_table, head_table):
+def scan_backward(ends, deal_row, seq_rows, states, dy, conv_table, head_table, freight):
     group_rows, width = seq_rows.shape
     channels = dy.shape[1]
     steps = group_rows // STRETCH
-    whole = lambda shape: pl.BlockSpec(shape, lambda step: (0,) * len(shape))
-    return pl.pallas_call(
+    return run(
         scan_backward_kernel,
+        (ends, deal_row, seq_rows, states, dy, conv_table, head_table),
         grid=(steps,),
         in_specs=[
             pl.BlockSpec(memory_space=pltpu.SMEM),
@@ -408,14 +413,19 @@
             jax.ShapeDtypeStruct(conv_table.shape, jnp.float32),
             jax.ShapeDtypeStruct(head_table.shape, jnp.float32),
         ],
-        scratch_shapes=[
+        scratch=[
             pltpu.VMEM((8, conv_table.shape[1]), jnp.float32),
             pltpu.VMEM((channels, LANES), jnp.float32),
             pltpu.VMEM((group_rows, width), jnp.float32),
         ],
-        compiler_params=pltpu.CompilerParams(vmem_limit_bytes=VMEM_BYTES),
+        freight=freight,
+        micros=40,
         name="scan_backward",
-    )(ends, deal_row, seq_rows, states, dy, conv_table, head_table)
+    )
+
+
+def whole(shape):
+    return pl.BlockSpec(shape, lambda *steps: (0,) * len(shape))
 
 
 MESH = pl.DeviceIdType.MESH
@@ -445,11 +455,11 @@
     return [lax.rem(place + shift, inner) for shift in range(1, inner)]
 
 
-def greet(inner):
+def greet(flips, inner):
     barrier = pltpu.get_barrier_semaphore()
     part = lax.axis_index("seq")
     place, first = own_shard_group(inner)
-    for flip in FLIPS:
+    for flip in flips:
         pl.semaphore_signal(
             barrier, inc=1, device_id={"seq": flipped(part, flip)}, device_id_type=MESH
         )
@@ -457,7 +467,162 @@
         pl.semaphore_signal(
             barrier, inc=1, device_id={"shard": first + peer}, device_id_type=MESH
         )
-    pl.semaphore_wait(barrier, len(FLIPS) + inner - 1)
+    pl.semaphore_wait(barrier, len(flips) + inner - 1)
+
+
+class Parcel:
+    flips = ()
+
+    def __init__(self, array, shift, inner):
+        self.array, self.shift, self.inner = array, shift, inner
+        self.sems = 1
+
+    def moves(self, source, target):
+        place, first = own_shard_group(self.inner)
+        to = lax.rem(place + self.shift, self.inner)
+        return [(source, target, target, {"shard": first + to})]
+
+    def stays(self, source, target):
+        return []
+
+
+class PlaneSwap:
+    flips = (1, 2, 3, 4, 5, 6, 7)
+    inner = 1
+    sems = 8
+
+    def __init__(self, array):
+        self.array = array
+
+    def moves(self, source, target):
+        part = lax.axis_index("seq")
+        return [
+            (
+                source.at[flipped(part, flip)],
+                target.at[part],
+                target.at[flipped(part, flip)],
+                {"seq": flipped(part, flip)},
+            )
+            for flip in self.flips
+        ]
+
+    def stays(self, source, target):
+        part = lax.axis_index("seq")
+        return [(source.at[part], target.at[part])]
+
+
+COLLECTIVES = []
+
+
+def run(
+    kernel,
+    args,
+    *,
+    in_specs,
+    out_specs,
+    out_shape,
+    name,
+    micros,
+    grid=(),
+    scratch=(),
+    freight=(),
+    flips=(),
+    inner=1,
+):
+    freight = list(freight)
+    flips = tuple(sorted(set(flips).union(*[item.flips for item in freight])))
+    inner = max([inner] + [item.inner for item in freight])
+    talks = bool(flips) or inner > 1
+    count_in, count_out, count_scratch = len(args), len(out_shape), len(scratch)
+    count = len(freight)
+
+    def wrapped(*refs):
+        ins, refs = refs[:count_in], refs[count_in:]
+        sources, refs = refs[:count], refs[count:]
+        outs, refs = refs[:count_out], refs[count_out:]
+        targets, refs = refs[:count], refs[count:]
+        own, refs = refs[:count_scratch], refs[count_scratch:]
+
+        def remote(item, place, order, source, target, device):
+            send, recv = refs[3 * place : 3 * place + 2]
+            return pltpu.make_async_remote_copy(
+                src_ref=source,
+                dst_ref=target,
+                send_sem=send.at[order],
+                recv_sem=recv.at[order],
+                device_id=device,
+                device_id_type=MESH,
+            )
+
+        def moves():
+            for place, item in enumerate(freight):
+                for order, move in enumerate(item.moves(sources[place], targets[place])):
+                    yield item, place, order, move
+
+        def stays():
+            for place, item in enumerate(freight):
+                for source, target in item.stays(sources[place], targets[place]):
+                    yield pltpu.make_async_copy(source, target, refs[3 * place + 2])
+
+        def depart():
+            if talks:
+                greet(flips, inner)
+            for item, place, order, (source, target, _, device) in moves():
+                remote(item, place, order, source, target, device).start()
+            for copy in stays():
+                copy.start()
+
+        def arrive():
+            for item, place, order, (source, target, arrival, device) in moves():
+                remote(item, place, order, source, arrival, device).wait_recv()
+                remote(item, place, order, source, target, device).wait_send()
+            for copy in stays():
+                copy.wait()
+
+        if grid:
+            at = [pl.program_id(axis) for axis in range(len(grid))]
+            first, last = at[0] == 0, at[0] == grid[0] - 1
+            for axis in range(1, len(grid)):
+                first = first & (at[axis] == 0)
+                last = last & (at[axis] == grid[axis] - 1)
+            if talks:
+                pl.when(first)(depart)
+            kernel(*ins, *outs, *own)
+            if talks:
+                pl.when(last)(arrive)
+        else:
+            depart()
+            kernel(*ins, *outs, *own)
+            arrive()
+
+    anywhere = pl.BlockSpec(memory_space=pl.ANY)
+    extra = {}
+    if talks:
+        COLLECTIVES.append(name)
+        extra = dict(collective_id=len(COLLECTIVES), has_side_effects=True)
+    sems = []
+    for item in freight:
+        sems += [
+            pltpu.SemaphoreType.DMA((item.sems,)),
+            pltpu.SemaphoreType.DMA((item.sems,)),
+            pltpu.SemaphoreType.DMA(()),
+        ]
+    results = pl.pallas_call(
+        wrapped,
+        grid=grid,
+        in_specs=list(in_specs) + [anywhere] * count,
+        out_specs=list(out_specs) + [anywhere] * count,
+        out_shape=list(out_shape)
+        + [jax.ShapeDtypeStruct(item.array.shape, item.array.dtype) for item in freight],
+        scratch_shapes=list(scratch) + sems,
+        compiler_params=pltpu.CompilerParams(vmem_limit_bytes=VMEM_BYTES, **extra),
+        cost_estimate=cost_of(micros),
+        name=name,
+    )(*args, *[item.array for item in freight])
+    results = list(results)
+    if freight:
+        return results[:count_out] + [results[count_out:]]
+    return results
 
 
 def gather_kernel(inner, x_ref, out_ref, own_sem, zsend, zrecv, send, recv):
@@ -468,7 +633,6 @@
     spans = [pl.ds(0, half), pl.ds(half, half)]
     others = peers_in_order(place, inner)
     sources = [place] + others
-    greet(inner)
     own = pltpu.make_async_copy(x_ref, out_ref.at[place, part], own_sem)
     own.start()
     across = []
@@ -574,30 +738,33 @@
     own.wait()
 
 
-def gather_rows(x, inner, collective):
+def gather_rows(x, inner, freight=()):
     rows, width = x.shape
     seq_devices = lax.axis_size("seq")
-    return pl.pallas_call(
+    return run(
         functools.partial(gather_kernel, inner),
+        (x,),
         in_specs=[pl.BlockSpec(memory_space=pl.ANY)],
-        out_specs=pl.BlockSpec(memory_space=pl.ANY),
-        out_shape=jax.ShapeDtypeStruct((inner, seq_devices, rows, width), x.dtype),
-        scratch_shapes=[
+        out_specs=[pl.BlockSpec(memory_space=pl.ANY)],
+        out_shape=[jax.ShapeDtypeStruct((inner, seq_devices, rows, width), x.dtype)],
+        scratch=[
             pltpu.SemaphoreType.DMA(()),
             pltpu.SemaphoreType.DMA((max(1, inner - 1),)),
             pltpu.SemaphoreType.DMA((inner,)),
             pltpu.SemaphoreType.DMA((inner, 14)),
             pltpu.SemaphoreType.DMA((inner, 14)),
         ],
-        compiler_params=pltpu.CompilerParams(collective_id=collective, has_side_effects=True),
+        freight=freight,
+        flips=FLIPS,
+        inner=inner,
+        micros=25 * inner,
         name="gather_rows",
-    )(x)
-
-
-def reduce_kernel(
+    )
+
+
+def reduce_body(
     inner,
     p_ref,
-    out_ref,
     held,
     paired,
     turned,
@@ -616,12 +783,11 @@
 ):
     part = lax.axis_index("seq")
     place, first = own_shard_group(inner)
-    rows = out_ref.shape[0]
+    rows = held.shape[2]
     half = rows // 2
     spans = [pl.ds(0, half), pl.ds(half, half)]
     targets = list(reversed(peers_in_order(place, inner))) + [place]
     evens = (6, 2, 4, 0)
-    greet(inner)
     loads, cores = {}, {}
     for order, target in enumerate(targets):
         for slot, flip in enumerate(evens):
@@ -741,84 +907,487 @@
         )
         arrive.wait_recv()
         total = total + to_full(summed[peer])
-    out_ref[...] = total
     for copy in sends:
         copy.wait_send()
     for copy in cores.values():
         copy.wait_send()
     for copy in across:
         copy.wait_send()
-
-
-def reduce_rows(partial, collective):
-    inner, seq_devices, rows, width = partial.shape
+    return total
+
+
+def reduce_scratch(inner, rows, width):
     low = jnp.bfloat16
     sems = lambda *shape: pltpu.SemaphoreType.DMA(shape)
+    return [
+        pltpu.VMEM((inner, 4, rows, width), low),
+        pltpu.VMEM((inner, 4, rows, width), low),
+        pltpu.VMEM((inner, 2, rows // 2, width), low),
+        pltpu.VMEM((inner, 4, rows // 2, width), low),
+        pltpu.VMEM((max(1, inner - 1), rows, width), low),
+        pltpu.VMEM((inner, rows, width), low),
+        sems(inner, 4),
+        sems(inner, 4),
+        sems(inner, 4),
+        sems(inner, 2),
+        sems(inner, 2),
+        sems(inner, 4),
+        sems(inner, 4),
+        sems(max(1, inner - 1)),
+        sems(inner),
+    ]
+
+
+def reduce_kernel(inner, p_ref, out_ref, *scratch):
+    out_ref[...] = reduce_body(inner, p_ref, *scratch)
+
+
+def reduce_rows(partial, freight=()):
+    inner, _, rows, width = partial.shape
+    return run(
+        functools.partial(reduce_kernel, inner),
+        (partial,),
+        in_specs=[pl.BlockSpec(memory_space=pl.ANY)],
+        out_specs=[pl.BlockSpec(memory_space=pltpu.VMEM)],
+        out_shape=[jax.ShapeDtypeStruct((rows, width), jnp.float32)],
+        scratch=reduce_scratch(inner, rows, width),
+        freight=freight,
+        flips=FLIPS,
+        inner=inner,
+        micros=25 * inner,
+        name="reduce_rows",
+    )
+
+
+def plane_gather(own, target, send, recv):
+    part = lax.axis_index("seq")
+    half = own.shape[0] // 2
+    spans = [pl.ds(0, half), pl.ds(half, half)]
+    started = []
+
+    def copy_of(kind, block, span, flip, from_own=False):
+        place = target(block).at[spans[span]]
+        return pltpu.make_async_remote_copy(
+            src_ref=own.at[spans[span]] if from_own else place,
+            dst_ref=place,
+            send_sem=send.at[kind],
+            recv_sem=recv.at[kind],
+            device_id={"seq": flipped(part, flip)},
+            device_id_type=MESH,
+        )
+
+    def push(kind, block, span, flip, from_own=False):
+        copy = copy_of(kind, block, span, flip, from_own)
+        copy.start()
+        started.append(copy)
+
+    def arrived(kind, block, span, flip):
+        copy_of(kind, block, span, flip).wait_recv()
+
+    def first():
+        for kind, span, flip in (
+            (3, 1, 2), (4, 0, 4), (2, 0, 2), (5, 1, 4), (0, 0, 1), (1, 1, 1)
+        ):
+            push(kind, part, span, flip, True)
+
+    def second():
+        side, over = flipped(part, 2), flipped(part, 4)
+        arrived(3, side, 1, 2)
+        push(6, side, 1, 4)
+        arrived(4, over, 0, 4)
+        push(7, over, 0, 2)
+        push(9, side, 1, 1)
+        push(10, over, 0, 1)
+        arrived(2, side, 0, 2)
+        push(8, side, 0, 1)
+        arrived(5, over, 1, 4)
+        push(11, over, 1, 1)
+
+    def third():
+        far = flipped(part, 6)
+        arrived(6, far, 1, 4)
+        push(13, far, 1, 1)
+        arrived(7, far, 0, 2)
+        push(12, far, 0, 1)
+
+    def last():
+        for kind, flip, span in (
+            (0, 1, 0), (1, 1, 1), (9, 3, 1), (10, 5, 0), (8, 3, 0), (11, 5, 1), (13, 7, 1), (12, 7, 0)
+        ):
+            arrived(kind, flipped(part, flip), span, 1)
+        for copy in started:
+            copy.wait_send()
+
+    return first, second, third, last
+
+
+def line_gather(inner, own, target, send, recv):
+    place, first = own_shard_group(inner)
+    half = own.shape[0] // 2
+    spans = [pl.ds(0, half), pl.ds(half, half)]
+
+    def copy_of(way, step, span):
+        block = place - step if way == 0 else place + step
+        to = place + 1 if way == 0 else place - 1
+        spot = target(block).at[spans[span]]
+        return pltpu.make_async_remote_copy(
+            src_ref=own.at[spans[span]] if step == 0 else spot,
+            dst_ref=spot,
+            send_sem=send.at[way, step, span],
+            recv_sem=recv.at[way, step, span],
+            device_id={"shard": first + to},
+            device_id_type=MESH,
+        )
+
+    def sends(way, step):
+        if way == 0:
+            return (place < inner - 1) & (place >= step)
+        return (place > 0) & (place + step < inner)
+
+    def receives(way, step):
+        return place >= step if way == 0 else place + step < inner
+
+    def start(step, span):
+        for way in range(2):
+
+            @pl.when(sends(way, step))
+            def _():
+                copy_of(way, step, span).start()
+
+    def begin():
+        for span in range(2):
+            start(0, span)
+
+    def onward(step):
+        for span in range(2):
+            for way in range(2):
+
+                @pl.when(receives(way, step))
+                def _():
+                    block = place - step if way == 0 else place + step
+                    spot = target(block).at[spans[span]]
+                    pltpu.make_async_remote_copy(
+                        src_ref=spot,
+                        dst_ref=spot,
+                        send_sem=send.at[way, step - 1, span],
+                        recv_sem=recv.at[way, step - 1, span],
+                        device_id={"shard": block + first},
+                        device_id_type=MESH,
+                    ).wait_recv()
+
+            if step < inner - 1:
+                start(step, span)
+
+    def finish():
+        for step in range(inner - 1):
+            for span in range(2):
+                for way in range(2):
+
+                    @pl.when(sends(way, step))
+                    def _():
+                        copy_of(way, step, span).wait_send()
+
+    return begin, onward, finish
+
+
+def greet_line(inner):
+    barrier = pltpu.get_barrier_semaphore()
+    part = lax.axis_index("seq")
+    place, first = own_shard_group(inner)
+    for flip in FLIPS:
+        pl.semaphore_signal(
+            barrier, inc=1, device_id={"seq": flipped(part, flip)}, device_id_type=MESH
+        )
+
+    @pl.when(place > 0)
+    def _():
+        pl.semaphore_signal(
+            barrier, inc=1, device_id={"shard": first + place - 1}, device_id_type=MESH
+        )
+
+    @pl.when(place < inner - 1)
+    def _():
+        pl.semaphore_signal(
+            barrier, inc=1, device_id={"shard": first + place + 1}, device_id_type=MESH
+        )
+
+    ends = (place == 0).astype(jnp.int32) + (place == inner - 1).astype(jnp.int32)
+    pl.semaphore_wait(barrier, len(FLIPS) + 2 - ends)
+
+
+def begin_kernel(
+    inner,
+    x_ref,
+    w_ref,
+    s_ref,
+    r_ref,
+    x_out,
+    w_out,
+    s_out,
+    r_out,
+    own_sems,
+    send,
+    recv,
+    wsend,
+    wrecv,
+    ssend,
+    srecv,
+    rsend,
+    rrecv,
+):
+    part = lax.axis_index("seq")
+    place, _ = own_shard_group(inner)
+    rows = w_ref.shape[0]
+    greet_line(inner)
+    w_target = lambda p: w_out.at[pl.ds(p * rows, rows)]
+    s_target = lambda p: s_out.at[p]
+    w_begin, w_onward, w_finish = line_gather(inner, w_ref, w_target, wsend, wrecv)
+    r_target = lambda p: r_out.at[p]
+    s_begin, s_onward, s_finish = line_gather(inner, s_ref, s_target, ssend, srecv)
+    r_begin, r_onward, r_finish = line_gather(inner, r_ref, r_target, rsend, rrecv)
+    first, second, third, last = plane_gather(x_ref, lambda b: x_out.at[b], send, recv)
+    s_begin()
+    w_begin()
+    first()
+    r_begin()
+    owns = [
+        pltpu.make_async_copy(x_ref, x_out.at[part], own_sems.at[0]),
+        pltpu.make_async_copy(w_ref, w_target(place), own_sems.at[1]),
+        pltpu.make_async_copy(s_ref, s_target(place), own_sems.at[2]),
+        pltpu.make_async_copy(r_ref, r_target(place), own_sems.at[3]),
+    ]
+    for copy in owns:
+        copy.start()
+    s_onward(1)
+    w_onward(1)
+    second()
+    third()
+    for step in range(2, inner):
+        s_onward(step)
+        w_onward(step)
+        r_onward(step - 1)
+    last()
+    r_onward(inner - 1)
+    s_finish()
+    w_finish()
+    r_finish()
+    for copy in owns:
+        copy.wait()
+
+
+def begin(x, weights, small, rows, inner):
+    seq_devices = lax.axis_size("seq")
+    anywhere = pl.BlockSpec(memory_space=pl.ANY)
+    steps = inner - 1
+    sems = lambda *shape: pltpu.SemaphoreType.DMA(shape)
+    COLLECTIVES.append("begin")
     return pl.pallas_call(
-        functools.partial(reduce_kernel, inner),
-        in_specs=[pl.BlockSpec(memory_space=pl.ANY)],
-        out_specs=pl.BlockSpec(memory_space=pltpu.VMEM),
-        out_shape=jax.ShapeDtypeStruct((rows, width), jnp.float32),
+        functools.partial(begin_kernel, inner),
+        in_specs=[anywhere] * 4,
+        out_specs=[anywhere] * 4,
+        out_shape=[
+            jax.ShapeDtypeStruct((seq_devices,) + x.shape, x.dtype),
+            jax.ShapeDtypeStruct((inner * weights.shape[0], weights.shape[1]), weights.dtype),
+            jax.ShapeDtypeStruct((inner,) + small.shape, small.dtype),
+            jax.ShapeDtypeStruct((inner,) + rows.shape, rows.dtype),
+        ],
         scratch_shapes=[
-            pltpu.VMEM((inner, 4, rows, width), low),
-            pltpu.VMEM((inner, 4, rows, width), low),
-            pltpu.VMEM((inner, 2, rows // 2, width), low),
-            pltpu.VMEM((inner, 4, rows // 2, width), low),
-            pltpu.VMEM((max(1, inner - 1), rows, width), low),
-            pltpu.VMEM((inner, rows, width), low),
-            sems(inner, 4),
-            sems(inner, 4),
-            sems(inner, 4),
-            sems(inner, 2),
-            sems(inner, 2),
-            sems(inner, 4),
-            sems(inner, 4),
-            sems(max(1, inner - 1)),
+            sems(4),
+            sems(14),
+            sems(14),
+            sems(2, steps, 2),
+            sems(2, steps, 2),
+            sems(2, steps, 2),
+            sems(2, steps, 2),
+            sems(2, steps, 2),
+            sems(2, steps, 2),
+        ],
+        compiler_params=pltpu.CompilerParams(
+            collective_id=len(COLLECTIVES), has_side_effects=True
+        ),
+        cost_estimate=cost_of(60),
+        name="begin",
+    )(x, weights, small, rows)
+
+
+def sum_across(inner, part_ref, own, inbox, total_low, sems, send, recv):
+    place, first = own_shard_group(inner)
+    peers = peers_in_order(place, inner)
+    mine = pltpu.make_async_copy(part_ref.at[place], own, sems)
+    outgoing = [
+        pltpu.make_async_remote_copy(
+            src_ref=part_ref.at[peer],
+            dst_ref=inbox.at[place],
+            send_sem=send.at[order],
+            recv_sem=recv.at[place],
+            device_id={"shard": first + peer},
+            device_id_type=MESH,
+        )
+        for order, peer in enumerate(peers)
+    ]
+
+    def depart():
+        mine.start()
+        for copy in reversed(outgoing):
+            copy.start()
+
+    def arrive():
+        mine.wait()
+        total = to_full(own[...])
+        for order, peer in enumerate(peers):
+            pltpu.make_async_remote_copy(
+                src_ref=part_ref.at[peer],
+                dst_ref=inbox.at[peer],
+                send_sem=send.at[order],
+                recv_sem=recv.at[peer],
+                device_id={"shard": first + peer},
+                device_id_type=MESH,
+            ).wait_recv()
+            total = total + to_full(inbox[peer])
+        total_low[...] = to_low(total)
+
+    def finish():
+        for copy in outgoing:
+            copy.wait_send()
+
+    return depart, arrive, finish
+
+
+def settle_kernel(inner, counts, *refs):
+    part = lax.axis_index("seq")
+    hidden_ref, refs = refs[0], refs[1:]
+    parts, refs = refs[:counts], refs[counts:]
+    hidden_out, refs = refs[0], refs[1:]
+    outs, refs = refs[:counts], refs[counts:]
+    reduce_refs, refs = refs[:15], refs[15:]
+    lines, planes, owns = [], [], []
+    for index in range(counts):
+        own, inbox, low, sem, send, recv, gsend, grecv, here = refs[9 * index : 9 * index + 9]
+        lines.append(sum_across(inner, parts[index], own, inbox, low, sem, send, recv))
+        out = outs[index]
+        planes.append(plane_gather(low, lambda b, out=out: out.at[b], gsend, grecv))
+        owns.append(pltpu.make_async_copy(low, out.at[part], here))
+    for line in lines:
+        line[0]()
+    hidden_out[...] = reduce_body(1, hidden_ref, *reduce_refs)
+    for index in range(counts):
+        lines[index][1]()
+        planes[index][0]()
+        owns[index].start()
+        if index:
+            planes[index - 1][1]()
+    planes[counts - 1][1]()
+    for stage in (2, 3):
+        for plane in planes:
+            plane[stage]()
+    for index in range(counts):
+        lines[index][2]()
+        owns[index].wait()
+
+
+def settle(hidden, parts, inner):
+    _, _, rows, width = hidden.shape
+    seq_devices = lax.axis_size("seq")
+    anywhere = pl.BlockSpec(memory_space=pl.ANY)
+    low = jnp.bfloat16
+    sems = lambda *shape: pltpu.SemaphoreType.DMA(shape)
+    scratch = reduce_scratch(1, rows, width)
+    for part in parts:
+        shape = part.shape[1:]
+        scratch += [
+            pltpu.VMEM(shape, low),
+            pltpu.VMEM(part.shape, low),
+            pltpu.VMEM(shape, low),
+            sems(),
             sems(inner),
-        ],
-        compiler_params=pltpu.CompilerParams(
-            collective_id=collective, has_side_effects=True, vmem_limit_bytes=VMEM_BYTES
-        ),
-        name="reduce_rows",
-    )(partial)
-
-
-def whole(shape):
-    return pl.BlockSpec(shape, lambda *steps: (0,) * len(shape))
+            sems(inner),
+            sems(14),
+            sems(14),
+            sems(),
+        ]
+    return run(
+        functools.partial(settle_kernel, inner, len(parts)),
+        (hidden,) + tuple(parts),
+        in_specs=[anywhere] * (1 + len(parts)),
+        out_specs=[pl.BlockSpec(memory_space=pltpu.VMEM)] + [anywhere] * len(parts),
+        out_shape=[jax.ShapeDtypeStruct((rows, width), jnp.float32)]
+        + [jax.ShapeDtypeStruct((seq_devices,) + part.shape[1:], low) for part in parts],
+        scratch=scratch,
+        flips=FLIPS,
+        inner=inner,
+        micros=90,
+        name="settle",
+    )
+
+
+def sum_all_kernel(inner, p_ref, out_ref, total_low, own_sem, send, recv, *reduce_refs):
+    part = lax.axis_index("seq")
+    total_low[...] = to_low(reduce_body(inner, p_ref, *reduce_refs))
+    stages = plane_gather(total_low, lambda b: out_ref.at[b], send, recv)
+    own = pltpu.make_async_copy(total_low, out_ref.at[part], own_sem)
+    own.start()
+    for stage in stages:
+        stage()
+    own.wait()
+
+
+def sum_all(partial):
+    inner, seq_devices, rows, width = partial.shape
+    sems = lambda *shape: pltpu.SemaphoreType.DMA(shape)
+    anywhere = pl.BlockSpec(memory_space=pl.ANY)
+    return run(
+        functools.partial(sum_all_kernel, inner),
+        (partial,),
+        in_specs=[anywhere],
+        out_specs=[anywhere],
+        out_shape=[jax.ShapeDtypeStruct((seq_devices, rows, width), jnp.bfloat16)],
+        scratch=[pltpu.VMEM((rows, width), jnp.bfloat16), sems(), sems(14), sems(14)]
+        + reduce_scratch(inner, rows, width),
+        flips=FLIPS,
+        inner=inner,
+        micros=25,
+        name="sum_all",
+    )[0]
 
 
 def params_of(limit=VMEM_BYTES):
     return pltpu.CompilerParams(vmem_limit_bytes=limit)
 
 
-def project_kernel(x_ref, gain_ref, w_ref, hidden_ref, gate_ref, rows_ref):
+def project_kernel(x_ref, gain_ref, w_ref, dt_ref, hidden_ref, gate_ref, rows_ref):
     x = to_full(x_ref[...])
     hidden = to_low(x * norm_scale(x) * gain_ref[...])
     hidden_ref[...] = hidden
     projected = dot_full(hidden, w_ref[...])
     gate_width = gate_ref.shape[1]
     gate_ref[...] = projected[:, :gate_width]
-    rows_ref[...] = to_low(projected[:, gate_width:])
-
-
-def project(x, gain, weights, gate_width):
+    rest = projected.shape[1] - gate_width
+    rows_ref[:, :rest] = to_low(projected[:, gate_width:])
+    rows_ref[:, rest:] = to_low(dot_full(hidden, dt_ref[...]))
+
+
+def project(x, gain, weights, dt_weights, gate_width, freight=()):
     rows, width = x.shape
-    columns = weights.shape[1]
+    columns = weights.shape[1] + LANES
     tile = 256
     block = lambda extent: pl.BlockSpec((tile, extent), lambda step: (step, 0))
-    return pl.pallas_call(
+    return run(
         project_kernel,
+        (x, gain, weights, dt_weights,),
         grid=(rows // tile,),
-        in_specs=[block(width), whole(gain.shape), whole(weights.shape)],
+        in_specs=[
+            block(width), whole(gain.shape), whole(weights.shape), whole(dt_weights.shape)
+        ],
         out_specs=[block(width), block(gate_width), block(columns - gate_width)],
         out_shape=[
             jax.ShapeDtypeStruct((rows, width), jnp.bfloat16),
             jax.ShapeDtypeStruct((rows, gate_width), jnp.float32),
             jax.ShapeDtypeStruct((rows, columns - gate_width), jnp.bfloat16),
         ],
-        compiler_params=params_of(),
+        freight=freight,
+        micros=11,
         name="project",
-    )(x, gain, weights)
+    )
 
 
 def put_split(columns, rows):
@@ -851,6 +1420,7 @@
         out_specs=pl.BlockSpec((1, tile, width + LANES), lambda step: (step, 0, 0)),
         out_shape=jax.ShapeDtypeStruct((blocks, tile, width + LANES), jnp.bfloat16),
         compiler_params=params_of(),
+        cost_estimate=cost_of(9),
         name="mix_out",
     )(y, gate, gain, weights)
 
@@ -888,12 +1458,13 @@
         w_grad_ref[...] = to_low(total[...])
 
 
-def mix_back(mix, y, gate, gain, weights):
+def mix_back(mix, y, gate, gain, weights, freight=()):
     blocks, tile, wide = mix.shape
     rows, channels = y.shape
     block = pl.BlockSpec((tile, channels), lambda step: (step, 0))
-    return pl.pallas_call(
+    return run(
         mix_back_kernel,
+        (mix, y, gate, gain, weights,),
         grid=(blocks,),
         in_specs=[
             pl.BlockSpec((1, tile, wide), lambda step: (step, 0, 0)),
@@ -909,13 +1480,16 @@
             jax.ShapeDtypeStruct(weights.shape, jnp.bfloat16),
             jax.ShapeDtypeStruct((8, channels), jnp.float32),
         ],
-        scratch_shapes=[pltpu.VMEM(weights.shape, jnp.float32)],
-        compiler_params=params_of(),
+        scratch=[pltpu.VMEM(weights.shape, jnp.float32)],
+        freight=freight,
+        micros=12,
         name="mix_back",
-    )(mix, y, gate, gain, weights)
-
-
-def project_back_kernel(dgate_ref, drows_ref, hidden_ref, w_ref, part_ref, w_grad_ref, total):
+    )
+
+
+def project_back_kernel(
+    dgate_ref, drows_ref, hidden_ref, w_ref, dt_ref, part_ref, main_grad_ref, rest_grad_ref, total
+):
     step = pl.program_id(0)
 
     @pl.when(step == 0)
@@ -923,43 +1497,55 @@
         total[...] = jnp.zeros_like(total)
 
     grads = jnp.concatenate([dgate_ref[...], drows_ref[...]], axis=1)
-    part_ref[0] = to_low(dot_lanes(grads, w_ref[...]))
+    columns = w_ref.shape[1]
+    part_ref[0] = to_low(
+        dot_lanes(grads[:, :columns], w_ref[...]) + dot_lanes(grads[:, columns:], dt_ref[...])
+    )
     total[...] += dot_rows(hidden_ref[...], grads)
 
     @pl.when(step == pl.num_programs(0) - 1)
     def _():
-        w_grad_ref[...] = to_low(total[...])
-
-
-def project_back(dgate, drows, hidden, weights, blocks):
+        main = main_grad_ref.shape[1]
+        main_grad_ref[...] = to_low(total[:, :main])
+        rest_grad_ref[...] = to_low(total[:, main:])
+
+
+def project_back(dgate, drows, hidden, weights, dt_weights, blocks, freight=()):
     rows, width = hidden.shape
     tile = rows // blocks
+    main = 2 * dgate.shape[1]
+    rest = weights.shape[1] + LANES - main
     block = lambda extent: pl.BlockSpec((tile, extent), lambda step: (step, 0))
-    return pl.pallas_call(
+    return run(
         project_back_kernel,
+        (dgate, drows, hidden, weights, dt_weights,),
         grid=(blocks,),
         in_specs=[
             block(dgate.shape[1]),
             block(drows.shape[1]),
             block(width),
             whole(weights.shape),
+            whole(dt_weights.shape),
         ],
         out_specs=[
             pl.BlockSpec((1, tile, width), lambda step: (step, 0, 0)),
-            whole(weights.shape),
+            whole((width, main)),
+            whole((width, rest)),
         ],
         out_shape=[
             jax.ShapeDtypeStruct((blocks, tile, width), jnp.bfloat16),
-            jax.ShapeDtypeStruct(weights.shape, jnp.bfloat16),
-        ],
-        scratch_shapes=[pltpu.VMEM(weights.shape, jnp.float32)],
-        compiler_params=params_of(),
+            jax.ShapeDtypeStruct((width, main), jnp.bfloat16),
+            jax.ShapeDtypeStruct((width, rest), jnp.bfloat16),
+        ],
+        scratch=[pltpu.VMEM((width, main + rest), jnp.float32)],
+        freight=freight,
+        micros=25,
         name="project_back",
-    )(dgate, drows, hidden, weights)
+    )
 
 
 def shared_kernel(
-    rows_ref, grad_ref, up_ref, down_ref, res_ref, back_ref, up_grad_ref, down_grad_ref, up_sum, down_sum
+    rows_ref, up_ref, down_ref, res_ref, back_ref, up_grad_ref, down_grad_ref, up_sum, down_sum
 ):
     step = pl.program_id(0)
 
@@ -968,10 +1554,9 @@
         up_sum[...] = jnp.zeros_like(up_sum)
         down_sum[...] = jnp.zeros_like(down_sum)
 
-    width = grad_ref.shape[2]
-    hidden = down_ref.shape[0]
+    hidden, width = down_ref.shape
     rows = rows_ref[0, :, :width]
-    grad = grad_ref[0]
+    grad = rows_ref[0, :, width + LANES :]
     joined = dot_full(rows, up_ref[...])
     gate, up = joined[:, :hidden], joined[:, hidden:]
     sig = jax.nn.sigmoid(gate)
@@ -994,134 +1579,172 @@
         down_grad_ref[...] = to_low(down_sum[...])
 
 
-def shared_expert(rows, grad, up, down):
-    blocks, tile, wide = rows.shape
-    width = grad.shape[2]
-    block = lambda extent: pl.BlockSpec((1, tile, extent), lambda step: (step, 0, 0))
-    return pl.pallas_call(
+def shared_expert(rows, up, down, blocks, inner, freight=()):
+    _, tile, wide = rows.shape
+    width = down.shape[1]
+    block = pl.BlockSpec((1, tile, width), lambda step: (step, 0, 0))
+    low = jnp.bfloat16
+    return run(
         shared_kernel,
+        (rows, up, down),
         grid=(blocks,),
-        in_specs=[block(wide), block(width), whole(up.shape), whole(down.shape)],
-        out_specs=[block(width), block(width), whole(up.shape), whole(down.shape)],
+        in_specs=[
+            pl.BlockSpec(
+                (1, tile, wide), lambda step: (own_shard_group(inner)[0] * blocks + step, 0, 0)
+            ),
+            whole(up.shape),
+            whole(down.shape),
+        ],
+        out_specs=[block, block, whole(up.shape), whole(down.shape)],
         out_shape=[
-            jax.ShapeDtypeStruct((blocks, tile, width), jnp.bfloat16),
-            jax.ShapeDtypeStruct((blocks, tile, width), jnp.bfloat16),
-            jax.ShapeDtypeStruct(up.shape, jnp.bfloat16),
-            jax.ShapeDtypeStruct(down.shape, jnp.bfloat16),
-        ],
-        scratch_shapes=[
-            pltpu.VMEM(up.shape, jnp.float32),
-            pltpu.VMEM(down.shape, jnp.float32),
-        ],
-        compiler_params=params_of(),
+            jax.ShapeDtypeStruct((blocks, tile, width), low),
+            jax.ShapeDtypeStruct((blocks, tile, width), low),
+            jax.ShapeDtypeStruct(up.shape, low),
+            jax.ShapeDtypeStruct(down.shape, low),
+        ],
+        scratch=[pltpu.VMEM(up.shape, jnp.float32), pltpu.VMEM(down.shape, jnp.float32)],
+        freight=freight,
+        micros=18,
         name="shared_expert",
-    )(rows, grad, up, down)
-
-
-def dispatch_kernel(
-    first_ref, rows_ref, grad_ref, x_ref, g_ref, picks_ref, *, top_count, slots
-):
+    )
+
+
+def dispatch_kernel(rows_ref, x_ref, g_ref, picks_ref, *, top_count, slots, own_first):
     per_device = x_ref.shape[0]
-    tok_rows = rows_ref.shape[1]
-    width = grad_ref.shape[2]
-    block = rows_ref[0]
-    extra = to_full(block[:, width:])
+    together, tok_rows, _ = rows_ref.shape
+    width = g_ref.shape[2]
+    wide = width + LANES
+    taken = per_device * slots
     lane = iota_of((tok_rows, LANES), 1)
     named = (lane >= 2 * top_count) & (lane < 3 * top_count)
-    member = jnp.zeros((tok_rows, LANES), jnp.float32)
-    for expert in range(per_device):
-        own = to_full(first_ref[0] + expert)
-        hit = jnp.sum(jnp.where(named & (extra == own), 1.0, 0.0), axis=1, keepdims=True)
-        member = jnp.where(lane // slots == expert, hit, member)
     before = iota_of((tok_rows, tok_rows), 0) > iota_of((tok_rows, tok_rows), 1)
-    ranks = dot_full(to_low(jnp.where(before, 1.0, 0.0)), to_low(member))
-    picks = jnp.where(
-        (ranks == to_full(lane % slots)) & (member > 0.0), 1.0, 0.0
-    ).astype(jnp.bfloat16)
-    picks_ref[0] = picks
-    rows = to_low(dot_rows(picks, block))
-    grads = to_low(dot_rows(picks, grad_ref[0]))
-    for expert in range(per_device):
-        x_ref[expert] = rows[expert * slots : (expert + 1) * slots]
-        g_ref[expert] = grads[expert * slots : (expert + 1) * slots]
-
-
-def dispatch(first, rows, grad, per_device, top_count, slots):
+    before = to_low(jnp.where(before, 1.0, 0.0))
+    first = own_first()
+    for index in range(together):
+        extra = to_full(rows_ref[index, :, width:wide])
+        member = jnp.zeros((tok_rows, LANES), jnp.float32)
+        for expert in range(per_device):
+            own = (first + expert).astype(jnp.float32)
+            hit = jnp.sum(jnp.where(named & (extra == own), 1.0, 0.0), axis=1, keepdims=True)
+            member = jnp.where(lane // slots == expert, hit, member)
+        ranks = dot_full(before, to_low(member))
+        picks = jnp.where(
+            (ranks == to_full(lane % slots)) & (member > 0.0), 1.0, 0.0
+        ).astype(jnp.bfloat16)
+        picks_ref[index] = picks
+        rows = to_low(dot_rows(picks[:, :taken], rows_ref[index]))
+        start = index * slots
+        for expert in range(per_device):
+            part = rows[expert * slots : (expert + 1) * slots]
+            x_ref[expert, start : start + slots] = part[:, :wide]
+            g_ref[expert, start : start + slots] = part[:, wide:]
+
+
+def dispatch(rows, width, per_device, top_count, slots, own_first, freight=()):
     blocks, tok_rows, wide = rows.shape
-    width = grad.shape[2]
-    block = lambda extent: pl.BlockSpec((1, tok_rows, extent), lambda step: (step, 0, 0))
-    taken = lambda extent: pl.BlockSpec((per_device, slots, extent), lambda step: (0, step, 0))
-    return pl.pallas_call(
-        functools.partial(dispatch_kernel, top_count=top_count, slots=slots),
-        grid=(blocks,),
-        in_specs=[pl.BlockSpec(memory_space=pltpu.SMEM), block(wide), block(width)],
-        out_specs=[taken(wide), taken(width), block(LANES)],
+    together = 4
+    block = lambda extent: pl.BlockSpec((together, tok_rows, extent), lambda step: (step, 0, 0))
+    taken = lambda extent: pl.BlockSpec(
+        (per_device, together * slots, extent), lambda step: (0, step, 0)
+    )
+    return run(
+        functools.partial(
+            dispatch_kernel, top_count=top_count, slots=slots, own_first=own_first
+        ),
+        (rows,),
+        grid=(blocks // together,),
+        in_specs=[block(wide)],
+        out_specs=[taken(width + LANES), taken(width), block(LANES)],
         out_shape=[
-            jax.ShapeDtypeStruct((per_device, blocks * slots, wide), jnp.bfloat16),
+            jax.ShapeDtypeStruct((per_device, blocks * slots, width + LANES), jnp.bfloat16),
             jax.ShapeDtypeStruct((per_device, blocks * slots, width), jnp.bfloat16),
             jax.ShapeDtypeStruct((blocks, tok_rows, LANES), jnp.bfloat16),
         ],
-        compiler_params=params_of(),
+        freight=freight,
+        micros=30,
         name="dispatch",
-    )(first, rows, grad)
-
-
-def experts_kernel(first_ref, place_ref, *refs, count, top_count):
+    )
+
+
+def join_piece(up, down):
+    double = up.shape[-1]
+    rows, width = down.shape[-2:]
+    half = rows // 2
+    rest = width - double
+    tail = jnp.concatenate([down[..., :half, double:], down[..., half:, double:]], axis=-1)
+    blank = jnp.zeros(tail.shape[:-1] + (double - 2 * rest,), tail.dtype)
+    tail = jnp.concatenate([tail, blank], axis=-1)
+    return jnp.concatenate([up, down[..., :double], tail], axis=-2)
+
+
+def piece_parts(piece, up, down, place, count):
+    depth, rows = up.shape[0] // count, down.shape[0] // count
+    double, width = up.shape[1], down.shape[1]
+    half, rest = rows // 2, width - double
+    up_start = pl.multiple_of(place * depth, depth)
+    down_start = pl.multiple_of(place * rows, rows)
+    tail = pl.ds(depth + rows, half)
+    return [
+        (piece.at[pl.ds(0, depth)], up.at[pl.ds(up_start, depth)]),
+        (piece.at[pl.ds(depth, rows)], down.at[pl.ds(down_start, rows), pl.ds(0, double)]),
+        (
+            piece.at[tail, pl.ds(0, rest)],
+            down.at[pl.ds(down_start, half), pl.ds(double, rest)],
+        ),
+        (
+            piece.at[tail, pl.ds(rest, rest)],
+            down.at[pl.ds(down_start + half, half), pl.ds(double, rest)],
+        ),
+    ]
+
+
+def experts_kernel(*refs, count, per_device, top_count, own_first, inner):
     x_ref, g_ref = refs[:2]
-    ups, downs = refs[2 : 2 + count], refs[2 + count : 2 + 2 * count]
-    refs = refs[2 + 2 * count :]
-    res_ref, dx_ref = refs[:2]
-    up_outs, down_outs = refs[2 : 2 + count], refs[2 + count : 2 + 2 * count]
-    up_held, down_held, up_sum, down_sum, up_low, down_low, up_sems, down_sems = refs[
-        2 + 2 * count :
-    ]
+    total = count * per_device
+    pieces = refs[2 : 2 + total]
+    res_ref, dx_ref = refs[2 + total : 4 + total]
+    outs = refs[4 + total : 4 + 2 * total]
+    up_held, down_held, up_sum, down_sum, up_low, down_low, sems = refs[4 + 2 * total :]
+    own_place, _ = own_shard_group(inner)
     expert, step = pl.program_id(0), pl.program_id(1)
-    experts, steps = pl.num_programs(0), pl.num_programs(1)
+    steps = pl.num_programs(1)
     slot = lax.rem(expert, 2)
     width, double = up_held.shape[1:]
     hidden = double // 2
     tile = x_ref.shape[1]
 
-    def spans(extent):
-        piece = extent // count
-        return [
-            pl.ds(
-                pl.multiple_of(lax.rem(place_ref[0] + count - shift, count) * piece, piece), piece
+    def fetch(which):
+        copies = []
+        for shift in range(count):
+            place = lax.rem(own_place + count - shift, count)
+            parts = piece_parts(
+                pieces[shift * per_device + which],
+                up_held.at[which % 2],
+                down_held.at[which % 2],
+                place,
+                count,
             )
-            for shift in range(count)
-        ]
-
-    def fetch(which, into):
-        copies = []
-        for shift, span in enumerate(spans(width)):
-            copies.append(
-                pltpu.make_async_copy(
-                    ups[shift].at[which], up_held.at[into, span], up_sems.at[into, shift]
+            for kind, (piece, held) in enumerate(parts):
+                copies.append(
+                    pltpu.make_async_copy(piece, held, sems.at[which % 2, shift, kind])
                 )
-            )
-        for shift, span in enumerate(spans(hidden)):
-            copies.append(
-                pltpu.make_async_copy(
-                    downs[shift].at[which], down_held.at[into, span], down_sems.at[into, shift]
-                )
-            )
         return copies
+
+    for which in range(per_device):
+
+        @pl.when((step == 0) & (expert == which))
+        def _():
+            if which == 0:
+                for copy in fetch(0):
+                    copy.start()
+            for copy in fetch(which):
+                copy.wait()
+            if which + 1 < per_device:
+                for copy in fetch(which + 1):
+                    copy.start()
 
     @pl.when(step == 0)
     def _():
-        @pl.when(expert == 0)
-        def _():
-            for copy in fetch(expert, slot):
-                copy.start()
-
-        for copy in fetch(expert, slot):
-            copy.wait()
-
-        @pl.when(expert + 1 < experts)
-        def _():
-            for copy in fetch(expert + 1, 1 - slot):
-                copy.start()
-
         up_sum[...] = jnp.zeros_like(up_sum)
         down_sum[...] = jnp.zeros_like(down_sum)
 
@@ -1129,8 +1752,8 @@
     rows = x_ref[0, :, :width]
     extra = to_full(x_ref[0, :, width:])
     lane = iota_of((tile, LANES), 1)
-    own = first_ref[0] + expert
-    hits = jnp.where((lane < 3 * top_count) & (extra == to_full(own)), 1.0, 0.0)
+    own = own_first() + expert
+    hits = jnp.where((lane < 3 * top_count) & (extra == own.astype(jnp.float32)), 1.0, 0.0)
     gate_slot = jnp.zeros((tile, 1), jnp.float32)
     for route in range(top_count):
         place = 2 * top_count + route
@@ -1163,95 +1786,109 @@
     )
     up_sum[...] += dot_rows(rows, joined_grad)
 
-    @pl.when(step == steps - 1)
-    def _():
-        up_low[...] = to_low(up_sum[...])
-        down_low[...] = to_low(down_sum[...])
-        copies = []
-        for shift, span in enumerate(spans(width)):
-            copies.append(
-                pltpu.make_async_copy(
-                    up_low.at[span], up_outs[shift].at[expert], up_sems.at[2, shift]
+    for which in range(per_device):
+
+        @pl.when((step == steps - 1) & (expert == which))
+        def _():
+            up_low[...] = to_low(up_sum[...])
+            down_low[...] = to_low(down_sum[...])
+            copies = []
+            for shift in range(count):
+                place = lax.rem(own_place + count - shift, count)
+                parts = piece_parts(
+                    outs[shift * per_device + which], up_low, down_low, place, count
                 )
-            )
-        for shift, span in enumerate(spans(hidden)):
-            copies.append(
-                pltpu.make_async_copy(
-                    down_low.at[span], down_outs[shift].at[expert], down_sems.at[2, shift]
-                )
-            )
-        for copy in copies:
-            copy.start()
-        for copy in copies:
-            copy.wait()
-
-
-def experts(first, place, x, g, ups, downs, top_count):
+                for kind, (piece, held) in enumerate(parts):
+                    copies.append(pltpu.make_async_copy(held, piece, sems.at[2, shift, kind]))
+            for copy in copies:
+                copy.start()
+            for copy in copies:
+                copy.wait()
+
+
+def experts(x, g, pieces, hidden, top_count, own_first, inner):
     per_device, rows, wide = x.shape
     width = g.shape[2]
-    count = len(ups)
-    double = ups[0].shape[2]
-    hidden = double // 2
+    count = len(pieces) // per_device
+    double = 2 * hidden
     tile = min(rows, 256)
     block = lambda extent: pl.BlockSpec((1, tile, extent), lambda e, step: (e, step, 0))
     anywhere = pl.BlockSpec(memory_space=pl.ANY)
-    scalars = pl.BlockSpec(memory_space=pltpu.SMEM)
     low = jnp.bfloat16
-    outs = pl.pallas_call(
-        functools.partial(experts_kernel, count=count, top_count=top_count),
+    outs = run(
+        functools.partial(
+            experts_kernel,
+            count=count,
+            per_device=per_device,
+            top_count=top_count,
+            own_first=own_first,
+            inner=inner,
+        ),
+        (x, g) + tuple(pieces),
         grid=(per_device, rows // tile),
-        in_specs=[scalars, scalars, block(wide), block(width)] + [anywhere] * (2 * count),
-        out_specs=[block(width), block(wide)] + [anywhere] * (2 * count),
+        in_specs=[block(wide), block(width)] + [anywhere] * len(pieces),
+        out_specs=[block(width), block(wide)] + [anywhere] * len(pieces),
         out_shape=[
             jax.ShapeDtypeStruct((per_device, rows, width), low),
             jax.ShapeDtypeStruct((per_device, rows, wide), low),
         ]
-        + [jax.ShapeDtypeStruct(piece.shape, low) for piece in list(ups) + list(downs)],
-        scratch_shapes=[
+        + [jax.ShapeDtypeStruct(piece.shape, low) for piece in pieces],
+        scratch=[
             pltpu.VMEM((2, width, double), low),
             pltpu.VMEM((2, hidden, width), low),
             pltpu.VMEM((width, double), jnp.float32),
             pltpu.VMEM((hidden, width), jnp.float32),
             pltpu.VMEM((width, double), low),
             pltpu.VMEM((hidden, width), low),
-            pltpu.SemaphoreType.DMA((3, count)),
-            pltpu.SemaphoreType.DMA((3, count)),
-        ],
-        compiler_params=params_of(),
+            pltpu.SemaphoreType.DMA((3, count, 4)),
+        ],
+        micros=45,
         name="experts",
-    )(first, place, x, g, *ups, *downs)
-    return outs[0], outs[1], outs[2 : 2 + count], outs[2 + count :]
-
-
-def combine_kernel(place_ref, picks_ref, res_ref, dx_ref, sres_ref, sback_ref, out_ref, back_ref):
+    )
+    return outs[0], outs[1], outs[2:]
+
+
+def combine_kernel(
+    picks_ref, res_ref, dx_ref, sres_ref, sback_ref, out_ref, back_ref, *, slots, inner
+):
     step = pl.program_id(0)
-    width = out_ref.shape[2]
-    per_device, slots = res_ref.shape[:2]
-    taken = per_device * slots
-    picks = picks_ref[0, :, :taken]
-    out = dot_full(picks, res_ref[...].reshape(taken, width))
-    back = dot_full(picks, dx_ref[...].reshape(taken, width + LANES))
-    out_ref[0] = to_low(out)
-    back_ref[0] = to_low(back)
-
-    @pl.when(lax.div(step, sres_ref.shape[0]) == place_ref[0])
+    together, _, width = out_ref.shape
+    per_device = res_ref.shape[0]
+    blocks = sres_ref.shape[0]
+    place, _ = own_shard_group(inner)
+    for index in range(together):
+        picks = picks_ref[index, :, : per_device * slots]
+        start = index * slots
+        stacked = lambda ref: jnp.concatenate(
+            [ref[expert, start : start + slots] for expert in range(per_device)], axis=0
+        )
+        out_ref[index] = to_low(dot_full(picks, stacked(res_ref)))
+        back_ref[index] = to_low(dot_full(picks, stacked(dx_ref)))
+
+    @pl.when(lax.div(step * together, blocks) == place)
     def _():
-        block = lax.rem(step, sres_ref.shape[0])
-        out_ref[0] = to_low(out + to_full(sres_ref[block]))
-        back_ref[0, :, :width] = to_low(back[:, :width] + to_full(sback_ref[block]))
-
-
-def combine(place, picks, res, dx, shared_res, shared_back):
+        first = lax.rem(step * together, blocks)
+        for index in range(together):
+            out_ref[index] = to_low(to_full(out_ref[index]) + to_full(sres_ref[first + index]))
+            back_ref[index, :, :width] = to_low(
+                to_full(back_ref[index, :, :width]) + to_full(sback_ref[first + index])
+            )
+
+
+def combine(picks, res, dx, shared_res, shared_back, inner, freight=()):
     blocks, tok_rows, _ = picks.shape
     per_device, rows, width = res.shape
     slots = rows // blocks
-    block = lambda extent: pl.BlockSpec((1, tok_rows, extent), lambda step: (step, 0, 0))
-    taken = lambda extent: pl.BlockSpec((per_device, slots, extent), lambda step: (0, step, 0))
-    return pl.pallas_call(
-        combine_kernel,
-        grid=(blocks,),
+    together = 4
+    block = lambda extent: pl.BlockSpec((together, tok_rows, extent), lambda step: (step, 0, 0))
+    taken = lambda extent: pl.BlockSpec(
+        (per_device, together * slots, extent), lambda step: (0, step, 0)
+    )
+    return run(
+        functools.partial(combine_kernel, slots=slots, inner=inner),
+        (picks, res, dx, shared_res, shared_back),
+        grid=(blocks // together,),
         in_specs=[
-            pl.BlockSpec(memory_space=pltpu.SMEM),
             block(LANES),
             taken(width),
             taken(width + LANES),
@@ -1263,14 +1900,91 @@
             jax.ShapeDtypeStruct((blocks, tok_rows, width), jnp.bfloat16),
             jax.ShapeDtypeStruct((blocks, tok_rows, width + LANES), jnp.bfloat16),
         ],
+        freight=freight,
+        micros=30,
+        name="combine",
+    )
+
+
+def assemble_kernel(main_ref, small_ref, out_ref):
+    seq_devices, rows, double = main_ref.shape
+    channels = double // 2
+    for device in range(seq_devices):
+        for side in range(2):
+            start = (side * seq_devices + device) * channels
+            out_ref[:, start : start + channels] = to_full(
+                main_ref[device, :, side * channels : (side + 1) * channels]
+            )
+    start = 2 * seq_devices * channels
+    out_ref[:, start:] = to_full(small_ref[0, :rows, : out_ref.shape[1] - start])
+
+
+def assemble(main, small, columns):
+    seq_devices, rows, double = main.shape
+    tile = rows // seq_devices
+    return pl.pallas_call(
+        assemble_kernel,
+        grid=(seq_devices,),
+        in_specs=[
+            pl.BlockSpec((seq_devices, tile, double), lambda step: (0, step, 0)),
+            pl.BlockSpec((1,) + small.shape[1:], lambda step: (step, 0, 0)),
+        ],
+        out_specs=pl.BlockSpec((tile, columns), lambda step: (step, 0)),
+        out_shape=jax.ShapeDtypeStruct((rows, columns), jnp.float32),
         compiler_params=params_of(),
-        name="combine",
-    )(place, picks, res, dx, shared_res, shared_back)
-
-
-def gather_small(arrays):
-    flat = jnp.concatenate([piece.reshape(-1) for piece in arrays])
-    joined = lax.all_gather(flat, "shard")
+        cost_estimate=cost_of(6),
+        name="assemble",
+    )(main, small)
+
+
+def collect_kernel(place_ref, *refs, per_device):
+    del place_ref
+    step = pl.program_id(0)
+    up_ref, down_ref = refs[-2:]
+    depth, double = up_ref.shape[1:]
+    rows, width = down_ref.shape[1:]
+    half, rest = rows // 2, width - double
+    for order, piece in enumerate(refs[:-2]):
+
+        @pl.when(step == order)
+        def _():
+            up_ref[0] = to_full(piece[:depth])
+            down_ref[0, :, :double] = to_full(piece[depth : depth + rows])
+            tail = to_full(piece[depth + rows :])
+            down_ref[0, :half, double:] = tail[:, :rest]
+            down_ref[0, half:, double:] = tail[:, rest : 2 * rest]
+
+
+def collect(place, pieces, per_device, depth, rows, width):
+    count = len(pieces)
+    shape = pieces[0].shape
+
+    def here(step, place):
+        shift, expert = lax.div(step, per_device), lax.rem(step, per_device)
+        return (
+            lax.rem(place[0] + shift, count // per_device) * per_device + expert, 0, 0
+        )
+
+    up, down = (depth, shape[1]), (rows, width)
+    return pl.pallas_call(
+        functools.partial(collect_kernel, per_device=per_device),
+        grid_spec=pltpu.PrefetchScalarGridSpec(
+            num_scalar_prefetch=1,
+            grid=(count,),
+            in_specs=[pl.BlockSpec(shape, lambda step, place: (0, 0))] * count,
+            out_specs=[pl.BlockSpec((1,) + up, here), pl.BlockSpec((1,) + down, here)],
+        ),
+        out_shape=[
+            jax.ShapeDtypeStruct((count,) + up, jnp.float32),
+            jax.ShapeDtypeStruct((count,) + down, jnp.float32),
+        ],
+        compiler_params=params_of(),
+        cost_estimate=cost_of(12),
+        name="collect",
+    )(place, *pieces)
+
+
+def split_small(joined, arrays):
     results, start = [], 0
     for piece in arrays:
         part = joined[:, start : start + piece.size]
@@ -1279,39 +1993,65 @@
     return results
 
 
-def rows_to_owner(shard_rows, part):
+def flat_of(arrays):
+    return jnp.concatenate([piece.reshape(-1) for piece in arrays])
+
+
+def rows_to_send(weights, columns, part):
+    seq_devices = lax.axis_size("seq")
+    halves = max(1, seq_devices // lax.axis_size("shard"))
+    mine = []
+    for weight in weights:
+        view = weight.reshape(halves, seq_devices, -1, weight.shape[1])
+        mine.append(lax.dynamic_index_in_dim(view, part, 1, keepdims=False))
+    width = weights[0].shape[1]
+    mine = jnp.concatenate(mine, axis=1).reshape(-1, width)
+    return jnp.concatenate([mine, columns.reshape(-1, width)], axis=0)
+
+
+def rows_by_owner(joined, weights):
+    seq_devices = lax.axis_size("seq")
+    halves = max(1, seq_devices // lax.axis_size("shard"))
+    count = halves * sum(weight.shape[0] // halves // seq_devices for weight in weights)
+    return joined[:, :count].reshape(seq_devices, -1, joined.shape[2])
+
+
+def rows_of_owner(taken, weights):
+    seq_devices = lax.axis_size("seq")
+    halves = max(1, seq_devices // lax.axis_size("shard"))
+    fine_rows = [weight.shape[0] // halves // seq_devices for weight in weights]
+    width = taken.shape[2]
+    taken = taken.reshape(seq_devices, -1, sum(fine_rows), width).transpose(1, 0, 2, 3)
+    results, start = [], 0
+    for fine in fine_rows:
+        results.append(taken[:, :, start : start + fine].reshape(-1, width))
+        start += fine
+    return results
+
+
+def rows_from_owner(grads):
     seq_devices = lax.axis_size("seq")
     shard_devices = lax.axis_size("shard")
-    rows, width = shard_rows.shape
-    own_rows = rows * shard_devices // seq_devices
-    halves = max(1, rows // own_rows)
-    fine = rows // halves // seq_devices
-    mine = lax.dynamic_index_in_dim(
-        shard_rows.reshape(halves, seq_devices, fine, width), part, 1, keepdims=False
-    )
-    spread = lax.all_gather(mine, "shard").reshape(seq_devices, -1, width)
-    return (
-        lax.all_to_all(spread, "seq", split_axis=0, concat_axis=0, tiled=True)
-        .reshape(seq_devices, own_rows // fine // seq_devices, fine, width)
-        .transpose(1, 0, 2, 3)
-        .reshape(own_rows, width)
-    )
-
-
-def rows_from_owner(own, part_rows):
+    width = grads[0].shape[1]
+    turns = shard_devices * max(1, seq_devices // shard_devices) // seq_devices
+    pieces = [
+        grad.reshape(turns, seq_devices, -1, width).transpose(1, 0, 2, 3) for grad in grads
+    ]
+    return jnp.concatenate(pieces, axis=2).reshape(seq_devices, -1, width)
+
+
+def rows_of_shard(joined, weights):
     seq_devices = lax.axis_size("seq")
-    shard_devices = lax.axis_size("shard")
-    own_rows, width = own.shape
-    halves = max(1, part_rows // own_rows)
-    fine = part_rows // halves // seq_devices
-    pieces = own.reshape(own_rows // fine // seq_devices, seq_devices, fine, width)
-    pieces = pieces.transpose(1, 0, 2, 3).reshape(seq_devices, -1, width)
-    spread = lax.all_to_all(pieces, "seq", split_axis=0, concat_axis=0, tiled=True)
-    mine = lax.psum_scatter(
-        spread.reshape(shard_devices, halves * fine, width), "shard", tiled=True
-    )
-    joined = lax.all_gather(mine.reshape(halves, fine, width), "seq", axis=1)
-    return joined.reshape(part_rows, width)
+    halves = max(1, seq_devices // lax.axis_size("shard"))
+    fine_rows = [weight.shape[0] // halves // seq_devices for weight in weights]
+    width = joined.shape[2]
+    count = halves * sum(fine_rows)
+    spread = joined[:, :count].reshape(seq_devices, halves, -1, width).transpose(1, 0, 2, 3)
+    results, start = [], 0
+    for fine in fine_rows:
+        results.append(to_full(spread[:, :, start : start + fine]).reshape(-1, width))
+        start += fine
+    return results, joined[:, count:]
 
 
 def inner_groups(inner):
@@ -1324,16 +2064,34 @@
     return [list(range(start, count, inner)) for start in range(inner)]
 
 
-def exchange(pieces, inner):
-    received = [pieces[0]]
-    for shift in range(1, inner):
-        pairs = [
-            (group[place], group[(place + shift) % inner])
-            for group in inner_groups(inner)
-            for place in range(inner)
-        ]
-        received.append(lax.ppermute(pieces[shift], "shard", pairs))
-    return received
+def stacked_pieces(received, place, inner, extents):
+    depth, rows, width = extents
+    own = jnp.stack(received)[lax.rem(place + inner - jnp.arange(inner), inner)]
+    joined = lax.all_gather(own, "shard", axis_index_groups=outer_groups(inner))
+    up, down = unjoin(joined.reshape((-1,) + joined.shape[2:]), depth, rows, width)
+    return join_piece(up.reshape(-1, up.shape[-1]), down.reshape(-1, width))
+
+
+def split_piece(grad, shift, place, inner, extents):
+    depth, rows, width = extents
+    shards = lax.axis_size("shard")
+    up, down = unjoin(grad, depth * shards, rows * shards, width)
+    up = up.reshape(shards // inner, inner, depth, -1)
+    down = down.reshape(shards // inner, inner, rows, width)
+    here = lax.rem(place + inner - shift, inner)
+    take = lambda array: lax.dynamic_index_in_dim(array, here, 1, keepdims=False)
+    return lax.psum_scatter(
+        join_piece(take(up), take(down)), "shard", axis_index_groups=outer_groups(inner)
+    )
+
+
+def unjoin(joined, depth, rows, width):
+    double = joined.shape[-1]
+    rest = width - double
+    tail = joined[..., depth + rows :, :]
+    tail = jnp.concatenate([tail[..., :rest], tail[..., rest : 2 * rest]], axis=-2)
+    down = jnp.concatenate([joined[..., depth : depth + rows, :], tail], axis=-1)
+    return joined[..., :depth, :], down
 
 
 def by_place(received, place, inner):
@@ -1387,6 +2145,7 @@
     top_count = routes.shape[2]
     per_device = local_experts // inner
     blocks = inner * seq_devices
+    COLLECTIVES.clear()
 
     def own_columns(array, start, extent):
         return lax.dynamic_slice_in_dim(array, start + part * extent, extent, 1)
@@ -1394,9 +2153,43 @@
     def own_rows(array, extent):
         return lax.dynamic_slice_in_dim(array, part * extent, extent, 0)
 
-    x_group = gather_rows(tokens[0], 1, 1).reshape(group_rows, width)
+    small_weights = [
+        norm_in, own_columns(w_dt, 0, heads), conv_w, conv_b, dt_bias, a_log, d_skip, norm_gate, norm_moe, w_router
+    ]
+    in_columns = jnp.concatenate(
+        [
+            own_columns(w_in, 0, channels),
+            own_columns(w_in, inner_width, channels),
+            w_in[:, 2 * inner_width :],
+        ],
+        axis=1,
+    )
+    flat = flat_of(small_weights)
+    shared_columns = jnp.concatenate(
+        [
+            own_columns(w_shared, 0, shared_part),
+            own_columns(w_shared, shared_width, shared_part),
+        ],
+        axis=1,
+    )
+    rows_sent = rows_to_send([w_out, w_shared_down], shared_columns, part)
+    if outer == 1:
+        wide = in_columns.shape[1]
+        flat_rows = -(-flat.size // (wide * 32)) * 32
+        flat = jnp.pad(flat, (0, flat_rows * wide - flat.size)).reshape(flat_rows, wide)
+        x_group, proj_in, joined, rows_joined = begin(
+            tokens[0], in_columns, flat, rows_sent, inner
+        )
+        joined = joined.reshape(inner, -1)
+        x_group = x_group.reshape(group_rows, width)
+    else:
+        x_group = gather_rows(tokens[0], 1)[0].reshape(group_rows, width)
+        proj_in = lax.all_gather(in_columns, "shard", tiled=True)
+        joined = lax.all_gather(flat, "shard")
+        rows_joined = lax.all_gather(rows_sent, "shard")
     (
         gain_in,
+        dt_columns,
         conv_weight,
         conv_bias,
         step_bias,
@@ -1405,63 +2198,33 @@
         gain_gate,
         gain_moe,
         router,
-    ) = gather_small(
-        [norm_in, conv_w, conv_b, dt_bias, a_log, d_skip, norm_gate, norm_moe, w_router]
-    )
-    in_columns = jnp.concatenate(
-        [
-            own_columns(w_in, 0, channels),
-            own_columns(w_in, inner_width, channels),
-            w_in[:, 2 * inner_width :],
-            own_columns(w_dt, 0, heads),
-            jnp.zeros((depth_rows, LANES - heads), jnp.bfloat16),
-        ],
-        axis=1,
-    )
-    proj_in = lax.all_gather(in_columns, "shard", tiled=True)
-    out_rows = rows_to_owner(w_out, part)
-    shared_up = lax.all_gather(
-        jnp.concatenate(
-            [
-                own_columns(w_shared, 0, shared_part),
-                own_columns(w_shared, shared_width, shared_part),
-            ],
-            axis=1,
-        ),
-        "shard",
-        tiled=True,
-    )
-    shared_down = rows_to_owner(w_shared_down, part)
-    if outer == 1:
-        grad_all = lax.all_gather(out_grad[0], ("shard", "seq"))
-    else:
-        grad_all = lax.all_gather(
-            lax.all_gather(out_grad[0], "shard", axis_index_groups=inner_groups(inner)),
-            "seq",
-            axis=1,
+    ) = split_small(joined, small_weights)
+    shared_up = rows_joined[:, rows_joined.shape[1] - shared_columns.size // width :]
+    shared_up = shared_up.reshape(-1, shared_columns.shape[1])
+    dt_columns = jnp.pad(dt_columns, ((0, 0), (0, LANES - heads)))
+    def piece_of(shift, expert):
+        here = lax.rem(place + shift, inner) * per_device + expert
+        return join_piece(
+            lax.dynamic_index_in_dim(w_experts, here, 0, keepdims=False),
+            lax.dynamic_index_in_dim(w_experts_down, here, 0, keepdims=False),
         )
-    grad_all = grad_all.reshape(blocks, tok_rows, width)
-
-    def experts_of(array, shift):
-        start = lax.rem(place + shift, inner) * per_device
-        return lax.dynamic_slice_in_dim(array, start, per_device, 0)
-
-    up_pieces = exchange([experts_of(w_experts, shift) for shift in range(inner)], inner)
-    down_pieces = exchange([experts_of(w_experts_down, shift) for shift in range(inner)], inner)
-    if outer > 1:
-
-        def assembled(pieces):
-            joined = lax.all_gather(
-                by_place(pieces, place, inner), "shard", axis_index_groups=outer_groups(inner)
-            )
-            return [
-                joined.transpose(2, 0, 1, 3, 4).reshape(per_device, -1, joined.shape[-1])
-            ]
-
-        up_pieces, down_pieces = assembled(up_pieces), assembled(down_pieces)
+
+    def own_first():
+        here, _ = own_shard_group(inner)
+        return lax.axis_index("seq") * local_experts + here * per_device
+
+    pieces = {(0, expert): piece_of(0, expert) for expert in range(per_device)}
+
+    def parcels(*keys):
+        return [Parcel(piece_of(*key), key[0], inner) for key in keys]
+
+    def unpack(keys, arrays):
+        pieces.update(zip(keys, arrays))
 
     gain_row = to_full(gain_in)[None]
-    hidden_in, gate_in, rows_in = project(x_group, gain_row, proj_in, channels)
+    hidden_in, gate_in, rows_in = project(
+        x_group, gain_row, proj_in, dt_columns, channels
+    )
     ends = jnp.cumsum(lengths[0]).astype(jnp.int32)
     conv_part = jnp.concatenate(
         [own_rows(conv_weight, channels), conv_weight[inner_width:]], axis=0
@@ -1480,11 +2243,24 @@
         ),
         ((0, 5), (0, LANES - heads)),
     )
-    y, seq_rows, states = scan_forward(
-        ends, deal_order, rows_in, conv_table, head_table, channels
-    )
+    keys = [(1, 0)]
+    y, seq_rows, states, (taken, *arrays) = scan_forward(
+        ends,
+        deal_order,
+        rows_in,
+        conv_table,
+        head_table,
+        channels,
+        [PlaneSwap(rows_by_owner(rows_joined, [w_out, w_shared_down]))] + parcels(*keys),
+    )
+    unpack(keys, arrays)
+    out_rows, shared_down = rows_of_owner(taken, [w_out, w_shared_down])
     gate_gain = to_full(own_rows(gain_gate, channels))[None]
-    mixed = reduce_rows(mix_out(y, gate_in, gate_gain, out_rows, seq_devices)[None], 2)
+    keys = [(inner - 1, 0)]
+    mixed, arrays = reduce_rows(
+        mix_out(y, gate_in, gate_gain, out_rows, seq_devices)[None], parcels(*keys)
+    )
+    unpack(keys, arrays)
     gate_scale = lax.rsqrt(
         (mixed[:, width : width + 1] + mixed[:, width + 1 : width + 2]) / inner_width + EPSILON
     )
@@ -1511,70 +2287,70 @@
         ],
         axis=1,
     )
-    moe_all = gather_rows(jnp.concatenate([moe_in, extra], axis=1), inner, 3)
-    moe_all = moe_all.reshape(blocks, tok_rows, width + LANES)
-    moe_group = lax.dynamic_slice_in_dim(moe_all, place * seq_devices, seq_devices, 0)
-    grad_group = lax.dynamic_slice_in_dim(grad_all, place * seq_devices, seq_devices, 0)
-    shared_res, shared_back, shared_up_grad, shared_down_grad = shared_expert(
-        moe_group, grad_group, shared_up, shared_down
-    )
+    keys = [(1, 1), (2, 0)]
+    both_all, arrays = gather_rows(
+        jnp.concatenate([moe_in, extra, out_grad[0]], axis=1), inner, parcels(*keys)
+    )
+    unpack(keys, arrays)
+    both_all = both_all.reshape(blocks, tok_rows, 2 * width + LANES)
     capacity = min(tok_rows, max(2, tok_rows * top_count * 5 // (expert_total * 3)))
     slots = -(-capacity // 16) * 16
-    first = (part * local_experts + place * per_device).astype(jnp.int32)[None]
-    place_row = place.astype(jnp.int32)[None]
-    expert_rows, grad_rows, picks = dispatch(
-        first, moe_all, grad_all, per_device, top_count, slots
-    )
-    expert_res, expert_back, up_grads, down_grads = experts(
-        first, place_row, expert_rows, grad_rows, up_pieces, down_pieces, top_count
-    )
-    out_part, back_part = combine(
-        place_row, picks, expert_res, expert_back, shared_res, shared_back
-    )
-    back = reduce_rows(back_part.reshape(inner, seq_devices, tok_rows, -1), 4)
-    if outer == 1:
-        out_sum = lax.psum_scatter(
-            out_part.reshape(blocks * tok_rows, width), ("shard", "seq"), tiled=True
-        )
-    else:
-        out_sum = lax.psum_scatter(
-            lax.psum_scatter(
-                out_part.reshape(inner, seq_devices, tok_rows, width),
-                "seq",
-                scatter_dimension=1,
-            ),
-            "shard",
-            axis_index_groups=inner_groups(inner),
-        )
+    keys = [(inner - 1, 1)]
+    expert_rows, grad_rows, picks, arrays = dispatch(
+        both_all, width, per_device, top_count, slots, own_first, parcels(*keys)
+    )
+    unpack(keys, arrays)
+    keys = [(2, 1)]
+    shared_res, shared_back, shared_up_grad, shared_down_grad, arrays = shared_expert(
+        both_all, shared_up, shared_down, seq_devices, inner, parcels(*keys)
+    )
+    unpack(keys, arrays)
+    order = [(shift, expert) for shift in range(inner) for expert in range(per_device)]
+    pieces = [pieces[key] for key in order]
+    if outer > 1:
+        pieces = [
+            stacked_pieces(
+                [pieces[shift * per_device + expert] for shift in range(inner)],
+                place,
+                inner,
+                (depth_rows, hidden_rows, width),
+            )
+            for expert in range(per_device)
+        ]
+    expert_res, expert_back, grads = experts(
+        expert_rows, grad_rows, pieces, hidden, top_count, own_first, inner
+    )
+    if outer > 1:
+        grads = [
+            split_piece(grads[expert], shift, place, inner, (depth_rows, hidden_rows, width))
+            for shift in range(inner)
+            for expert in range(per_device)
+        ]
+    grads = dict(zip(order, grads))
+    returned = {(0, expert): grads[0, expert] for expert in range(per_device)}
+
+    def back_parcels(*keys):
+        return [Parcel(grads[key], inner - key[0], inner) for key in keys]
+
+    def unpack_back(keys, arrays):
+        returned.update(zip(keys, arrays))
+
+    keys = [(1, 0)]
+    out_part, back_part, arrays = combine(
+        picks, expert_res, expert_back, shared_res, shared_back, inner, back_parcels(*keys)
+    )
+    unpack_back(keys, arrays)
+    keys = [(2, 0)]
+    back, arrays = reduce_rows(
+        back_part.reshape(inner, seq_devices, tok_rows, -1), back_parcels(*keys)
+    )
+    unpack_back(keys, arrays)
+    keys = [(inner - 1, 0)]
+    out_sum, arrays = reduce_rows(
+        out_part.reshape(inner, seq_devices, tok_rows, -1), back_parcels(*keys)
+    )
+    unpack_back(keys, arrays)
     layer_out = to_low(after_mix + to_full(out_sum))
-
-    if outer > 1:
-
-        def scattered(grads):
-            full = grads[0]
-            piece = full.shape[1] // shard_devices
-            split = full.reshape(per_device, outer, inner, piece, full.shape[2])
-            own = lax.psum_scatter(
-                split.transpose(1, 2, 0, 3, 4),
-                "shard",
-                axis_index_groups=outer_groups(inner),
-            )
-            return [
-                lax.dynamic_index_in_dim(own, lax.rem(place + shift, inner), 0, keepdims=False)
-                for shift in range(inner)
-            ]
-
-        up_back, down_back = scattered(up_grads), scattered(down_grads)
-    else:
-        turned = lambda pieces: [pieces[(inner - shift) % inner] for shift in range(inner)]
-        up_back, down_back = turned(up_grads), turned(down_grads)
-
-    def whole_shard(pieces):
-        received = by_place(exchange(pieces, inner), place, inner)
-        return to_full(received.reshape((local_experts,) + received.shape[2:]))
-
-    experts_grad = whole_shard(up_back)
-    experts_down_grad = whole_shard(down_back)
 
     half = LANES // 2
     gate_grad_all = (
@@ -1597,17 +2373,57 @@
     share = jnp.sum(to_full(mix_low) * mix_sum, axis=1, keepdims=True) / inner_width
     carried = put_split([share, gate_scale], tok_rows)
 
-    mix_group = gather_rows(jnp.concatenate([mix_low, carried], axis=1), 1, 5)[0]
+    keys = [(inner - 1, 1)]
+    mix_group, arrays = gather_rows(
+        jnp.concatenate([mix_low, carried], axis=1), 1, back_parcels(*keys)
+    )
+    unpack_back(keys, arrays)
     dy, gate_in_grad, proj_out_grad, gain_gate_grad = mix_back(
-        mix_group, y, gate_in, gate_gain, out_rows
-    )
-    rows_grad, conv_grad, head_grad = scan_backward(
-        ends, deal_order, seq_rows, states, dy, conv_table, head_table
-    )
-    hidden_part, proj_in_grad = project_back(
-        gate_in_grad, rows_grad, hidden_in, proj_in, seq_devices
-    )
-    hidden_grad = reduce_rows(hidden_part[None], 6)
+        mix_group[0], y, gate_in, gate_gain, out_rows
+    )
+    keys = [(2, 1)]
+    rows_grad, conv_grad, head_grad, (taken, *arrays) = scan_backward(
+        ends,
+        deal_order,
+        seq_rows,
+        states,
+        dy,
+        conv_table,
+        head_table,
+        [PlaneSwap(rows_from_owner([proj_out_grad, shared_down_grad]))] + back_parcels(*keys),
+    )
+    unpack_back(keys, arrays)
+    keys = [(1, 1)]
+    hidden_part, main_grad, rest_grad, arrays = project_back(
+        gate_in_grad, rows_grad, hidden_in, proj_in, dt_columns, seq_devices, back_parcels(*keys)
+    )
+    unpack_back(keys, arrays)
+    experts_grad, experts_down_grad = collect(
+        place[None], [returned[key] for key in order], per_device, depth_rows, hidden_rows, width
+    )
+    rows_part = jnp.concatenate(
+        [
+            taken.reshape(shard_devices, -1, width),
+            shared_up_grad.reshape(shard_devices, -1, width),
+        ],
+        axis=1,
+    )
+    main_part = main_grad.reshape(shard_devices, depth_rows, 2 * channels)
+    if outer == 1:
+        hidden_grad, main_all, rows_all = settle(hidden_part[None], [main_part, rows_part], inner)
+    else:
+        hidden_grad = reduce_rows(hidden_part[None])[0]
+        main_all = lax.all_gather(lax.psum_scatter(main_part, "shard"), "seq")
+        rows_all = lax.all_gather(lax.psum_scatter(rows_part, "shard"), "seq")
+    (w_out_grad, w_shared_down_grad), shared_columns = rows_of_shard(
+        rows_all, [w_out, w_shared_down]
+    )
+    w_shared_grad = (
+        to_full(shared_columns)
+        .reshape(seq_devices, depth_rows, 2, shared_part)
+        .transpose(1, 2, 0, 3)
+        .reshape(depth_rows, 2 * shared_width)
+    )
     own_scale = norm_scale(residual)
     own_unit = residual * own_scale
     gain_in_grad = jnp.sum(hidden_grad * own_unit, axis=0)
@@ -1618,76 +2434,93 @@
         * (hidden_scaled - own_unit * jnp.mean(hidden_scaled * own_unit, axis=1, keepdims=True))
     )
 
-    own_in_grad = lax.all_gather(
-        lax.psum_scatter(proj_in_grad[:, : 2 * channels], "shard", tiled=True), "seq"
-    )
-    w_in_main = (
-        own_in_grad.reshape(seq_devices, depth_rows, 2, channels)
-        .transpose(1, 2, 0, 3)
-        .reshape(depth_rows, 2 * inner_width)
-    )
-    own_shared_grad = lax.all_gather(
-        lax.psum_scatter(shared_up_grad, "shard", tiled=True), "seq"
-    )
-    w_shared_grad = to_full(
-        own_shared_grad.reshape(seq_devices, depth_rows, 2, shared_part)
-        .transpose(1, 2, 0, 3)
-        .reshape(depth_rows, 2 * shared_width)
-    )
-    w_out_grad = to_full(rows_from_owner(proj_out_grad, w_out.shape[0]))
-    w_shared_down_grad = to_full(rows_from_owner(shared_down_grad, w_shared_down.shape[0]))
-
     def spread(values, length, axis=0):
         shape = values.shape[:axis] + (length,) + values.shape[axis + 1 :]
         return lax.dynamic_update_slice_in_dim(
             jnp.zeros(shape, values.dtype), values, part * values.shape[axis], axis
         )
 
+    state_columns = rest_grad.shape[1] - LANES
     conv_rows_grad = conv_grad[:5].T
     conv_full = jnp.concatenate(
         [spread(conv_rows_grad[:channels], inner_width), conv_rows_grad[channels:]], axis=0
     )
-    small = [
-        gain_in_grad,
-        spread(proj_in_grad[:, -LANES:][:, :heads], head_total, 1),
+    by_depth = [
+        rest_grad[:, :state_columns],
+        to_low(router_grad),
+        spread(rest_grad[:, state_columns : state_columns + heads], head_total, 1),
+        to_low(jnp.stack([gain_in_grad, gain_moe_grad], axis=1)),
+    ]
+    by_shard = [
         conv_full[:, :4],
         conv_full[:, 4],
         spread(head_grad[0, :heads], head_total),
         spread(head_grad[1, :heads], head_total),
         spread(head_grad[2, :heads], head_total),
         spread(gain_gate_grad[0], inner_width),
-        gain_moe_grad,
-        router_grad,
-        proj_in_grad[:, 2 * channels : -LANES],
     ]
-    shapes = [(piece.shape[0] // shard_devices,) + piece.shape[1:] for piece in small]
-    packed = jnp.concatenate(
-        [to_low(piece).reshape(shard_devices, -1) for piece in small], axis=1
-    )
-    summed = lax.psum(lax.psum_scatter(packed, "shard", tiled=True), "seq").reshape(-1)
+    shapes = [(piece.shape[0] // shard_devices,) + piece.shape[1:] for piece in by_shard]
+    by_shard = jnp.concatenate(
+        [to_low(piece).reshape(shard_devices, -1) for piece in by_shard], axis=1
+    )
+    extents = [piece.shape[1] for piece in by_depth]
+    used = sum(extents)
+    if outer == 1:
+        wide = -(-used // LANES) * LANES
+        by_depth.append(jnp.zeros((width, wide - used), jnp.bfloat16))
+        by_depth = jnp.concatenate(by_depth, axis=1).reshape(inner, seq_devices, -1, wide)
+        depth_each = by_depth.shape[2]
+        size = by_shard.shape[1]
+        each = -(-size // (seq_devices * wide))
+        padded = -(-each // 16) * 16
+        by_shard = jnp.pad(by_shard, ((0, 0), (0, each * seq_devices * wide - size)))
+        by_shard = by_shard.reshape(inner, seq_devices, each, wide)
+        by_shard = jnp.pad(by_shard, ((0, 0), (0, 0), (0, padded - each), (0, 0)))
+        small_all = sum_all(jnp.concatenate([by_depth, by_shard], axis=2))
+        w_in_grad = assemble(main_all, small_all, w_in.shape[1])
+        depth_sum = to_full(small_all[:, :depth_each].reshape(depth_rows, wide))
+        shard_sum = small_all[:, depth_each : depth_each + each].reshape(-1)
+    else:
+        by_depth = jnp.concatenate(by_depth, axis=1).reshape(shard_devices, -1)
+        packed = jnp.concatenate([by_depth, by_shard], axis=1)
+        summed = lax.psum(lax.psum_scatter(packed, "shard", tiled=True), "seq").reshape(-1)
+        depth_sum = to_full(summed[: depth_rows * used]).reshape(depth_rows, used)
+        shard_sum = summed[depth_rows * used :]
+        w_in_main = (
+            main_all.reshape(seq_devices, depth_rows, 2, channels)
+            .transpose(1, 2, 0, 3)
+            .reshape(depth_rows, 2 * inner_width)
+        )
+        w_in_grad = jnp.concatenate([to_full(w_in_main), depth_sum[:, :state_columns]], axis=1)
     results, start = [], 0
     for shape in shapes:
         size = 1
         for extent in shape:
             size *= extent
-        results.append(to_full(summed[start : start + size]).reshape(shape))
+        results.append(to_full(shard_sum[start : start + size]).reshape(shape))
         start += size
-    w_in_grad = jnp.concatenate([to_full(w_in_main), results[10]], axis=1)
+    conv_w_grad, conv_b_grad, dt_bias_grad, a_log_grad, d_skip_grad, norm_gate_grad = results
+    start = state_columns
+    w_router_grad = depth_sum[:, start : start + expert_total]
+    start += expert_total
+    w_dt_grad = depth_sum[:, start : start + head_total]
+    start += head_total
+    norm_in_grad, norm_moe_grad = depth_sum[:, start], depth_sum[:, start + 1]
     return (
         layer_out[None],
         tokens_grad[None],
-        results[0],
+        norm_in_grad,
         w_in_grad,
-        results[1],
-        results[2],
-        results[3],
-        results[4],
-        results[5],
-        results[6],
-        results[7],
+        w_dt_grad,
+        conv_w_grad,
+        conv_b_grad,
+        dt_bias_grad,
+        a_log_grad,
+        d_skip_grad,
+        norm_gate_grad,
         w_out_grad,
-        results[8],
-        results[9],
+        norm_moe_grad,
+        w_router_grad,
         w_shared_grad,
         w_shared_down_grad,
         experts_grad,

time: 1660 us -> 1280 us (0.77)
  Pallas kernels: 617 us -> 1140 us
  waiting for transfers between devices: 477 us -> 0 us
  blocking collectives: 312 us -> 0 us
  local copies, waits for them, and re-layouts: 133 us -> 82.6 us
  starting transfers between devices: 32.3 us -> 0 us
  other arithmetic: 61.6 us -> 40 us
    pallas_call x15 -> x19, Pallas kernels: 607 us -> 1130 us  [the longest x16 1010 us: run(): pl.pallas_call(wrapped, grid=grid, in_specs=list(in_specs) + [anywhere] *...]
    reduce_scatter x5 -> x0, waiting for transfers between devices: 292 us -> none  [the longest x1 190 us: local(): lax.psum_scatter(out_part.reshape(blocks * tok_rows, width), ('shard', 's...]
    all_gather x3 -> x0, blocking collectives: 280 us -> none  [the longest x1 244 us: rows_to_owner(): spread = lax.all_gather(mine, 'shard').reshape(seq_devices, -1, width)]
    ppermute x12 -> x0, waiting for transfers between devices: 108 us -> none  [exchange(): received.append(lax.ppermute(pieces[shift], 'shard', pairs))]
    psum x1 -> x0, waiting for transfers between devices: 51.3 us -> none  [local(): lax.psum(lax.psum_scatter(packed, 'shard', tiled=True), 'seq').reshape(-1)]
    all_to_all x2 -> x0, blocking collectives: 32 us -> none  [rows_from_owner(): lax.all_to_all(pieces, 'seq', split_axis=0, concat_axis=0, tiled=True)]
    convert_element_type x10 -> x2, local copies, waits for them, and re-layouts: 27.3 us -> 0.02 us  [to_full(): return values.astype(jnp.float32)]
    convert_element_type x14 -> x8, other arithmetic: 29.5 us -> 3.23 us  [to_full(): return values.astype(jnp.float32)]
  transfers between devices with their start and end apart: 28 -> 0, of which waited for: 10 -> 0; matrix products, arithmetic and copies ran while one was open for 8% -> 0% of each run, Pallas kernels for 19% -> 0%
where the time goes in v2:
time: 1280 us; the launch traced here: 1270 us
  Pallas kernels  1140 us (89%)
  local copies, waits for them, and re-layouts  82.6 us (6%)
  other arithmetic  40 us (3%)
    pallas_call x16, Pallas kernels, run(): pl.pallas_call(wrapped, grid=grid, in_specs=list(in_specs) + [anywhere] *...  1010 us
    pallas_call x1, Pallas kernels, begin(): pl.pallas_call(functools.partial(begin_kernel, inner), in_specs=[anywhere...  99 us

profile of v2, /device:TPU:0, one launch (start us, length us, event | category | flops | bytes accessed | tf_op | source)
XLA Modules:
  0.0 1269.6 jit_solution(4810440571116641116)
XLA Ops:
  0.8 3.4 dynamic-slice_bitcast_fusion.8
  18.8 99.0 %begin.1 = (bf16[8,192,1536]{2,1,0:T(8,128)(2,1)}, bf16[1536,1024]{1,0:T(8,128)(2,1)}, bf16[4,32,1024]{2,1,0:T(8,128)(2,1)}, bf16[4,192,1536]{2,1,0:T(8,128)(2,1)}) custom-call(bf16[192,1536]{1,0:T(8,128)(2,1)} %bitcast.153, bf16[384,1024]{1,0:T(8,128)(2,1)} %pad_maximum_fusion.1.w_ref, bf16[32,1024]{1,0:T(8,128)(2,1)} %reshape.439.s_ref, ...), custom_call_target="tpu_custom_call" | custom-call | bytes 216000000 | tf_op jit(solution)/shard_map/begin/pallas_call | solution.py:1184
  126.0 11.6 project.1
  139.5 34.6 %scan_forward.1 = (bf16[1536,384]{1,0:T(8,128)(2,1)}, bf16[1536,768]{1,0:T(8,128)(2,1)}, f32[6,384,128]{2,1,0:T(8,128)}, bf16[8,64,1536]{2,1,0:T(8,128)(2,1)}, bf16[576,1024]{1,0:T(8,128)(2,1)}) custom-call(s32[4]{0:T(128)} %bitcast.184, s32[1,1536]{1,0:T(1,128)} %refs_1_.3, bf16[1536,768]{1,0:T(8,128)(2,1)} %get-tuple-element.84.refs_2_, ...), custom_call_target="tpu_custom_call" | custom-call | bytes 90000000 | tf_op jit(solution)/shard_map/scan_forward/pallas_call | solution.py:610
  177.3 8.8 mix_out.1
  187.3 29.1 %reduce_rows.3 = (f32[192,1664]{1,0:T(8,128)}, bf16[576,1024]{1,0:T(8,128)(2,1)}) custom-call(bf16[1,8,192,1664]{3,2,1,0:T(8,128)(2,1)} %bitcast.144, bf16[576,1024]{1,0:T(8,128)(2,1)} %maximum_maximum_fusion.1.refs_1_), custom_call_target="tpu_custom_call" | custom-call | bytes 90000000 | tf_op jit(solution)/shard_map/reduce_rows/pallas_call | solution.py:610
  231.8 269.0 %gather_rows.2 = (bf16[4,8,192,3200]{3,2,1,0:T(8,128)(2,1)}, bf16[576,1024]{1,0:T(8,128)(2,1)}, bf16[576,1024]{1,0:T(8,128)(2,1)}) custom-call(bf16[192,3200]{1,0:T(8,128)(2,1)} %concatenate.109.refs_0_, bf16[576,1024]{1,0:T(8,128)(2,1)} %maximum_maximum_fusion.2.refs_1_, bf16[576,1024]{1,0:T(8,128)(2,1)} %maximum_maximum_fusion.3.refs_2_), custom_call_target="tpu_custom_call" | custom-call | bytes 360000000 | tf_op jit(solution)/shard_map/gather_rows/pallas_call | solution.py:610
  507.3 58.1 %shared_expert.1 = (bf16[8,192,1536]{2,1,0:T(8,128)(2,1)}, bf16[8,192,1536]{2,1,0:T(8,128)(2,1)}, bf16[1536,256]{1,0:T(8,128)(2,1)}, bf16[128,1536]{1,0:T(8,128)(2,1)}, bf16[576,1024]{1,0:T(8,128)(2,1)}) custom-call(bf16[32,192,3200]{2,1,0:T(8,128)(2,1)} %bitcast.142, bf16[1536,256]{1,0:T(8,128)(2,1)} %reshape.458.refs_1_, bf16[128,1536]{1,0:T(8,128)(2,1)} %bitcast.163, ...), custom_call_target="tpu_custom_call" | custom-call | bytes 64800000 | tf_op jit(solution)/shard_map/shared_expert/pallas_call | solution.py:610
  567.6 32.1 %dispatch.1 = (bf16[2,1024,1664]{2,1,0:T(8,128)(2,1)}, bf16[2,1024,1536]{2,1,0:T(8,128)(2,1)}, bf16[32,192,128]{2,1,0:T(8,128)(2,1)}, bf16[576,1024]{1,0:T(8,128)(2,1)}) custom-call(bf16[32,192,3200]{2,1,0:T(8,128)(2,1)} %bitcast.143, bf16[576,1024]{1,0:T(8,128)(2,1)} %maximum_maximum_fusion.4.refs_1_), custom_call_target="tpu_custom_call" | custom-call | bytes 108000000 | tf_op jit(solution)/shard_map/dispatch/pallas_call | solution.py:610
  602.3 44.9 %experts.1 = (bf16[2,1024,1536]{2,1,0:T(8,128)(2,1)}, bf16[2,1024,1664]{2,1,0:T(8,128)(2,1)}, bf16[576,1024]{1,0:T(8,128)(2,1)}, bf16[576,1024]{1,0:T(8,128)(2,1...) custom-call(bf16[2,1024,1664]{2,1,0:T(8,128)(2,1)} %get-tuple-elemen, ...), custom_call_target="tpu_custom_call" | custom-call | bytes 162000000 | tf_op jit(solution)/shard_map/experts/pallas_call | solution.py:610
  647.2 36.2 %combine.1 = (bf16[32,192,1536]{2,1,0:T(8,128)(2,1)}, bf16[32,192,1664]{2,1,0:T(8,128)(2,1)}, bf16[576,1024]{1,0:T(8,128)(2,1)}) custom-call(bf16[32,192,128]{2,1,0:T(8,128)(2,1)} %get-tuple-element.91.refs_0_, bf16[2,1024,1536]{2,1,0:T(8,128)(2,1)} %get-tuple-element.100.refs_1_, bf16[2,1024,1664]{2,1,0:T(8,128)(2,1)} %get-tuple-element.101.refs_2_, ...), custom_call_target="tpu_custom_call" | custom-call | bytes 108000000 | tf_op jit(solution)/shard_map/combine/pallas_call | solution.py:610
  683.4 93.8 %reduce_rows.4 = (f32[192,1536]{1,0:T(8,128)}, bf16[576,1024]{1,0:T(8,128)(2,1)}) custom-call(bf16[4,8,192,1536]{3,2,1,0:T(8,128)(2,1)} %bitcast.146, bf16[576,1024]{1,0:T(8,128)(2,1)} %get-tuple-element.106.refs_1_), custom_call_target="tpu_custom_call" | custom-call | bytes 360000000 | tf_op jit(solution)/shard_map/reduce_rows/pallas_call | solution.py:610
  777.3 112.0 %reduce_rows.5 = (f32[192,1664]{1,0:T(8,128)}, bf16[576,1024]{1,0:T(8,128)(2,1)}) custom-call(bf16[4,8,192,1664]{3,2,1,0:T(8,128)(2,1)} %bitcast.145, bf16[576,1024]{1,0:T(8,128)(2,1)} %get-tuple-element.109.refs_1_), custom_call_target="tpu_custom_call" | custom-call | bytes 360000000 | tf_op jit(solution)/shard_map/reduce_rows/pallas_call | solution.py:610
  895.7 30.4 %gather_rows.3 = (bf16[1,8,192,1664]{3,2,1,0:T(8,128)(2,1)}, bf16[576,1024]{1,0:T(8,128)(2,1)}) custom-call(bf16[192,1664]{1,0:T(8,128)(2,1)} %pad_maximum_fusion.2.refs_0_, bf16[576,1024]{1,0:T(8,128)(2,1)} %get-tuple-element.111.refs_1_), custom_call_target="tpu_custom_call" | custom-call | bytes 90000000 | tf_op jit(solution)/shard_map/gather_rows/pallas_call | solution.py:610
  926.1 12.2 mix_back.1
  940.8 57.7 %scan_backward.1 = (bf16[1536,768]{1,0:T(8,128)(2,1)}, f32[8,640]{1,0:T(8,128)}, f32[8,128]{1,0:T(8,128)}, bf16[8,64,1536]{2,1,0:T(8,128)(2,1)}, bf16[576,1024]{1,0:T(8,128)(2,1)}) custom-call(s32[4]{0:T(128)} %bitcast.185, s32[1,1536]{1,0:T(1,128)} %refs_1_.3, bf16[1536,768]{1,0:T(8,128)(2,1)} %get-tuple-element.114.refs_2_, ...), custom_call_target="tpu_custom_call" | custom-call | bytes 144000000 | tf_op jit(solution)/shard_map/scan_backward/pallas_call | solution.py:610
  998.6 33.4 %project_back.1 = (bf16[8,192,1536]{2,1,0:T(8,128)(2,1)}, bf16[1536,768]{1,0:T(8,128)(2,1)}, bf16[1536,384]{1,0:T(8,128)(2,1)}, bf16[576,1024]{1,0:T(8,128)(2,1)}) custom-call(bf16[1536,384]{1,0:T(8,128)(2,1)} %get-tuple-element.113.refs_0_, bf16[1536,768]{1,0:T(8,128)(2,1)} %get-tuple-element.120.refs_1_, bf16[1536,1536]{1,0:T(8,128)(2,1)} %get-tuple-element.121.refs_2_, ...), custom_call_target="tpu_custom_call" | custom-call | bytes 90000000 | tf_op jit(solution)/shard_map/project_back/pallas_call | solution.py:610
  1031.9 10.7 collect.1
  1047.9 121.7 %settle.1 = (f32[192,1536]{1,0:T(8,128)}, bf16[8,384,768]{2,1,0:T(8,128)(2,1)}, bf16[8,192,1536]{2,1,0:T(8,128)(2,1)}) custom-call(bf16[1,8,192,1536]{3,2,1,0:T(8,128)(2,1)} %bitcast.159, bf16[4,384,768]{2,1,0:T(8,128)(2,1)} %bitcast.162, bf16[4,192,1536]{2,1,0:T(8,128)(2,1)} %pad_maximum_fusion.refs_2_), custom_call_target="tpu_custom_call" | custom-call | bytes 324000000 | tf_op jit(solution)/shard_map/settle/pallas_call | solution.py:610
  1189.9 38.1 %sum_all.1.small_ref = bf16[8,64,384]{2,1,0:T(8,128)(2,1)} custom-call(bf16[4,8,64,384]{3,2,1,0:T(8,128)(2,1)} %fusion.4.refs_0_), custom_call_target="tpu_custom_call" | custom-call | bytes 90000000 | tf_op jit(solution)/shard_map/sum_all/pallas_call | solution.py:610
  1228.0 7.8 assemble.1
  1237.5 3.5 slice_convert_fusion.1
  1241.0 5.1 reshape.497
  1246.1 3.7 copy.137
  (326 shorter events, 110.2 us)
Async XLA Ops:
  0.7 13.5 %copy-start = (bf16[768,1536]{1,0:T(8,128)(2,1)S(1)}, bf16[768,1536]{1,0:T(8,128)(2,1)}, u32[]{:S(2)}) copy-start(bf16[768,1536]{1,0:T(8,128)(2,1)} %param.35) | copy-start | bytes 7077892
  0.7 4.9 copy-start.7
  119.0 5.3 copy-start.31
  126.0 11.6 copy-start.21
  177.3 8.8 copy-start.29
  177.3 8.8 copy-start.35
  177.3 8.8 copy-start.36
  187.3 30.9 %copy-start.5 = (bf16[1,192,1536]{2,1,0:T(8,128)(2,1)S(1)}, bf16[1,192,1536]{2,1,0:T(8,128)(2,1)}, u32[]{:S(2)}) copy-start(bf16[1,192,1536]{2,1,0:T(8,128)(2,1)} %param.21) | copy-start | bytes 1769476
  220.8 3.7 copy-start.8
  221.2 5.8 copy-start.13
  231.8 270.9 %copy-start.23 = (bf16[128,1536]{1,0:T(8,128)(2,1)S(1)}, bf16[128,1536]{1,0:T(8,128)(2,1)}, u32[]{:S(2)}) copy-start(bf16[128,1536]{1,0:T(8,128)(2,1)} %get-tuple-element.246) | copy-start | bytes 1179652
  231.8 270.9 %copy-start.26 = (bf16[128,1536]{1,0:T(8,128)(2,1)S(1)}, bf16[128,1536]{1,0:T(8,128)(2,1)}, u32[]{:S(2)}) copy-start(bf16[128,1536]{1,0:T(8,128)(2,1)} %get-tuple-element.239) | copy-start | bytes 1179652
  507.3 58.1 %copy-start.24 = (bf16[128,1536]{1,0:T(8,128)(2,1)S(1)}, bf16[128,1536]{1,0:T(8,128)(2,1)}, u32[]{:S(2)}) copy-start(bf16[128,1536]{1,0:T(8,128)(2,1)} %get-tuple-element.240) | copy-start | bytes 1179652
  507.3 58.1 %copy-start.25 = (bf16[128,1536]{1,0:T(8,128)(2,1)S(1)}, bf16[128,1536]{1,0:T(8,128)(2,1)}, u32[]{:S(2)}) copy-start(bf16[128,1536]{1,0:T(8,128)(2,1)} %get-tuple-element.241) | copy-start | bytes 1179652
  567.6 32.1 %copy-start.15 = (bf16[384,1024]{1,0:T(8,128)(2,1)S(1)}, bf16[384,1024]{1,0:T(8,128)(2,1)}, u32[]{:S(2)}) copy-start(bf16[384,1024]{1,0:T(8,128)(2,1)} %get-tuple-element.230) | copy-start | bytes 2359300
  777.2 113.2 %copy-start.40 = (s32[1,192,6]{1,2,0:T(8,128)S(1)}, s32[1,192,6]{1,2,0:T(8,128)}, u32[]{:S(2)}) copy-start(s32[1,192,6]{1,2,0:T(8,128)} %copy-done.39) | copy-start | bytes 13828
  777.3 113.3 %copy-start.43 = (f32[192]{0:T(256)S(1)}, f32[192]{0:T(256)}, u32[]{:S(2)}) copy-start(f32[192]{0:T(256)} %copy-done.42) | copy-start | bytes 2308
  777.3 113.3 %copy-start.50 = (f32[192]{0:T(256)S(1)}, f32[192]{0:T(256)}, u32[]{:S(2)}) copy-start(f32[192]{0:T(256)} %copy-done.49) | copy-start | bytes 2308
  926.1 12.2 copy-start.34
  1047.9 121.7 %copy-start.59 = (f32[192]{0:T(256)S(1)}, f32[192]{0:T(256)}, u32[]{:S(2)}) copy-start(f32[192]{0:T(256)} %get-tuple-element.251) | copy-start | bytes 2308
  1047.9 121.8 %copy-start.47 = (f32[4,384]{1,0:T(4,128)S(1)}, f32[4,384]{1,0:T(4,128)}, u32[]{:S(2)}) copy-start(f32[4,384]{1,0:T(4,128)} %get-tuple-element.268) | copy-start | bytes 18436
  1169.6 3.3 copy-start.52
  1228.0 7.8 slice-start
  1256.6 3.5 copy-start.20
  (48 other events, 94.1 us)

commit v3 on v2

v3 whole, which is shorter than its diff:
```python
import functools

import jax
import jax.numpy as jnp
from jax import lax
from jax.experimental import pallas as pl
from jax.experimental.pallas import tpu as pltpu
from jax.sharding import PartitionSpec as P

STRETCH = 256
INNER = 4
UP, DOWN = 0, 1
EPSILON = 1e-05
HIGHEST = lax.Precision.HIGHEST


def matmul(left_side, right_side):
    return jnp.dot(left_side, right_side, preferred_element_type=jnp.float32)


def left_contract(left_side, right_side):
    return lax.dot_general(
        left_side, right_side, (((0,), (0,)), ((), ())), preferred_element_type=jnp.float32
    )


def right_contract(left_side, right_side):
    return lax.dot_general(
        left_side, right_side, (((1,), (1,)), ((), ())), preferred_element_type=jnp.float32
    )


def to_low(values):
    return values.astype(jnp.bfloat16)


def to_full(values):
    return values.astype(jnp.float32)


def norm_scale(values):
    return lax.rsqrt(jnp.mean(values * values, axis=-1, keepdims=True) + EPSILON)


LANES = 128
VMEM_BYTES = 56 * 1024 * 1024


def cost_of(micros):
    return pl.CostEstimate(flops=0, transcendentals=0, bytes_accessed=int(micros * 3.6e6))


def dot_rows(left_side, right_side, precision=None):
    return lax.dot_general(
        left_side,
        right_side,
        (((0,), (0,)), ((), ())),
        precision=precision,
        preferred_element_type=jnp.float32,
    )


def dot_lanes(left_side, right_side, precision=None):
    return lax.dot_general(
        left_side,
        right_side,
        (((1,), (1,)), ((), ())),
        precision=precision,
        preferred_element_type=jnp.float32,
    )


def dot_full(left_side, right_side, precision=None):
    return jnp.dot(
        left_side, right_side, precision=precision, preferred_element_type=jnp.float32
    )


def iota_of(shape, axis):
    return lax.broadcasted_iota(jnp.int32, shape, axis)


def ids_at(places, ends_ref):
    total = jnp.zeros(places.shape, jnp.int32)
    for seq in range(ends_ref.shape[0]):
        total = total + (places >= ends_ref[seq]).astype(jnp.int32)
    return total


def id_at(place, ends_ref):
    total = jnp.int32(0)
    for seq in range(ends_ref.shape[0]):
        total = total + (place >= ends_ref[seq]).astype(jnp.int32)
    return total


class Stretch:
    def __init__(self, start, rows, before, conv_ref, head_ref, ends_ref, channels):
        length = rows.shape[0]
        self.channels = channels
        self.heads = channels // 64
        width = conv_ref.shape[1]
        state = (width - channels) // 2
        places = start + iota_of((length, 1), 0)
        self.ids = ids_at(places, ends_ref)
        self.ids_row = ids_at(start + iota_of((1, length), 1), ends_ref)
        inputs = rows[:, :width]
        joined = jnp.concatenate([before[:, :width], inputs], axis=0)
        self.shifted = [inputs]
        value = conv_ref[4:5, :] + inputs * conv_ref[3:4, :]
        for offset in range(1, 4):
            same = (ids_at(places - offset, ends_ref) == self.ids) & (places >= offset)
            moved = pltpu.roll(joined, offset, 0)[8:, :]
            moved = jnp.where(same, moved, 0.0)
            self.shifted.append(moved)
            value = value + moved * conv_ref[3 - offset : 4 - offset, :]
        self.value = value
        self.sig = jax.nn.sigmoid(value)
        act = value * self.sig
        self.x = act[:, :channels]
        self.b = act[:, channels : channels + state]
        self.c = act[:, channels + state :]
        self.b_low = to_low(self.b)
        self.c_low = to_low(self.c)
        self.dt_in = rows[:, width:] + head_ref[0:1, :]
        self.dt = jnp.maximum(self.dt_in, 0.0) + jnp.log1p(jnp.exp(-jnp.abs(self.dt_in)))
        self.rate = head_ref[1:2, :]
        rows_at = iota_of((length, length), 0)
        columns_at = iota_of((length, length), 1)
        lower = (rows_at >= columns_at).astype(jnp.float32)
        self.cum = dot_full(lower, self.dt * self.rate, HIGHEST)
        self.cum_rows = self.cum.T[:8, :]
        self.dt_rows = self.dt.T[:8, :]
        self.causal = (self.ids == self.ids_row) & (rows_at >= columns_at)
        self.scores = dot_lanes(self.c_low, self.b_low)
        last_id = jnp.where(start > 0, id_at(start - 1, ends_ref), -1)
        end_id = id_at(start + length - 1, ends_ref)
        self.enter = jnp.where(self.ids == last_id, jnp.exp(self.cum), 0.0)
        end_cum = self.cum[length - 1 : length, :]
        self.tail = jnp.where(self.ids == end_id, jnp.exp(end_cum - self.cum), 0.0)
        self.tail_weight = self.tail * self.dt
        self.keep = jnp.where(last_id == end_id, jnp.exp(end_cum), 0.0)

    def decay(self, head):
        spread = self.cum[:, head : head + 1] - self.cum_rows[head : head + 1, :]
        return jnp.where(self.causal, jnp.exp(jnp.minimum(spread, 0.0)), 0.0)

    def per_channel(self, by_head):
        return jnp.concatenate(
            [
                jnp.broadcast_to(by_head[:, head : head + 1], (by_head.shape[0], 64))
                for head in range(self.heads)
            ],
            axis=1,
        )

    def state_keep(self):
        return jnp.concatenate(
            [
                jnp.broadcast_to(self.keep[:, head : head + 1], (64, LANES))
                for head in range(self.heads)
            ],
            axis=0,
        )


def head_lanes(channels):
    return (iota_of((channels, LANES), 0) // 64 == iota_of((channels, LANES), 1)).astype(
        jnp.float32
    )


def pick_rows(deal_ref, start, length):
    places = start + iota_of((length, 1), 0)
    return jnp.where(deal_ref[...] == places, 1.0, 0.0).astype(jnp.bfloat16)


def scan_forward_kernel(
    ends_ref, deal_ref, rows_ref, conv_ref, head_ref, y_ref, seq_ref, states_ref, before, state, total
):
    step = pl.program_id(0)
    length = seq_ref.shape[0]
    channels = y_ref.shape[1]
    start = step * length

    @pl.when(step == 0)
    def _():
        before[...] = jnp.zeros_like(before)
        state[...] = jnp.zeros_like(state)
        total[...] = jnp.zeros_like(total)

    picks = pick_rows(deal_ref, start, length)
    rows = dot_full(picks, rows_ref[...])
    seq_ref[...] = to_low(rows)
    part = Stretch(start, rows, before[...], conv_ref, head_ref, ends_ref, channels)
    before[...] = rows[length - 8 :, :]
    state_now = state[...]
    states_ref[0] = state_now
    x_low = to_low(part.x)
    outs = []
    lane = iota_of((length, LANES), 1)
    for pair in range(channels // LANES):
        x_pair = x_low[:, pair * LANES : (pair + 1) * LANES]
        halves = []
        for head in (2 * pair, 2 * pair + 1):
            weights = part.decay(head) * part.scores * part.dt_rows[head : head + 1, :]
            halves.append(dot_full(to_low(weights), x_pair))
        outs.append(jnp.where(lane < 64, halves[0], halves[1]))
    earlier = dot_lanes(part.c_low, to_low(state_now))
    skip = part.per_channel(head_ref[2:3, :])
    y = jnp.concatenate(outs, axis=1) + part.per_channel(part.enter) * earlier + skip * part.x
    state[...] = part.state_keep() * state_now + dot_rows(
        to_low(part.per_channel(part.tail_weight) * part.x), part.b_low
    )
    total[...] += dot_rows(picks, to_low(y))

    @pl.when(step == pl.num_programs(0) - 1)
    def _():
        y_ref[...] = to_low(total[...])


def scan_forward(ends, deal_row, rows, conv_table, head_table, channels, freight):
    group_rows, width = rows.shape
    steps = group_rows // STRETCH
    state_rows = (channels, LANES)
    return run(
        scan_forward_kernel,
        (ends, deal_row, rows, conv_table, head_table),
        grid=(steps,),
        in_specs=[
            pl.BlockSpec(memory_space=pltpu.SMEM),
            whole(deal_row.shape),
            whole(rows.shape),
            whole(conv_table.shape),
            whole(head_table.shape),
        ],
        out_specs=[
            whole((group_rows, channels)),
            pl.BlockSpec((STRETCH, width), lambda step: (step, 0)),
            pl.BlockSpec((1,) + state_rows, lambda step: (step, 0, 0)),
        ],
        out_shape=[
            jax.ShapeDtypeStruct((group_rows, channels), jnp.bfloat16),
            jax.ShapeDtypeStruct((group_rows, width), jnp.bfloat16),
            jax.ShapeDtypeStruct((steps,) + state_rows, jnp.float32),
        ],
        scratch=[
            pltpu.VMEM((8, width), jnp.float32),
            pltpu.VMEM(state_rows, jnp.float32),
            pltpu.VMEM((group_rows, channels), jnp.float32),
        ],
        freight=freight,
        micros=25,
        name="scan_forward",
    )


def scan_backward_kernel(
    ends_ref,
    deal_ref,
    seq_ref,
    states_ref,
    dy_ref,
    conv_ref,
    head_ref,
    other_ref,
    drows_ref,
    conv_grad_ref,
    head_grad_ref,
    other_sum_ref,
    after,
    state_grad,
    *other_scratch,
):
    order = pl.program_id(0)
    steps = pl.num_programs(0)
    reducer = Reducer(other_ref.shape[0], other_ref, other_sum_ref, other_scratch)

    @pl.when(order == 0)
    def _():
        reducer.begin()

    step = steps - 1 - order
    length = STRETCH
    channels = dy_ref.shape[1]
    width = conv_ref.shape[1]
    state_width = (width - channels) // 2
    start = pl.multiple_of(step * length, length)

    @pl.when(order == 0)
    def _():
        after[...] = jnp.zeros_like(after)
        state_grad[...] = jnp.zeros_like(state_grad)
        drows_ref[...] = jnp.zeros_like(drows_ref)
        conv_grad_ref[...] = jnp.zeros_like(conv_grad_ref)
        head_grad_ref[...] = jnp.zeros_like(head_grad_ref)

    picks = pick_rows(deal_ref, start, length)
    dy = dot_full(picks, dy_ref[...])
    rows = seq_ref[pl.ds(start, length), :].astype(jnp.float32)
    place = pl.multiple_of(jnp.maximum(start - 16, 0), 16)
    before = seq_ref[pl.ds(place, 16), :].astype(jnp.float32)[8:, :]
    part = Stretch(start, rows, before, conv_ref, head_ref, ends_ref, channels)
    state_now = states_ref[0]
    state_low = to_low(state_now)
    next_grad = state_grad[...]
    next_low = to_low(next_grad)
    lanes_of = head_lanes(channels)
    x_low = to_low(part.x)
    dy_low = to_low(dy)
    lane = iota_of((length, LANES), 1)

    enter = part.per_channel(part.enter)
    tail_weight = part.per_channel(part.tail_weight)
    earlier = dot_lanes(part.c_low, state_low)
    enter_grad = dot_full(dy * earlier, lanes_of, HIGHEST)
    entered = to_low(enter * dy)
    c_grad = dot_full(entered, state_low)
    state_grad[...] = part.state_keep() * next_grad + dot_rows(entered, part.c_low)
    onward = dot_lanes(part.b_low, next_low)
    x_grad = part.per_channel(head_ref[2:3, :]) * dy + tail_weight * onward
    tail_grad = dot_full(part.x * onward, lanes_of, HIGHEST)
    b_grad = dot_full(to_low(tail_weight * part.x), next_low)
    tail_part = tail_grad * part.tail_weight
    cum_grad = enter_grad * part.enter - tail_part
    dt_grad = tail_grad * part.tail
    kept = dot_lanes(jnp.ones((8, LANES), jnp.float32), next_grad * state_now, HIGHEST)
    keep_grad = dot_full(kept, lanes_of, HIGHEST)[:1, :]
    end_grad = jnp.sum(tail_part, axis=0, keepdims=True) + keep_grad * part.keep

    score_grad = jnp.zeros((length, length), jnp.float32)
    cum_columns, cum_rows, dt_rows, outs = [], [], [], []
    for pair in range(channels // LANES):
        x_pair = x_low[:, pair * LANES : (pair + 1) * LANES]
        dy_pair = dy_low[:, pair * LANES : (pair + 1) * LANES]
        halves = []
        for half, head in enumerate((2 * pair, 2 * pair + 1)):
            mine = (lane < 64) if half == 0 else (lane >= 64)
            weight_grad = dot_lanes(jnp.where(mine, dy_pair, jnp.zeros_like(dy_pair)), x_pair)
            decay = part.decay(head)
            dt_row = part.dt_rows[head : head + 1, :]
            by_decay = weight_grad * decay
            by_dt = by_decay * part.scores
            by_spread = by_dt * dt_row
            dt_rows.append(jnp.sum(by_dt, axis=0, keepdims=True))
            cum_rows.append(jnp.sum(by_spread, axis=0, keepdims=True))
            cum_columns.append(jnp.sum(by_spread, axis=1, keepdims=True))
            score_grad = score_grad + by_decay * dt_row
            halves.append(dot_rows(to_low(decay * part.scores * dt_row), dy_pair))
        outs.append(jnp.where(lane < 64, halves[0], halves[1]))
    x_grad = x_grad + jnp.concatenate(outs, axis=1)
    score_low = to_low(score_grad)
    c_grad = c_grad + dot_full(score_low, part.b_low)
    b_grad = b_grad + dot_rows(score_low, part.c_low)

    heads = len(dt_rows)
    blank = jnp.zeros((LANES - heads, length), jnp.float32)
    dt_grad = dt_grad + jnp.concatenate(dt_rows + [blank], axis=0).T
    cum_grad = cum_grad - jnp.concatenate(cum_rows + [blank], axis=0).T
    for head in range(heads):
        cum_grad = cum_grad + jnp.where(lane == head, cum_columns[head], 0.0)
    at_end = iota_of((length, 1), 0) == length - 1
    cum_grad = cum_grad + jnp.where(at_end, end_grad, 0.0)
    upper = (iota_of((length, length), 1) >= iota_of((length, length), 0)).astype(jnp.float32)
    log_grad = dot_full(upper, cum_grad, HIGHEST)
    dt_grad = dt_grad + log_grad * part.rate
    dt_in_grad = dt_grad * jax.nn.sigmoid(part.dt_in)
    dt_in_grad = jnp.where(lane < heads, dt_in_grad, 0.0)
    head_grad_ref[0:1, :] += jnp.sum(dt_in_grad, axis=0, keepdims=True)
    head_grad_ref[1:2, :] += jnp.sum(log_grad * part.dt, axis=0, keepdims=True) * part.rate
    skip_sum = jnp.broadcast_to(jnp.sum(dy * part.x, axis=0, keepdims=True), (8, channels))
    head_grad_ref[2:3, :] += dot_full(skip_sum, lanes_of, HIGHEST)[:1, :]

    act_grad = jnp.concatenate([x_grad, b_grad, c_grad], axis=1)
    value_grad = act_grad * part.sig * (1.0 + part.value * (1.0 - part.sig))
    conv_grad_ref[4:5, :] += jnp.sum(value_grad, axis=0, keepdims=True)
    for offset in range(4):
        conv_grad_ref[3 - offset : 4 - offset, :] += jnp.sum(
            value_grad * part.shifted[offset], axis=0, keepdims=True
        )
    joined = jnp.concatenate([value_grad, after[...]], axis=0)
    places = start + iota_of((length, 1), 0)
    rows_grad = value_grad * conv_ref[3:4, :]
    for offset in range(1, 4):
        moved = pltpu.roll(joined, length + 8 - offset, 0)[:length, :]
        same = (ids_at(places + offset, ends_ref) == part.ids) & (
            places + offset < steps * length
        )
        rows_grad = rows_grad + jnp.where(same, moved, 0.0) * conv_ref[3 - offset : 4 - offset, :]
    after[...] = value_grad[:8, :]
    drows_ref[...] += to_low(
        dot_rows(picks, to_low(jnp.concatenate([rows_grad, dt_in_grad], axis=1)))
    )

    stages = reducer.inner + 3
    last = dy_ref.shape[0] // length - 1
    for count in range(stages):

        @pl.when(order == min(count, last))
        def _():
            reducer.step(count)

    @pl.when(order == steps - 1)
    def _():
        reducer.finish()


def scan_backward(
    ends, deal_row, seq_rows, states, dy, conv_table, head_table, other, freight
):
    group_rows, width = seq_rows.shape
    channels = dy.shape[1]
    steps = group_rows // STRETCH
    return run(
        scan_backward_kernel,
        (ends, deal_row, seq_rows, states, dy, conv_table, head_table, other),
        grid=(steps,),
        in_specs=[
            pl.BlockSpec(memory_space=pltpu.SMEM),
            whole(deal_row.shape),
            once(seq_rows.shape),
            pl.BlockSpec((1, channels, LANES), lambda step: (steps - 1 - step, 0, 0)),
            once(dy.shape),
            whole(conv_table.shape),
            whole(head_table.shape),
            pl.BlockSpec(memory_space=pl.ANY),
        ],
        out_specs=[
            whole((group_rows, width)),
            whole(conv_table.shape),
            whole(head_table.shape),
            whole(other.shape[2:]),
        ],
        out_shape=[
            jax.ShapeDtypeStruct((group_rows, width), jnp.bfloat16),
            jax.ShapeDtypeStruct(conv_table.shape, jnp.float32),
            jax.ShapeDtypeStruct(head_table.shape, jnp.float32),
            jax.ShapeDtypeStruct(other.shape[2:], jnp.float32),
        ],
        scratch=[
            pltpu.VMEM((8, conv_table.shape[1]), jnp.float32),
            pltpu.VMEM((channels, LANES), jnp.float32),
        ]
        + Reducer.scratch(other.shape[0], *other.shape[2:]),
        freight=freight,
        flips=FLIPS,
        inner=other.shape[0],
        micros=40,
        name="scan_backward",
    )


def whole(shape):
    return pl.BlockSpec(shape, lambda *steps: (0,) * len(shape))


def once(shape):
    return pl.BlockSpec(
        shape, lambda *steps: (0,) * len(shape), pipeline_mode=pl.Buffered(buffer_count=1)
    )


MESH = pl.DeviceIdType.MESH
FLIPS = (1, 2, 4)


def flipped(place, flip):
    result = place
    for bit in FLIPS:
        if flip & bit:
            result = result + bit - 2 * bit * lax.rem(lax.div(place, bit), 2)
    return result


def own_shard_group(inner):
    shard = lax.axis_index("shard")
    place = lax.rem(shard, inner)
    return place, shard - place


def peers_in_order(place, inner):
    if inner == 1:
        return []
    if inner == 4:
        half = lax.div(place, 2)
        return [flipped(place, 1), 2 - half, 3 - 3 * half]
    return [lax.rem(place + shift, inner) for shift in range(1, inner)]


def greet(flips, inner):
    barrier = pltpu.get_barrier_semaphore()
    part = lax.axis_index("seq")
    place, first = own_shard_group(inner)
    for flip in flips:
        pl.semaphore_signal(
            barrier, inc=1, device_id={"seq": flipped(part, flip)}, device_id_type=MESH
        )
    for peer in peers_in_order(place, inner):
        pl.semaphore_signal(
            barrier, inc=1, device_id={"shard": first + peer}, device_id_type=MESH
        )
    pl.semaphore_wait(barrier, len(flips) + inner - 1)


class Parcel:
    flips = ()
    sems = 1

    def __init__(self, array, shift, inner, index=None, output=None):
        self.array, self.shift, self.inner, self.index = array, shift, inner, index
        self.shape = array.shape if index is None else array.shape[1:]
        self.output = output

    def moves(self, source, target):
        place, first = own_shard_group(self.inner)
        to = lax.rem(place + self.shift, self.inner)
        if self.index is not None:
            source = source.at[self.index(to)]
        return [(source, target, target, {"shard": first + to})]

    def stays(self, source, target):
        return []


class PlaneSwap:
    flips = (1, 2, 3, 4, 5, 6, 7)
    inner = 1
    sems = 8

    output = None

    def __init__(self, array):
        self.array, self.shape = array, array.shape

    def moves(self, source, target):
        part = lax.axis_index("seq")
        return [
            (
                source.at[flipped(part, flip)],
                target.at[part],
                target.at[flipped(part, flip)],
                {"seq": flipped(part, flip)},
            )
            for flip in self.flips
        ]

    def stays(self, source, target):
        part = lax.axis_index("seq")
        return [(source.at[part], target.at[part])]


COLLECTIVES = []


def run(
    kernel,
    args,
    *,
    in_specs,
    out_specs,
    out_shape,
    name,
    micros,
    grid=(),
    scratch=(),
    freight=(),
    flips=(),
    inner=1,
    late=False,
):
    freight = list(freight)
    flips = tuple(sorted(set(flips).union(*[item.flips for item in freight])))
    inner = max([inner] + [item.inner for item in freight])
    talks = bool(flips) or inner > 1
    count_in, count_out, count_scratch = len(args), len(out_shape), len(scratch)
    count = len(freight)
    loaded = [item for item in freight if item.output is None]

    def wrapped(*refs):
        ins, refs = refs[:count_in], refs[count_in:]
        sources, refs = list(refs[: len(loaded)]), refs[len(loaded) :]
        outs, refs = refs[:count_out], refs[count_out:]
        sources = [
            sources.pop(0) if item.output is None else outs[item.output] for item in freight
        ]
        targets, refs = refs[:count], refs[count:]
        own, refs = refs[:count_scratch], refs[count_scratch:]

        def remote(item, place, order, source, target, device):
            send, recv = refs[3 * place : 3 * place + 2]
            return pltpu.make_async_remote_copy(
                src_ref=source,
                dst_ref=target,
                send_sem=send.at[order],
                recv_sem=recv.at[order],
                device_id=device,
                device_id_type=MESH,
            )

        def moves(chosen):
            for place, item in enumerate(freight):
                if not chosen(item):
                    continue
                for order, move in enumerate(item.moves(sources[place], targets[place])):
                    yield item, place, order, move

        def stays(chosen):
            for place, item in enumerate(freight):
                if not chosen(item):
                    continue
                for source, target in item.stays(sources[place], targets[place]):
                    yield pltpu.make_async_copy(source, target, refs[3 * place + 2])

        def depart(chosen=lambda item: True):
            for item, place, order, (source, target, _, device) in moves(chosen):
                remote(item, place, order, source, target, device).start()
            for copy in stays(chosen):
                copy.start()

        def arrive(chosen=lambda item: True):
            for item, place, order, (source, target, arrival, device) in moves(chosen):
                remote(item, place, order, source, arrival, device).wait_recv()
                remote(item, place, order, source, target, device).wait_send()
            for copy in stays(chosen):
                copy.wait()

        if grid:
            at = [pl.program_id(axis) for axis in range(len(grid))]
            first, last = at[0] == 0, at[0] == grid[0] - 1
            for axis in range(1, len(grid)):
                first = first & (at[axis] == 0)
                last = last & (at[axis] == grid[axis] - 1)
            if talks:

                @pl.when(first)
                def _():
                    greet(flips, inner)
                    if not late:
                        depart()

            if late:
                kernel(depart, arrive, targets, *ins, *outs, *own)
            else:
                kernel(*ins, *outs, *own)
            if talks and not late:
                pl.when(last)(arrive)
        else:
            if talks:
                greet(flips, inner)
            if late:
                kernel(depart, *ins, *outs, *own)
            else:
                depart()
                kernel(*ins, *outs, *own)
            arrive()

    anywhere = pl.BlockSpec(memory_space=pl.ANY)
    extra = {}
    if talks:
        COLLECTIVES.append(name)
        extra = dict(collective_id=len(COLLECTIVES), has_side_effects=True)
    sems = []
    for item in freight:
        sems += [
            pltpu.SemaphoreType.DMA((item.sems,)),
            pltpu.SemaphoreType.DMA((item.sems,)),
            pltpu.SemaphoreType.DMA(()),
        ]
    results = pl.pallas_call(
        wrapped,
        grid=grid,
        in_specs=list(in_specs) + [anywhere] * len(loaded),
        out_specs=list(out_specs) + [anywhere] * count,
        out_shape=list(out_shape)
        + [jax.ShapeDtypeStruct(item.shape, item.array.dtype) for item in freight],
        scratch_shapes=list(scratch) + sems,
        compiler_params=pltpu.CompilerParams(vmem_limit_bytes=VMEM_BYTES, **extra),
        cost_estimate=cost_of(micros),
        name=name,
    )(*args, *[item.array for item in loaded])
    results = list(results)
    if freight:
        return results[:count_out] + [results[count_out:]]
    return results


class LineSum:
    def __init__(self, inner, sums, from_below, from_above, send, below_recv, above_recv):
        self.inner = inner
        self.sums, self.from_below, self.from_above = sums, from_below, from_above
        self.send, self.below_recv, self.above_recv = send, below_recv, above_recv
        self.place, self.first = own_shard_group(inner)
        self.targets = list(reversed(peers_in_order(self.place, inner))) + [self.place]

    def copy(self, order, up):
        target = self.targets[order]
        inbox = self.from_below if up else self.from_above
        recv = self.below_recv if up else self.above_recv
        return pltpu.make_async_remote_copy(
            src_ref=self.sums.at[order],
            dst_ref=inbox.at[target],
            send_sem=self.send.at[order],
            recv_sem=recv.at[target],
            device_id={"shard": self.first + self.place + (1 if up else -1)},
            device_id_type=MESH,
        )

    def arrived(self, target, up):
        inbox = self.from_below if up else self.from_above
        recv = self.below_recv if up else self.above_recv
        pltpu.make_async_remote_copy(
            src_ref=inbox.at[target],
            dst_ref=inbox.at[target],
            send_sem=self.send.at[0],
            recv_sem=recv.at[target],
            device_id={"shard": self.first + self.place + (-1 if up else 1)},
            device_id_type=MESH,
        ).wait_recv()
        return to_full(inbox[target])

    def ways(self):
        return ((True, self.place > 0), (False, self.place < self.inner - 1))

    def push(self, order):
        target = self.targets[order]
        for up, comes in self.ways():
            heads = (target > self.place) if up else (target < self.place)

            @pl.when(heads & comes)
            def _():
                self.sums[order] = to_low(
                    to_full(self.sums[order]) + self.arrived(target, up)
                )

            @pl.when(heads)
            def _():
                self.copy(order, up).start()

    def add_own(self, total):
        for up, comes in self.ways():

            @pl.when(comes)
            def _():
                total[...] += self.arrived(self.place, up)

    def finish(self):
        for order in range(self.inner - 1):
            for up in (True, False):
                target = self.targets[order]

                @pl.when((target > self.place) if up else (target < self.place))
                def _():
                    self.copy(order, up).wait_send()

    @staticmethod
    def scratch(inner, rows, width):
        sems = lambda *shape: pltpu.SemaphoreType.DMA(shape)
        return [
            pltpu.VMEM((max(1, inner - 1), rows, width), jnp.bfloat16),
            pltpu.VMEM((inner, rows, width), jnp.bfloat16),
            pltpu.VMEM((inner, rows, width), jnp.bfloat16),
            sems(max(1, inner - 1)),
            sems(inner),
            sems(inner),
        ]


class Reducer:
    def __init__(self, inner, p_ref, total, refs):
        self.inner, self.p_ref, self.total = inner, p_ref, total
        self.held, self.paired, self.turned, self.crossed = refs[:4]
        self.load, self.core_send, self.core_recv = refs[4:7]
        self.turn_send, self.turn_recv, self.cross_send, self.cross_recv = refs[7:11]
        self.line = LineSum(inner, *refs[11:])
        self.part = lax.axis_index("seq")
        half = self.held.shape[2] // 2
        self.spans = [pl.ds(0, half), pl.ds(half, half)]

    @staticmethod
    def scratch(inner, rows, width):
        low = jnp.bfloat16
        sems = lambda *shape: pltpu.SemaphoreType.DMA(shape)
        return [
            pltpu.VMEM((inner, 4, rows, width), low),
            pltpu.VMEM((inner, 4, rows, width), low),
            pltpu.VMEM((inner, 2, rows // 2, width), low),
            pltpu.VMEM((inner, 4, rows // 2, width), low),
            sems(inner, 4),
            sems(inner, 4),
            sems(inner, 4),
            sems(inner, 2),
            sems(inner, 2),
            sems(inner, 4),
            sems(inner, 4),
        ] + LineSum.scratch(inner, rows, width)

    EVENS = (6, 2, 4, 0)

    def to_core(self, order, slot):
        return pltpu.make_async_remote_copy(
            src_ref=self.p_ref.at[
                self.line.targets[order], flipped(self.part, self.EVENS[slot] + 1)
            ],
            dst_ref=self.paired.at[order, slot],
            send_sem=self.core_send.at[order, slot],
            recv_sem=self.core_recv.at[order, slot],
            device_id={"seq": flipped(self.part, 1)},
            device_id_type=MESH,
        )

    def loading(self, order, slot):
        return pltpu.make_async_copy(
            self.p_ref.at[self.line.targets[order], flipped(self.part, self.EVENS[slot])],
            self.held.at[order, slot],
            self.load.at[order, slot],
        )

    def turn(self, order, span):
        return pltpu.make_async_remote_copy(
            src_ref=self.held.at[order, 0, self.spans[span]],
            dst_ref=self.turned.at[order, span],
            send_sem=self.turn_send.at[order, span],
            recv_sem=self.turn_recv.at[order, span],
            device_id={"seq": flipped(self.part, (2, 4)[span])},
            device_id_type=MESH,
        )

    CROSSINGS = ((1, 2, 0), (2, 4, 1), (2, 4, 0), (1, 2, 1))

    def cross(self, order, kind):
        slot, flip, span = self.CROSSINGS[kind]
        return pltpu.make_async_remote_copy(
            src_ref=self.held.at[order, slot, self.spans[span]],
            dst_ref=self.crossed.at[order, kind],
            send_sem=self.cross_send.at[order, kind],
            recv_sem=self.cross_recv.at[order, kind],
            device_id={"seq": flipped(self.part, flip)},
            device_id_type=MESH,
        )

    def begin(self):
        for order in range(self.inner):
            for slot in range(4):
                self.to_core(order, slot).start()
                self.loading(order, slot).start()

    def total_of(self, order, slot):
        self.loading(order, slot).wait()
        self.to_core(order, slot).wait_recv()
        return to_full(self.held[order, slot]) + to_full(self.paired[order, slot])

    def stage_a(self, order):
        self.held[order, 0] = to_low(self.total_of(order, 0))
        for span in range(2):
            self.turn(order, span).start()
        for slot in (1, 2):
            self.held[order, slot] = to_low(self.total_of(order, slot))
            self.cross(order, slot - 1).start()

    def stage_b(self, order):
        for kind in (2, 3):
            slot, _, span = self.CROSSINGS[kind]
            self.turn(order, span).wait_recv()
            at = self.spans[span]
            self.held[order, slot, at] = to_low(
                to_full(self.held[order, slot, at]) + to_full(self.turned[order, span])
            )
            self.cross(order, kind).start()

    def stage_c(self, order):
        total = self.total_of(order, 3)
        for kind in range(4):
            self.cross(order, kind).wait_recv()
        crossed = [to_full(self.crossed[order, kind]) for kind in range(4)]
        total = total + jnp.concatenate(
            [crossed[0] + crossed[2], crossed[1] + crossed[3]], axis=0
        )
        if order == self.inner - 1:
            self.total[...] = total
        else:
            self.line.sums[order] = to_low(total)

    def stage_d(self, order):
        if order == self.inner - 1:
            self.line.add_own(self.total)
        else:
            self.line.push(order)

    def step(self, count):
        for stage, late in (
            (self.stage_a, 0),
            (self.stage_b, 1),
            (self.stage_c, 2),
            (self.stage_d, 3),
        ):
            if 0 <= count - late < self.inner:
                stage(count - late)

    def finish(self):
        for order in range(self.inner):
            for slot in range(4):
                self.to_core(order, slot).wait_send()
            for span in range(2):
                self.turn(order, span).wait_send()
            for kind in range(4):
                self.cross(order, kind).wait_send()
        self.line.finish()

    def whole(self):
        self.begin()
        for count in range(self.inner + 3):
            self.step(count)
        self.finish()


def reduce_kernel(inner, p_ref, out_ref, *scratch):
    Reducer(inner, p_ref, out_ref, scratch).whole()


def reduce_rows(partial, freight=()):
    inner, _, rows, width = partial.shape
    return run(
        functools.partial(reduce_kernel, inner),
        (partial,),
        in_specs=[pl.BlockSpec(memory_space=pl.ANY)],
        out_specs=[pl.BlockSpec(memory_space=pltpu.VMEM)],
        out_shape=[jax.ShapeDtypeStruct((rows, width), jnp.float32)],
        scratch=Reducer.scratch(inner, rows, width),
        freight=freight,
        flips=FLIPS,
        inner=inner,
        micros=25 * inner,
        name="reduce_rows",
    )


def plane_gather(own, target, send, recv):
    part = lax.axis_index("seq")
    half = own.shape[0] // 2
    spans = [pl.ds(0, half), pl.ds(half, half)]
    started = []

    def copy_of(kind, block, span, flip, from_own=False):
        place = target(block).at[spans[span]]
        return pltpu.make_async_remote_copy(
            src_ref=own.at[spans[span]] if from_own else place,
            dst_ref=place,
            send_sem=send.at[kind],
            recv_sem=recv.at[kind],
            device_id={"seq": flipped(part, flip)},
            device_id_type=MESH,
        )

    def push(kind, block, span, flip, from_own=False):
        copy = copy_of(kind, block, span, flip, from_own)
        copy.start()
        started.append(copy)

    def arrived(kind, block, span, flip):
        copy_of(kind, block, span, flip).wait_recv()

    def first():
        for kind, span, flip in (
            (3, 1, 2), (4, 0, 4), (2, 0, 2), (5, 1, 4), (0, 0, 1), (1, 1, 1)
        ):
            push(kind, part, span, flip, True)

    def second():
        side, over = flipped(part, 2), flipped(part, 4)
        arrived(3, side, 1, 2)
        push(6, side, 1, 4)
        arrived(4, over, 0, 4)
        push(7, over, 0, 2)
        push(9, side, 1, 1)
        push(10, over, 0, 1)
        arrived(2, side, 0, 2)
        push(8, side, 0, 1)
        arrived(5, over, 1, 4)
        push(11, over, 1, 1)

    def third():
        far = flipped(part, 6)
        arrived(6, far, 1, 4)
        push(13, far, 1, 1)
        arrived(7, far, 0, 2)
        push(12, far, 0, 1)

    def last():
        for kind, flip, span in (
            (0, 1, 0), (1, 1, 1), (9, 3, 1), (10, 5, 0), (8, 3, 0), (11, 5, 1), (13, 7, 1), (12, 7, 0)
        ):
            arrived(kind, flipped(part, flip), span, 1)
        for copy in started:
            copy.wait_send()

    return first, second, third, last


def line_gather(inner, own, target, send, recv):
    place, first = own_shard_group(inner)
    half = own.shape[0] // 2
    spans = [pl.ds(0, half), pl.ds(half, half)]

    def copy_of(way, step, span):
        block = place - step if way == 0 else place + step
        to = place + 1 if way == 0 else place - 1
        spot = target(block).at[spans[span]]
        return pltpu.make_async_remote_copy(
            src_ref=own.at[spans[span]] if step == 0 else spot,
            dst_ref=spot,
            send_sem=send.at[way, step, span],
            recv_sem=recv.at[way, step, span],
            device_id={"shard": first + to},
            device_id_type=MESH,
        )

    def sends(way, step):
        if way == 0:
            return (place < inner - 1) & (place >= step)
        return (place > 0) & (place + step < inner)

    def receives(way, step):
        return place >= step if way == 0 else place + step < inner

    def start(step, span):
        for way in range(2):

            @pl.when(sends(way, step))
            def _():
                copy_of(way, step, span).start()

    def begin():
        for span in range(2):
            start(0, span)

    def onward(step):
        for span in range(2):
            for way in range(2):

                @pl.when(receives(way, step))
                def _():
                    block = place - step if way == 0 else place + step
                    spot = target(block).at[spans[span]]
                    pltpu.make_async_remote_copy(
                        src_ref=spot,
                        dst_ref=spot,
                        send_sem=send.at[way, step - 1, span],
                        recv_sem=recv.at[way, step - 1, span],
                        device_id={"shard": block + first},
                        device_id_type=MESH,
                    ).wait_recv()

            if step < inner - 1:
                start(step, span)

    def finish():
        for step in range(inner - 1):
            for span in range(2):
                for way in range(2):

                    @pl.when(sends(way, step))
                    def _():
                        copy_of(way, step, span).wait_send()

    return begin, onward, finish


def group_gather(inner, own, target, sems):
    part = lax.axis_index("seq")
    place, _ = own_shard_group(inner)
    sources = [place] + peers_in_order(place, inner)
    line_send, line_recv, send, recv = sems
    line = line_gather(inner, own, lambda p: target(p, part), line_send, line_recv)
    planes = [
        plane_gather(
            own if order == 0 else target(source, part),
            lambda b, source=source: target(source, b),
            send.at[order],
            recv.at[order],
        )
        for order, source in enumerate(sources)
    ]
    return line, planes


def group_sems(inner):
    sems = lambda *shape: pltpu.SemaphoreType.DMA(shape)
    steps = max(1, inner - 1)
    return [sems(2, steps, 2), sems(2, steps, 2), sems(inner, 14), sems(inner, 14)]


def gather_kernel(inner, depart, x_ref, out_ref, own_sem, *sems):
    part = lax.axis_index("seq")
    place, _ = own_shard_group(inner)
    own = pltpu.make_async_copy(x_ref, out_ref.at[place, part], own_sem)
    (begin, onward, finish), planes = group_gather(
        inner, x_ref, lambda p, b: out_ref.at[p, b], sems
    )
    if inner > 1:
        begin()
    planes[0][0]()
    own.start()
    planes[0][1]()
    for order in range(1, inner):
        onward(order)
        if order == inner - 1:
            depart()
        planes[order][0]()
        planes[order - 1][2]()
        planes[order][1]()
    if inner == 1:
        depart()
    planes[inner - 1][2]()
    for stages in planes:
        stages[3]()
    if inner > 1:
        finish()
    own.wait()


def gather_rows(x, inner, freight=()):
    rows, width = x.shape
    seq_devices = lax.axis_size("seq")
    return run(
        functools.partial(gather_kernel, inner),
        (x,),
        in_specs=[pl.BlockSpec(memory_space=pl.ANY)],
        out_specs=[pl.BlockSpec(memory_space=pl.ANY)],
        out_shape=[jax.ShapeDtypeStruct((inner, seq_devices, rows, width), x.dtype)],
        scratch=[pltpu.SemaphoreType.DMA(())] + group_sems(inner),
        freight=freight,
        flips=FLIPS,
        inner=inner,
        late=True,
        micros=25 * inner,
        name="gather_rows",
    )


def begin_kernel(
    inner, x_ref, g_ref, w_ref, s_ref, r_ref, x_out, g_out, w_out, s_out, r_out, own_sems, *sems
):
    part = lax.axis_index("seq")
    place, _ = own_shard_group(inner)
    rows = w_ref.shape[0]
    targets = [
        lambda p: s_out.at[p],
        lambda p: w_out.at[pl.ds(p * rows, rows)],
        lambda p: r_out.at[p],
    ]
    sources = [s_ref, w_ref, r_ref]
    lines = [
        line_gather(inner, source, target, sems[2 * order], sems[2 * order + 1])
        for order, (source, target) in enumerate(zip(sources, targets))
    ]
    line, planes = group_gather(inner, g_ref, lambda p, b: g_out.at[p, b], sems[6:10])
    lines.append(line)
    x_plane = plane_gather(x_ref, lambda b: x_out.at[b], sems[10], sems[11])
    rows_line = lines.pop(2)
    for begin_line, _, _ in lines:
        begin_line()
    x_plane[0]()
    planes[0][0]()
    owns = [
        pltpu.make_async_copy(source, target(place), own_sems.at[order])
        for order, (source, target) in enumerate(zip(sources, targets))
    ]
    owns.append(pltpu.make_async_copy(x_ref, x_out.at[part], own_sems.at[3]))
    owns.append(pltpu.make_async_copy(g_ref, g_out.at[place, part], own_sems.at[4]))
    for copy in owns:
        copy.start()
    x_plane[1]()
    planes[0][1]()
    x_plane[2]()
    planes[0][2]()
    for step in range(1, inner):
        for _, onward, _ in reversed(lines):
            onward(step)
        if step == max(1, inner - 2):
            rows_line[0]()
        planes[step][0]()
        if step > 1:
            planes[step - 1][2]()
        planes[step][1]()
    rows_line[1](1)
    planes[inner - 1][2]()
    for step in range(2, inner):
        rows_line[1](step)
    x_plane[3]()
    for stages in planes:
        stages[3]()
    for _, _, finish in lines + [rows_line]:
        finish()
    for copy in owns:
        copy.wait()


def begin(x, grad, weights, small, rows, inner):
    seq_devices = lax.axis_size("seq")
    anywhere = pl.BlockSpec(memory_space=pl.ANY)
    sems = lambda *shape: pltpu.SemaphoreType.DMA(shape)
    line_sems = [sems(2, inner - 1, 2)] * 6
    return run(
        functools.partial(begin_kernel, inner),
        (x, grad, weights, small, rows),
        in_specs=[anywhere] * 5,
        out_specs=[anywhere] * 5,
        out_shape=[
            jax.ShapeDtypeStruct((seq_devices,) + x.shape, x.dtype),
            jax.ShapeDtypeStruct((inner, seq_devices) + grad.shape, grad.dtype),
            jax.ShapeDtypeStruct((inner * weights.shape[0], weights.shape[1]), weights.dtype),
            jax.ShapeDtypeStruct((inner,) + small.shape, small.dtype),
            jax.ShapeDtypeStruct((inner,) + rows.shape, rows.dtype),
        ],
        scratch=[sems(5)] + line_sems + group_sems(inner) + [sems(14), sems(14)],
        flips=FLIPS,
        inner=inner,
        micros=130,
        name="begin",
    )


def settle_kernel(
    inner,
    counts,
    spot,
    hidden_ref,
    small_ref,
    x_ref,
    mix_ref,
    gain_ref,
    *refs,
):
    part = lax.axis_index("seq")
    place, _ = own_shard_group(inner)
    parts, refs = refs[:counts], refs[counts:]
    tokens_out, refs = refs[0], refs[1:]
    outs, refs = refs[: counts + 1], refs[counts + 1 :]
    hidden_sum, small_held, small_sum, small_load = refs[:4]
    refs = refs[4:]
    take = len(Reducer.scratch(1, 16, LANES))
    hidden = Reducer(1, hidden_ref, hidden_sum, refs[:take])
    small = Reducer(inner, small_held, small_sum, refs[take : 2 * take])
    refs = refs[2 * take :]
    lines, totals, planes, owns = [], [], [], []
    for index in range(counts + 1):
        low, gsend, grecv, here = refs[:4]
        refs = refs[4:]
        out = outs[index]
        planes.append(plane_gather(low, lambda b, out=out: out.at[b], gsend, grecv))
        owns.append((low, pltpu.make_async_copy(low, out.at[part], here)))
    loads = []
    for index in range(counts):
        total, load = refs[:2]
        line = LineSum(inner, *refs[2:8])
        refs = refs[8:]
        lines.append(line)
        totals.append(total)
        for order in range(inner - 1):
            loads.append(
                pltpu.make_async_copy(
                    parts[index].at[line.targets[order]], line.sums.at[order], load.at[order]
                )
            )
        loads.append(
            pltpu.make_async_copy(parts[index].at[place], owns[index][0], load.at[inner - 1])
        )
    small_loading = pltpu.make_async_copy(small_ref, small_held, small_load)
    for copy in loads:
        copy.start()
    small_loading.start()
    hidden.begin()

    def send_part(index):
        for copy in loads[index * inner : (index + 1) * inner]:
            copy.wait()
        totals[index][...] = to_full(owns[index][0][...])
        for order in range(inner - 1):
            lines[index].push(order)

    def gather_part(index):
        lines[index].add_own(totals[index])
        owns[index][0][...] = to_low(totals[index][...])
        planes[index][0]()
        owns[index][1].start()

    hidden.step(0)
    send_part(0)
    for count in range(1, 4):
        hidden.step(count)
    x = to_full(x_ref[...])
    scale = norm_scale(x)
    unit = x * scale
    grad = hidden_sum[...]
    gain_grad = jnp.sum(grad * unit, axis=0, keepdims=True)
    scaled = grad * gain_ref[...]
    mean = jnp.mean(scaled * unit, axis=1, keepdims=True)
    tokens_out[...] = to_low(mix_ref[...] + scale * (scaled - unit * mean))
    small_loading.wait()
    wide = small_held.shape[3]
    depth = gain_grad.shape[1] // inner
    rows16 = pl.ds(spot // 16 * 16, 16)
    at_row = iota_of((16, wide), 0) == spot % 16
    for shard in range(inner):
        row = gain_grad[:, shard * depth : (shard + 1) * depth]
        if depth < wide:
            row = jnp.concatenate([row, jnp.zeros((1, wide - depth), jnp.float32)], axis=1)
        old = to_full(small_held[shard, 0, rows16])
        small_held[shard, 0, rows16] = to_low(jnp.where(at_row, old + row, old))
    small.begin()
    small.step(0)
    for index in range(1, counts):
        send_part(index)
        small.step(index)
        gather_part(index - 1)
        if index > 1:
            planes[index - 2][1]()
    for count in range(counts, inner + 3):
        small.step(count)
    owns[counts][0][...] = to_low(small_sum[...])
    planes[counts][0]()
    owns[counts][1].start()
    if counts > 1:
        planes[counts - 2][1]()
        planes[counts - 2][2]()
    gather_part(counts - 1)
    planes[counts][1]()
    planes[counts][2]()
    planes[counts - 1][1]()
    for index in range(counts - 2):
        planes[index][2]()
    planes[counts - 1][2]()
    for plane in planes:
        plane[3]()
    hidden.finish()
    small.finish()
    for line in lines:
        line.finish()
    for _, copy in owns:
        copy.wait()


def settle(hidden, small, x, mix, gain, parts, spot, inner):
    _, _, rows, width = hidden.shape
    seq_devices = lax.axis_size("seq")
    anywhere = pl.BlockSpec(memory_space=pl.ANY)
    inside = pl.BlockSpec(memory_space=pltpu.VMEM)
    low = jnp.bfloat16
    sems = lambda *shape: pltpu.SemaphoreType.DMA(shape)
    small_rows, small_wide = small.shape[2:]
    shapes = [part.shape[1:] for part in parts] + [(small_rows, small_wide)]
    scratch = [
        pltpu.VMEM((rows, width), jnp.float32),
        pltpu.VMEM(small.shape, low),
        pltpu.VMEM((small_rows, small_wide), jnp.float32),
        sems(),
    ]
    scratch += Reducer.scratch(1, rows, width)
    scratch += Reducer.scratch(inner, small_rows, small_wide)
    for shape in shapes:
        scratch += [pltpu.VMEM(shape, low), sems(14), sems(14), sems()]
    for shape in shapes[:-1]:
        scratch += [pltpu.VMEM(shape, jnp.float32), sems(inner)]
        scratch += LineSum.scratch(inner, *shape)
    return run(
        functools.partial(settle_kernel, inner, len(parts), spot),
        (hidden, small, x, mix, gain) + tuple(parts),
        in_specs=[anywhere] * 2 + [inside] * 3 + [anywhere] * len(parts),
        out_specs=[inside] + [anywhere] * len(shapes),
        out_shape=[jax.ShapeDtypeStruct((rows, width), low)]
        + [jax.ShapeDtypeStruct((seq_devices,) + shape, low) for shape in shapes],
        scratch=scratch,
        flips=FLIPS,
        inner=inner,
        micros=90,
        name="settle",
    )


def params_of(limit=VMEM_BYTES):
    return pltpu.CompilerParams(vmem_limit_bytes=limit)


def project_kernel(x_ref, gain_ref, w_ref, dt_ref, hidden_ref, gate_ref, rows_ref):
    x = to_full(x_ref[...])
    hidden = to_low(x * norm_scale(x) * gain_ref[...])
    hidden_ref[...] = hidden
    gate_width = gate_ref.shape[1]
    used = gate_width + rows_ref.shape[1] - LANES
    projected = dot_full(hidden, w_ref[:, :used])
    gate_ref[...] = projected[:, :gate_width]
    rest = used - gate_width
    rows_ref[:, :rest] = to_low(projected[:, gate_width:])
    rows_ref[:, rest:] = to_low(dot_full(hidden, dt_ref[...]))


def project(x, gain, weights, dt_weights, gate_width, columns, freight=()):
    rows, width = x.shape
    columns = columns + LANES
    tile = 256
    block = lambda extent: pl.BlockSpec((tile, extent), lambda step: (step, 0))
    return run(
        project_kernel,
        (x, gain, weights, dt_weights,),
        grid=(rows // tile,),
        in_specs=[
            block(width), whole(gain.shape), whole(weights.shape), whole(dt_weights.shape)
        ],
        out_specs=[block(width), block(gate_width), block(columns - gate_width)],
        out_shape=[
            jax.ShapeDtypeStruct((rows, width), jnp.bfloat16),
            jax.ShapeDtypeStruct((rows, gate_width), jnp.float32),
            jax.ShapeDtypeStruct((rows, columns - gate_width), jnp.bfloat16),
        ],
        freight=freight,
        micros=11,
        name="project",
    )


def put_split(columns, rows):
    lane = iota_of((rows, LANES), 1)
    result = jnp.zeros((rows, LANES), jnp.float32)
    for place, column in enumerate(columns):
        high = to_full(to_low(column))
        result = jnp.where(lane == 2 * place, high, result)
        result = jnp.where(lane == 2 * place + 1, column - high, result)
    return to_low(result)


def mix_out_kernel(y_ref, gate_ref, gain_ref, packed_ref, part_ref, w_ref):
    width = w_ref.shape[1]

    @pl.when(pl.program_id(0) == 0)
    def _():
        unpack_rows(packed_ref, w_ref, True)

    gated = to_full(y_ref[...]) * jax.nn.silu(gate_ref[...])
    part_ref[0, :, :width] = to_low(dot_full(to_low(gated * gain_ref[...]), w_ref[...]))
    squares = jnp.sum(gated * gated, axis=1, keepdims=True)
    part_ref[0, :, width:] = put_split([squares], y_ref.shape[0])


def mix_out(y, gate, gain, weights, blocks, freight=()):
    rows, channels = y.shape
    width = weights.shape[2]
    tile = rows // blocks
    block = pl.BlockSpec((tile, channels), lambda step: (step, 0))
    return run(
        mix_out_kernel,
        (y, gate, gain, weights),
        grid=(blocks,),
        in_specs=[block, block, whole(gain.shape), whole(weights.shape)],
        out_specs=[pl.BlockSpec((1, tile, width + LANES), lambda step: (step, 0, 0))],
        out_shape=[jax.ShapeDtypeStruct((blocks, tile, width + LANES), jnp.bfloat16)],
        scratch=[pltpu.VMEM((channels, width), jnp.bfloat16)],
        freight=freight,
        micros=9,
        name="mix_out",
    )


def mix_back_kernel(
    mix_ref,
    y_ref,
    gate_ref,
    gain_ref,
    packed_ref,
    dy_ref,
    dgate_ref,
    w_grad_ref,
    gain_grad_ref,
    total,
    w_ref,
):
    step = pl.program_id(0)
    width = w_ref.shape[1]

    @pl.when(step == 0)
    def _():
        unpack_rows(packed_ref, w_ref, True)
        total[...] = jnp.zeros_like(total)
        gain_grad_ref[...] = jnp.zeros_like(gain_grad_ref)

    mix = mix_ref[0, :, :width]
    extra = to_full(mix_ref[0, :, width:])
    share = extra[:, 0:1] + extra[:, 1:2]
    scale = extra[:, 2:3] + extra[:, 3:4]
    normed_grad = dot_lanes(mix, w_ref[...])
    y = to_full(y_ref[...])
    gate = gate_ref[...]
    sig = jax.nn.sigmoid(gate)
    act = gate * sig
    unit = y * act * scale
    gain = gain_ref[...]
    gain_grad_ref[0:1, :] += jnp.sum(normed_grad * unit, axis=0, keepdims=True)
    gated_grad = scale * (normed_grad * gain - unit * share)
    dy_ref[...] = to_low(gated_grad * act)
    dgate_ref[...] = to_low(gated_grad * y * sig * (1.0 + gate * (1.0 - sig)))
    total[...] += dot_rows(to_low(unit * gain), mix)

    @pl.when(step == pl.num_programs(0) - 1)
    def _():
        w_grad_ref[...] = to_low(total[...])


def mix_back(mix, y, gate, gain, weights, freight=()):
    blocks, tile, wide = mix.shape
    rows, channels = y.shape
    shape = (channels, weights.shape[2])
    block = pl.BlockSpec((tile, channels), lambda step: (step, 0))
    return run(
        mix_back_kernel,
        (mix, y, gate, gain, weights,),
        grid=(blocks,),
        in_specs=[
            pl.BlockSpec((1, tile, wide), lambda step: (step, 0, 0)),
            block,
            block,
            whole(gain.shape),
            whole(weights.shape),
        ],
        out_specs=[block, block, whole(shape), whole((8, channels))],
        out_shape=[
            jax.ShapeDtypeStruct((rows, channels), jnp.bfloat16),
            jax.ShapeDtypeStruct((rows, channels), jnp.bfloat16),
            jax.ShapeDtypeStruct(shape, jnp.bfloat16),
            jax.ShapeDtypeStruct((8, channels), jnp.float32),
        ],
        scratch=[pltpu.VMEM(shape, jnp.float32), pltpu.VMEM(shape, jnp.bfloat16)],
        freight=freight,
        micros=12,
        name="mix_back",
    )


def project_back_kernel(
    dgate_ref, drows_ref, hidden_ref, w_ref, dt_ref, part_ref, main_grad_ref, rest_grad_ref, total
):
    step = pl.program_id(0)

    @pl.when(step == 0)
    def _():
        total[...] = jnp.zeros_like(total)

    grads = jnp.concatenate([dgate_ref[...], drows_ref[...]], axis=1)
    columns = grads.shape[1] - LANES
    part_ref[0] = to_low(
        dot_lanes(grads[:, :columns], w_ref[:, :columns])
        + dot_lanes(grads[:, columns:], dt_ref[...])
    )
    total[...] += dot_rows(hidden_ref[...], grads)

    @pl.when(step == pl.num_programs(0) - 1)
    def _():
        main = main_grad_ref.shape[1]
        main_grad_ref[...] = to_low(total[:, :main])
        rest_grad_ref[...] = to_low(total[:, main:])


def project_back(dgate, drows, hidden, weights, dt_weights, blocks, freight=()):
    rows, width = hidden.shape
    tile = rows // blocks
    main = 2 * dgate.shape[1]
    rest = dgate.shape[1] + drows.shape[1] - main
    block = lambda extent: pl.BlockSpec((tile, extent), lambda step: (step, 0))
    return run(
        project_back_kernel,
        (dgate, drows, hidden, weights, dt_weights,),
        grid=(blocks,),
        in_specs=[
            block(dgate.shape[1]),
            block(drows.shape[1]),
            block(width),
            whole(weights.shape),
            whole(dt_weights.shape),
        ],
        out_specs=[
            pl.BlockSpec((1, tile, width), lambda step: (step, 0, 0)),
            whole((width, main)),
            whole((width, rest)),
        ],
        out_shape=[
            jax.ShapeDtypeStruct((blocks, tile, width), jnp.bfloat16),
            jax.ShapeDtypeStruct((width, main), jnp.bfloat16),
            jax.ShapeDtypeStruct((width, rest), jnp.bfloat16),
        ],
        scratch=[pltpu.VMEM((width, main + rest), jnp.float32)],
        freight=freight,
        micros=25,
        name="project_back",
    )


def unpack_rows(packed_ref, held_ref, first):
    blocks, both, _ = packed_ref.shape
    fine = held_ref.shape[0] // blocks
    start = 0 if first else both - fine
    for block in range(blocks):
        held_ref[block * fine : (block + 1) * fine] = packed_ref[block, start : start + fine]


def shared_kernel(
    rows_ref,
    grad_ref,
    up_ref,
    down_ref,
    res_ref,
    back_ref,
    up_grad_ref,
    down_grad_ref,
    up_sum,
    down_sum,
    down_held,
):
    step = pl.program_id(0)

    @pl.when(step == 0)
    def _():
        up_sum[...] = jnp.zeros_like(up_sum)
        down_sum[...] = jnp.zeros_like(down_sum)
        unpack_rows(down_ref, down_held, False)

    hidden, width = down_held.shape
    rows = rows_ref[0, :, :width]
    grad = grad_ref[0]
    joined = dot_full(rows, up_ref[...])
    gate, up = joined[:, :hidden], joined[:, hidden:]
    sig = jax.nn.sigmoid(gate)
    act = gate * sig
    acted = to_low(act * up)
    res_ref[0] = to_low(dot_full(acted, down_held[...]))
    down_sum[...] += dot_rows(acted, grad)
    act_grad = dot_lanes(grad, down_held[...])
    joined_grad = to_low(
        jnp.concatenate(
            [act_grad * up * sig * (1.0 + gate * (1.0 - sig)), act_grad * act], axis=1
        )
    )
    up_sum[...] += dot_rows(rows, joined_grad)
    back_ref[0] = to_low(dot_lanes(joined_grad, up_ref[...]))

    @pl.when(step == pl.num_programs(0) - 1)
    def _():
        up_grad_ref[...] = to_low(up_sum[...])
        down_grad_ref[...] = to_low(down_sum[...])


def shared_expert(rows, grad, up, down, hidden, blocks, inner, freight=()):
    _, tile, wide = rows.shape
    width = down.shape[2]
    down_shape = (hidden, width)
    up_shape = (width, 2 * hidden)
    block = pl.BlockSpec((1, tile, width), lambda step: (step, 0, 0))
    low = jnp.bfloat16
    own = lambda extent: pl.BlockSpec(
        (1, tile, extent), lambda step: (own_shard_group(inner)[0] * blocks + step, 0, 0)
    )
    return run(
        shared_kernel,
        (rows, grad, up, down),
        grid=(blocks,),
        in_specs=[
            own(wide),
            own(width),
            pl.BlockSpec((width, up_shape[1]), lambda step: (0, up.shape[1] // up_shape[1] - 1)),
            whole(down.shape),
        ],
        out_specs=[block, block, whole(up_shape), whole(down_shape)],
        out_shape=[
            jax.ShapeDtypeStruct((blocks, tile, width), low),
            jax.ShapeDtypeStruct((blocks, tile, width), low),
            jax.ShapeDtypeStruct(up_shape, low),
            jax.ShapeDtypeStruct(down_shape, low),
        ],
        scratch=[
            pltpu.VMEM(up_shape, jnp.float32),
            pltpu.VMEM(down_shape, jnp.float32),
            pltpu.VMEM(down_shape, low),
        ],
        freight=freight,
        micros=18,
        name="shared_expert",
    )


def dispatch_kernel(
    rows_ref, grad_ref, x_ref, g_ref, picks_ref, *, top_count, slots, own_first
):
    per_device = x_ref.shape[0]
    together, tok_rows, _ = rows_ref.shape
    width = g_ref.shape[2]
    wide = width + LANES
    taken = per_device * slots
    lane = iota_of((tok_rows, LANES), 1)
    named = (lane >= 2 * top_count) & (lane < 3 * top_count)
    before = iota_of((tok_rows, tok_rows), 0) > iota_of((tok_rows, tok_rows), 1)
    before = to_low(jnp.where(before, 1.0, 0.0))
    first = own_first()
    for index in range(together):
        extra = to_full(rows_ref[index, :, width:wide])
        member = jnp.zeros((tok_rows, LANES), jnp.float32)
        for expert in range(per_device):
            own = (first + expert).astype(jnp.float32)
            hit = jnp.sum(jnp.where(named & (extra == own), 1.0, 0.0), axis=1, keepdims=True)
            member = jnp.where(lane // slots == expert, hit, member)
        ranks = dot_full(before, to_low(member))
        picks = jnp.where(
            (ranks == to_full(lane % slots)) & (member > 0.0), 1.0, 0.0
        ).astype(jnp.bfloat16)
        picks_ref[index] = picks
        rows = to_low(dot_rows(picks[:, :taken], rows_ref[index]))
        grads = to_low(dot_rows(picks[:, :taken], grad_ref[index]))
        start = index * slots
        for expert in range(per_device):
            span = slice(expert * slots, (expert + 1) * slots)
            x_ref[expert, start : start + slots] = rows[span]
            g_ref[expert, start : start + slots] = grads[span]


def dispatch(rows, grad, per_device, top_count, slots, own_first, freight=()):
    blocks, tok_rows, wide = rows.shape
    width = grad.shape[2]
    together = 4
    block = lambda extent: pl.BlockSpec((together, tok_rows, extent), lambda step: (step, 0, 0))
    taken = lambda extent: pl.BlockSpec(
        (per_device, together * slots, extent), lambda step: (0, step, 0)
    )
    return run(
        functools.partial(
            dispatch_kernel, top_count=top_count, slots=slots, own_first=own_first
        ),
        (rows, grad),
        grid=(blocks // together,),
        in_specs=[block(wide), block(width)],
        out_specs=[taken(width + LANES), taken(width), block(LANES)],
        out_shape=[
            jax.ShapeDtypeStruct((per_device, blocks * slots, width + LANES), jnp.bfloat16),
            jax.ShapeDtypeStruct((per_device, blocks * slots, width), jnp.bfloat16),
            jax.ShapeDtypeStruct((blocks, tok_rows, LANES), jnp.bfloat16),
        ],
        freight=freight,
        micros=30,
        name="dispatch",
    )


def experts_kernel(
    depart, arrive, targets, *refs, count, per_device, top_count, own_first, inner, incoming, outgoing
):
    x_ref, g_ref = refs[:2]
    total = 2 * count * per_device
    given = total - len(incoming)
    pieces, refs = list(refs[2 : 2 + given]), refs[2 + given :]
    for order, key in enumerate(incoming):
        pieces.insert(key, targets[order])
    res_ref, dx_ref = refs[:2]
    outs = refs[2 : 2 + total]
    up_held, down_held, up_sum, down_sum, up_low, down_low, sems = refs[2 + total :]
    own_place, _ = own_shard_group(inner)
    is_incoming = lambda item: item.output is None
    is_outgoing = lambda item: item.output is not None
    expert, step = pl.program_id(0), pl.program_id(1)
    steps = pl.num_programs(1)
    slot = lax.rem(expert, 2)
    width, double = up_held.shape[1:]
    hidden = double // 2
    tile = x_ref.shape[1]

    def parts(refs_of, which, up, down):
        result = []
        for shift in range(count):
            from_place = lax.rem(own_place + count - shift, count)
            for kind, held in enumerate((up, down)):
                extent = held.shape[0] // count
                start = pl.multiple_of(from_place * extent, extent)
                piece = refs_of[(shift * per_device + which) * 2 + kind]
                if len(piece.shape) == 3:
                    piece = piece.at[own_place * per_device + which]
                result.append((piece, held.at[pl.ds(start, extent)], (shift, kind)))
        return result

    def fetch(which):
        half = which % 2
        return [
            pltpu.make_async_copy(piece, held, sems.at[half, at[0], at[1]])
            for piece, held, at in parts(pieces, which, up_held.at[half], down_held.at[half])
        ]

    for which in range(per_device):

        @pl.when((step == 0) & (expert == which))
        def _():
            if which == 0:
                for copy in fetch(0):
                    copy.start()
                depart(is_incoming)
            if which == 1:
                arrive(is_incoming)
                depart(is_outgoing)
                for copy in fetch(1):
                    copy.start()
            for copy in fetch(which):
                copy.wait()
            if 1 <= which < per_device - 1:
                for copy in fetch(which + 1):
                    copy.start()

    @pl.when(step == 0)
    def _():
        up_sum[...] = jnp.zeros_like(up_sum)
        down_sum[...] = jnp.zeros_like(down_sum)

    up, down = up_held.at[slot], down_held.at[slot]
    rows = x_ref[0, :, :width]
    extra = to_full(x_ref[0, :, width:])
    lane = iota_of((tile, LANES), 1)
    own = own_first() + expert
    hits = jnp.where((lane < 3 * top_count) & (extra == own.astype(jnp.float32)), 1.0, 0.0)
    gate_slot = jnp.zeros((tile, 1), jnp.float32)
    for route in range(top_count):
        place = 2 * top_count + route
        value = extra[:, 2 * route : 2 * route + 1] + extra[:, 2 * route + 1 : 2 * route + 2]
        gate_slot = gate_slot + hits[:, place : place + 1] * value
    joined = dot_full(rows, up[...])
    gate, lift = joined[:, :hidden], joined[:, hidden:]
    sig = jax.nn.sigmoid(gate)
    act = gate * sig
    acted = to_low(act * lift)
    res = to_low(dot_full(acted, down[...]))
    grads = g_ref[0]
    wide_grads = to_full(grads)
    wide_res = to_full(res)
    gate_grad = jnp.sum(wide_res * wide_grads, axis=1, keepdims=True)
    res_ref[0] = to_low(wide_res * gate_slot)
    weighted = to_low(wide_grads * gate_slot)
    act_grad = dot_lanes(weighted, down[...])
    down_sum[...] += dot_rows(acted, weighted)
    joined_grad = to_low(
        jnp.concatenate(
            [act_grad * lift * sig * (1.0 + gate * (1.0 - sig)), act_grad * act], axis=1
        )
    )
    dx_ref[0, :, :width] = to_low(dot_lanes(joined_grad, up[...]))
    high = to_full(to_low(gate_grad))
    half = LANES // 2
    dx_ref[0, :, width:] = to_low(
        jnp.where(lane == own, high, 0.0) + jnp.where(lane == own + half, gate_grad - high, 0.0)
    )
    up_sum[...] += dot_rows(rows, joined_grad)

    for which in range(per_device):

        @pl.when((step == steps - 1) & (expert == which))
        def _():
            up_low[...] = to_low(up_sum[...])
            down_low[...] = to_low(down_sum[...])
            copies = [
                pltpu.make_async_copy(held, piece, sems.at[2, at[0], at[1]])
                for piece, held, at in parts(outs, which, up_low, down_low)
            ]
            for copy in copies:
                copy.start()
            for copy in copies:
                copy.wait()

    if outgoing:

        @pl.when((step == steps - 1) & (expert == per_device - 1))
        def _():
            arrive(is_outgoing)


def experts(x, g, pieces, hidden, top_count, own_first, inner, incoming=(), outgoing=()):
    per_device, rows, wide = x.shape
    width = g.shape[2]
    count = (len(pieces) + len(incoming)) // per_device // 2
    incoming = sorted(incoming, key=lambda entry: entry[0])
    full_list = list(pieces)
    for key, item in incoming:
        full_list.insert(key, jax.ShapeDtypeStruct(item.shape, item.array.dtype))
    low = jnp.bfloat16
    shapes = [jax.ShapeDtypeStruct(piece.shape[-2:], low) for piece in full_list]
    freight = [item for _, item in incoming] + [
        Parcel(shapes[key], shift, inner, output=2 + key) for key, shift in outgoing
    ]
    double = 2 * hidden
    tile = min(rows, 256)
    block = lambda extent: pl.BlockSpec((1, tile, extent), lambda e, step: (e, step, 0))
    anywhere = pl.BlockSpec(memory_space=pl.ANY)
    low = jnp.bfloat16
    outs = run(
        functools.partial(
            experts_kernel,
            count=count,
            per_device=per_device,
            top_count=top_count,
            own_first=own_first,
            inner=inner,
            incoming=[key for key, _ in incoming],
            outgoing=outgoing,
        ),
        (x, g) + tuple(pieces),
        grid=(per_device, rows // tile),
        in_specs=[block(wide), block(width)] + [anywhere] * len(pieces),
        out_specs=[block(width), block(wide)] + [anywhere] * len(shapes),
        out_shape=[
            jax.ShapeDtypeStruct((per_device, rows, width), low),
            jax.ShapeDtypeStruct((per_device, rows, wide), low),
        ]
        + shapes,
        scratch=[
            pltpu.VMEM((2, width, double), low),
            pltpu.VMEM((2, hidden, width), low),
            pltpu.VMEM((width, double), jnp.float32),
            pltpu.VMEM((hidden, width), jnp.float32),
            pltpu.VMEM((width, double), low),
            pltpu.VMEM((hidden, width), low),
            pltpu.SemaphoreType.DMA((3, count, 2)),
        ],
        freight=freight,
        inner=inner if freight else 1,
        late=True,
        micros=45,
        name="experts",
    )
    sent = outs.pop()[len(incoming) :] if freight else []
    return outs[0], outs[1], outs[2:], sent


def combine_kernel(
    picks_ref, res_ref, dx_ref, sres_ref, sback_ref, out_ref, back_ref, *, slots, inner
):
    step = pl.program_id(0)
    together, _, width = out_ref.shape
    per_device = res_ref.shape[0]
    blocks = sres_ref.shape[0]
    place, _ = own_shard_group(inner)
    for index in range(together):
        picks = picks_ref[index, :, : per_device * slots]
        start = index * slots
        stacked = lambda ref: jnp.concatenate(
            [ref[expert, start : start + slots] for expert in range(per_device)], axis=0
        )
        out_ref[index] = to_low(dot_full(picks, stacked(res_ref)))
        back_ref[index] = to_low(dot_full(picks, stacked(dx_ref)))

    @pl.when(lax.div(step * together, blocks) == place)
    def _():
        first = lax.rem(step * together, blocks)
        for index in range(together):
            out_ref[index] = to_low(to_full(out_ref[index]) + to_full(sres_ref[first + index]))
            back_ref[index, :, :width] = to_low(
                to_full(back_ref[index, :, :width]) + to_full(sback_ref[first + index])
            )


def combine(picks, res, dx, shared_res, shared_back, inner, freight=()):
    blocks, tok_rows, _ = picks.shape
    per_device, rows, width = res.shape
    slots = rows // blocks
    together = 4
    block = lambda extent: pl.BlockSpec((together, tok_rows, extent), lambda step: (step, 0, 0))
    taken = lambda extent: pl.BlockSpec(
        (per_device, together * slots, extent), lambda step: (0, step, 0)
    )
    return run(
        functools.partial(combine_kernel, slots=slots, inner=inner),
        (picks, res, dx, shared_res, shared_back),
        grid=(blocks // together,),
        in_specs=[
            block(LANES),
            taken(width),
            taken(width + LANES),
            whole(shared_res.shape),
            whole(shared_back.shape),
        ],
        out_specs=[block(width), block(width + LANES)],
        out_shape=[
            jax.ShapeDtypeStruct((blocks, tok_rows, width), jnp.bfloat16),
            jax.ShapeDtypeStruct((blocks, tok_rows, width + LANES), jnp.bfloat16),
        ],
        freight=freight,
        micros=30,
        name="combine",
    )


def assemble_kernel(
    main_ref, shared_in_ref, small_ref, rows_ref, w_in_ref, shared_ref, out_ref, down_ref
):
    seq_devices, rows, double = main_ref.shape
    channels = double // 2
    for device in range(seq_devices):
        for target, source in ((w_in_ref, main_ref), (shared_ref, shared_in_ref)):
            extent = source.shape[2] // 2
            for side in range(2):
                start = (side * seq_devices + device) * extent
                target[:, start : start + extent] = to_full(
                    source[device, :, side * extent : (side + 1) * extent]
                )
    start = 2 * seq_devices * channels
    w_in_ref[:, start:] = to_full(small_ref[0, :rows, : w_in_ref.shape[1] - start])
    halves, _, out_rows, _ = out_ref.shape
    down_rows = down_ref.shape[2]
    for half in range(halves):
        at = half * (out_rows + down_rows)
        out_ref[half, 0] = to_full(rows_ref[0, at : at + out_rows])
        down_ref[half, 0] = to_full(rows_ref[0, at + out_rows : at + out_rows + down_rows])


def assemble(main, shared, small, rows, columns, shared_columns, out_rows, down_rows, halves):
    seq_devices, depth_rows, _ = main.shape
    tile = depth_rows // seq_devices
    width = rows.shape[2]
    out_fine = out_rows // halves // seq_devices
    down_fine = down_rows // halves // seq_devices
    flat = lambda extent: pl.BlockSpec((tile, extent), lambda step: (step, 0))
    fine = lambda extent: pl.BlockSpec(
        (halves, 1, extent, width), lambda step: (0, step, 0, 0)
    )
    full = jnp.float32
    results = pl.pallas_call(
        assemble_kernel,
        grid=(seq_devices,),
        in_specs=[
            pl.BlockSpec((seq_devices, tile, main.shape[2]), lambda step: (0, step, 0)),
            pl.BlockSpec((seq_devices, tile, shared.shape[2]), lambda step: (0, step, 0)),
            pl.BlockSpec((1,) + small.shape[1:], lambda step: (step, 0, 0)),
            pl.BlockSpec((1,) + rows.shape[1:], lambda step: (step, 0, 0)),
        ],
        out_specs=[flat(columns), flat(shared_columns), fine(out_fine), fine(down_fine)],
        out_shape=[
            jax.ShapeDtypeStruct((depth_rows, columns), full),
            jax.ShapeDtypeStruct((depth_rows, shared_columns), full),
            jax.ShapeDtypeStruct((halves, seq_devices, out_fine, width), full),
            jax.ShapeDtypeStruct((halves, seq_devices, down_fine, width), full),
        ],
        compiler_params=params_of(),
        cost_estimate=cost_of(10),
        name="assemble",
    )(main, shared, small, rows)
    return results[0], results[1], results[2].reshape(-1, width), results[3].reshape(-1, width)


def collect_kernel(place_ref, *refs):
    del place_ref
    step = pl.program_id(0)
    up_ref, down_ref = refs[-2:]
    for order in range(len(refs) // 2 - 1):

        @pl.when(step == order)
        def _():
            up_ref[0] = to_full(refs[2 * order][...])
            down_ref[0] = to_full(refs[2 * order + 1][...])


def collect(place, pieces, per_device):
    count = len(pieces) // 2
    up, down = pieces[0].shape, pieces[1].shape

    def here(step, place):
        shift, expert = lax.div(step, per_device), lax.rem(step, per_device)
        return (
            lax.rem(place[0] + shift, count // per_device) * per_device + expert, 0, 0
        )

    still = lambda shape: pl.BlockSpec(shape, lambda step, place: (0, 0))
    return pl.pallas_call(
        collect_kernel,
        grid_spec=pltpu.PrefetchScalarGridSpec(
            num_scalar_prefetch=1,
            grid=(count,),
            in_specs=[still(up), still(down)] * count,
            out_specs=[pl.BlockSpec((1,) + up, here), pl.BlockSpec((1,) + down, here)],
        ),
        out_shape=[
            jax.ShapeDtypeStruct((count,) + up, jnp.float32),
            jax.ShapeDtypeStruct((count,) + down, jnp.float32),
        ],
        compiler_params=params_of(),
        cost_estimate=cost_of(12),
        name="collect",
    )(place, *pieces)


def route_hits(routes, route, lane):
    return lane == routes[:, route : route + 1]


def token_forward_kernel(
    mixed_ref, x_ref, gain_ref, router_ref, routes_ref, after_ref, wide_ref, gates_ref, *, inner_width, top_count
):
    width = x_ref.shape[1]
    rows = x_ref.shape[0]
    squares = mixed_ref[:, width : width + 1] + mixed_ref[:, width + 1 : width + 2]
    scale = lax.rsqrt(squares / inner_width + EPSILON)
    after = to_full(x_ref[...]) + mixed_ref[:, :width] * scale
    after_ref[...] = after
    moe_in = to_low(after * norm_scale(after) * gain_ref[...])
    wide_ref[:, :width] = moe_in
    logits = dot_full(moe_in, router_ref[...])
    lane = iota_of((rows, LANES), 1)
    routes = routes_ref[...]
    picked = [
        jnp.sum(jnp.where(route_hits(routes, k, lane), logits, 0.0), axis=1, keepdims=True)
        for k in range(top_count)
    ]
    largest = functools.reduce(jnp.maximum, picked)
    powers = [jnp.exp(value - largest) for value in picked]
    total = sum(powers)
    gates = jnp.zeros((rows, LANES), jnp.float32)
    extra = jnp.zeros((rows, LANES), jnp.float32)
    for k in range(top_count):
        value = powers[k] / total
        high = to_full(to_low(value))
        gates = jnp.where(lane == k, value, gates)
        extra = jnp.where(lane == 2 * k, high, extra)
        extra = jnp.where(lane == 2 * k + 1, value - high, extra)
        extra = jnp.where(lane == 2 * top_count + k, to_full(routes[:, k : k + 1]), extra)
    gates_ref[...] = jnp.where(lane == top_count, scale, gates)
    wide_ref[:, width:] = to_low(extra)


def token_forward(mixed, x, gain, router, routes, inner_width, top_count):
    rows, width = x.shape
    arrays = (mixed, x, gain, router, routes)
    return pl.pallas_call(
        functools.partial(
            token_forward_kernel, inner_width=inner_width, top_count=top_count
        ),
        in_specs=[whole(array.shape) for array in arrays],
        out_specs=[whole((rows, width)), whole((rows, width + LANES)), whole((rows, LANES))],
        out_shape=[
            jax.ShapeDtypeStruct((rows, width), jnp.float32),
            jax.ShapeDtypeStruct((rows, width + LANES), jnp.bfloat16),
            jax.ShapeDtypeStruct((rows, LANES), jnp.float32),
        ],
        compiler_params=params_of(),
        cost_estimate=cost_of(5),
        name="token_forward",
    )(*arrays)


def token_back_kernel(
    back_ref,
    mixed_ref,
    after_ref,
    wide_ref,
    gates_ref,
    grad_ref,
    gain_ref,
    router_ref,
    routes_ref,
    mix_ref,
    mix_wide_ref,
    router_grad_ref,
    gain_grad_ref,
    *,
    inner_width,
    top_count,
):
    rows, width = grad_ref.shape
    lane = iota_of((rows, LANES), 1)
    half = LANES // 2
    routes = routes_ref[...]
    gates = gates_ref[...]
    all_grads = back_ref[:, width:]
    values = [gates[:, k : k + 1] for k in range(top_count)]
    grads = [
        jnp.sum(
            jnp.where(
                route_hits(routes, k, lane) | route_hits(routes, k, lane - half), all_grads, 0.0
            ),
            axis=1,
            keepdims=True,
        )
        for k in range(top_count)
    ]
    common = sum(value * grad for value, grad in zip(values, grads))
    logit_grad = jnp.zeros((rows, LANES), jnp.float32)
    for k in range(top_count):
        logit_grad = jnp.where(
            route_hits(routes, k, lane), values[k] * (grads[k] - common), logit_grad
        )
    logit_grad = to_low(logit_grad)
    router_grad_ref[...] = to_low(dot_rows(wide_ref[:, :width], logit_grad))
    moe_grad = back_ref[:, :width] + dot_lanes(logit_grad, router_ref[...])
    after = after_ref[...]
    scale = norm_scale(after)
    unit = after * scale
    gain_grad_ref[...] = jnp.broadcast_to(
        jnp.sum(moe_grad * unit, axis=0, keepdims=True), (8, width)
    )
    scaled = moe_grad * gain_ref[...]
    mean = jnp.mean(scaled * unit, axis=1, keepdims=True)
    mix = to_full(grad_ref[...]) + scale * (scaled - unit * mean)
    mix_ref[...] = mix
    mix_low = to_low(mix)
    mix_wide_ref[:, :width] = mix_low
    mix_scale = gates[:, top_count : top_count + 1]
    share = jnp.sum(to_full(mix_low) * mixed_ref[:, :width], axis=1, keepdims=True)
    mix_wide_ref[:, width:] = put_split([share * mix_scale / inner_width, mix_scale], rows)


def token_back(back, mixed, after, wide, gates, grad, gain, router, routes, inner_width, top_count):
    rows, width = grad.shape
    arrays = (back, mixed, after, wide, gates, grad, gain, router, routes)
    return pl.pallas_call(
        functools.partial(token_back_kernel, inner_width=inner_width, top_count=top_count),
        in_specs=[whole(array.shape) for array in arrays],
        out_specs=[
            whole((rows, width)),
            whole((rows, width + LANES)),
            whole((width, LANES)),
            whole((8, width)),
        ],
        out_shape=[
            jax.ShapeDtypeStruct((rows, width), jnp.float32),
            jax.ShapeDtypeStruct((rows, width + LANES), jnp.bfloat16),
            jax.ShapeDtypeStruct((width, LANES), jnp.bfloat16),
            jax.ShapeDtypeStruct((8, width), jnp.float32),
        ],
        compiler_params=params_of(),
        cost_estimate=cost_of(6),
        name="token_back",
    )(*arrays)


def split_small(joined, arrays):
    results, start = [], 0
    for piece in arrays:
        part = joined[:, start : start + piece.size]
        results.append(part.reshape((-1,) + piece.shape[1:]))
        start += piece.size
    return results


def flat_of(arrays):
    return jnp.concatenate([piece.reshape(-1) for piece in arrays])


def rows_to_send(weights, part):
    seq_devices = lax.axis_size("seq")
    halves = max(1, seq_devices // lax.axis_size("shard"))
    mine = []
    for weight in weights:
        view = weight.reshape(halves, seq_devices, -1, weight.shape[1])
        mine.append(lax.dynamic_index_in_dim(view, part, 1, keepdims=False))
    return jnp.concatenate(mine, axis=1).reshape(-1, weights[0].shape[1])


def rows_by_owner(joined):
    seq_devices = lax.axis_size("seq")
    return joined.reshape(seq_devices, -1, joined.shape[2])


def rows_of_owner(taken, weights):
    seq_devices = lax.axis_size("seq")
    halves = max(1, seq_devices // lax.axis_size("shard"))
    fine_rows = [weight.shape[0] // halves // seq_devices for weight in weights]
    width = taken.shape[2]
    taken = taken.reshape(seq_devices, -1, sum(fine_rows), width).transpose(1, 0, 2, 3)
    results, start = [], 0
    for fine in fine_rows:
        results.append(taken[:, :, start : start + fine].reshape(-1, width))
        start += fine
    return results


def rows_from_owner(grads):
    seq_devices = lax.axis_size("seq")
    shard_devices = lax.axis_size("shard")
    width = grads[0].shape[1]
    turns = shard_devices * max(1, seq_devices // shard_devices) // seq_devices
    pieces = [
        grad.reshape(turns, seq_devices, -1, width).transpose(1, 0, 2, 3) for grad in grads
    ]
    return jnp.concatenate(pieces, axis=2).reshape(seq_devices, -1, width)


def rows_of_shard(joined, weights):
    seq_devices = lax.axis_size("seq")
    halves = max(1, seq_devices // lax.axis_size("shard"))
    fine_rows = [weight.shape[0] // halves // seq_devices for weight in weights]
    width = joined.shape[2]
    spread = joined.reshape(seq_devices, halves, -1, width).transpose(1, 0, 2, 3)
    results, start = [], 0
    for fine in fine_rows:
        results.append(to_full(spread[:, :, start : start + fine]).reshape(-1, width))
        start += fine
    return results


def inner_groups(inner):
    count = lax.axis_size("shard")
    return [list(range(start, start + inner)) for start in range(0, count, inner)]


def outer_groups(inner):
    count = lax.axis_size("shard")
    return [list(range(start, count, inner)) for start in range(inner)]


def carry(array, freight):
    result, arrays = run(
        lambda source, target: None,
        (array,),
        in_specs=[pl.BlockSpec(memory_space=pl.ANY)],
        out_specs=[pl.BlockSpec(memory_space=pl.ANY)],
        out_shape=[jax.ShapeDtypeStruct((8, LANES), jnp.float32)],
        freight=freight,
        micros=30,
        name="carry",
    )
    del result
    return array, arrays


def stacked_pieces(received, place, inner):
    own = jnp.stack(received)[lax.rem(place + inner - jnp.arange(inner), inner)]
    joined = lax.all_gather(own, "shard", axis_index_groups=outer_groups(inner))
    return joined.reshape(-1, joined.shape[-1])


def split_piece(grad, shift, place, inner):
    outer = lax.axis_size("shard") // inner
    rows = grad.reshape(outer, inner, -1, grad.shape[1])
    here = lax.rem(place + inner - shift, inner)
    return lax.psum_scatter(
        lax.dynamic_index_in_dim(rows, here, 1, keepdims=False),
        "shard",
        axis_index_groups=outer_groups(inner),
    )


def local(
    tokens,
    out_grad,
    deal_order,
    lengths,
    routes,
    norm_in,
    w_in,
    w_dt,
    conv_w,
    conv_b,
    dt_bias,
    a_log,
    d_skip,
    norm_gate,
    w_out,
    norm_moe,
    w_router,
    w_shared,
    w_shared_down,
    w_experts,
    w_experts_down,
):
    seq_devices = lax.axis_size("seq")
    shard_devices = lax.axis_size("shard")
    part = lax.axis_index("seq")
    shard = lax.axis_index("shard")
    inner = min(shard_devices, INNER)
    outer = shard_devices // inner
    place = lax.rem(shard, inner)
    _, tok_rows, width = tokens.shape
    group_rows = tok_rows * seq_devices
    inner_width = w_out.shape[0] * shard_devices
    channels = inner_width // seq_devices
    head_total = w_dt.shape[1]
    heads = head_total // seq_devices
    shared_width = w_shared_down.shape[0] * shard_devices
    shared_part = shared_width // seq_devices
    depth_rows = w_in.shape[0]
    expert_total = w_router.shape[1]
    local_experts, _, double = w_experts.shape
    hidden = double // 2
    hidden_rows = w_experts_down.shape[1]
    top_count = routes.shape[2]
    per_device = local_experts // inner
    blocks = inner * seq_devices
    COLLECTIVES.clear()

    def own_columns(array, start, extent):
        return lax.dynamic_slice_in_dim(array, start + part * extent, extent, 1)

    def own_rows(array, extent):
        return lax.dynamic_slice_in_dim(array, part * extent, extent, 0)

    small_weights = [
        norm_in, own_columns(w_dt, 0, heads), conv_w, conv_b, dt_bias, a_log, d_skip, norm_gate, norm_moe, w_router
    ]
    in_columns = jnp.concatenate(
        [
            own_columns(w_in, 0, channels),
            own_columns(w_in, inner_width, channels),
            w_in[:, 2 * inner_width :],
            own_columns(w_shared, 0, shared_part),
            own_columns(w_shared, shared_width, shared_part),
        ],
        axis=1,
    )
    flat = flat_of(small_weights)
    rows_sent = rows_to_send([w_out, w_shared_down], part)
    if outer == 1:
        wide = in_columns.shape[1]
        flat_rows = -(-flat.size // (wide * 32)) * 32
        flat = jnp.pad(flat, (0, flat_rows * wide - flat.size)).reshape(flat_rows, wide)
        x_group, grad_all, proj_in, joined, rows_joined = begin(
            tokens[0], out_grad[0], in_columns, flat, rows_sent, inner
        )
        joined = joined.reshape(inner, -1)
        x_group = x_group.reshape(group_rows, width)
    else:
        x_group = gather_rows(tokens[0], 1)[0].reshape(group_rows, width)
        grad_all = gather_rows(out_grad[0], inner)[0]
        proj_in = lax.all_gather(in_columns, "shard", tiled=True)
        joined = lax.all_gather(flat, "shard")
        rows_joined = lax.all_gather(rows_sent, "shard")
    (
        gain_in,
        dt_columns,
        conv_weight,
        conv_bias,
        step_bias,
        decay_log,
        skip_gain,
        gain_gate,
        gain_moe,
        router,
    ) = split_small(joined, small_weights)
    dt_columns = jnp.pad(dt_columns, ((0, 0), (0, LANES - heads)))
    grad_all = grad_all.reshape(blocks, tok_rows, width)

    weights_of = (w_experts, w_experts_down)

    def own_first():
        here, _ = own_shard_group(inner)
        return lax.axis_index("seq") * local_experts + here * per_device

    pieces = {
        (0, expert, kind): weights_of[kind] for expert in range(per_device) for kind in range(2)
    }

    def parcels(*keys):
        return [
            Parcel(
                weights_of[kind],
                shift,
                inner,
                lambda to, expert=expert: to * per_device + expert,
            )
            for shift, expert, kind in keys
        ]

    def unpack(keys, arrays):
        pieces.update(zip(keys, arrays))

    last = inner - 1

    gain_row = to_full(gain_in)[None]
    in_width = in_columns.shape[1] - 2 * shared_part
    keys = [(1, 0, DOWN)]
    hidden_in, gate_in, rows_in, arrays = project(
        x_group, gain_row, proj_in, dt_columns, channels, in_width, parcels(*keys)
    )
    unpack(keys, arrays)
    ends = jnp.cumsum(lengths[0]).astype(jnp.int32)
    conv_part = jnp.concatenate(
        [own_rows(conv_weight, channels), conv_weight[inner_width:]], axis=0
    )
    bias_part = jnp.concatenate([own_rows(conv_bias, channels), conv_bias[inner_width:]], axis=0)
    conv_table = to_full(
        jnp.pad(jnp.concatenate([conv_part.T, bias_part[None]], axis=0), ((0, 3), (0, 0)))
    )
    head_table = jnp.pad(
        jnp.stack(
            [
                to_full(own_rows(step_bias, heads)),
                -jnp.exp(to_full(own_rows(decay_log, heads))),
                to_full(own_rows(skip_gain, heads)),
            ]
        ),
        ((0, 5), (0, LANES - heads)),
    )
    keys = [(1, 0, UP), (last, 0, DOWN)]
    y, seq_rows, states, (taken, *arrays) = scan_forward(
        ends,
        deal_order,
        rows_in,
        conv_table,
        head_table,
        channels,
        [PlaneSwap(rows_by_owner(rows_joined))] + parcels(*keys),
    )
    unpack(keys, arrays)
    if outer > 1:
        out_rows, down_rows = rows_of_owner(taken, [w_out, w_shared_down])
        taken = jnp.concatenate(
            [
                out_rows.reshape(seq_devices, -1, width),
                down_rows.reshape(seq_devices, -1, width),
            ],
            axis=1,
        )
    own_weights = taken
    gate_gain = to_full(own_rows(gain_gate, channels))[None]
    keys = [(1, 1, DOWN)]
    mix_part, arrays = mix_out(y, gate_in, gate_gain, own_weights, seq_devices, parcels(*keys))
    unpack(keys, arrays)
    keys = [(last, 0, UP), (last, 1, DOWN)]
    mixed, arrays = reduce_rows(mix_part[None], parcels(*keys))
    unpack(keys, arrays)

    moe_row = to_full(gain_moe)[None]
    router_wide = jnp.pad(router, ((0, 0), (0, LANES - expert_total)))
    route_ids = jnp.pad(routes[0], ((0, 0), (0, LANES - top_count)))
    after_mix, moe_wide, gates = token_forward(
        mixed, tokens[0], moe_row, router_wide, route_ids, inner_width, top_count
    )
    keys = [(2, 0, UP), (2, 0, DOWN), (last, 1, UP)]
    moe_all, arrays = gather_rows(moe_wide, inner, parcels(*keys))
    unpack(keys, arrays)
    moe_all = moe_all.reshape(blocks, tok_rows, width + LANES)
    capacity = min(tok_rows, max(2, tok_rows * top_count * 5 // (expert_total * 3)))
    slots = -(-capacity // 16) * 16
    keys = [(2, 1, UP)]
    expert_rows, grad_rows, picks, arrays = dispatch(
        moe_all, grad_all, per_device, top_count, slots, own_first, parcels(*keys)
    )
    unpack(keys, arrays)
    keys = [(2, 1, DOWN)]
    shared_res, shared_back, shared_up_grad, shared_down_grad, arrays = shared_expert(
        moe_all,
        grad_all,
        proj_in,
        own_weights,
        shared_part,
        seq_devices,
        inner,
        parcels(*keys),
    )
    unpack(keys, arrays)
    order = [
        (shift, expert, kind)
        for shift in range(inner)
        for expert in range(per_device)
        for kind in range(2)
    ]
    if outer == 1:
        late_keys = [(1, 1, UP)]
        early_keys = [(1, 0, UP), (last, 0, DOWN)]
        expert_res, expert_back, grads, sent = experts(
            expert_rows,
            grad_rows,
            [pieces[key] for key in order if key not in late_keys],
            hidden,
            top_count,
            own_first,
            inner,
            [(order.index(key), parcels(key)[0]) for key in late_keys],
            [(order.index(key), inner - key[0]) for key in early_keys],
        )
    else:
        for expert in range(per_device):
            for kind in range(2):
                pieces[0, expert, kind] = lax.dynamic_index_in_dim(
                    weights_of[kind], place * per_device + expert, 0, keepdims=False
                )
        keys = [(1, 1, UP)]
        moe_all, arrays = carry(moe_all, parcels(*keys))
        unpack(keys, arrays)
        early_keys, sent = [], []
        held = [
            stacked_pieces([pieces[shift, expert, kind] for shift in range(inner)], place, inner)
            for expert in range(per_device)
            for kind in range(2)
        ]
        expert_res, expert_back, grads, _ = experts(
            expert_rows, grad_rows, held, hidden, top_count, own_first, inner
        )
        grads = [
            split_piece(grads[expert * 2 + kind], shift, place, inner)
            for shift, expert, kind in order
        ]
    grads = dict(zip(order, grads))
    returned = {key: grads[key] for key in order if key[0] == 0}
    returned.update(zip(early_keys, sent))

    def back_parcels(*keys):
        keys = [key for key in keys if key not in early_keys]
        return [Parcel(grads[key], inner - key[0], inner) for key in keys]

    def unpack_back(keys, arrays):
        keys = [key for key in keys if key not in early_keys]
        returned.update(zip(keys, arrays))

    keys = [(1, 0, UP), (last, 0, DOWN), (last, 0, UP), (1, 0, DOWN), (1, 1, DOWN)]
    out_part, back_part, arrays = combine(
        picks, expert_res, expert_back, shared_res, shared_back, inner, back_parcels(*keys)
    )
    unpack_back(keys, arrays)
    keys = [(2, 0, UP), (last, 1, UP)]
    back, arrays = reduce_rows(
        back_part.reshape(inner, seq_devices, tok_rows, -1), back_parcels(*keys)
    )
    unpack_back(keys, arrays)
    mix_grad, mix_wide, router_grad, gain_moe_grad = token_back(
        back,
        mixed,
        after_mix,
        moe_wide,
        gates,
        out_grad[0],
        moe_row,
        router_wide,
        route_ids,
        inner_width,
        top_count,
    )

    keys = [(1, 1, UP), (last, 1, DOWN)]
    mix_group, arrays = gather_rows(mix_wide, 1, back_parcels(*keys))
    unpack_back(keys, arrays)
    keys = [(2, 0, DOWN)]
    dy, gate_in_grad, proj_out_grad, gain_gate_grad, arrays = mix_back(
        mix_group[0], y, gate_in, gate_gain, own_weights, back_parcels(*keys)
    )
    unpack_back(keys, arrays)
    keys = [(2, 1, UP)]
    rows_grad, conv_grad, head_grad, out_sum, (taken, *arrays) = scan_backward(
        ends,
        deal_order,
        seq_rows,
        states,
        dy,
        conv_table,
        head_table,
        out_part.reshape(inner, seq_devices, tok_rows, -1),
        [PlaneSwap(rows_from_owner([proj_out_grad, shared_down_grad]))] + back_parcels(*keys),
    )
    unpack_back(keys, arrays)
    layer_out = to_low(after_mix + out_sum)
    keys = [(2, 1, DOWN)]
    hidden_part, main_grad, rest_grad, arrays = project_back(
        gate_in_grad, rows_grad, hidden_in, proj_in, dt_columns, seq_devices, back_parcels(*keys)
    )
    unpack_back(keys, arrays)
    experts_grad, experts_down_grad = collect(
        place[None], [returned[key] for key in order], per_device
    )
    def spread(values, length, axis=0):
        shape = values.shape[:axis] + (length,) + values.shape[axis + 1 :]
        return lax.dynamic_update_slice_in_dim(
            jnp.zeros(shape, values.dtype), values, part * values.shape[axis], axis
        )

    state_columns = rest_grad.shape[1] - LANES
    conv_rows_grad = conv_grad[:5].T
    conv_full = jnp.concatenate(
        [spread(conv_rows_grad[:channels], inner_width), conv_rows_grad[channels:]], axis=0
    )
    by_depth = [
        rest_grad[:, :state_columns],
        router_grad[:, :expert_total],
        spread(rest_grad[:, state_columns : state_columns + heads], head_total, 1),
        to_low(gain_moe_grad[0])[:, None],
    ]
    by_shard = [
        conv_full[:, :4],
        conv_full[:, 4],
        spread(head_grad[0, :heads], head_total),
        spread(head_grad[1, :heads], head_total),
        spread(head_grad[2, :heads], head_total),
        spread(gain_gate_grad[0], inner_width),
    ]
    shapes = [(piece.shape[0] // shard_devices,) + piece.shape[1:] for piece in by_shard]
    by_shard = jnp.concatenate(
        [to_low(piece).reshape(shard_devices, -1) for piece in by_shard], axis=1
    )
    extents = [piece.shape[1] for piece in by_depth]
    used = sum(extents)
    if outer == 1:
        wide = -(-max(used, depth_rows) // LANES) * LANES
        by_depth.append(jnp.zeros((width, wide - used), jnp.bfloat16))
        by_depth = jnp.concatenate(by_depth, axis=1).reshape(inner, seq_devices, -1, wide)
        depth_each = by_depth.shape[2]
        size = by_shard.shape[1]
        each = -(-size // (seq_devices * wide))
        padded = -(-each // 16) * 16
        by_shard = jnp.pad(by_shard, ((0, 0), (0, each * seq_devices * wide - size)))
        by_shard = by_shard.reshape(inner, seq_devices, each, wide)
        by_shard = jnp.pad(by_shard, ((0, 0), (0, 0), (0, padded - each), (0, 0)))
        tokens_grad, rows_all, shared_all, main_all, small_all = settle(
            hidden_part[None],
            jnp.concatenate([by_depth, by_shard], axis=2),
            tokens[0],
            mix_grad,
            gain_row,
            [
                taken.reshape(inner, -1, width),
                shared_up_grad.reshape(inner, depth_rows, -1),
                main_grad.reshape(inner, depth_rows, -1),
            ],
            depth_each + each,
            inner,
        )
        w_in_grad, w_shared_grad, w_out_grad, w_shared_down_grad = assemble(
            main_all,
            shared_all,
            small_all,
            rows_all,
            w_in.shape[1],
            2 * shared_width,
            w_out.shape[0],
            w_shared_down.shape[0],
            max(1, seq_devices // shard_devices),
        )
        depth_sum = to_full(small_all[:, :depth_each].reshape(depth_rows, wide))
        shard_sum = small_all[:, depth_each : depth_each + each].reshape(-1)
        norm_in_grad = to_full(small_all[0, depth_each + each, :depth_rows])
    else:
        hidden_grad = reduce_rows(hidden_part[None])[0]
        residual = to_full(tokens[0])
        own_scale = norm_scale(residual)
        own_unit = residual * own_scale
        scaled = hidden_grad * gain_row
        tokens_grad = to_low(
            mix_grad
            + own_scale
            * (scaled - own_unit * jnp.mean(scaled * own_unit, axis=1, keepdims=True))
        )
        by_depth.append(to_low(jnp.sum(hidden_grad * own_unit, axis=0))[:, None])
        by_depth = jnp.concatenate(by_depth, axis=1).reshape(shard_devices, -1)
        packed = jnp.concatenate([by_depth, by_shard], axis=1)
        summed = lax.psum(lax.psum_scatter(packed, "shard", tiled=True), "seq").reshape(-1)
        count = depth_rows * (used + 1)
        depth_sum = to_full(summed[:count]).reshape(depth_rows, used + 1)
        shard_sum = summed[count:]
        norm_in_grad = depth_sum[:, used]

        def from_line(part, rows):
            own = lax.psum_scatter(part.reshape(shard_devices, rows, -1), "shard")
            return lax.all_gather(own, "seq")

        def columns_of(joined, extent):
            joined = joined.reshape(seq_devices, depth_rows, 2, extent).transpose(1, 2, 0, 3)
            return to_full(joined.reshape(depth_rows, -1))

        w_in_main = columns_of(from_line(main_grad, depth_rows), channels)
        w_in_grad = jnp.concatenate([w_in_main, depth_sum[:, :state_columns]], axis=1)
        w_shared_grad = columns_of(from_line(shared_up_grad, depth_rows), shared_part)
        rows_each = taken.shape[0] * taken.shape[1] // shard_devices
        w_out_grad, w_shared_down_grad = rows_of_shard(
            from_line(taken, rows_each), [w_out, w_shared_down]
        )
    results, start = [], 0
    for shape in shapes:
        size = 1
        for extent in shape:
            size *= extent
        results.append(to_full(shard_sum[start : start + size]).reshape(shape))
        start += size
    conv_w_grad, conv_b_grad, dt_bias_grad, a_log_grad, d_skip_grad, norm_gate_grad = results
    start = state_columns
    w_router_grad = depth_sum[:, start : start + expert_total]
    start += expert_total
    w_dt_grad = depth_sum[:, start : start + head_total]
    start += head_total
    norm_moe_grad = depth_sum[:, start]
    return (
        layer_out[None],
        tokens_grad[None],
        norm_in_grad,
        w_in_grad,
        w_dt_grad,
        conv_w_grad,
        conv_b_grad,
        dt_bias_grad,
        a_log_grad,
        d_skip_grad,
        norm_gate_grad,
        w_out_grad,
        norm_moe_grad,
        w_router_grad,
        w_shared_grad,
        w_shared_down_grad,
        experts_grad,
        experts_down_grad,
    )


def solution(mesh):
    placed = (
        P("shard", "seq", None),
        P("shard", "seq", None),
        P("shard", None),
        P("shard", None),
        P("shard", "seq", None),
        P("shard"),
        P("shard", None),
        P("shard", None),
        P("shard", None),
        P("shard"),
        P("shard"),
        P("shard"),
        P("shard"),
        P("shard"),
        P("shard", None),
        P("shard"),
        P("shard", None),
        P("shard", None),
        P("shard", None),
        P("seq", "shard", None),
        P("seq", "shard", None),
    )
    return jax.shard_map(
        local,
        mesh=mesh,
        in_specs=placed,
        out_specs=(
            P("shard", "seq", None),
            P("shard", "seq", None),
            P("shard"),
            P("shard", None),
            P("shard", None),
            P("shard", None),
            P("shard"),
            P("shard"),
            P("shard"),
            P("shard"),
            P("shard"),
            P("shard", None),
            P("shard"),
            P("shard", None),
            P("shard", None),
            P("shard", None),
            P("seq", "shard", None),
            P("seq", "shard", None),
        ),
        check_vma=False,
    )
```

time: 1280 us -> 1090 us (0.85)
  Pallas kernels: 1140 us -> 1020 us
  local copies, waits for them, and re-layouts: 82.6 us -> 42.3 us
  other arithmetic: 40 us -> 14.1 us
    pallas_call x3, Pallas kernels: 119 us -> 20.6 us  [the longest x1 10.8 us: collect(): pl.pallas_call(collect_kernel, grid_spec=pltpu.PrefetchScalarGridSpec(num...]
    pallas_call x16, Pallas kernels: 1010 us -> 989 us  [run(): pl.pallas_call(wrapped, grid=grid, in_specs=list(in_specs) + [anywhere] *...]
    reshape x9 -> x0, local copies, waits for them, and re-layouts: 17 us -> none  [the longest x2 8.8 us: local(): w_shared_grad = to_full(shared_columns).reshape(seq_devices, depth_rows,...]
    concatenate x15 -> x2, other arithmetic: 16 us -> 2.98 us  [the longest x1 2.2 us: local(): jnp.concatenate([by_depth, by_shard], axis=2)]
where the time goes in v3:
time: 1090 us; the launch traced here: 1080 us
  Pallas kernels  1020 us (94%)
  local copies, waits for them, and re-layouts  42.3 us (4%)
  other arithmetic  14.1 us (1%)
    pallas_call x16, Pallas kernels, run(): pl.pallas_call(wrapped, grid=grid, in_specs=list(in_specs) + [anywhere] *...  989 us

profile of v3, /device:TPU:0, one launch (start us, length us, event | category | flops | bytes accessed | tf_op | source)
XLA Modules:
  0.0 1079.6 jit_solution(1749084076711177132)
XLA Ops:
  11.5 6.3 concatenate.41
  20.2 144.5 %begin.1 = (bf16[8,192,1536]{2,1,0:T(8,128)(2,1)}, bf16[4,8,192,1536]{3,2,1,0:T(8,128)(2,1)}, bf16[1536,1280]{1,0:T(8,128)(2,1)}, bf16[4,32,1280]{2,1,0:T(8,128)(2,1)}, bf16[4,128,1536]{2,1,0:T(8,128)(2,1)}) custom-call(bf16[192,1536]{1,0:T(8,128)(2,1)} %bitcast.76, bf16[192,1536]{1,0:T(8,128)(2,1)} %bitcast.84, bf16[384,1280]{1,0:T(8,128)(2,1)} %copy-done.3, ...), custom_call_target="tpu_custom_call" | custom-call | bytes 468000000 | tf_op jit(solution)/shard_map/begin/pallas_call | solution.py:669
  168.3 15.2 %project.1 = (bf16[1536,1536]{1,0:T(8,128)(2,1)}, f32[1536,384]{1,0:T(8,128)}, bf16[1536,768]{1,0:T(8,128)(2,1)}, bf16[128,1536]{1,0:T(8,128)(2,1)}) custom-call(bf16[1536,1536]{1,0:T(8,128)(2,1)} %bitcast.82, f32[1,1536]{1,0:T(1,128)} %bitcast.105, bf16[1536,1280]{1,0:T(8,128)(2,1)} %get-tuple-element.115.refs_2_.refs_3_, ...), custom_call_target="tpu_custom_call" | custom-call | bytes 39600000 | tf_op jit(solution)/shard_map/project/pallas_call | solution.py:669
  187.5 30.9 %scan_forward.1 = (bf16[1536,384]{1,0:T(8,128)(2,1)}, bf16[1536,768]{1,0:T(8,128)(2,1)}, f32[6,384,128]{2,1,0:T(8,128)}, bf16[8,64,1536]{2,1,0:T(8,128)(2,1)}, b...) custom-call(s32[4]{0:T(128)} %bitcast.110, s32[1,1536]{1,0:T(1,128)} %refs_1_.7, ...), custom_call_target="tpu_custom_call" | custom-call | bytes 90000000 | tf_op jit(solution)/shard_map/scan_forward/pallas_call | solution.py:669
  219.2 16.0 %mix_out.1 = (bf16[8,192,1664]{2,1,0:T(8,128)(2,1)}, bf16[128,1536]{1,0:T(8,128)(2,1)}) custom-call(bf16[1536,384]{1,0:T(8,128)(2,1)} %get-tuple-element.118.refs_0_.refs_1_, f32[1536,384]{1,0:T(8,128)} %get-tuple-element.119.refs_1_.refs_2_, f32[1,384]{1,0:T(1,128)} %reshape.263.refs_2_.refs_3_, bf16[8,64,1536]{2,1,0:T(8,128)(2,1)} %get-tuple-element.120.refs_3_.refs_4_, ...), custom_call_target="tpu_custom_call" | custom-call | bytes 32400000 | tf_op jit(solution)/shard_map/mix_out/pallas_call | solution.py:669
  235.2 30.2 %reduce_rows.2 = (f32[192,1664]{1,0:T(8,128)}, bf16[384,1024]{1,0:T(8,128)(2,1)}, bf16[128,1536]{1,0:T(8,128)(2,1)}) custom-call(bf16[1,8,192,1664]{3,2,1,0:T(8,128)(2,1)} %bitcast.79, bf16[8,384,1024]{2,1,0:T(8,128)(2,1)} %refs_17_.1, bf16[8,128,1536]{2,1,0:T(8,128)(2,1)} %refs_5_.1), custom_call_target="tpu_custom_call" | custom-call | bytes 90000000 | tf_op jit(solution)/shard_map/reduce_rows/pallas_call | solution.py:669
  268.1 3.6 token_forward.1
  271.8 111.9 %gather_rows.2 = (bf16[4,8,192,1664]{3,2,1,0:T(8,128)(2,1)}, bf16[384,1024]{1,0:T(8,128)(2,1)}, bf16[128,1536]{1,0:T(8,128)(2,1)}, bf16[384,1024]{1,0:T(8,128)(2,1)}) custom-call(bf16[192,1664]{1,0:T(8,128)(2,1)} %get-tuple-element.126.refs_0_.wide_ref, bf16[8,384,1024]{2,1,0:T(8,128)(2,1)} %refs_17_.1, bf16[8,128,1536]{2,1,0:T(8,128)(2,1)} %refs_5_.1, ...), custom_call_target="tpu_custom_call" | custom-call | bytes 360000000 | tf_op jit(solution)/shard_map/gather_rows/pallas_call | solution.py:669
  383.7 55.2 %dispatch.1 = (bf16[2,1024,1664]{2,1,0:T(8,128)(2,1)}, bf16[2,1024,1536]{2,1,0:T(8,128)(2,1)}, bf16[32,192,128]{2,1,0:T(8,128)(2,1)}, bf16[384,1024]{1,0:T(8,128)(2,1)}) custom-call(bf16[32,192,1664]{2,1,0:T(8,128)(2,1)} %bitcast.70, bf16[32,192,1536]{2,1,0:T(8,128)(2,1)} %bitcast.72, bf16[8,384,1024]{2,1,0:T(8,128)(2,1)} %refs_17_.1), custom_call_target="tpu_custom_call" | custom-call | bytes 108000000 | tf_op jit(solution)/shard_map/dispatch/pallas_call | solution.py:669
  438.9 23.4 %shared_expert.1 = (bf16[8,192,1536]{2,1,0:T(8,128)(2,1)}, bf16[8,192,1536]{2,1,0:T(8,128)(2,1)}, bf16[1536,256]{1,0:T(8,128)(2,1)}, bf16[128,1536]{1,0:T(8,128)(2,1)}, bf16[128,1536]{1,0:T(8,128)(2,1)}) custom-call(bf16[32,192,1664]{2,1,0:T(8,128)(2,1)} %bitcast.71, bf16[32,192,1536]{2,1,0:T(8,128)(2,1)} %bitcast.73, ...), custom_call_target="tpu_custom_call" | custom-call | bytes 64800000 | tf_op jit(solution)/shard_map/shared_expert/pallas_call | solution.py:669
  462.3 54.2 %experts.1 = (bf16[2,1024,1536]{2,1,0:T(8,128)(2,1)}, bf16[2,1024,1664]{2,1,0:T(8,128)(2,1)}, bf16[384,1024]{1,0:T(8,128)(2,1)}, bf16[128,1536]{1,0:T(8,128)(2,1...) custom-call(bf16[2,1024,1664]{2,1,0:T(8,128)(2,1)} %get-tuple-elemen, ...), custom_call_target="tpu_custom_call" | custom-call | bytes 162000000 | tf_op jit(solution)/shard_map/experts/pallas_call | solution.py:669
  516.6 41.4 %combine.1 = (bf16[32,192,1536]{2,1,0:T(8,128)(2,1)}, bf16[32,192,1664]{2,1,0:T(8,128)(2,1)}, bf16[384,1024]{1,0:T(8,128)(2,1)}, bf16[128,1536]{1,0:T(8,128)(2,1)}, bf16[128,1536]{1,0:T(8,128)(2,1)}) custom-call(bf16[32,192,128]{2,1,0:T(8,128)(2,1)} %get-tuple-element.129.refs_0_, bf16[2,1024,1536]{2,1,0:T(8,128)(2,1)} %get-tuple-element.143.refs_1_, ...), custom_call_target="tpu_custom_call" | custom-call | bytes 108000000 | tf_op jit(solution)/shard_map/combine/pallas_call | solution.py:669
  558.0 117.1 %reduce_rows.3 = (f32[192,1664]{1,0:T(8,128)}, bf16[384,1024]{1,0:T(8,128)(2,1)}, bf16[384,1024]{1,0:T(8,128)(2,1)}) custom-call(bf16[4,8,192,1664]{3,2,1,0:T(8,128)(2,1)} %bitcast.74, bf16[384,1024]{1,0:T(8,128)(2,1)} %get-tuple-element.151.refs_1_, bf16[384,1024]{1,0:T(8,128)(2,1)} %get-tuple-element.152.refs_2_), custom_call_target="tpu_custom_call" | custom-call | bytes 360000000 | tf_op jit(solution)/shard_map/reduce_rows/pallas_call | solution.py:669
  675.1 6.2 token_back.1
  681.3 45.6 %gather_rows.3 = (bf16[1,8,192,1664]{3,2,1,0:T(8,128)(2,1)}, bf16[384,1024]{1,0:T(8,128)(2,1)}, bf16[128,1536]{1,0:T(8,128)(2,1)}) custom-call(bf16[192,1664]{1,0:T(8,128)(2,1)} %get-tuple-element.155.refs_0_, bf16[384,1024]{1,0:T(8,128)(2,1)} %get-tuple-element.156.refs_1_, bf16[128,1536]{1,0:T(8,128)(2,1)} %get-tuple-element.157.refs_2_), custom_call_target="tpu_custom_call" | custom-call | bytes 90000000 | tf_op jit(solution)/shard_map/gather_rows/pallas_call | solution.py:669
  726.9 21.6 %mix_back.1 = (bf16[1536,384]{1,0:T(8,128)(2,1)}, bf16[1536,384]{1,0:T(8,128)(2,1)}, bf16[384,1536]{1,0:T(8,128)(2,1)}, f32[8,384]{1,0:T(8,128)}, bf16[128,1536]{1,0:T(8,128)(2,1)}) custom-call(bf16[8,192,1664]{2,1,0:T(8,128)(2,1)} %bitcast.80, bf16[1536,384]{1,0:T(8,128)(2,1)} %get-tuple-element.118.refs_0_.refs_1_, ...), custom_call_target="tpu_custom_call" | custom-call | bytes 43200000 | tf_op jit(solution)/shard_map/mix_back/pallas_call | solution.py:669
  748.4 2.5 maximum_bitcast_fusion.refs_8_
  751.0 128.3 %scan_backward.1 = (bf16[1536,768]{1,0:T(8,128)(2,1)}, f32[8,640]{1,0:T(8,128)}, f32[8,128]{1,0:T(8,128)}, f32[192,1536]{1,0:T(8,128)}, bf16[8,64,1536]{2,1,0:T(8,128)(2,1)}, /*index=5*/bf16[384,1024]{1,0:T(8,128)(2,1)}) custom-call(s32[4]{0:T(128)} %bitcast.111, s32[1,1536]{1,0:T(1,128)} %refs_1_.7, bf16[1536,768]{1,0:T(8,128)(2,1)} %get-tuple-element.124.refs_2_, ...), custom_call_target="tpu_custom_call" | custom-call | bytes 144000000 | tf_op jit(solution)/shard_map/scan_backward/pallas_call | solution.py:669
  879.3 2.2 fusion.2
  881.6 28.5 %project_back.1 = (bf16[8,192,1536]{2,1,0:T(8,128)(2,1)}, bf16[1536,768]{1,0:T(8,128)(2,1)}, bf16[1536,384]{1,0:T(8,128)(2,1)}, bf16[128,1536]{1,0:T(8,128)(2,1)}) custom-call(bf16[1536,384]{1,0:T(8,128)(2,1)} %get-tuple-element.166.refs_0_, bf16[1536,768]{1,0:T(8,128)(2,1)} %get-tuple-element.167.refs_1_, bf16[1536,1536]{1,0:T(8,128)(2,1)} %get-tuple-element.168.refs_2_, ...), custom_call_target="tpu_custom_call" | custom-call | bytes 90000000 | tf_op jit(solution)/shard_map/project_back/pallas_call | solution.py:669
  921.0 2.2 fusion.1.refs_1_
  923.2 125.4 %settle.1 = (bf16[192,1536]{1,0:T(8,128)(2,1)}, bf16[8,128,1536]{2,1,0:T(8,128)(2,1)}, bf16[8,384,256]{2,1,0:T(8,128)(2,1)}, bf16[8,384,768]{2,1,0:T(8,128)(2,1)}, bf16[8,64,384]{2,1,0:T(8,128)(2,1)}) custom-call(bf16[1,8,192,1536]{3,2,1,0:T(8,128)(2,1)} %bitcast.81, bf16[4,8,64,384]{3,2,1,0:T(8,128)(2,1)} %fusion.1.refs_1_, bf16[192,1536]{1,0:T(8,128)(2,1)} %bitcast.78, ...), custom_call_target="tpu_custom_call" | custom-call | bytes 324000000 | tf_op jit(solution)/shard_map/settle/pallas_call | solution.py:669
  1050.0 11.4 %assemble.1 = (f32[384,6400]{1,0:T(8,128)}, f32[384,2048]{1,0:T(8,128)}, f32[2,8,48,1536]{3,2,1,0:T(8,128)}, f32[2,8,16,1536]{3,2,1,0:T(8,128)}) custom-call(bf16[8,384,768]{2,1,0:T(8,128)(2,1)} %get-tuple-element.183.main_ref, bf16[8,384,256]{2,1,0:T(8,128)(2,1)} %get-tuple-element.184.shared_in_ref, bf16[8,64,384]{2,1,0:T(8,128)(2,1)} %get-tuple-element.182.small_ref, ...), custom_call_target="tpu_custom_call" | custom-call | bytes 36000000 | tf_op jit(solution)/shard_map/assemble/pallas_call | solution.py:2023
  1067.5 10.8 %collect.1 = (f32[8,384,1024]{2,1,0:T(8,128)}, f32[8,128,1536]{2,1,0:T(8,128)}) custom-call(s32[1]{0:T(128)} %bitcast.41.place_ref, bf16[384,1024]{1,0:T(8,128)(2,1)} %get-tuple-element.190.refs_0_, bf16[128,1536]{1,0:T(8,128)(2,1)} %get-tuple-element.191.refs_1_, bf16[384,1024]{1,0:T(8,128)(2,1)} %get-tuple-element.192.refs_2_, ...), custom_call_target="tpu_custom_call" | custom-call | bytes 43200000 | tf_op jit(solution)/shard_map/collect/pallas_call | solution.py:2069
  (131 shorter events, 43.2 us)
Async XLA Ops:
  0.7 18.8 %copy-start = (bf16[768,1536]{1,0:T(8,128)(2,1)S(1)}, bf16[768,1536]{1,0:T(8,128)(2,1)}, u32[]{:S(2)}) copy-start(bf16[768,1536]{1,0:T(8,128)(2,1)} %param.35) | copy-start | bytes 7077892
  7.0 13.3 %copy-start.3 = (bf16[384,1280]{1,0:T(8,128)(2,1)}, bf16[384,1280]{1,0:T(8,128)(2,1)S(1)}, u32[]{:S(2)}) copy-start(bf16[384,1280]{1,0:T(8,128)(2,1)S(1)} %dynamic-slice_dynamic-update-slice_fusion.2.refs_2_) | copy-start | bytes 2949124
  235.2 32.2 %copy-start.9 = (s32[1,192,6]{1,0,2:T(1,128)S(1)}, s32[1,192,6]{1,0,2:T(1,128)}, u32[]{:S(2)}) copy-start(s32[1,192,6]{1,0,2:T(1,128)} %param.25) | copy-start | bytes 13828
  726.9 21.6 %copy-start.8 = (bf16[128,1536]{1,0:T(8,128)(2,1)S(1)}, bf16[128,1536]{1,0:T(8,128)(2,1)}, u32[]{:S(2)}) copy-start(bf16[128,1536]{1,0:T(8,128)(2,1)} %get-tuple-element.163) | copy-start | bytes 1179652
  751.0 128.3 %copy-start.2 = (f32[192,1536]{1,0:T(8,128)S(1)}, f32[192,1536]{1,0:T(8,128)}, u32[]{:S(2)}) copy-start(f32[192,1536]{1,0:T(8,128)} %get-tuple-element.123.after_ref) | copy-start | bytes 3538948
  881.5 28.5 %copy-start.10 = (f32[8,640]{1,0:T(8,128)S(1)}, f32[8,640]{1,0:T(8,128)}, u32[]{:S(2)}) copy-start(f32[8,640]{1,0:T(8,128)} %get-tuple-element.174) | copy-start | bytes 61444
  910.1 6.7 copy-start.5
  912.3 7.7 copy-start.7
  1050.0 11.4 %copy-start.4 = (bf16[8,64,384]{2,1,0:T(8,128)(2,1)S(1)}, bf16[8,64,384]{2,1,0:T(8,128)(2,1)}, u32[]{:S(2)}) copy-start(bf16[8,64,384]{2,1,0:T(8,128)(2,1)} %get-tuple-element.182.small_ref) | copy-start | bytes 1179652
  1067.5 10.8 %copy-start.6 = (bf16[192,1536]{1,0:T(8,128)(2,1)S(1)}, bf16[192,1536]{1,0:T(8,128)(2,1)}, u32[]{:S(2)}) copy-start(bf16[192,1536]{1,0:T(8,128)(2,1)} %get-tuple-element.181) | copy-start | bytes 1769476
  1067.5 11.6 %copy-start.1 = (bf16[768,1536]{1,0:T(8,128)(2,1)S(1)}, bf16[768,1536]{1,0:T(8,128)(2,1)}, u32[]{:S(2)}) copy-start(bf16[768,1536]{1,0:T(8,128)(2,1)} %param.35) | copy-start | bytes 7077892

commit v4 on v3

--- a/solution.py
+++ b/solution.py
@@ -80,36 +80,38 @@
     return lax.broadcasted_iota(jnp.int32, shape, axis)
 
 
-def ids_at(places, ends_ref):
-    total = jnp.zeros(places.shape, jnp.int32)
-    for seq in range(ends_ref.shape[0]):
-        total = total + (places >= ends_ref[seq]).astype(jnp.int32)
+def ids_at(places, lengths_ref):
+    total, end = jnp.zeros(places.shape, jnp.int32), 0
+    for seq in range(lengths_ref.shape[0]):
+        end = end + lengths_ref[seq]
+        total = total + (places >= end).astype(jnp.int32)
     return total
 
 
-def id_at(place, ends_ref):
-    total = jnp.int32(0)
-    for seq in range(ends_ref.shape[0]):
-        total = total + (place >= ends_ref[seq]).astype(jnp.int32)
+def id_at(place, lengths_ref):
+    total, end = jnp.int32(0), 0
+    for seq in range(lengths_ref.shape[0]):
+        end = end + lengths_ref[seq]
+        total = total + (place >= end).astype(jnp.int32)
     return total
 
 
 class Stretch:
-    def __init__(self, start, rows, before, conv_ref, head_ref, ends_ref, channels):
+    def __init__(self, start, rows, before, conv_ref, head_ref, lengths_ref, channels):
         length = rows.shape[0]
         self.channels = channels
         self.heads = channels // 64
         width = conv_ref.shape[1]
         state = (width - channels) // 2
         places = start + iota_of((length, 1), 0)
-        self.ids = ids_at(places, ends_ref)
-        self.ids_row = ids_at(start + iota_of((1, length), 1), ends_ref)
+        self.ids = ids_at(places, lengths_ref)
+        self.ids_row = ids_at(start + iota_of((1, length), 1), lengths_ref)
         inputs = rows[:, :width]
         joined = jnp.concatenate([before[:, :width], inputs], axis=0)
         self.shifted = [inputs]
         value = conv_ref[4:5, :] + inputs * conv_ref[3:4, :]
         for offset in range(1, 4):
-            same = (ids_at(places - offset, ends_ref) == self.ids) & (places >= offset)
+            same = (ids_at(places - offset, lengths_ref) == self.ids) & (places >= offset)
             moved = pltpu.roll(joined, offset, 0)[8:, :]
             moved = jnp.where(same, moved, 0.0)
             self.shifted.append(moved)
@@ -133,8 +135,8 @@
         self.dt_rows = self.dt.T[:8, :]
         self.causal = (self.ids == self.ids_row) & (rows_at >= columns_at)
         self.scores = dot_lanes(self.c_low, self.b_low)
-        last_id = jnp.where(start > 0, id_at(start - 1, ends_ref), -1)
-        end_id = id_at(start + length - 1, ends_ref)
+        last_id = jnp.where(start > 0, id_at(start - 1, lengths_ref), -1)
+        end_id = id_at(start + length - 1, lengths_ref)
         self.enter = jnp.where(self.ids == last_id, jnp.exp(self.cum), 0.0)
         end_cum = self.cum[length - 1 : length, :]
         self.tail = jnp.where(self.ids == end_id, jnp.exp(end_cum - self.cum), 0.0)
@@ -176,7 +178,7 @@
 
 
 def scan_forward_kernel(
-    ends_ref, deal_ref, rows_ref, conv_ref, head_ref, y_ref, seq_ref, states_ref, before, state, total
+    lengths_ref, deal_ref, rows_ref, conv_ref, head_ref, y_ref, seq_ref, states_ref, before, state, total
 ):
     step = pl.program_id(0)
     length = seq_ref.shape[0]
@@ -192,7 +194,7 @@
     picks = pick_rows(deal_ref, start, length)
     rows = dot_full(picks, rows_ref[...])
     seq_ref[...] = to_low(rows)
-    part = Stretch(start, rows, before[...], conv_ref, head_ref, ends_ref, channels)
+    part = Stretch(start, rows, before[...], conv_ref, head_ref, lengths_ref, channels)
     before[...] = rows[length - 8 :, :]
     state_now = state[...]
     states_ref[0] = state_now
@@ -219,13 +221,13 @@
         y_ref[...] = to_low(total[...])
 
 
-def scan_forward(ends, deal_row, rows, conv_table, head_table, channels, freight):
+def scan_forward(lengths, deal_row, rows, conv_table, head_table, channels, freight):
     group_rows, width = rows.shape
     steps = group_rows // STRETCH
     state_rows = (channels, LANES)
     return run(
         scan_forward_kernel,
-        (ends, deal_row, rows, conv_table, head_table),
+        (lengths, deal_row, rows, conv_table, head_table),
         grid=(steps,),
         in_specs=[
             pl.BlockSpec(memory_space=pltpu.SMEM),
@@ -256,7 +258,7 @@
 
 
 def scan_backward_kernel(
-    ends_ref,
+    lengths_ref,
     deal_ref,
     seq_ref,
     states_ref,
@@ -276,9 +278,17 @@
     steps = pl.num_programs(0)
     reducer = Reducer(other_ref.shape[0], other_ref, other_sum_ref, other_scratch)
 
+    last = dy_ref.shape[0] // STRETCH - 1
+
     @pl.when(order == 0)
     def _():
         reducer.begin()
+
+    for count in range(min(last + 1, reducer.inner + 3)):
+
+        @pl.when(order == count)
+        def _():
+            reducer.step(count)
 
     step = steps - 1 - order
     length = STRETCH
@@ -300,7 +310,7 @@
     rows = seq_ref[pl.ds(start, length), :].astype(jnp.float32)
     place = pl.multiple_of(jnp.maximum(start - 16, 0), 16)
     before = seq_ref[pl.ds(place, 16), :].astype(jnp.float32)[8:, :]
-    part = Stretch(start, rows, before, conv_ref, head_ref, ends_ref, channels)
+    part = Stretch(start, rows, before, conv_ref, head_ref, lengths_ref, channels)
     state_now = states_ref[0]
     state_low = to_low(state_now)
     next_grad = state_grad[...]
@@ -383,7 +393,7 @@
     rows_grad = value_grad * conv_ref[3:4, :]
     for offset in range(1, 4):
         moved = pltpu.roll(joined, length + 8 - offset, 0)[:length, :]
-        same = (ids_at(places + offset, ends_ref) == part.ids) & (
+        same = (ids_at(places + offset, lengths_ref) == part.ids) & (
             places + offset < steps * length
         )
         rows_grad = rows_grad + jnp.where(same, moved, 0.0) * conv_ref[3 - offset : 4 - offset, :]
@@ -392,11 +402,9 @@
         dot_rows(picks, to_low(jnp.concatenate([rows_grad, dt_in_grad], axis=1)))
     )
 
-    stages = reducer.inner + 3
-    last = dy_ref.shape[0] // length - 1
-    for count in range(stages):
-
-        @pl.when(order == min(count, last))
+    for count in range(last + 1, reducer.inner + 3):
+
+        @pl.when(order == last)
         def _():
             reducer.step(count)
 
@@ -406,14 +414,14 @@
 
 
 def scan_backward(
-    ends, deal_row, seq_rows, states, dy, conv_table, head_table, other, freight
+    lengths, deal_row, seq_rows, states, dy, conv_table, head_table, other, freight
 ):
     group_rows, width = seq_rows.shape
     channels = dy.shape[1]
     steps = group_rows // STRETCH
     return run(
         scan_backward_kernel,
-        (ends, deal_row, seq_rows, states, dy, conv_table, head_table, other),
+        (lengths, deal_row, seq_rows, states, dy, conv_table, head_table, other),
         grid=(steps,),
         in_specs=[
             pl.BlockSpec(memory_space=pltpu.SMEM),
@@ -569,6 +577,8 @@
     late=False,
 ):
     freight = list(freight)
+    for place, item in enumerate(freight):
+        item.rank = place
     flips = tuple(sorted(set(flips).union(*[item.flips for item in freight])))
     inner = max([inner] + [item.inner for item in freight])
     talks = bool(flips) or inner > 1
@@ -721,7 +731,16 @@
     def ways(self):
         return ((True, self.place > 0), (False, self.place < self.inner - 1))
 
-    def push(self, order):
+    def push_free(self, order):
+        target = self.targets[order]
+        for up, comes in self.ways():
+            heads = (target > self.place) if up else (target < self.place)
+
+            @pl.when(heads & jnp.logical_not(comes))
+            def _():
+                self.copy(order, up).start()
+
+    def push_rest(self, order):
         target = self.targets[order]
         for up, comes in self.ways():
             heads = (target > self.place) if up else (target < self.place)
@@ -731,9 +750,6 @@
                 self.sums[order] = to_low(
                     to_full(self.sums[order]) + self.arrived(target, up)
                 )
-
-            @pl.when(heads)
-            def _():
                 self.copy(order, up).start()
 
     def add_own(self, total):
@@ -879,22 +895,26 @@
             self.total[...] = total
         else:
             self.line.sums[order] = to_low(total)
+            self.line.push_free(order)
 
     def stage_d(self, order):
         if order == self.inner - 1:
             self.line.add_own(self.total)
         else:
-            self.line.push(order)
+            self.line.push_rest(order)
 
     def step(self, count):
         for stage, late in (
+            (self.stage_b, 1),
             (self.stage_a, 0),
-            (self.stage_b, 1),
             (self.stage_c, 2),
             (self.stage_d, 3),
         ):
             if 0 <= count - late < self.inner:
                 stage(count - late)
+
+    def steps(self):
+        return self.inner + 3
 
     def finish(self):
         for order in range(self.inner):
@@ -906,21 +926,30 @@
                 self.cross(order, kind).wait_send()
         self.line.finish()
 
-    def whole(self):
+    def whole(self, depart):
         self.begin()
+        depart(0)
         for count in range(self.inner + 3):
             self.step(count)
+            if count >= 2:
+                depart(count - 1)
         self.finish()
 
 
-def reduce_kernel(inner, p_ref, out_ref, *scratch):
-    Reducer(inner, p_ref, out_ref, scratch).whole()
+def reduce_kernel(inner, staged, depart, p_ref, out_ref, *scratch):
+    def leave(number):
+        if staged:
+            depart(lambda item: item.rank == number)
+
+    if not staged:
+        depart()
+    Reducer(inner, p_ref, out_ref, scratch).whole(leave)
 
 
 def reduce_rows(partial, freight=()):
     inner, _, rows, width = partial.shape
     return run(
-        functools.partial(reduce_kernel, inner),
+        functools.partial(reduce_kernel, inner, inner > 1),
         (partial,),
         in_specs=[pl.BlockSpec(memory_space=pl.ANY)],
         out_specs=[pl.BlockSpec(memory_space=pltpu.VMEM)],
@@ -929,6 +958,7 @@
         freight=freight,
         flips=FLIPS,
         inner=inner,
+        late=True,
         micros=25 * inner,
         name="reduce_rows",
     )
@@ -1098,6 +1128,8 @@
     )
     if inner > 1:
         begin()
+    else:
+        depart()
     planes[0][0]()
     own.start()
     planes[0][1]()
@@ -1108,8 +1140,6 @@
         planes[order][0]()
         planes[order - 1][2]()
         planes[order][1]()
-    if inner == 1:
-        depart()
     planes[inner - 1][2]()
     for stages in planes:
         stages[3]()
@@ -1138,35 +1168,91 @@
 
 
 def begin_kernel(
-    inner, x_ref, g_ref, w_ref, s_ref, r_ref, x_out, g_out, w_out, s_out, r_out, own_sems, *sems
+    inner,
+    x_ref,
+    g_ref,
+    s_ref,
+    d_ref,
+    in_ref,
+    shared_ref,
+    out_ref,
+    down_ref,
+    x_out,
+    g_out,
+    w_out,
+    s_out,
+    d_out,
+    r_out,
+    w_ref,
+    r_ref,
+    own_sems,
+    pick_sems,
+    *sems,
 ):
     part = lax.axis_index("seq")
     place, _ = own_shard_group(inner)
     rows = w_ref.shape[0]
+    seq_devices = x_out.shape[0]
+    picks = []
+
+    def pick(source, target):
+        picks.append(pltpu.make_async_copy(source, target, pick_sems.at[len(picks)]))
+
+    shared = shared_ref.shape[1] // seq_devices // 2
+    state = w_ref.shape[1] - 2 * shared
+    channels = (in_ref.shape[1] - state) // (2 * seq_devices - 2)
+    state -= 2 * channels
+    at = 0
+    for source, extent in ((in_ref, channels), (shared_ref, shared)):
+        for side in range(2):
+            start = pl.multiple_of((side * seq_devices + part) * extent, extent)
+            pick(source.at[:, pl.ds(start, extent)], w_ref.at[:, pl.ds(at, extent)])
+            at += extent
+        if source is in_ref:
+            pick(
+                source.at[:, pl.ds(in_ref.shape[1] - state, state)],
+                w_ref.at[:, pl.ds(at, state)],
+            )
+            at += state
+    halves = seq_devices // inner
+    at = 0
+    for half in range(halves):
+        for source in (out_ref, down_ref):
+            fine = source.shape[0] // halves // seq_devices
+            start = pl.multiple_of((half * seq_devices + part) * fine, fine)
+            pick(source.at[pl.ds(start, fine)], r_ref.at[pl.ds(at, fine)])
+            at += fine
+    for copy in picks:
+        copy.start()
     targets = [
         lambda p: s_out.at[p],
         lambda p: w_out.at[pl.ds(p * rows, rows)],
         lambda p: r_out.at[p],
+        lambda p: d_out.at[p],
     ]
-    sources = [s_ref, w_ref, r_ref]
+    sources = [s_ref, w_ref, r_ref, d_ref]
     lines = [
         line_gather(inner, source, target, sems[2 * order], sems[2 * order + 1])
         for order, (source, target) in enumerate(zip(sources, targets))
     ]
-    line, planes = group_gather(inner, g_ref, lambda p, b: g_out.at[p, b], sems[6:10])
+    line, planes = group_gather(inner, g_ref, lambda p, b: g_out.at[p, b], sems[8:12])
     lines.append(line)
-    x_plane = plane_gather(x_ref, lambda b: x_out.at[b], sems[10], sems[11])
+    x_plane = plane_gather(x_ref, lambda b: x_out.at[b], sems[12], sems[13])
     rows_line = lines.pop(2)
-    for begin_line, _, _ in lines:
-        begin_line()
+    lines[0][0]()
+    lines[2][0]()
+    lines[3][0]()
     x_plane[0]()
     planes[0][0]()
+    for copy in picks:
+        copy.wait()
+    lines[1][0]()
     owns = [
         pltpu.make_async_copy(source, target(place), own_sems.at[order])
         for order, (source, target) in enumerate(zip(sources, targets))
     ]
-    owns.append(pltpu.make_async_copy(x_ref, x_out.at[part], own_sems.at[3]))
-    owns.append(pltpu.make_async_copy(g_ref, g_out.at[place, part], own_sems.at[4]))
+    owns.append(pltpu.make_async_copy(x_ref, x_out.at[part], own_sems.at[4]))
+    owns.append(pltpu.make_async_copy(g_ref, g_out.at[place, part], own_sems.at[5]))
     for copy in owns:
         copy.start()
     x_plane[1]()
@@ -1195,24 +1281,31 @@
         copy.wait()
 
 
-def begin(x, grad, weights, small, rows, inner):
+def begin(x, grad, small, by_depth, w_in, w_shared, w_out, w_down, in_width, shared_part, inner):
     seq_devices = lax.axis_size("seq")
+    low = jnp.bfloat16
+    depth, width = w_in.shape[0], w_out.shape[1]
+    columns = in_width + 2 * shared_part
+    rows = (w_out.shape[0] + w_down.shape[0]) // seq_devices
     anywhere = pl.BlockSpec(memory_space=pl.ANY)
     sems = lambda *shape: pltpu.SemaphoreType.DMA(shape)
-    line_sems = [sems(2, inner - 1, 2)] * 6
+    line_sems = [sems(2, inner - 1, 2)] * 8
     return run(
         functools.partial(begin_kernel, inner),
-        (x, grad, weights, small, rows),
-        in_specs=[anywhere] * 5,
-        out_specs=[anywhere] * 5,
+        (x, grad, small, by_depth, w_in, w_shared, w_out, w_down),
+        in_specs=[anywhere] * 8,
+        out_specs=[anywhere] * 6,
         out_shape=[
             jax.ShapeDtypeStruct((seq_devices,) + x.shape, x.dtype),
             jax.ShapeDtypeStruct((inner, seq_devices) + grad.shape, grad.dtype),
-            jax.ShapeDtypeStruct((inner * weights.shape[0], weights.shape[1]), weights.dtype),
+            jax.ShapeDtypeStruct((inner * depth, columns), low),
             jax.ShapeDtypeStruct((inner,) + small.shape, small.dtype),
-            jax.ShapeDtypeStruct((inner,) + rows.shape, rows.dtype),
+            jax.ShapeDtypeStruct((inner,) + by_depth.shape, low),
+            jax.ShapeDtypeStruct((inner, rows, width), low),
         ],
-        scratch=[sems(5)] + line_sems + group_sems(inner) + [sems(14), sems(14)],
+        scratch=[pltpu.VMEM((depth, columns), low), pltpu.VMEM((rows, width), low)]
+        + [sems(6), sems(5 + 2 * (seq_devices // inner))]
+        + line_sems + group_sems(inner) + [sems(14), sems(14)],
         flips=FLIPS,
         inner=inner,
         micros=130,
@@ -1223,7 +1316,6 @@
 def settle_kernel(
     inner,
     counts,
-    spot,
     hidden_ref,
     small_ref,
     x_ref,
@@ -1236,11 +1328,11 @@
     parts, refs = refs[:counts], refs[counts:]
     tokens_out, refs = refs[0], refs[1:]
     outs, refs = refs[: counts + 1], refs[counts + 1 :]
-    hidden_sum, small_held, small_sum, small_load = refs[:4]
-    refs = refs[4:]
+    hidden_sum, small_sum = refs[:2]
+    refs = refs[2:]
     take = len(Reducer.scratch(1, 16, LANES))
     hidden = Reducer(1, hidden_ref, hidden_sum, refs[:take])
-    small = Reducer(inner, small_held, small_sum, refs[take : 2 * take])
+    small = Reducer(inner, small_ref, small_sum, refs[take : 2 * take])
     refs = refs[2 * take :]
     lines, totals, planes, owns = [], [], [], []
     for index in range(counts + 1):
@@ -1265,18 +1357,23 @@
         loads.append(
             pltpu.make_async_copy(parts[index].at[place], owns[index][0], load.at[inner - 1])
         )
-    small_loading = pltpu.make_async_copy(small_ref, small_held, small_load)
     for copy in loads:
         copy.start()
-    small_loading.start()
+    small.begin()
     hidden.begin()
 
-    def send_part(index):
+    def load(index):
         for copy in loads[index * inner : (index + 1) * inner]:
             copy.wait()
         totals[index][...] = to_full(owns[index][0][...])
-        for order in range(inner - 1):
-            lines[index].push(order)
+
+    def push_free(index, orders):
+        for order in orders:
+            lines[index].push_free(order)
+
+    def push_rest(index, orders):
+        for order in orders:
+            lines[index].push_rest(order)
 
     def gather_part(index):
         lines[index].add_own(totals[index])
@@ -1284,51 +1381,51 @@
         planes[index][0]()
         owns[index][1].start()
 
+    every = range(inner - 1)
+    small.step(0)
+    small.step(1)
+    load(0)
+    push_free(0, every[:1])
+    for count in range(2, small.steps() - 2):
+        small.step(count)
     hidden.step(0)
-    send_part(0)
-    for count in range(1, 4):
-        hidden.step(count)
-    x = to_full(x_ref[...])
-    scale = norm_scale(x)
-    unit = x * scale
-    grad = hidden_sum[...]
-    gain_grad = jnp.sum(grad * unit, axis=0, keepdims=True)
-    scaled = grad * gain_ref[...]
-    mean = jnp.mean(scaled * unit, axis=1, keepdims=True)
-    tokens_out[...] = to_low(mix_ref[...] + scale * (scaled - unit * mean))
-    small_loading.wait()
-    wide = small_held.shape[3]
-    depth = gain_grad.shape[1] // inner
-    rows16 = pl.ds(spot // 16 * 16, 16)
-    at_row = iota_of((16, wide), 0) == spot % 16
-    for shard in range(inner):
-        row = gain_grad[:, shard * depth : (shard + 1) * depth]
-        if depth < wide:
-            row = jnp.concatenate([row, jnp.zeros((1, wide - depth), jnp.float32)], axis=1)
-        old = to_full(small_held[shard, 0, rows16])
-        small_held[shard, 0, rows16] = to_low(jnp.where(at_row, old + row, old))
-    small.begin()
-    small.step(0)
+    push_free(0, every[1:])
     for index in range(1, counts):
-        send_part(index)
-        small.step(index)
-        gather_part(index - 1)
-        if index > 1:
-            planes[index - 2][1]()
-    for count in range(counts, inner + 3):
+        load(index)
+        push_free(index, every)
+    push_rest(0, every[:1])
+    for count in range(small.steps() - 2, small.steps()):
         small.step(count)
     owns[counts][0][...] = to_low(small_sum[...])
     planes[counts][0]()
     owns[counts][1].start()
+    hidden.step(1)
+    push_rest(0, every[1:])
+    planes[counts][1]()
+    hidden.step(2)
+    hidden.step(3)
+    planes[counts][2]()
+    x = to_full(x_ref[...])
+    scale = norm_scale(x)
+    unit = x * scale
+    scaled = hidden_sum[...] * gain_ref[...]
+    mean = jnp.mean(scaled * unit, axis=1, keepdims=True)
+    tokens_out[...] = to_low(mix_ref[...] + scale * (scaled - unit * mean))
     if counts > 1:
-        planes[counts - 2][1]()
+        push_rest(1, every[:1])
+    gather_part(0)
+    if counts > 1:
+        push_rest(1, every[1:])
+    for index in range(1, counts):
+        planes[index - 1][1]()
+        if index > 1:
+            planes[index - 2][2]()
+        gather_part(index)
+        if index + 1 < counts:
+            push_rest(index + 1, every)
+    if counts > 1:
         planes[counts - 2][2]()
-    gather_part(counts - 1)
-    planes[counts][1]()
-    planes[counts][2]()
     planes[counts - 1][1]()
-    for index in range(counts - 2):
-        planes[index][2]()
     planes[counts - 1][2]()
     for plane in planes:
         plane[3]()
@@ -1340,7 +1437,7 @@
         copy.wait()
 
 
-def settle(hidden, small, x, mix, gain, parts, spot, inner):
+def settle(hidden, small, x, mix, gain, parts, inner):
     _, _, rows, width = hidden.shape
     seq_devices = lax.axis_size("seq")
     anywhere = pl.BlockSpec(memory_space=pl.ANY)
@@ -1351,9 +1448,7 @@
     shapes = [part.shape[1:] for part in parts] + [(small_rows, small_wide)]
     scratch = [
         pltpu.VMEM((rows, width), jnp.float32),
-        pltpu.VMEM(small.shape, low),
         pltpu.VMEM((small_rows, small_wide), jnp.float32),
-        sems(),
     ]
     scratch += Reducer.scratch(1, rows, width)
     scratch += Reducer.scratch(inner, small_rows, small_wide)
@@ -1363,7 +1458,7 @@
         scratch += [pltpu.VMEM(shape, jnp.float32), sems(inner)]
         scratch += LineSum.scratch(inner, *shape)
     return run(
-        functools.partial(settle_kernel, inner, len(parts), spot),
+        functools.partial(settle_kernel, inner, len(parts)),
         (hidden, small, x, mix, gain) + tuple(parts),
         in_specs=[anywhere] * 2 + [inside] * 3 + [anywhere] * len(parts),
         out_specs=[inside] + [anywhere] * len(shapes),
@@ -1556,6 +1651,13 @@
         main = main_grad_ref.shape[1]
         main_grad_ref[...] = to_low(total[:, :main])
         rest_grad_ref[...] = to_low(total[:, main:])
+        by_gain = jnp.sum(total[:, :columns] * to_full(w_ref[:, :columns]), axis=1, keepdims=True)
+        by_gain += jnp.sum(total[:, columns:] * to_full(dt_ref[...]), axis=1, keepdims=True)
+        rest = rest_grad_ref.shape[1]
+        lane = iota_of((rest_grad_ref.shape[0], LANES), 1)
+        rest_grad_ref[:, rest - LANES :] = to_low(
+            jnp.where(lane == LANES - 1, by_gain, total[:, columns:])
+        )
 
 
 def project_back(dgate, drows, hidden, weights, dt_weights, blocks, freight=()):
@@ -2388,39 +2490,54 @@
     def own_rows(array, extent):
         return lax.dynamic_slice_in_dim(array, part * extent, extent, 0)
 
-    small_weights = [
-        norm_in, own_columns(w_dt, 0, heads), conv_w, conv_b, dt_bias, a_log, d_skip, norm_gate, norm_moe, w_router
-    ]
-    in_columns = jnp.concatenate(
+    small_weights = [norm_in, conv_w, conv_b, dt_bias, a_log, d_skip, norm_gate, norm_moe]
+    by_depth = jnp.concatenate(
         [
-            own_columns(w_in, 0, channels),
-            own_columns(w_in, inner_width, channels),
-            w_in[:, 2 * inner_width :],
-            own_columns(w_shared, 0, shared_part),
-            own_columns(w_shared, shared_width, shared_part),
+            w_router,
+            own_columns(w_dt, 0, heads),
+            jnp.zeros((depth_rows, LANES - expert_total - heads), jnp.bfloat16),
         ],
         axis=1,
     )
+    in_width = 2 * channels + w_in.shape[1] - 2 * inner_width
     flat = flat_of(small_weights)
-    rows_sent = rows_to_send([w_out, w_shared_down], part)
     if outer == 1:
-        wide = in_columns.shape[1]
-        flat_rows = -(-flat.size // (wide * 32)) * 32
-        flat = jnp.pad(flat, (0, flat_rows * wide - flat.size)).reshape(flat_rows, wide)
-        x_group, grad_all, proj_in, joined, rows_joined = begin(
-            tokens[0], out_grad[0], in_columns, flat, rows_sent, inner
+        flat_rows = -(-flat.size // (LANES * 32)) * 32
+        flat = jnp.pad(flat, (0, flat_rows * LANES - flat.size)).reshape(flat_rows, LANES)
+        x_group, grad_all, proj_in, joined, depth_joined, rows_joined = begin(
+            tokens[0],
+            out_grad[0],
+            flat,
+            by_depth,
+            w_in,
+            w_shared,
+            w_out,
+            w_shared_down,
+            in_width,
+            shared_part,
+            inner,
         )
         joined = joined.reshape(inner, -1)
         x_group = x_group.reshape(group_rows, width)
     else:
         x_group = gather_rows(tokens[0], 1)[0].reshape(group_rows, width)
         grad_all = gather_rows(out_grad[0], inner)[0]
+        in_columns = jnp.concatenate(
+            [
+                own_columns(w_in, 0, channels),
+                own_columns(w_in, inner_width, channels),
+                w_in[:, 2 * inner_width :],
+                own_columns(w_shared, 0, shared_part),
+                own_columns(w_shared, shared_width, shared_part),
+            ],
+            axis=1,
+        )
         proj_in = lax.all_gather(in_columns, "shard", tiled=True)
         joined = lax.all_gather(flat, "shard")
-        rows_joined = lax.all_gather(rows_sent, "shard")
+        depth_joined = lax.all_gather(by_depth, "shard")
+        rows_joined = lax.all_gather(rows_to_send([w_out, w_shared_down], part), "shard")
     (
         gain_in,
-        dt_columns,
         conv_weight,
         conv_bias,
         step_bias,
@@ -2428,9 +2545,11 @@
         skip_gain,
         gain_gate,
         gain_moe,
-        router,
     ) = split_small(joined, small_weights)
-    dt_columns = jnp.pad(dt_columns, ((0, 0), (0, LANES - heads)))
+    depth_joined = depth_joined.reshape(width, LANES)
+    lane = jnp.arange(LANES)[None]
+    router_wide = jnp.where(lane < expert_total, depth_joined, 0)
+    dt_columns = jnp.where(lane < heads, jnp.roll(depth_joined, -expert_total, axis=1), 0)
     grad_all = grad_all.reshape(blocks, tok_rows, width)
 
     weights_of = (w_experts, w_experts_down)
@@ -2460,13 +2579,11 @@
     last = inner - 1
 
     gain_row = to_full(gain_in)[None]
-    in_width = in_columns.shape[1] - 2 * shared_part
     keys = [(1, 0, DOWN)]
     hidden_in, gate_in, rows_in, arrays = project(
         x_group, gain_row, proj_in, dt_columns, channels, in_width, parcels(*keys)
     )
     unpack(keys, arrays)
-    ends = jnp.cumsum(lengths[0]).astype(jnp.int32)
     conv_part = jnp.concatenate(
         [own_rows(conv_weight, channels), conv_weight[inner_width:]], axis=0
     )
@@ -2486,7 +2603,7 @@
     )
     keys = [(1, 0, UP), (last, 0, DOWN)]
     y, seq_rows, states, (taken, *arrays) = scan_forward(
-        ends,
+        lengths[0],
         deal_order,
         rows_in,
         conv_table,
@@ -2506,15 +2623,12 @@
         )
     own_weights = taken
     gate_gain = to_full(own_rows(gain_gate, channels))[None]
-    keys = [(1, 1, DOWN)]
-    mix_part, arrays = mix_out(y, gate_in, gate_gain, own_weights, seq_devices, parcels(*keys))
-    unpack(keys, arrays)
+    (mix_part,) = mix_out(y, gate_in, gate_gain, own_weights, seq_devices)
     keys = [(last, 0, UP), (last, 1, DOWN)]
     mixed, arrays = reduce_rows(mix_part[None], parcels(*keys))
     unpack(keys, arrays)
 
     moe_row = to_full(gain_moe)[None]
-    router_wide = jnp.pad(router, ((0, 0), (0, LANES - expert_total)))
     route_ids = jnp.pad(routes[0], ((0, 0), (0, LANES - top_count)))
     after_mix, moe_wide, gates = token_forward(
         mixed, tokens[0], moe_row, router_wide, route_ids, inner_width, top_count
@@ -2549,7 +2663,7 @@
         for kind in range(2)
     ]
     if outer == 1:
-        late_keys = [(1, 1, UP)]
+        late_keys = [(1, 1, UP), (1, 1, DOWN)]
         early_keys = [(1, 0, UP), (last, 0, DOWN)]
         expert_res, expert_back, grads, sent = experts(
             expert_rows,
@@ -2568,7 +2682,7 @@
                 pieces[0, expert, kind] = lax.dynamic_index_in_dim(
                     weights_of[kind], place * per_device + expert, 0, keepdims=False
                 )
-        keys = [(1, 1, UP)]
+        keys = [(1, 1, UP), (1, 1, DOWN)]
         moe_all, arrays = carry(moe_all, parcels(*keys))
         unpack(keys, arrays)
         early_keys, sent = [], []
@@ -2596,12 +2710,12 @@
         keys = [key for key in keys if key not in early_keys]
         returned.update(zip(keys, arrays))
 
-    keys = [(1, 0, UP), (last, 0, DOWN), (last, 0, UP), (1, 0, DOWN), (1, 1, DOWN)]
+    keys = [(1, 0, UP), (last, 0, DOWN), (last, 0, UP), (1, 0, DOWN)]
     out_part, back_part, arrays = combine(
         picks, expert_res, expert_back, shared_res, shared_back, inner, back_parcels(*keys)
     )
     unpack_back(keys, arrays)
-    keys = [(2, 0, UP), (last, 1, UP)]
+    keys = [(last, 1, UP), (2, 0, DOWN), (1, 1, UP)]
     back, arrays = reduce_rows(
         back_part.reshape(inner, seq_devices, tok_rows, -1), back_parcels(*keys)
     )
@@ -2620,17 +2734,17 @@
         top_count,
     )
 
-    keys = [(1, 1, UP), (last, 1, DOWN)]
+    keys = [(2, 0, UP)]
     mix_group, arrays = gather_rows(mix_wide, 1, back_parcels(*keys))
     unpack_back(keys, arrays)
-    keys = [(2, 0, DOWN)]
+    keys = [(last, 1, DOWN)]
     dy, gate_in_grad, proj_out_grad, gain_gate_grad, arrays = mix_back(
         mix_group[0], y, gate_in, gate_gain, own_weights, back_parcels(*keys)
     )
     unpack_back(keys, arrays)
-    keys = [(2, 1, UP)]
-    rows_grad, conv_grad, head_grad, out_sum, (taken, *arrays) = scan_backward(
-        ends,
+    keys = [(2, 1, UP), (1, 1, DOWN)]
+    rows_grad, conv_grad, head_grad, out_sum, arrays = scan_backward(
+        lengths[0],
         deal_order,
         seq_rows,
         states,
@@ -2638,13 +2752,14 @@
         conv_table,
         head_table,
         out_part.reshape(inner, seq_devices, tok_rows, -1),
-        [PlaneSwap(rows_from_owner([proj_out_grad, shared_down_grad]))] + back_parcels(*keys),
+        back_parcels(*keys),
     )
     unpack_back(keys, arrays)
     layer_out = to_low(after_mix + out_sum)
     keys = [(2, 1, DOWN)]
-    hidden_part, main_grad, rest_grad, arrays = project_back(
-        gate_in_grad, rows_grad, hidden_in, proj_in, dt_columns, seq_devices, back_parcels(*keys)
+    swap = [PlaneSwap(rows_from_owner([proj_out_grad, shared_down_grad]))]
+    hidden_part, main_grad, rest_grad, (taken, *arrays) = project_back(
+        gate_in_grad, rows_grad, hidden_in, proj_in, dt_columns, seq_devices, swap + back_parcels(*keys)
     )
     unpack_back(keys, arrays)
     experts_grad, experts_down_grad = collect(
@@ -2665,6 +2780,7 @@
         rest_grad[:, :state_columns],
         router_grad[:, :expert_total],
         spread(rest_grad[:, state_columns : state_columns + heads], head_total, 1),
+        rest_grad[:, -1:],
         to_low(gain_moe_grad[0])[:, None],
     ]
     by_shard = [
@@ -2682,7 +2798,7 @@
     extents = [piece.shape[1] for piece in by_depth]
     used = sum(extents)
     if outer == 1:
-        wide = -(-max(used, depth_rows) // LANES) * LANES
+        wide = -(-used // LANES) * LANES
         by_depth.append(jnp.zeros((width, wide - used), jnp.bfloat16))
         by_depth = jnp.concatenate(by_depth, axis=1).reshape(inner, seq_devices, -1, wide)
         depth_each = by_depth.shape[2]
@@ -2692,18 +2808,17 @@
         by_shard = jnp.pad(by_shard, ((0, 0), (0, each * seq_devices * wide - size)))
         by_shard = by_shard.reshape(inner, seq_devices, each, wide)
         by_shard = jnp.pad(by_shard, ((0, 0), (0, 0), (0, padded - each), (0, 0)))
-        tokens_grad, rows_all, shared_all, main_all, small_all = settle(
+        tokens_grad, main_all, rows_all, shared_all, small_all = settle(
             hidden_part[None],
             jnp.concatenate([by_depth, by_shard], axis=2),
             tokens[0],
             mix_grad,
             gain_row,
             [
+                main_grad.reshape(inner, depth_rows, -1),
                 taken.reshape(inner, -1, width),
                 shared_up_grad.reshape(inner, depth_rows, -1),
-                main_grad.reshape(inner, depth_rows, -1),
             ],
-            depth_each + each,
             inner,
         )
         w_in_grad, w_shared_grad, w_out_grad, w_shared_down_grad = assemble(
@@ -2719,7 +2834,6 @@
         )
         depth_sum = to_full(small_all[:, :depth_each].reshape(depth_rows, wide))
         shard_sum = small_all[:, depth_each : depth_each + each].reshape(-1)
-        norm_in_grad = to_full(small_all[0, depth_each + each, :depth_rows])
     else:
         hidden_grad = reduce_rows(hidden_part[None])[0]
         residual = to_full(tokens[0])
@@ -2731,14 +2845,12 @@
             + own_scale
             * (scaled - own_unit * jnp.mean(scaled * own_unit, axis=1, keepdims=True))
         )
-        by_depth.append(to_low(jnp.sum(hidden_grad * own_unit, axis=0))[:, None])
         by_depth = jnp.concatenate(by_depth, axis=1).reshape(shard_devices, -1)
         packed = jnp.concatenate([by_depth, by_shard], axis=1)
         summed = lax.psum(lax.psum_scatter(packed, "shard", tiled=True), "seq").reshape(-1)
-        count = depth_rows * (used + 1)
-        depth_sum = to_full(summed[:count]).reshape(depth_rows, used + 1)
+        count = depth_rows * used
+        depth_sum = to_full(summed[:count]).reshape(depth_rows, used)
         shard_sum = summed[count:]
-        norm_in_grad = depth_sum[:, used]
 
         def from_line(part, rows):
             own = lax.psum_scatter(part.reshape(shard_devices, rows, -1), "shard")
@@ -2768,7 +2880,8 @@
     start += expert_total
     w_dt_grad = depth_sum[:, start : start + head_total]
     start += head_total
-    norm_moe_grad = depth_sum[:, start]
+    norm_in_grad = depth_sum[:, start] / to_full(norm_in)
+    norm_moe_grad = depth_sum[:, start + 1]
     return (
         layer_out[None],
         tokens_grad[None],

time: 1090 us -> 996 us (0.914)
  Pallas kernels: 1020 us -> 944 us
    pallas_call x16, Pallas kernels: 989 us -> 912 us  [run(): pl.pallas_call(wrapped, grid=grid, in_specs=list(in_specs) + [anywhere] *...]
where the time goes in v4:
time: 996 us; the launch traced here: 991 us
  Pallas kernels  944 us (95%)
  local copies, waits for them, and re-layouts  34.5 us (3%)
  other arithmetic  11.8 us (1%)
    pallas_call x16, Pallas kernels, run(): pl.pallas_call(wrapped, grid=grid, in_specs=list(in_specs) + [anywhere] *...  912 us

profile of v4, /device:TPU:0, one launch (start us, length us, event | category | flops | bytes accessed | tf_op | source)
XLA Modules:
  0.0 991.4 jit_solution(2626698500007112569)
XLA Ops:
  1.8 4.8 concatenate.43
  9.2 146.2 %begin.1 = (bf16[8,192,1536]{2,1,0:T(8,128)(2,1)}, bf16[4,8,192,1536]{3,2,1,0:T(8,128)(2,1)}, bf16[1536,1280]{1,0:T(8,128)(2,1)}, bf16[4,64,128]{2,1,0:T(8,128)(...) custom-call(bf16[192,1536]{1,0:T(8,128)(2,1)} %bitcast.75, bf16[192,1536]{1,0:T(8,128)(2,1)} %bitcast.84, ...), custom_call_target="tpu_custom_call" | custom-call | bytes 468000000 | tf_op jit(solution)/shard_map/begin/pallas_call | solution.py:679
  159.3 15.4 %project.1 = (bf16[1536,1536]{1,0:T(8,128)(2,1)}, f32[1536,384]{1,0:T(8,128)}, bf16[1536,768]{1,0:T(8,128)(2,1)}, bf16[128,1536]{1,0:T(8,128)(2,1)}) custom-call(bf16[1536,1536]{1,0:T(8,128)(2,1)} %bitcast.80, f32[1,1536]{1,0:T(1,128)} %bitcast.102, bf16[1536,1280]{1,0:T(8,128)(2,1)} %get-tuple-element.114.refs_2_.refs_3_, ...), custom_call_target="tpu_custom_call" | custom-call | bytes 39600000 | tf_op jit(solution)/shard_map/project/pallas_call | solution.py:679
  175.0 1.8 reshape.192
  178.8 30.9 %scan_forward.1 = (bf16[1536,384]{1,0:T(8,128)(2,1)}, bf16[1536,768]{1,0:T(8,128)(2,1)}, f32[6,384,128]{2,1,0:T(8,128)}, bf16[8,64,1536]{2,1,0:T(8,128)(2,1)}, b...) custom-call(s32[4]{0:T(128)} %bitcast.106, s32[1,1536]{1,0:T(1,128)} %refs_1_.7, ...), custom_call_target="tpu_custom_call" | custom-call | bytes 90000000 | tf_op jit(solution)/shard_map/scan_forward/pallas_call | solution.py:679
  210.4 9.0 mix_out.1
  219.4 32.0 %reduce_rows.2 = (f32[192,1664]{1,0:T(8,128)}, bf16[384,1024]{1,0:T(8,128)(2,1)}, bf16[128,1536]{1,0:T(8,128)(2,1)}) custom-call(bf16[1,8,192,1664]{3,2,1,0:T(8,128)(2,1)} %bitcast.72, bf16[8,384,1024]{2,1,0:T(8,128)(2,1)} %refs_16_.1, bf16[8,128,1536]{2,1,0:T(8,128)(2,1)} %refs_17_.1), custom_call_target="tpu_custom_call" | custom-call | bytes 90000000 | tf_op jit(solution)/shard_map/reduce_rows/pallas_call | solution.py:679
  253.6 3.6 token_forward.1
  257.2 113.8 %gather_rows.2 = (bf16[4,8,192,1664]{3,2,1,0:T(8,128)(2,1)}, bf16[384,1024]{1,0:T(8,128)(2,1)}, bf16[128,1536]{1,0:T(8,128)(2,1)}, bf16[384,1024]{1,0:T(8,128)(2,1)}) custom-call(bf16[192,1664]{1,0:T(8,128)(2,1)} %get-tuple-element.125.refs_0_.wide_ref, bf16[8,384,1024]{2,1,0:T(8,128)(2,1)} %refs_16_.1, bf16[8,128,1536]{2,1,0:T(8,128)(2,1)} %refs_17_.1, ...), custom_call_target="tpu_custom_call" | custom-call | bytes 360000000 | tf_op jit(solution)/shard_map/gather_rows/pallas_call | solution.py:679
  371.1 54.3 %dispatch.1 = (bf16[2,1024,1664]{2,1,0:T(8,128)(2,1)}, bf16[2,1024,1536]{2,1,0:T(8,128)(2,1)}, bf16[32,192,128]{2,1,0:T(8,128)(2,1)}, bf16[384,1024]{1,0:T(8,128)(2,1)}) custom-call(bf16[32,192,1664]{2,1,0:T(8,128)(2,1)} %bitcast.68, bf16[32,192,1536]{2,1,0:T(8,128)(2,1)} %bitcast.70, bf16[8,384,1024]{2,1,0:T(8,128)(2,1)} %refs_16_.1), custom_call_target="tpu_custom_call" | custom-call | bytes 108000000 | tf_op jit(solution)/shard_map/dispatch/pallas_call | solution.py:679
  425.3 24.3 %shared_expert.1 = (bf16[8,192,1536]{2,1,0:T(8,128)(2,1)}, bf16[8,192,1536]{2,1,0:T(8,128)(2,1)}, bf16[1536,256]{1,0:T(8,128)(2,1)}, bf16[128,1536]{1,0:T(8,128)(2,1)}, bf16[128,1536]{1,0:T(8,128)(2,1)}) custom-call(bf16[32,192,1664]{2,1,0:T(8,128)(2,1)} %bitcast.69, bf16[32,192,1536]{2,1,0:T(8,128)(2,1)} %bitcast.71, ...), custom_call_target="tpu_custom_call" | custom-call | bytes 64800000 | tf_op jit(solution)/shard_map/shared_expert/pallas_call | solution.py:679
  449.6 57.4 %experts.1 = (bf16[2,1024,1536]{2,1,0:T(8,128)(2,1)}, bf16[2,1024,1664]{2,1,0:T(8,128)(2,1)}, bf16[384,1024]{1,0:T(8,128)(2,1)}, bf16[128,1536]{1,0:T(8,128)(2,1...) custom-call(bf16[2,1024,1664]{2,1,0:T(8,128)(2,1)} %get-tuple-elemen, ...), custom_call_target="tpu_custom_call" | custom-call | bytes 162000000 | tf_op jit(solution)/shard_map/experts/pallas_call | solution.py:679
  507.0 32.6 %combine.1 = (bf16[32,192,1536]{2,1,0:T(8,128)(2,1)}, bf16[32,192,1664]{2,1,0:T(8,128)(2,1)}, bf16[384,1024]{1,0:T(8,128)(2,1)}, bf16[128,1536]{1,0:T(8,128)(2,1)}) custom-call(bf16[32,192,128]{2,1,0:T(8,128)(2,1)} %get-tuple-element.128.refs_0_, bf16[2,1024,1536]{2,1,0:T(8,128)(2,1)} %get-tuple-element.141.refs_1_, ...), custom_call_target="tpu_custom_call" | custom-call | bytes 108000000 | tf_op jit(solution)/shard_map/combine/pallas_call | solution.py:679
  539.6 106.6 %reduce_rows.3 = (f32[192,1664]{1,0:T(8,128)}, bf16[384,1024]{1,0:T(8,128)(2,1)}, bf16[128,1536]{1,0:T(8,128)(2,1)}, bf16[384,1024]{1,0:T(8,128)(2,1)}) custom-call(bf16[4,8,192,1664]{3,2,1,0:T(8,128)(2,1)} %bitcast.73, bf16[384,1024]{1,0:T(8,128)(2,1)} %get-tuple-element.148.refs_1_, bf16[128,1536]{1,0:T(8,128)(2,1)} %get-tuple-element.149.refs_2_, ...), custom_call_target="tpu_custom_call" | custom-call | bytes 360000000 | tf_op jit(solution)/shard_map/reduce_rows/pallas_call | solution.py:679
  646.2 6.2 token_back.1
  652.4 38.0 %gather_rows.3 = (bf16[1,8,192,1664]{3,2,1,0:T(8,128)(2,1)}, bf16[384,1024]{1,0:T(8,128)(2,1)}) custom-call(bf16[192,1664]{1,0:T(8,128)(2,1)} %get-tuple-element.153.refs_0_, bf16[384,1024]{1,0:T(8,128)(2,1)} %get-tuple-element.154.refs_1_), custom_call_target="tpu_custom_call" | custom-call | bytes 90000000 | tf_op jit(solution)/shard_map/gather_rows/pallas_call | solution.py:679
  690.4 15.4 %mix_back.1 = (bf16[1536,384]{1,0:T(8,128)(2,1)}, bf16[1536,384]{1,0:T(8,128)(2,1)}, bf16[384,1536]{1,0:T(8,128)(2,1)}, f32[8,384]{1,0:T(8,128)}, bf16[128,1536]{1,0:T(8,128)(2,1)}) custom-call(bf16[8,192,1664]{2,1,0:T(8,128)(2,1)} %bitcast.78, bf16[1536,384]{1,0:T(8,128)(2,1)} %get-tuple-element.118.refs_0_.refs_1_, ...), custom_call_target="tpu_custom_call" | custom-call | bytes 43200000 | tf_op jit(solution)/shard_map/mix_back/pallas_call | solution.py:679
  705.8 101.9 %scan_backward.1 = (bf16[1536,768]{1,0:T(8,128)(2,1)}, f32[8,640]{1,0:T(8,128)}, f32[8,128]{1,0:T(8,128)}, f32[192,1536]{1,0:T(8,128)}, bf16[384,1024]{1,0:T(8,128)(2,1)}, /*index=5*/bf16[128,1536]{1,0:T(8,128)(2,1)}) custom-call(s32[4]{0:T(128)} %bitcast.107, s32[1,1536]{1,0:T(1,128)} %refs_1_.7, bf16[1536,768]{1,0:T(8,128)(2,1)} %get-tuple-element.123.refs_2_, ...), custom_call_target="tpu_custom_call" | custom-call | bytes 144000000 | tf_op jit(solution)/shard_map/scan_backward/pallas_call | solution.py:679
  807.8 2.3 fusion.2
  811.4 28.2 %project_back.1 = (bf16[8,192,1536]{2,1,0:T(8,128)(2,1)}, bf16[1536,768]{1,0:T(8,128)(2,1)}, bf16[1536,384]{1,0:T(8,128)(2,1)}, bf16[8,64,1536]{2,1,0:T(8,128)(2,1)}, bf16[128,1536]{1,0:T(8,128)(2,1)}) custom-call(bf16[1536,384]{1,0:T(8,128)(2,1)} %get-tuple-element.162.refs_0_, bf16[1536,768]{1,0:T(8,128)(2,1)} %get-tuple-element.163.refs_1_, ...), custom_call_target="tpu_custom_call" | custom-call | bytes 90000000 | tf_op jit(solution)/shard_map/project_back/pallas_call | solution.py:679
  849.7 2.7 concatenate.54
  853.8 106.0 %settle.1 = (bf16[192,1536]{1,0:T(8,128)(2,1)}, bf16[8,384,768]{2,1,0:T(8,128)(2,1)}, bf16[8,128,1536]{2,1,0:T(8,128)(2,1)}, bf16[8,384,256]{2,1,0:T(8,128)(2,1)}, bf16[8,64,384]{2,1,0:T(8,128)(2,1)}) custom-call(bf16[1,8,192,1536]{3,2,1,0:T(8,128)(2,1)} %bitcast.79, bf16[4,8,64,384]{3,2,1,0:T(8,128)(2,1)} %fusion.1.refs_1_, bf16[192,1536]{1,0:T(8,128)(2,1)} %bitcast.77, ...), custom_call_target="tpu_custom_call" | custom-call | bytes 324000000 | tf_op jit(solution)/shard_map/settle/pallas_call | solution.py:679
  962.3 11.4 %assemble.1 = (f32[384,6400]{1,0:T(8,128)}, f32[384,2048]{1,0:T(8,128)}, f32[2,8,48,1536]{3,2,1,0:T(8,128)}, f32[2,8,16,1536]{3,2,1,0:T(8,128)}) custom-call(bf16[8,384,768]{2,1,0:T(8,128)(2,1)} %get-tuple-element.181.main_ref, bf16[8,384,256]{2,1,0:T(8,128)(2,1)} %get-tuple-element.182.shared_in_ref, bf16[8,64,384]{2,1,0:T(8,128)(2,1)} %get-tuple-element.180.small_ref, ...), custom_call_target="tpu_custom_call" | custom-call | bytes 36000000 | tf_op jit(solution)/shard_map/assemble/pallas_call | solution.py:2125
  979.7 10.7 %collect.1 = (f32[8,384,1024]{2,1,0:T(8,128)}, f32[8,128,1536]{2,1,0:T(8,128)}) custom-call(s32[1]{0:T(128)} %bitcast.38.place_ref, bf16[384,1024]{1,0:T(8,128)(2,1)} %get-tuple-element.188.refs_0_, bf16[128,1536]{1,0:T(8,128)(2,1)} %get-tuple-element.189.refs_1_, bf16[384,1024]{1,0:T(8,128)(2,1)} %get-tuple-element.190.refs_2_, ...), custom_call_target="tpu_custom_call" | custom-call | bytes 43200000 | tf_op jit(solution)/shard_map/collect/pallas_call | solution.py:2171
  (126 shorter events, 34.6 us)
Async XLA Ops:
  0.7 6.6 copy-start
  219.4 32.6 %copy-start.3 = (bf16[4,384,128]{2,1,0:T(8,128)(2,1)S(1)}, bf16[4,384,128]{2,1,0:T(8,128)(2,1)}, u32[]{:S(2)}) copy-start(bf16[4,384,128]{2,1,0:T(8,128)(2,1)} %get-tuple-element.115) | copy-start | bytes 1179652
  219.4 33.4 %copy-start.10 = (s32[1,192,6]{1,0,2:T(1,128)S(1)}, s32[1,192,6]{1,0,2:T(1,128)}, u32[]{:S(2)}) copy-start(s32[1,192,6]{1,0,2:T(1,128)} %param.25) | copy-start | bytes 13828
  705.8 102.0 %copy-start.2 = (f32[192,1536]{1,0:T(8,128)S(1)}, f32[192,1536]{1,0:T(8,128)}, u32[]{:S(2)}) copy-start(f32[192,1536]{1,0:T(8,128)} %get-tuple-element.122.after_ref) | copy-start | bytes 3538948
  807.7 2.4 copy-start.6
  807.7 2.4 copy-start.8
  811.4 28.2 %copy-start.11 = (f32[8,640]{1,0:T(8,128)S(1)}, f32[8,640]{1,0:T(8,128)}, u32[]{:S(2)}) copy-start(f32[8,640]{1,0:T(8,128)} %get-tuple-element.172) | copy-start | bytes 61444
  839.6 6.7 copy-start.4
  847.9 1.7 copy-start.5
  848.9 3.5 copy-start.9
  853.8 107.9 %copy-start.12 = (bf16[384]{0:T(512)(128)(2,1)S(1)}, bf16[384]{0:T(512)(128)(2,1)}, u32[]{:S(2)}) copy-start(bf16[384]{0:T(512)(128)(2,1)} %param.26) | copy-start | bytes 2308
  979.7 10.7 %copy-start.7 = (bf16[192,1536]{1,0:T(8,128)(2,1)S(1)}, bf16[192,1536]{1,0:T(8,128)(2,1)}, u32[]{:S(2)}) copy-start(bf16[192,1536]{1,0:T(8,128)(2,1)} %get-tuple-element.179) | copy-start | bytes 1769476
  979.7 11.5 %copy-start.1 = (bf16[384,48]{0,1:T(8,128)(2,1)S(1)}, bf16[384,48]{0,1:T(8,128)(2,1)}, u32[]{:S(2)}) copy-start(bf16[384,48]{0,1:T(8,128)(2,1)} %param.28) | copy-start | bytes 110596

commit v5 on v4

--- a/solution.py
+++ b/solution.py
@@ -510,12 +510,26 @@
     pl.semaphore_wait(barrier, len(flips) + inner - 1)
 
 
+def among(place, places):
+    if places is None:
+        return None
+    return functools.reduce(jnp.logical_or, [place == one for one in places])
+
+
+def do_if(condition, action):
+    if condition is None:
+        action()
+    else:
+        pl.when(condition)(action)
+
+
 class Parcel:
     flips = ()
     sems = 1
 
-    def __init__(self, array, shift, inner, index=None, output=None):
+    def __init__(self, array, shift, inner, index=None, output=None, senders=None):
         self.array, self.shift, self.inner, self.index = array, shift, inner, index
+        self.senders = senders
         self.shape = array.shape if index is None else array.shape[1:]
         self.output = output
 
@@ -526,6 +540,13 @@
             source = source.at[self.index(to)]
         return [(source, target, target, {"shard": first + to})]
 
+    def sends(self):
+        return among(own_shard_group(self.inner)[0], self.senders)
+
+    def comes(self):
+        place, _ = own_shard_group(self.inner)
+        return among(lax.rem(place + self.inner - self.shift, self.inner), self.senders)
+
     def stays(self, source, target):
         return []
 
@@ -539,6 +560,12 @@
 
     def __init__(self, array):
         self.array, self.shape = array, array.shape
+
+    def sends(self):
+        return None
+
+    def comes(self):
+        return None
 
     def moves(self, source, target):
         part = lax.axis_index("seq")
@@ -621,16 +648,28 @@
                 for source, target in item.stays(sources[place], targets[place]):
                     yield pltpu.make_async_copy(source, target, refs[3 * place + 2])
 
-        def depart(chosen=lambda item: True):
+        def depart(chosen=lambda item: True, gate=None):
             for item, place, order, (source, target, _, device) in moves(chosen):
-                remote(item, place, order, source, target, device).start()
+                allowed = item.sends()
+                if gate is not None:
+                    allowed = gate if allowed is None else allowed & gate
+                do_if(
+                    allowed,
+                    lambda: remote(item, place, order, source, target, device).start(),
+                )
             for copy in stays(chosen):
                 copy.start()
 
         def arrive(chosen=lambda item: True):
             for item, place, order, (source, target, arrival, device) in moves(chosen):
-                remote(item, place, order, source, arrival, device).wait_recv()
-                remote(item, place, order, source, target, device).wait_send()
+                do_if(
+                    item.comes(),
+                    lambda: remote(item, place, order, source, arrival, device).wait_recv(),
+                )
+                do_if(
+                    item.sends(),
+                    lambda: remote(item, place, order, source, target, device).wait_send(),
+                )
             for copy in stays(chosen):
                 copy.wait()
 
@@ -782,8 +821,8 @@
 
 
 class Reducer:
-    def __init__(self, inner, p_ref, total, refs):
-        self.inner, self.p_ref, self.total = inner, p_ref, total
+    def __init__(self, inner, p_ref, total, refs, make=None):
+        self.inner, self.p_ref, self.total, self.make = inner, p_ref, total, make
         self.held, self.paired, self.turned, self.crossed = refs[:4]
         self.load, self.core_send, self.core_recv = refs[4:7]
         self.turn_send, self.turn_recv, self.cross_send, self.cross_recv = refs[7:11]
@@ -814,7 +853,9 @@
 
     def to_core(self, order, slot):
         return pltpu.make_async_remote_copy(
-            src_ref=self.p_ref.at[
+            src_ref=self.p_ref.at[order, slot]
+            if self.make
+            else self.p_ref.at[
                 self.line.targets[order], flipped(self.part, self.EVENS[slot] + 1)
             ],
             dst_ref=self.paired.at[order, slot],
@@ -857,11 +898,21 @@
     def begin(self):
         for order in range(self.inner):
             for slot in range(4):
+                if self.make:
+                    target = self.line.targets[order]
+                    block = flipped(self.part, self.EVENS[slot] + 1)
+                    self.make(target, block, self.p_ref.at[order, slot])
                 self.to_core(order, slot).start()
-                self.loading(order, slot).start()
+                if not self.make:
+                    self.loading(order, slot).start()
+            if self.make:
+                for slot in range(4):
+                    block = flipped(self.part, self.EVENS[slot])
+                    self.make(self.line.targets[order], block, self.held.at[order, slot])
 
     def total_of(self, order, slot):
-        self.loading(order, slot).wait()
+        if not self.make:
+            self.loading(order, slot).wait()
         self.to_core(order, slot).wait_recv()
         return to_full(self.held[order, slot]) + to_full(self.paired[order, slot])
 
@@ -1026,10 +1077,10 @@
     return first, second, third, last
 
 
-def line_gather(inner, own, target, send, recv):
+def line_gather(inner, own, target, send, recv, split=2):
     place, first = own_shard_group(inner)
-    half = own.shape[0] // 2
-    spans = [pl.ds(0, half), pl.ds(half, half)]
+    half = own.shape[0] // split
+    spans = [pl.ds(span * half, half) for span in range(split)]
 
     def copy_of(way, step, span):
         block = place - step if way == 0 else place + step
@@ -1060,11 +1111,11 @@
                 copy_of(way, step, span).start()
 
     def begin():
-        for span in range(2):
+        for span in range(split):
             start(0, span)
 
     def onward(step):
-        for span in range(2):
+        for span in range(split):
             for way in range(2):
 
                 @pl.when(receives(way, step))
@@ -1085,7 +1136,7 @@
 
     def finish():
         for step in range(inner - 1):
-            for span in range(2):
+            for span in range(split):
                 for way in range(2):
 
                     @pl.when(sends(way, step))
@@ -1135,8 +1186,10 @@
     planes[0][1]()
     for order in range(1, inner):
         onward(order)
-        if order == inner - 1:
-            depart()
+        if order < inner - 1:
+            depart(lambda item: item.rank == order - 1)
+        else:
+            depart(lambda item: item.rank >= order - 1)
         planes[order][0]()
         planes[order - 1][2]()
         planes[order][1]()
@@ -1169,6 +1222,7 @@
 
 def begin_kernel(
     inner,
+    depart,
     x_ref,
     g_ref,
     s_ref,
@@ -1185,8 +1239,12 @@
     r_out,
     w_ref,
     r_ref,
+    b_ref,
+    b_line,
+    b_all,
     own_sems,
     pick_sems,
+    place_sems,
     *sems,
 ):
     part = lax.axis_index("seq")
@@ -1199,21 +1257,16 @@
         picks.append(pltpu.make_async_copy(source, target, pick_sems.at[len(picks)]))
 
     shared = shared_ref.shape[1] // seq_devices // 2
-    state = w_ref.shape[1] - 2 * shared
-    channels = (in_ref.shape[1] - state) // (2 * seq_devices - 2)
-    state -= 2 * channels
+    channels = w_ref.shape[1] // 2 - shared
+    share, state = b_ref.shape
     at = 0
     for source, extent in ((in_ref, channels), (shared_ref, shared)):
         for side in range(2):
             start = pl.multiple_of((side * seq_devices + part) * extent, extent)
             pick(source.at[:, pl.ds(start, extent)], w_ref.at[:, pl.ds(at, extent)])
             at += extent
-        if source is in_ref:
-            pick(
-                source.at[:, pl.ds(in_ref.shape[1] - state, state)],
-                w_ref.at[:, pl.ds(at, state)],
-            )
-            at += state
+    start = pl.multiple_of(part * share, share)
+    pick(in_ref.at[pl.ds(start, share), pl.ds(in_ref.shape[1] - state, state)], b_ref)
     halves = seq_devices // inner
     at = 0
     for half in range(halves):
@@ -1226,70 +1279,110 @@
         copy.start()
     targets = [
         lambda p: s_out.at[p],
-        lambda p: w_out.at[pl.ds(p * rows, rows)],
+        lambda p: w_out.at[pl.ds(p * rows, rows), pl.ds(0, w_ref.shape[1])],
         lambda p: r_out.at[p],
         lambda p: d_out.at[p],
+        lambda p: b_line.at[pl.ds(p * share, share)],
     ]
-    sources = [s_ref, w_ref, r_ref, d_ref]
+    sources = [s_ref, w_ref, r_ref, d_ref, b_ref]
     lines = [
-        line_gather(inner, source, target, sems[2 * order], sems[2 * order + 1])
+        line_gather(
+            inner, source, target, sems[2 * order], sems[2 * order + 1], 1 if order == 4 else 2
+        )
         for order, (source, target) in enumerate(zip(sources, targets))
     ]
-    line, planes = group_gather(inner, g_ref, lambda p, b: g_out.at[p, b], sems[8:12])
+    b_plane = plane_gather(b_line, lambda b: b_all.at[b], sems[16], sems[17])
+    line, planes = group_gather(inner, g_ref, lambda p, b: g_out.at[p, b], sems[10:14])
     lines.append(line)
-    x_plane = plane_gather(x_ref, lambda b: x_out.at[b], sems[12], sems[13])
+    x_plane = plane_gather(x_ref, lambda b: x_out.at[b], sems[14], sems[15])
     rows_line = lines.pop(2)
     lines[0][0]()
     lines[2][0]()
-    lines[3][0]()
+    lines[4][0]()
     x_plane[0]()
     planes[0][0]()
     for copy in picks:
         copy.wait()
+    lines[3][0]()
     lines[1][0]()
+    rows_line[0]()
+    at_end = (place == 0) | (place == inner - 1)
+    depart(gate=at_end)
     owns = [
         pltpu.make_async_copy(source, target(place), own_sems.at[order])
         for order, (source, target) in enumerate(zip(sources, targets))
     ]
-    owns.append(pltpu.make_async_copy(x_ref, x_out.at[part], own_sems.at[4]))
-    owns.append(pltpu.make_async_copy(g_ref, g_out.at[place, part], own_sems.at[5]))
+    owns.append(pltpu.make_async_copy(x_ref, x_out.at[part], own_sems.at[5]))
+    owns.append(pltpu.make_async_copy(g_ref, g_out.at[place, part], own_sems.at[6]))
     for copy in owns:
         copy.start()
     x_plane[1]()
     planes[0][1]()
     x_plane[2]()
     planes[0][2]()
+    *other_lines, g_line = lines
     for step in range(1, inner):
-        for _, onward, _ in reversed(lines):
-            onward(step)
-        if step == max(1, inner - 2):
-            rows_line[0]()
+        g_line[1](step)
         planes[step][0]()
         if step > 1:
             planes[step - 1][2]()
         planes[step][1]()
-    rows_line[1](1)
+        for _, onward, _ in reversed(other_lines):
+            onward(step)
+        if step == 1:
+            rows_line[1](1)
+            depart(gate=jnp.logical_not(at_end))
     planes[inner - 1][2]()
+    owns[4].wait()
+    b_plane[0]()
     for step in range(2, inner):
         rows_line[1](step)
+    b_plane[1]()
+    b_plane[2]()
     x_plane[3]()
     for stages in planes:
         stages[3]()
+    b_plane[3]()
+    own_b = pltpu.make_async_copy(b_line, b_all.at[part], own_sems.at[7])
+    own_b.start()
+    own_b.wait()
+    spread = []
+    for device in range(seq_devices):
+        for shard in range(inner):
+            spread.append(
+                pltpu.make_async_copy(
+                    b_all.at[device, pl.ds(shard * share, share)],
+                    w_out.at[
+                        pl.ds(shard * rows + device * share, share), pl.ds(w_ref.shape[1], state)
+                    ],
+                    place_sems.at[device, shard],
+                )
+            )
+    for copy in spread:
+        copy.start()
     for _, _, finish in lines + [rows_line]:
         finish()
-    for copy in owns:
+    for order, copy in enumerate(owns):
+        if order != 4:
+            copy.wait()
+    for copy in spread:
         copy.wait()
 
 
-def begin(x, grad, small, by_depth, w_in, w_shared, w_out, w_down, in_width, shared_part, inner):
+def begin(
+    x, grad, small, by_depth, w_in, w_shared, w_out, w_down, in_width, shared_part, inner, freight
+):
     seq_devices = lax.axis_size("seq")
     low = jnp.bfloat16
     depth, width = w_in.shape[0], w_out.shape[1]
     columns = in_width + 2 * shared_part
+    w_columns = 2 * w_out.shape[0] * inner // seq_devices + 2 * shared_part
     rows = (w_out.shape[0] + w_down.shape[0]) // seq_devices
     anywhere = pl.BlockSpec(memory_space=pl.ANY)
     sems = lambda *shape: pltpu.SemaphoreType.DMA(shape)
-    line_sems = [sems(2, inner - 1, 2)] * 8
+    line_sems = [sems(2, inner - 1, 2)] * 10
+    state = in_width + 2 * shared_part - w_columns
+    fine = depth // seq_devices
     return run(
         functools.partial(begin_kernel, inner),
         (x, grad, small, by_depth, w_in, w_shared, w_out, w_down),
@@ -1303,11 +1396,23 @@
             jax.ShapeDtypeStruct((inner,) + by_depth.shape, low),
             jax.ShapeDtypeStruct((inner, rows, width), low),
         ],
-        scratch=[pltpu.VMEM((depth, columns), low), pltpu.VMEM((rows, width), low)]
-        + [sems(6), sems(5 + 2 * (seq_devices // inner))]
-        + line_sems + group_sems(inner) + [sems(14), sems(14)],
+        scratch=[
+            pltpu.VMEM((depth, w_columns), low),
+            pltpu.VMEM((rows, width), low),
+            pltpu.VMEM((fine, state), low),
+            pltpu.VMEM((inner * fine, state), low),
+            pltpu.VMEM((seq_devices, inner * fine, state), low),
+            sems(8),
+            sems(5 + 2 * (seq_devices // inner)),
+            sems(seq_devices, inner),
+        ]
+        + line_sems
+        + group_sems(inner)
+        + [sems(14)] * 4,
+        freight=freight,
         flips=FLIPS,
         inner=inner,
+        late=True,
         micros=130,
         name="begin",
     )
@@ -1481,12 +1586,15 @@
     hidden = to_low(x * norm_scale(x) * gain_ref[...])
     hidden_ref[...] = hidden
     gate_width = gate_ref.shape[1]
-    used = gate_width + rows_ref.shape[1] - LANES
+    used = 2 * gate_width
+    state = rows_ref.shape[1] - LANES - gate_width
     projected = dot_full(hidden, w_ref[:, :used])
     gate_ref[...] = projected[:, :gate_width]
-    rest = used - gate_width
-    rows_ref[:, :rest] = to_low(projected[:, gate_width:])
-    rows_ref[:, rest:] = to_low(dot_full(hidden, dt_ref[...]))
+    rows_ref[:, :gate_width] = to_low(projected[:, gate_width:])
+    rows_ref[:, gate_width : gate_width + state] = to_low(
+        dot_full(hidden, w_ref[:, w_ref.shape[1] - state :])
+    )
+    rows_ref[:, gate_width + state :] = to_low(dot_full(hidden, dt_ref[...]))
 
 
 def project(x, gain, weights, dt_weights, gate_width, columns, freight=()):
@@ -1523,34 +1631,40 @@
     return to_low(result)
 
 
-def mix_out_kernel(y_ref, gate_ref, gain_ref, packed_ref, part_ref, w_ref):
+def mix_out_kernel(y_ref, gate_ref, gain_ref, packed_ref, out_ref, w_ref, sent, *scratch):
     width = w_ref.shape[1]
-
-    @pl.when(pl.program_id(0) == 0)
-    def _():
-        unpack_rows(packed_ref, w_ref, True)
-
-    gated = to_full(y_ref[...]) * jax.nn.silu(gate_ref[...])
-    part_ref[0, :, :width] = to_low(dot_full(to_low(gated * gain_ref[...]), w_ref[...]))
-    squares = jnp.sum(gated * gated, axis=1, keepdims=True)
-    part_ref[0, :, width:] = put_split([squares], y_ref.shape[0])
+    rows = out_ref.shape[0]
+    unpack_rows(packed_ref, w_ref, True)
+
+    def make(_, block, place):
+        at = pl.ds(pl.multiple_of(block * rows, rows), rows)
+        gated = to_full(y_ref[at, :]) * jax.nn.silu(gate_ref[at, :])
+        place[:, :width] = to_low(dot_full(to_low(gated * gain_ref[...]), w_ref[...]))
+        squares = jnp.sum(gated * gated, axis=1, keepdims=True)
+        place[:, width:] = put_split([squares], rows)
+
+    Reducer(1, sent, out_ref, scratch, make).whole(lambda number: None)
 
 
 def mix_out(y, gate, gain, weights, blocks, freight=()):
     rows, channels = y.shape
     width = weights.shape[2]
     tile = rows // blocks
-    block = pl.BlockSpec((tile, channels), lambda step: (step, 0))
+    inside = pl.BlockSpec(memory_space=pltpu.VMEM)
     return run(
         mix_out_kernel,
         (y, gate, gain, weights),
-        grid=(blocks,),
-        in_specs=[block, block, whole(gain.shape), whole(weights.shape)],
-        out_specs=[pl.BlockSpec((1, tile, width + LANES), lambda step: (step, 0, 0))],
-        out_shape=[jax.ShapeDtypeStruct((blocks, tile, width + LANES), jnp.bfloat16)],
-        scratch=[pltpu.VMEM((channels, width), jnp.bfloat16)],
+        in_specs=[inside] * 4,
+        out_specs=[inside],
+        out_shape=[jax.ShapeDtypeStruct((tile, width + LANES), jnp.float32)],
+        scratch=[
+            pltpu.VMEM((channels, width), jnp.bfloat16),
+            pltpu.VMEM((1, 4, tile, width + LANES), jnp.bfloat16),
+        ]
+        + Reducer.scratch(1, tile, width + LANES),
         freight=freight,
-        micros=9,
+        flips=FLIPS,
+        micros=35,
         name="mix_out",
     )
 
@@ -1639,19 +1753,24 @@
         total[...] = jnp.zeros_like(total)
 
     grads = jnp.concatenate([dgate_ref[...], drows_ref[...]], axis=1)
+    main = 2 * dgate_ref.shape[1]
     columns = grads.shape[1] - LANES
+    state_at = w_ref.shape[1] - (columns - main)
     part_ref[0] = to_low(
-        dot_lanes(grads[:, :columns], w_ref[:, :columns])
+        dot_lanes(grads[:, :main], w_ref[:, :main])
+        + dot_lanes(grads[:, main:columns], w_ref[:, state_at:])
         + dot_lanes(grads[:, columns:], dt_ref[...])
     )
     total[...] += dot_rows(hidden_ref[...], grads)
 
     @pl.when(step == pl.num_programs(0) - 1)
     def _():
-        main = main_grad_ref.shape[1]
         main_grad_ref[...] = to_low(total[:, :main])
         rest_grad_ref[...] = to_low(total[:, main:])
-        by_gain = jnp.sum(total[:, :columns] * to_full(w_ref[:, :columns]), axis=1, keepdims=True)
+        by_gain = jnp.sum(total[:, :main] * to_full(w_ref[:, :main]), axis=1, keepdims=True)
+        by_gain += jnp.sum(
+            total[:, main:columns] * to_full(w_ref[:, state_at:]), axis=1, keepdims=True
+        )
         by_gain += jnp.sum(total[:, columns:] * to_full(dt_ref[...]), axis=1, keepdims=True)
         rest = rest_grad_ref.shape[1]
         lane = iota_of((rest_grad_ref.shape[0], LANES), 1)
@@ -1748,7 +1867,7 @@
         down_grad_ref[...] = to_low(down_sum[...])
 
 
-def shared_expert(rows, grad, up, down, hidden, blocks, inner, freight=()):
+def shared_expert(rows, grad, up, up_at, down, hidden, blocks, inner, freight=()):
     _, tile, wide = rows.shape
     width = down.shape[2]
     down_shape = (hidden, width)
@@ -1765,7 +1884,7 @@
         in_specs=[
             own(wide),
             own(width),
-            pl.BlockSpec((width, up_shape[1]), lambda step: (0, up.shape[1] // up_shape[1] - 1)),
+            pl.BlockSpec((width, up_shape[1]), lambda step: (0, up_at // up_shape[1])),
             whole(down.shape),
         ],
         out_specs=[block, block, whole(up_shape), whole(down_shape)],
@@ -1848,20 +1967,16 @@
 
 
 def experts_kernel(
-    depart, arrive, targets, *refs, count, per_device, top_count, own_first, inner, incoming, outgoing
+    depart, arrive, targets, *refs, count, per_device, top_count, own_first, inner, doubles, outgoing
 ):
     x_ref, g_ref = refs[:2]
     total = 2 * count * per_device
-    given = total - len(incoming)
-    pieces, refs = list(refs[2 : 2 + given]), refs[2 + given :]
-    for order, key in enumerate(incoming):
-        pieces.insert(key, targets[order])
+    pieces, refs = refs[2 : 2 + total], refs[2 + total :]
+    seconds, refs = dict(zip(doubles, refs[: len(doubles)])), refs[len(doubles) :]
     res_ref, dx_ref = refs[:2]
     outs = refs[2 : 2 + total]
     up_held, down_held, up_sum, down_sum, up_low, down_low, sems = refs[2 + total :]
     own_place, _ = own_shard_group(inner)
-    is_incoming = lambda item: item.output is None
-    is_outgoing = lambda item: item.output is not None
     expert, step = pl.program_id(0), pl.program_id(1)
     steps = pl.num_programs(1)
     slot = lax.rem(expert, 2)
@@ -1869,44 +1984,49 @@
     hidden = double // 2
     tile = x_ref.shape[1]
 
-    def parts(refs_of, which, up, down):
+    def parts(which, up, down):
         result = []
         for shift in range(count):
             from_place = lax.rem(own_place + count - shift, count)
             for kind, held in enumerate((up, down)):
                 extent = held.shape[0] // count
                 start = pl.multiple_of(from_place * extent, extent)
-                piece = refs_of[(shift * per_device + which) * 2 + kind]
-                if len(piece.shape) == 3:
-                    piece = piece.at[own_place * per_device + which]
-                result.append((piece, held.at[pl.ds(start, extent)], (shift, kind)))
+                number = (shift * per_device + which) * 2 + kind
+                result.append((number, held.at[pl.ds(start, extent)], (shift, kind)))
         return result
 
-    def fetch(which):
+    def fetch(which, action):
         half = which % 2
-        return [
-            pltpu.make_async_copy(piece, held, sems.at[half, at[0], at[1]])
-            for piece, held, at in parts(pieces, which, up_held.at[half], down_held.at[half])
-        ]
+        for number, held, at in parts(which, up_held.at[half], down_held.at[half]):
+            sem = sems.at[half, at[0], at[1]]
+            piece = pieces[number]
+            if len(piece.shape) == 3:
+                piece = piece.at[own_place * per_device + which]
+            if number in seconds:
+                early = among(own_place, doubles[number])
+                pl.when(early)(
+                    lambda: action(pltpu.make_async_copy(piece, held, sem))
+                )
+                pl.when(jnp.logical_not(early))(
+                    lambda: action(pltpu.make_async_copy(seconds[number], held, sem))
+                )
+            else:
+                action(pltpu.make_async_copy(piece, held, sem))
+
+    begin_copy = lambda copy: copy.start()
+    end_copy = lambda copy: copy.wait()
 
     for which in range(per_device):
 
         @pl.when((step == 0) & (expert == which))
         def _():
             if which == 0:
-                for copy in fetch(0):
-                    copy.start()
-                depart(is_incoming)
+                fetch(0, begin_copy)
             if which == 1:
-                arrive(is_incoming)
-                depart(is_outgoing)
-                for copy in fetch(1):
-                    copy.start()
-            for copy in fetch(which):
-                copy.wait()
-            if 1 <= which < per_device - 1:
-                for copy in fetch(which + 1):
-                    copy.start()
+                depart()
+            fetch(which, end_copy)
+            if which + 1 < per_device:
+                fetch(which + 1, begin_copy)
 
     @pl.when(step == 0)
     def _():
@@ -1958,8 +2078,8 @@
             up_low[...] = to_low(up_sum[...])
             down_low[...] = to_low(down_sum[...])
             copies = [
-                pltpu.make_async_copy(held, piece, sems.at[2, at[0], at[1]])
-                for piece, held, at in parts(outs, which, up_low, down_low)
+                pltpu.make_async_copy(held, outs[number], sems.at[2, at[0], at[1]])
+                for number, held, at in parts(which, up_low, down_low)
             ]
             for copy in copies:
                 copy.start()
@@ -1970,22 +2090,17 @@
 
         @pl.when((step == steps - 1) & (expert == per_device - 1))
         def _():
-            arrive(is_outgoing)
-
-
-def experts(x, g, pieces, hidden, top_count, own_first, inner, incoming=(), outgoing=()):
+            arrive()
+
+
+def experts(x, g, pieces, hidden, top_count, own_first, inner, doubles=(), outgoing=()):
     per_device, rows, wide = x.shape
     width = g.shape[2]
-    count = (len(pieces) + len(incoming)) // per_device // 2
-    incoming = sorted(incoming, key=lambda entry: entry[0])
-    full_list = list(pieces)
-    for key, item in incoming:
-        full_list.insert(key, jax.ShapeDtypeStruct(item.shape, item.array.dtype))
+    count = len(pieces) // per_device // 2
     low = jnp.bfloat16
-    shapes = [jax.ShapeDtypeStruct(piece.shape[-2:], low) for piece in full_list]
-    freight = [item for _, item in incoming] + [
-        Parcel(shapes[key], shift, inner, output=2 + key) for key, shift in outgoing
-    ]
+    shapes = [jax.ShapeDtypeStruct(piece.shape[-2:], low) for piece in pieces]
+    freight = [Parcel(shapes[key], shift, inner, output=2 + key) for key, shift in outgoing]
+    others = [other for _, other, _ in doubles]
     double = 2 * hidden
     tile = min(rows, 256)
     block = lambda extent: pl.BlockSpec((1, tile, extent), lambda e, step: (e, step, 0))
@@ -1999,12 +2114,12 @@
             top_count=top_count,
             own_first=own_first,
             inner=inner,
-            incoming=[key for key, _ in incoming],
+            doubles={number: places for number, _, places in doubles},
             outgoing=outgoing,
         ),
-        (x, g) + tuple(pieces),
+        (x, g) + tuple(pieces) + tuple(others),
         grid=(per_device, rows // tile),
-        in_specs=[block(wide), block(width)] + [anywhere] * len(pieces),
+        in_specs=[block(wide), block(width)] + [anywhere] * (len(pieces) + len(others)),
         out_specs=[block(width), block(wide)] + [anywhere] * len(shapes),
         out_shape=[
             jax.ShapeDtypeStruct((per_device, rows, width), low),
@@ -2026,7 +2141,7 @@
         micros=45,
         name="experts",
     )
-    sent = outs.pop()[len(incoming) :] if freight else []
+    sent = outs.pop() if freight else []
     return outs[0], outs[1], outs[2:], sent
 
 
@@ -2329,17 +2444,86 @@
     )(*arrays)
 
 
-def split_small(joined, arrays):
-    results, start = [], 0
-    for piece in arrays:
-        part = joined[:, start : start + piece.size]
-        results.append(part.reshape((-1,) + piece.shape[1:]))
-        start += piece.size
-    return results
-
-
-def flat_of(arrays):
-    return jnp.concatenate([piece.reshape(-1) for piece in arrays])
+ROWS_AFTER = 16
+
+
+def pack_kernel(
+    rest_ref, router_ref, conv_ref, head_ref, gate_ref, moe_ref, out_ref, wide, *, inner_width, experts, heads
+):
+    part = lax.axis_index("seq")
+    inner, seq_devices, block_rows, columns = out_ref.shape
+    depth = block_rows - ROWS_AFTER
+    state = columns - LANES
+    lane = iota_of((rest_ref.shape[0], LANES), 1)
+    last = to_full(rest_ref[:, state:])
+    steps = jnp.where(lane < heads, last, 0.0)
+    extra = to_full(router_ref[...]) + pltpu.roll(steps, experts + heads * part, 1)
+    extra = to_low(jnp.where(lane == LANES - 1, last, extra))
+    for shard in range(inner):
+        for device in range(seq_devices):
+            start = (shard * seq_devices + device) * depth
+            out_ref[shard, device, :depth, :state] = rest_ref[start : start + depth, :state]
+            out_ref[shard, device, :depth, state:] = extra[start : start + depth]
+    channels = gate_ref.shape[1]
+    others = conv_ref.shape[1] - channels
+    wide[...] = jnp.zeros_like(wide)
+    own = pl.ds(pl.multiple_of(part * channels, channels), channels)
+    wide[:8, own] = conv_ref[:, :channels]
+    wide[:8, inner_width : inner_width + others] = conv_ref[:, channels:]
+    wide[8:, own] = gate_ref[...]
+    convs = wide[:8, :]
+    gates = wide[8:, :]
+    per_conv = (inner_width + others) // inner
+    per_gate = inner_width // inner
+    width = moe_ref.shape[1] // inner
+    row = iota_of((ROWS_AFTER, columns), 0)
+    blank = jnp.zeros((1, columns), jnp.float32)
+    head_lane = iota_of((8, LANES), 1)
+    values = jnp.where(head_lane < heads, head_ref[...], 0.0)
+    values = [
+        jnp.concatenate([pltpu.roll(values, heads * part, 1)[k : k + 1], blank[:, LANES:]], axis=1)
+        for k in range(3)
+    ]
+    moe = moe_ref[...]
+
+    def pieces(rows, at, start, extent):
+        count = -(-extent // columns)
+        return [rows[at : at + 1, start + k * columns : start + (k + 1) * columns] for k in range(count)]
+
+    for shard in range(inner):
+        for device in range(seq_devices):
+            if device < 5:
+                lines = pieces(convs, device, shard * per_conv, per_conv)
+            elif device == 5:
+                lines = pieces(gates, 0, shard * per_gate, per_gate)
+            elif device == 6:
+                lines = values
+            else:
+                lines = [moe[:1, shard * width : (shard + 1) * width]]
+                lines = [jnp.concatenate([lines[0], blank[:, width:]], axis=1) if width < columns else lines[0]]
+            tile = jnp.zeros((ROWS_AFTER, columns), jnp.float32)
+            for k, line in enumerate(lines):
+                tile = jnp.where(row == k, line, tile)
+            out_ref[shard, device, depth:] = to_low(tile)
+
+
+def pack(rest, router, conv, head, gate, moe, inner, seq_devices, inner_width, experts, heads):
+    depth = rest.shape[0] // inner // seq_devices
+    columns = rest.shape[1]
+    arrays = (rest, router, conv, head, gate, moe)
+    reach = inner_width + conv.shape[1] - gate.shape[1] + columns
+    return pl.pallas_call(
+        functools.partial(pack_kernel, inner_width=inner_width, experts=experts, heads=heads),
+        in_specs=[whole(array.shape) for array in arrays],
+        out_specs=whole((inner, seq_devices, depth + ROWS_AFTER, columns)),
+        out_shape=jax.ShapeDtypeStruct(
+            (inner, seq_devices, depth + ROWS_AFTER, columns), jnp.bfloat16
+        ),
+        scratch_shapes=[pltpu.VMEM((16, -(-reach // LANES) * LANES), jnp.float32)],
+        compiler_params=params_of(),
+        cost_estimate=cost_of(3),
+        name="pack",
+    )(*arrays)
 
 
 def rows_to_send(weights, part):
@@ -2402,21 +2586,6 @@
 def outer_groups(inner):
     count = lax.axis_size("shard")
     return [list(range(start, count, inner)) for start in range(inner)]
-
-
-def carry(array, freight):
-    result, arrays = run(
-        lambda source, target: None,
-        (array,),
-        in_specs=[pl.BlockSpec(memory_space=pl.ANY)],
-        out_specs=[pl.BlockSpec(memory_space=pl.ANY)],
-        out_shape=[jax.ShapeDtypeStruct((8, LANES), jnp.float32)],
-        freight=freight,
-        micros=30,
-        name="carry",
-    )
-    del result
-    return array, arrays
 
 
 def stacked_pieces(received, place, inner):
@@ -2490,7 +2659,10 @@
     def own_rows(array, extent):
         return lax.dynamic_slice_in_dim(array, part * extent, extent, 0)
 
-    small_weights = [norm_in, conv_w, conv_b, dt_bias, a_log, d_skip, norm_gate, norm_moe]
+    row_wide = -(-max(conv_w.shape[0], norm_gate.shape[0]) // LANES) * LANES
+    row_of = lambda piece: jnp.pad(piece, ((0, 0), (0, row_wide - piece.shape[1])))
+    vectors = [conv_b, norm_gate, norm_in, norm_moe, dt_bias, a_log, d_skip]
+    flat = jnp.concatenate([row_of(conv_w.T)] + [row_of(vector[None]) for vector in vectors])
     by_depth = jnp.concatenate(
         [
             w_router,
@@ -2499,12 +2671,53 @@
         ],
         axis=1,
     )
+    weights_of = (w_experts, w_experts_down)
+
+    def own_first():
+        here, _ = own_shard_group(inner)
+        return lax.axis_index("seq") * local_experts + here * per_device
+
+    pieces = {
+        (0, expert, kind): weights_of[kind] for expert in range(per_device) for kind in range(2)
+    }
+
+    last = inner - 1
+    early_from = {1: range(inner // 2), last: range(inner - inner // 2, inner)} if outer == 1 else {}
+    early = {}
+
+    def parcels(*keys, first=False):
+        result = []
+        for shift, expert, kind in keys:
+            senders = None
+            if shift in early_from:
+                senders = [
+                    place for place in range(inner) if (place in early_from[shift]) == first
+                ]
+            result.append(
+                Parcel(
+                    weights_of[kind],
+                    shift,
+                    inner,
+                    lambda to, expert=expert: to * per_device + expert,
+                    senders=senders,
+                )
+            )
+        return result
+
+    def unpack(keys, arrays):
+        pieces.update(zip(keys, arrays))
+
+
     in_width = 2 * channels + w_in.shape[1] - 2 * inner_width
-    flat = flat_of(small_weights)
     if outer == 1:
-        flat_rows = -(-flat.size // (LANES * 32)) * 32
-        flat = jnp.pad(flat, (0, flat_rows * LANES - flat.size)).reshape(flat_rows, LANES)
-        x_group, grad_all, proj_in, joined, depth_joined, rows_joined = begin(
+        flat = jnp.pad(flat, ((0, -flat.shape[0] % 32), (0, 0)))
+        early_keys = [
+            (shift, expert, kind)
+            for expert in range(per_device)
+            for kind in range(2)
+            for shift in early_from
+        ]
+        x_group, grad_all, proj_in, joined, depth_joined, rows_joined, arrays = begin(
             tokens[0],
             out_grad[0],
             flat,
@@ -2516,8 +2729,9 @@
             in_width,
             shared_part,
             inner,
-        )
-        joined = joined.reshape(inner, -1)
+            parcels(*early_keys, first=True),
+        )
+        early.update(zip(early_keys, arrays))
         x_group = x_group.reshape(group_rows, width)
     else:
         x_group = gather_rows(tokens[0], 1)[0].reshape(group_rows, width)
@@ -2526,9 +2740,9 @@
             [
                 own_columns(w_in, 0, channels),
                 own_columns(w_in, inner_width, channels),
-                w_in[:, 2 * inner_width :],
                 own_columns(w_shared, 0, shared_part),
                 own_columns(w_shared, shared_width, shared_part),
+                w_in[:, 2 * inner_width :],
             ],
             axis=1,
         )
@@ -2536,60 +2750,28 @@
         joined = lax.all_gather(flat, "shard")
         depth_joined = lax.all_gather(by_depth, "shard")
         rows_joined = lax.all_gather(rows_to_send([w_out, w_shared_down], part), "shard")
-    (
-        gain_in,
-        conv_weight,
-        conv_bias,
-        step_bias,
-        decay_log,
-        skip_gain,
-        gain_gate,
-        gain_moe,
-    ) = split_small(joined, small_weights)
+    taps = conv_w.shape[1]
+    conv_rows = joined[:, :taps, : conv_w.shape[0]].transpose(1, 0, 2).reshape(taps, -1)
+    conv_bias, gain_gate, gain_in, gain_moe, step_bias, decay_log, skip_gain = (
+        joined[:, taps + order, : vector.shape[0]].reshape(-1)
+        for order, vector in enumerate(vectors)
+    )
     depth_joined = depth_joined.reshape(width, LANES)
     lane = jnp.arange(LANES)[None]
     router_wide = jnp.where(lane < expert_total, depth_joined, 0)
     dt_columns = jnp.where(lane < heads, jnp.roll(depth_joined, -expert_total, axis=1), 0)
     grad_all = grad_all.reshape(blocks, tok_rows, width)
 
-    weights_of = (w_experts, w_experts_down)
-
-    def own_first():
-        here, _ = own_shard_group(inner)
-        return lax.axis_index("seq") * local_experts + here * per_device
-
-    pieces = {
-        (0, expert, kind): weights_of[kind] for expert in range(per_device) for kind in range(2)
-    }
-
-    def parcels(*keys):
-        return [
-            Parcel(
-                weights_of[kind],
-                shift,
-                inner,
-                lambda to, expert=expert: to * per_device + expert,
-            )
-            for shift, expert, kind in keys
-        ]
-
-    def unpack(keys, arrays):
-        pieces.update(zip(keys, arrays))
-
-    last = inner - 1
-
     gain_row = to_full(gain_in)[None]
-    keys = [(1, 0, DOWN)]
-    hidden_in, gate_in, rows_in, arrays = project(
-        x_group, gain_row, proj_in, dt_columns, channels, in_width, parcels(*keys)
-    )
-    unpack(keys, arrays)
-    conv_part = jnp.concatenate(
-        [own_rows(conv_weight, channels), conv_weight[inner_width:]], axis=0
-    )
-    bias_part = jnp.concatenate([own_rows(conv_bias, channels), conv_bias[inner_width:]], axis=0)
+    hidden_in, gate_in, rows_in = project(
+        x_group, gain_row, proj_in, dt_columns, channels, in_width
+    )
+    conv_all = jnp.concatenate([conv_rows, conv_bias[None]], axis=0)
     conv_table = to_full(
-        jnp.pad(jnp.concatenate([conv_part.T, bias_part[None]], axis=0), ((0, 3), (0, 0)))
+        jnp.pad(
+            jnp.concatenate([own_columns(conv_all, 0, channels), conv_all[:, inner_width:]], axis=1),
+            ((0, 3), (0, 0)),
+        )
     )
     head_table = jnp.pad(
         jnp.stack(
@@ -2601,7 +2783,7 @@
         ),
         ((0, 5), (0, LANES - heads)),
     )
-    keys = [(1, 0, UP), (last, 0, DOWN)]
+    keys = [(2, 0, DOWN), (1, 0, DOWN), (last, 0, DOWN)]
     y, seq_rows, states, (taken, *arrays) = scan_forward(
         lengths[0],
         deal_order,
@@ -2623,9 +2805,10 @@
         )
     own_weights = taken
     gate_gain = to_full(own_rows(gain_gate, channels))[None]
-    (mix_part,) = mix_out(y, gate_in, gate_gain, own_weights, seq_devices)
-    keys = [(last, 0, UP), (last, 1, DOWN)]
-    mixed, arrays = reduce_rows(mix_part[None], parcels(*keys))
+    keys = [(2, 1, DOWN), (1, 1, DOWN), (last, 1, DOWN)]
+    mixed, arrays = mix_out(
+        y, gate_in, gate_gain, own_weights, seq_devices, parcels(*keys)
+    )
     unpack(keys, arrays)
 
     moe_row = to_full(gain_moe)[None]
@@ -2633,29 +2816,27 @@
     after_mix, moe_wide, gates = token_forward(
         mixed, tokens[0], moe_row, router_wide, route_ids, inner_width, top_count
     )
-    keys = [(2, 0, UP), (2, 0, DOWN), (last, 1, UP)]
+    keys = [(2, 0, UP), (1, 0, UP), (last, 0, UP)]
     moe_all, arrays = gather_rows(moe_wide, inner, parcels(*keys))
     unpack(keys, arrays)
     moe_all = moe_all.reshape(blocks, tok_rows, width + LANES)
     capacity = min(tok_rows, max(2, tok_rows * top_count * 5 // (expert_total * 3)))
     slots = -(-capacity // 16) * 16
-    keys = [(2, 1, UP)]
+    keys = [(2, 1, UP), (1, 1, UP), (last, 1, UP)]
     expert_rows, grad_rows, picks, arrays = dispatch(
         moe_all, grad_all, per_device, top_count, slots, own_first, parcels(*keys)
     )
     unpack(keys, arrays)
-    keys = [(2, 1, DOWN)]
-    shared_res, shared_back, shared_up_grad, shared_down_grad, arrays = shared_expert(
+    shared_res, shared_back, shared_up_grad, shared_down_grad = shared_expert(
         moe_all,
         grad_all,
         proj_in,
+        2 * channels,
         own_weights,
         shared_part,
         seq_devices,
         inner,
-        parcels(*keys),
-    )
-    unpack(keys, arrays)
+    )
     order = [
         (shift, expert, kind)
         for shift in range(inner)
@@ -2663,17 +2844,24 @@
         for kind in range(2)
     ]
     if outer == 1:
-        late_keys = [(1, 1, UP), (1, 1, DOWN)]
         early_keys = [(1, 0, UP), (last, 0, DOWN)]
         expert_res, expert_back, grads, sent = experts(
             expert_rows,
             grad_rows,
-            [pieces[key] for key in order if key not in late_keys],
+            [early.get(key, pieces[key]) for key in order],
             hidden,
             top_count,
             own_first,
             inner,
-            [(order.index(key), parcels(key)[0]) for key in late_keys],
+            [
+                (
+                    order.index(key),
+                    pieces[key],
+                    [(place_of + key[0]) % inner for place_of in early_from[key[0]]],
+                )
+                for key in order
+                if key in early
+            ],
             [(order.index(key), inner - key[0]) for key in early_keys],
         )
     else:
@@ -2682,9 +2870,6 @@
                 pieces[0, expert, kind] = lax.dynamic_index_in_dim(
                     weights_of[kind], place * per_device + expert, 0, keepdims=False
                 )
-        keys = [(1, 1, UP), (1, 1, DOWN)]
-        moe_all, arrays = carry(moe_all, parcels(*keys))
-        unpack(keys, arrays)
         early_keys, sent = [], []
         held = [
             stacked_pieces([pieces[shift, expert, kind] for shift in range(inner)], place, inner)
@@ -2715,7 +2900,7 @@
         picks, expert_res, expert_back, shared_res, shared_back, inner, back_parcels(*keys)
     )
     unpack_back(keys, arrays)
-    keys = [(last, 1, UP), (2, 0, DOWN), (1, 1, UP)]
+    keys = [(last, 1, UP), (2, 1, DOWN), (1, 1, UP)]
     back, arrays = reduce_rows(
         back_part.reshape(inner, seq_devices, tok_rows, -1), back_parcels(*keys)
     )
@@ -2734,15 +2919,14 @@
         top_count,
     )
 
-    keys = [(2, 0, UP)]
+    keys = [(2, 0, DOWN), (last, 1, DOWN)]
     mix_group, arrays = gather_rows(mix_wide, 1, back_parcels(*keys))
     unpack_back(keys, arrays)
-    keys = [(last, 1, DOWN)]
-    dy, gate_in_grad, proj_out_grad, gain_gate_grad, arrays = mix_back(
-        mix_group[0], y, gate_in, gate_gain, own_weights, back_parcels(*keys)
-    )
-    unpack_back(keys, arrays)
-    keys = [(2, 1, UP), (1, 1, DOWN)]
+    keys = []
+    dy, gate_in_grad, proj_out_grad, gain_gate_grad = mix_back(
+        mix_group[0], y, gate_in, gate_gain, own_weights
+    )
+    keys = [(2, 1, UP), (2, 0, UP)]
     rows_grad, conv_grad, head_grad, out_sum, arrays = scan_backward(
         lengths[0],
         deal_order,
@@ -2756,7 +2940,7 @@
     )
     unpack_back(keys, arrays)
     layer_out = to_low(after_mix + out_sum)
-    keys = [(2, 1, DOWN)]
+    keys = [(1, 1, DOWN)]
     swap = [PlaneSwap(rows_from_owner([proj_out_grad, shared_down_grad]))]
     hidden_part, main_grad, rest_grad, (taken, *arrays) = project_back(
         gate_in_grad, rows_grad, hidden_in, proj_in, dt_columns, seq_devices, swap + back_parcels(*keys)
@@ -2772,45 +2956,23 @@
         )
 
     state_columns = rest_grad.shape[1] - LANES
-    conv_rows_grad = conv_grad[:5].T
-    conv_full = jnp.concatenate(
-        [spread(conv_rows_grad[:channels], inner_width), conv_rows_grad[channels:]], axis=0
-    )
-    by_depth = [
-        rest_grad[:, :state_columns],
-        router_grad[:, :expert_total],
-        spread(rest_grad[:, state_columns : state_columns + heads], head_total, 1),
-        rest_grad[:, -1:],
-        to_low(gain_moe_grad[0])[:, None],
-    ]
-    by_shard = [
-        conv_full[:, :4],
-        conv_full[:, 4],
-        spread(head_grad[0, :heads], head_total),
-        spread(head_grad[1, :heads], head_total),
-        spread(head_grad[2, :heads], head_total),
-        spread(gain_gate_grad[0], inner_width),
-    ]
-    shapes = [(piece.shape[0] // shard_devices,) + piece.shape[1:] for piece in by_shard]
-    by_shard = jnp.concatenate(
-        [to_low(piece).reshape(shard_devices, -1) for piece in by_shard], axis=1
-    )
-    extents = [piece.shape[1] for piece in by_depth]
-    used = sum(extents)
     if outer == 1:
-        wide = -(-used // LANES) * LANES
-        by_depth.append(jnp.zeros((width, wide - used), jnp.bfloat16))
-        by_depth = jnp.concatenate(by_depth, axis=1).reshape(inner, seq_devices, -1, wide)
-        depth_each = by_depth.shape[2]
-        size = by_shard.shape[1]
-        each = -(-size // (seq_devices * wide))
-        padded = -(-each // 16) * 16
-        by_shard = jnp.pad(by_shard, ((0, 0), (0, each * seq_devices * wide - size)))
-        by_shard = by_shard.reshape(inner, seq_devices, each, wide)
-        by_shard = jnp.pad(by_shard, ((0, 0), (0, 0), (0, padded - each), (0, 0)))
+        small = pack(
+            rest_grad,
+            router_grad,
+            conv_grad,
+            head_grad,
+            gain_gate_grad,
+            gain_moe_grad,
+            inner,
+            seq_devices,
+            inner_width,
+            expert_total,
+            heads,
+        )
         tokens_grad, main_all, rows_all, shared_all, small_all = settle(
             hidden_part[None],
-            jnp.concatenate([by_depth, by_shard], axis=2),
+            small,
             tokens[0],
             mix_grad,
             gain_row,
@@ -2832,9 +2994,43 @@
             w_shared_down.shape[0],
             max(1, seq_devices // shard_devices),
         )
-        depth_sum = to_full(small_all[:, :depth_each].reshape(depth_rows, wide))
-        shard_sum = small_all[:, depth_each : depth_each + each].reshape(-1)
+        depth_each = small_all.shape[1] - ROWS_AFTER
+        depth_sum = to_full(small_all[:, :depth_each].reshape(depth_rows, -1))
+        after = to_full(small_all[:, depth_each:])
+        conv_w_grad = after[:4].reshape(4, -1)[:, : conv_w.shape[0]].T
+        conv_b_grad = after[4].reshape(-1)[: conv_b.shape[0]]
+        norm_gate_grad = after[5].reshape(-1)[: norm_gate.shape[0]]
+        here = shard * dt_bias.shape[0]
+        of_heads = lax.dynamic_slice_in_dim(after[6, :3], here, dt_bias.shape[0], 1)
+        dt_bias_grad, a_log_grad, d_skip_grad = of_heads[0], of_heads[1], of_heads[2]
+        norm_moe_grad = after[7, 0, :depth_rows]
+        last_lane = rest_grad.shape[1] - 1
     else:
+        conv_rows_grad = conv_grad[:5].T
+        conv_full = jnp.concatenate(
+            [spread(conv_rows_grad[:channels], inner_width), conv_rows_grad[channels:]], axis=0
+        )
+        by_depth = [
+            rest_grad[:, :state_columns],
+            router_grad[:, :expert_total],
+            spread(rest_grad[:, state_columns : state_columns + heads], head_total, 1),
+            rest_grad[:, -1:],
+            to_low(gain_moe_grad[0])[:, None],
+        ]
+        by_shard = [
+            conv_full[:, :4],
+            conv_full[:, 4],
+            spread(head_grad[0, :heads], head_total),
+            spread(head_grad[1, :heads], head_total),
+            spread(head_grad[2, :heads], head_total),
+            spread(gain_gate_grad[0], inner_width),
+        ]
+        shapes = [(piece.shape[0] // shard_devices,) + piece.shape[1:] for piece in by_shard]
+        by_shard = jnp.concatenate(
+            [to_low(piece).reshape(shard_devices, -1) for piece in by_shard], axis=1
+        )
+        extents = [piece.shape[1] for piece in by_depth]
+        used = sum(extents)
         hidden_grad = reduce_rows(hidden_part[None])[0]
         residual = to_full(tokens[0])
         own_scale = norm_scale(residual)
@@ -2867,21 +3063,21 @@
         w_out_grad, w_shared_down_grad = rows_of_shard(
             from_line(taken, rows_each), [w_out, w_shared_down]
         )
-    results, start = [], 0
-    for shape in shapes:
-        size = 1
-        for extent in shape:
-            size *= extent
-        results.append(to_full(shard_sum[start : start + size]).reshape(shape))
-        start += size
-    conv_w_grad, conv_b_grad, dt_bias_grad, a_log_grad, d_skip_grad, norm_gate_grad = results
+        results, start = [], 0
+        for shape in shapes:
+            size = 1
+            for extent in shape:
+                size *= extent
+            results.append(to_full(shard_sum[start : start + size]).reshape(shape))
+            start += size
+        conv_w_grad, conv_b_grad, dt_bias_grad, a_log_grad, d_skip_grad, norm_gate_grad = results
+        norm_moe_grad = depth_sum[:, used - 1]
+        last_lane = used - 2
     start = state_columns
     w_router_grad = depth_sum[:, start : start + expert_total]
     start += expert_total
     w_dt_grad = depth_sum[:, start : start + head_total]
-    start += head_total
-    norm_in_grad = depth_sum[:, start] / to_full(norm_in)
-    norm_moe_grad = depth_sum[:, start + 1]
+    norm_in_grad = depth_sum[:, last_lane] / to_full(norm_in)
     return (
         layer_out[None],
         tokens_grad[None],

time: 996 us -> 966 us (0.970)
  Pallas kernels: 944 us -> 921 us
    pallas_call x16 -> x15, Pallas kernels: 912 us -> 886 us  [run(): pl.pallas_call(wrapped, grid=grid, in_specs=list(in_specs) + [anywhere] *...]
where the time goes in v5:
time: 966 us; the launch traced here: 958 us
  Pallas kernels  921 us (95%)
  local copies, waits for them, and re-layouts  26.6 us (3%)
    pallas_call x15, Pallas kernels, run(): pl.pallas_call(wrapped, grid=grid, in_specs=list(in_specs) + [anywhere] *...  886 us

profile of v5, /device:TPU:0, one launch (start us, length us, event | category | flops | bytes accessed | tf_op | source)
XLA Modules:
  0.0 958.0 jit_solution(14615260156554540141)
XLA Ops:
  9.6 140.7 %begin.1 = (bf16[8,192,1536]{2,1,0:T(8,128)(2,1)}, bf16[4,8,192,1536]{3,2,1,0:T(8,128)(2,1)}, bf16[1536,1280]{1,0:T(8,128)(2,1)}, bf16[4,32,896]{2,1,0:T(8,128)(...) custom-call(bf16[192,1536]{1,0:T(8,128)(2,1)} %bitcast.65, ...), custom_call_target="tpu_custom_call" | custom-call | bytes 468000000 | tf_op jit(solution)/shard_map/begin/pallas_call | solution.py:718
  155.9 11.5 %project.1 = (bf16[1536,1536]{1,0:T(8,128)(2,1)}, f32[1536,384]{1,0:T(8,128)}, bf16[1536,768]{1,0:T(8,128)(2,1)}) custom-call(bf16[1536,1536]{1,0:T(8,128)(2,1)} %bitcast.70, f32[1,1536]{1,0:T(1,128)} %convert.7.refs_1_.refs_4_, bf16[1536,1280]{1,0:T(8,128)(2,1)} %get-tuple-element.124.refs_2_.refs_3_, bf16[1536,128]{1,0:T(8,128)(2,1)} %maximum_select_fusion.refs_3_.refs_4_), custom_call_target="tpu_custom_call" | custom-call | bytes 39600000 | tf_op jit(solution)/shard_map/project/pallas_call | solution.py:718
  170.0 36.5 %scan_forward.1 = (bf16[1536,384]{1,0:T(8,128)(2,1)}, bf16[1536,768]{1,0:T(8,128)(2,1)}, f32[6,384,128]{2,1,0:T(8,128)}, bf16[8,64,1536]{2,1,0:T(8,128)(2,1)}, b...) custom-call(s32[4]{0:T(128)} %bitcast.86, s32[1,1536]{1,0:T(1,128)} %refs_1_.5, ...), custom_call_target="tpu_custom_call" | custom-call | bytes 90000000 | tf_op jit(solution)/shard_map/scan_forward/pallas_call | solution.py:718
  208.0 32.7 %mix_out.1 = (f32[192,1664]{1,0:T(8,128)}, bf16[128,1536]{1,0:T(8,128)(2,1)}, bf16[128,1536]{1,0:T(8,128)(2,1)}, bf16[128,1536]{1,0:T(8,128)(2,1)}) custom-call(bf16[1536,384]{1,0:T(8,128)(2,1)} %get-tuple-element.128.refs_0_.refs_1_, f32[1536,384]{1,0:T(8,128)} %get-tuple-element.129.refs_1_.refs_2_, f32[1,384]{1,0:T(1,128)} %reshape.144.refs_2_.refs_3_, ...), custom_call_target="tpu_custom_call" | custom-call | bytes 126000000 | tf_op jit(solution)/shard_map/mix_out/pallas_call | solution.py:718
  243.0 3.6 token_forward.1
  246.6 113.8 %gather_rows.2 = (bf16[4,8,192,1664]{3,2,1,0:T(8,128)(2,1)}, bf16[384,1024]{1,0:T(8,128)(2,1)}, bf16[384,1024]{1,0:T(8,128)(2,1)}, bf16[384,1024]{1,0:T(8,128)(2,1)}) custom-call(bf16[192,1664]{1,0:T(8,128)(2,1)} %get-tuple-element.135.refs_0_.wide_ref, bf16[8,384,1024]{2,1,0:T(8,128)(2,1)} %refs_4_.7, bf16[8,384,1024]{2,1,0:T(8,128)(2,1)} %refs_4_.7, ...), custom_call_target="tpu_custom_call" | custom-call | bytes 360000000 | tf_op jit(solution)/shard_map/gather_rows/pallas_call | solution.py:718
  360.4 19.5 %shared_expert.1 = (bf16[8,192,1536]{2,1,0:T(8,128)(2,1)}, bf16[8,192,1536]{2,1,0:T(8,128)(2,1)}, bf16[1536,256]{1,0:T(8,128)(2,1)}, bf16[128,1536]{1,0:T(8,128)(2,1)}) custom-call(bf16[32,192,1664]{2,1,0:T(8,128)(2,1)} %bitcast.59, bf16[32,192,1536]{2,1,0:T(8,128)(2,1)} %bitcast.61, bf16[1536,1280]{1,0:T(8,128)(2,1)} %get-tuple-element.124.refs_2_.refs_3_, ...), custom_call_target="tpu_custom_call" | custom-call | bytes 64800000 | tf_op jit(solution)/shard_map/shared_expert/pallas_call | solution.py:718
  379.9 58.7 %dispatch.1 = (bf16[2,1024,1664]{2,1,0:T(8,128)(2,1)}, bf16[2,1024,1536]{2,1,0:T(8,128)(2,1)}, bf16[32,192,128]{2,1,0:T(8,128)(2,1)}, bf16[384,1024]{1,0:T(8,128...) custom-call(bf16[32,192,1664]{2,1,0:T(8,128)(2,1)} %bitcast.60, bf16[32,192,1536]{2,1,0:T(8,128)(2,1)} %bitcast.62, ...), custom_call_target="tpu_custom_call" | custom-call | bytes 108000000 | tf_op jit(solution)/shard_map/dispatch/pallas_call | solution.py:718
  438.5 55.4 %experts.1 = (bf16[2,1024,1536]{2,1,0:T(8,128)(2,1)}, bf16[2,1024,1664]{2,1,0:T(8,128)(2,1)}, bf16[384,1024]{1,0:T(8,128)(2,1)}, bf16[128,1536]{1,0:T(8,128)(2,1...) custom-call(bf16[2,1024,1664]{2,1,0:T(8,128)(2,1)} %get-tuple-elemen, ...), custom_call_target="tpu_custom_call" | custom-call | bytes 162000000 | tf_op jit(solution)/shard_map/experts/pallas_call | solution.py:718
  493.9 33.7 %combine.1 = (bf16[32,192,1536]{2,1,0:T(8,128)(2,1)}, bf16[32,192,1664]{2,1,0:T(8,128)(2,1)}, bf16[384,1024]{1,0:T(8,128)(2,1)}, bf16[128,1536]{1,0:T(8,128)(2,1)}) custom-call(bf16[32,192,128]{2,1,0:T(8,128)(2,1)} %get-tuple-element.138.refs_0_, bf16[2,1024,1536]{2,1,0:T(8,128)(2,1)} %get-tuple-element.161.refs_1_, ...), custom_call_target="tpu_custom_call" | custom-call | bytes 108000000 | tf_op jit(solution)/shard_map/combine/pallas_call | solution.py:718
  527.7 106.3 %reduce_rows.1 = (f32[192,1664]{1,0:T(8,128)}, bf16[384,1024]{1,0:T(8,128)(2,1)}, bf16[128,1536]{1,0:T(8,128)(2,1)}, bf16[384,1024]{1,0:T(8,128)(2,1)}) custom-call(bf16[4,8,192,1664]{3,2,1,0:T(8,128)(2,1)} %bitcast.63, bf16[384,1024]{1,0:T(8,128)(2,1)} %get-tuple-element.168.refs_1_, bf16[128,1536]{1,0:T(8,128)(2,1)} %get-tuple-element.169.refs_2_, ...), custom_call_target="tpu_custom_call" | custom-call | bytes 360000000 | tf_op jit(solution)/shard_map/reduce_rows/pallas_call | solution.py:718
  633.9 6.2 token_back.1
  640.1 29.6 %gather_rows.3 = (bf16[1,8,192,1664]{3,2,1,0:T(8,128)(2,1)}, bf16[128,1536]{1,0:T(8,128)(2,1)}, bf16[128,1536]{1,0:T(8,128)(2,1)}) custom-call(bf16[192,1664]{1,0:T(8,128)(2,1)} %get-tuple-element.173.refs_0_, bf16[128,1536]{1,0:T(8,128)(2,1)} %get-tuple-element.174.refs_1_, bf16[128,1536]{1,0:T(8,128)(2,1)} %get-tuple-element.175.refs_2_), custom_call_target="tpu_custom_call" | custom-call | bytes 90000000 | tf_op jit(solution)/shard_map/gather_rows/pallas_call | solution.py:718
  669.7 12.4 %mix_back.1 = (bf16[1536,384]{1,0:T(8,128)(2,1)}, bf16[1536,384]{1,0:T(8,128)(2,1)}, bf16[384,1536]{1,0:T(8,128)(2,1)}, f32[8,384]{1,0:T(8,128)}) custom-call(bf16[8,192,1664]{2,1,0:T(8,128)(2,1)} %bitcast.68, bf16[1536,384]{1,0:T(8,128)(2,1)} %get-tuple-element.128.refs_0_.refs_1_, f32[1536,384]{1,0:T(8,128)} %get-tuple-element.129.refs_1_.refs_2_, ...), custom_call_target="tpu_custom_call" | custom-call | bytes 43200000 | tf_op jit(solution)/shard_map/mix_back/pallas_call | solution.py:718
  682.1 2.5 maximum_bitcast_fusion.refs_5_
  684.7 102.0 %scan_backward.1 = (bf16[1536,768]{1,0:T(8,128)(2,1)}, f32[8,640]{1,0:T(8,128)}, f32[8,128]{1,0:T(8,128)}, f32[192,1536]{1,0:T(8,128)}, bf16[384,1024]{1,0:T(8,128)(2,1)}, /*index=5*/bf16[384,1024]{1,0:T(8,128)(2,1)}) custom-call(s32[4]{0:T(128)} %bitcast.87, s32[1,1536]{1,0:T(1,128)} %refs_1_.5, bf16[1536,768]{1,0:T(8,128)(2,1)} %get-tuple-element.133.refs_2_, ...), custom_call_target="tpu_custom_call" | custom-call | bytes 144000000 | tf_op jit(solution)/shard_map/scan_backward/pallas_call | solution.py:718
  786.7 27.8 %project_back.1 = (bf16[8,192,1536]{2,1,0:T(8,128)(2,1)}, bf16[1536,768]{1,0:T(8,128)(2,1)}, bf16[1536,384]{1,0:T(8,128)(2,1)}, bf16[8,64,1536]{2,1,0:T(8,128)(2,1)}, bf16[128,1536]{1,0:T(8,128)(2,1)}) custom-call(bf16[1536,384]{1,0:T(8,128)(2,1)} %get-tuple-element.182.refs_0_, bf16[1536,768]{1,0:T(8,128)(2,1)} %get-tuple-element.183.refs_1_, ...), custom_call_target="tpu_custom_call" | custom-call | bytes 90000000 | tf_op jit(solution)/shard_map/project_back/pallas_call | solution.py:718
  814.5 10.8 %collect.1 = (f32[8,384,1024]{2,1,0:T(8,128)}, f32[8,128,1536]{2,1,0:T(8,128)}) custom-call(s32[1]{0:T(128)} %bitcast.40.place_ref, bf16[384,1024]{1,0:T(8,128)(2,1)} %get-tuple-element.208.refs_0_, bf16[128,1536]{1,0:T(8,128)(2,1)} %get-tuple-element.209.refs_1_, bf16[384,1024]{1,0:T(8,128)(2,1)} %get-tuple-element.210.refs_2_, ...), custom_call_target="tpu_custom_call" | custom-call | bytes 43200000 | tf_op jit(solution)/shard_map/collect/pallas_call | solution.py:2286
  825.3 2.9 pack.1.refs_1_
  828.2 105.4 %settle.1 = (bf16[192,1536]{1,0:T(8,128)(2,1)}, bf16[8,384,768]{2,1,0:T(8,128)(2,1)}, bf16[8,128,1536]{2,1,0:T(8,128)(2,1)}, bf16[8,384,256]{2,1,0:T(8,128)(2,1)}, bf16[8,64,384]{2,1,0:T(8,128)(2,1)}) custom-call(bf16[1,8,192,1536]{3,2,1,0:T(8,128)(2,1)} %bitcast.69, bf16[4,8,64,384]{3,2,1,0:T(8,128)(2,1)} %pack.1.refs_1_, bf16[192,1536]{1,0:T(8,128)(2,1)} %bitcast.67, ...), custom_call_target="tpu_custom_call" | custom-call | bytes 324000000 | tf_op jit(solution)/shard_map/settle/pallas_call | solution.py:718
  933.6 11.4 %assemble.1 = (f32[384,6400]{1,0:T(8,128)}, f32[384,2048]{1,0:T(8,128)}, f32[2,8,48,1536]{3,2,1,0:T(8,128)}, f32[2,8,16,1536]{3,2,1,0:T(8,128)}) custom-call(bf16[8,384,768]{2,1,0:T(8,128)(2,1)} %get-tuple-element.201.main_ref, bf16[8,384,256]{2,1,0:T(8,128)(2,1)} %get-tuple-element.202.shared_in_ref, bf16[8,64,384]{2,1,0:T(8,128)(2,1)} %get-tuple-element.200.small_ref, ...), custom_call_target="tpu_custom_call" | custom-call | bytes 36000000 | tf_op jit(solution)/shard_map/assemble/pallas_call | solution.py:2240
  945.9 1.7 copy.55
  948.3 1.7 copy.54
  954.8 1.3 slice_reduce_fusion.6
  (91 shorter events, 28.8 us)
Async XLA Ops:
  0.7 0.8 copy-start
  208.0 33.4 %copy-start.3 = (bf16[4,384,128]{2,1,0:T(8,128)(2,1)S(1)}, bf16[4,384,128]{2,1,0:T(8,128)(2,1)}, u32[]{:S(2)}) copy-start(bf16[4,384,128]{2,1,0:T(8,128)(2,1)} %get-tuple-element.125) | copy-start | bytes 1179652
  208.0 34.2 %copy-start.9 = (s32[1,192,6]{1,0,2:T(1,128)S(1)}, s32[1,192,6]{1,0,2:T(1,128)}, u32[]{:S(2)}) copy-start(s32[1,192,6]{1,0,2:T(1,128)} %param.25) | copy-start | bytes 13828
  669.7 12.5 %copy-start.8 = (bf16[128,1536]{1,0:T(8,128)(2,1)S(1)}, bf16[128,1536]{1,0:T(8,128)(2,1)}, u32[]{:S(2)}) copy-start(bf16[128,1536]{1,0:T(8,128)(2,1)} %get-tuple-element.186) | copy-start | bytes 1179652
  933.6 11.4 %copy-start.4 = (bf16[8,64,384]{2,1,0:T(8,128)(2,1)S(1)}, bf16[8,64,384]{2,1,0:T(8,128)(2,1)}, u32[]{:S(2)}) copy-start(bf16[8,64,384]{2,1,0:T(8,128)(2,1)} %get-tuple-element.200.small_ref) | copy-start | bytes 1179652
  945.0 5.2 copy-start.10
  945.0 11.0 %copy-start.2 = (f32[192,1536]{1,0:T(8,128)S(1)}, f32[192,1536]{1,0:T(8,128)}, u32[]{:S(2)}) copy-start(f32[192,1536]{1,0:T(8,128)} %get-tuple-element.132.after_ref) | copy-start | bytes 3538948
  945.0 11.0 %copy-start.5 = (f32[192,1536]{1,0:T(8,128)S(1)}, f32[192,1536]{1,0:T(8,128)}, u32[]{:S(2)}) copy-start(f32[192,1536]{1,0:T(8,128)} %get-tuple-element.181) | copy-start | bytes 3538948
  950.3 6.8 copy-start.6
  950.9 7.0 copy-start.1
  950.9 0.7 copy-start.7

commit v6 on v5

--- a/solution.py
+++ b/solution.py
@@ -1426,13 +1426,14 @@
     x_ref,
     mix_ref,
     gain_ref,
+    done_ref,
     *refs,
 ):
     part = lax.axis_index("seq")
     place, _ = own_shard_group(inner)
     parts, refs = refs[:counts], refs[counts:]
     tokens_out, refs = refs[0], refs[1:]
-    outs, refs = refs[: counts + 1], refs[counts + 1 :]
+    outs, refs = refs[: counts + 2], refs[counts + 2 :]
     hidden_sum, small_sum = refs[:2]
     refs = refs[2:]
     take = len(Reducer.scratch(1, 16, LANES))
@@ -1440,7 +1441,7 @@
     small = Reducer(inner, small_ref, small_sum, refs[take : 2 * take])
     refs = refs[2 * take :]
     lines, totals, planes, owns = [], [], [], []
-    for index in range(counts + 1):
+    for index in range(counts + 2):
         low, gsend, grecv, here = refs[:4]
         refs = refs[4:]
         out = outs[index]
@@ -1487,6 +1488,7 @@
         owns[index][1].start()
 
     every = range(inner - 1)
+    owns[counts + 1][0][...] = done_ref[...]
     small.step(0)
     small.step(1)
     load(0)
@@ -1504,12 +1506,16 @@
     owns[counts][0][...] = to_low(small_sum[...])
     planes[counts][0]()
     owns[counts][1].start()
+    planes[counts + 1][0]()
+    owns[counts + 1][1].start()
     hidden.step(1)
     push_rest(0, every[1:])
     planes[counts][1]()
+    planes[counts + 1][1]()
     hidden.step(2)
     hidden.step(3)
     planes[counts][2]()
+    planes[counts + 1][2]()
     x = to_full(x_ref[...])
     scale = norm_scale(x)
     unit = x * scale
@@ -1542,7 +1548,7 @@
         copy.wait()
 
 
-def settle(hidden, small, x, mix, gain, parts, inner):
+def settle(hidden, small, x, mix, gain, done, parts, inner):
     _, _, rows, width = hidden.shape
     seq_devices = lax.axis_size("seq")
     anywhere = pl.BlockSpec(memory_space=pl.ANY)
@@ -1550,7 +1556,7 @@
     low = jnp.bfloat16
     sems = lambda *shape: pltpu.SemaphoreType.DMA(shape)
     small_rows, small_wide = small.shape[2:]
-    shapes = [part.shape[1:] for part in parts] + [(small_rows, small_wide)]
+    shapes = [part.shape[1:] for part in parts] + [(small_rows, small_wide), done.shape]
     scratch = [
         pltpu.VMEM((rows, width), jnp.float32),
         pltpu.VMEM((small_rows, small_wide), jnp.float32),
@@ -1559,13 +1565,13 @@
     scratch += Reducer.scratch(inner, small_rows, small_wide)
     for shape in shapes:
         scratch += [pltpu.VMEM(shape, low), sems(14), sems(14), sems()]
-    for shape in shapes[:-1]:
+    for shape in shapes[: len(parts)]:
         scratch += [pltpu.VMEM(shape, jnp.float32), sems(inner)]
         scratch += LineSum.scratch(inner, *shape)
     return run(
         functools.partial(settle_kernel, inner, len(parts)),
-        (hidden, small, x, mix, gain) + tuple(parts),
-        in_specs=[anywhere] * 2 + [inside] * 3 + [anywhere] * len(parts),
+        (hidden, small, x, mix, gain, done) + tuple(parts),
+        in_specs=[anywhere] * 2 + [inside] * 4 + [anywhere] * len(parts),
         out_specs=[inside] + [anywhere] * len(shapes),
         out_shape=[jax.ShapeDtypeStruct((rows, width), low)]
         + [jax.ShapeDtypeStruct((seq_devices,) + shape, low) for shape in shapes],
@@ -1972,7 +1978,15 @@
     x_ref, g_ref = refs[:2]
     total = 2 * count * per_device
     pieces, refs = refs[2 : 2 + total], refs[2 + total :]
-    seconds, refs = dict(zip(doubles, refs[: len(doubles)])), refs[len(doubles) :]
+    seconds, came = {}, list(targets)
+    for number, (_, carried) in doubles.items():
+        if carried:
+            seconds[number] = came.pop(0)
+        else:
+            seconds[number], refs = refs[0], refs[1:]
+    is_incoming = lambda item: item.output is None
+    is_outgoing = lambda item: item.output is not None
+    late = any(carried for _, carried in doubles.values())
     res_ref, dx_ref = refs[:2]
     outs = refs[2 : 2 + total]
     up_held, down_held, up_sum, down_sum, up_low, down_low, sems = refs[2 + total :]
@@ -2003,7 +2017,7 @@
             if len(piece.shape) == 3:
                 piece = piece.at[own_place * per_device + which]
             if number in seconds:
-                early = among(own_place, doubles[number])
+                early = among(own_place, doubles[number][0])
                 pl.when(early)(
                     lambda: action(pltpu.make_async_copy(piece, held, sem))
                 )
@@ -2022,10 +2036,14 @@
         def _():
             if which == 0:
                 fetch(0, begin_copy)
+                depart(is_incoming)
             if which == 1:
-                depart()
+                arrive(is_incoming)
+                depart(is_outgoing)
+                if late:
+                    fetch(1, begin_copy)
             fetch(which, end_copy)
-            if which + 1 < per_device:
+            if which + 1 < per_device and not (late and which == 0):
                 fetch(which + 1, begin_copy)
 
     @pl.when(step == 0)
@@ -2090,7 +2108,7 @@
 
         @pl.when((step == steps - 1) & (expert == per_device - 1))
         def _():
-            arrive()
+            arrive(is_outgoing)
 
 
 def experts(x, g, pieces, hidden, top_count, own_first, inner, doubles=(), outgoing=()):
@@ -2099,8 +2117,11 @@
     count = len(pieces) // per_device // 2
     low = jnp.bfloat16
     shapes = [jax.ShapeDtypeStruct(piece.shape[-2:], low) for piece in pieces]
-    freight = [Parcel(shapes[key], shift, inner, output=2 + key) for key, shift in outgoing]
-    others = [other for _, other, _ in doubles]
+    carried = [other for _, other, _ in doubles if isinstance(other, Parcel)]
+    freight = carried + [
+        Parcel(shapes[key], shift, inner, output=2 + key) for key, shift in outgoing
+    ]
+    others = [other for _, other, _ in doubles if not isinstance(other, Parcel)]
     double = 2 * hidden
     tile = min(rows, 256)
     block = lambda extent: pl.BlockSpec((1, tile, extent), lambda e, step: (e, step, 0))
@@ -2114,7 +2135,9 @@
             top_count=top_count,
             own_first=own_first,
             inner=inner,
-            doubles={number: places for number, _, places in doubles},
+            doubles={
+                number: (places, isinstance(other, Parcel)) for number, other, places in doubles
+            },
             outgoing=outgoing,
         ),
         (x, g) + tuple(pieces) + tuple(others),
@@ -2141,7 +2164,7 @@
         micros=45,
         name="experts",
     )
-    sent = outs.pop() if freight else []
+    sent = outs.pop()[len(carried) :] if freight else []
     return outs[0], outs[1], outs[2:], sent
 
 
@@ -2822,12 +2845,14 @@
     moe_all = moe_all.reshape(blocks, tok_rows, width + LANES)
     capacity = min(tok_rows, max(2, tok_rows * top_count * 5 // (expert_total * 3)))
     slots = -(-capacity // 16) * 16
-    keys = [(2, 1, UP), (1, 1, UP), (last, 1, UP)]
+    late_keys = [(1, 1, UP)] if outer == 1 else []
+    keys = [key for key in [(2, 1, UP), (1, 1, UP)] if key not in late_keys]
     expert_rows, grad_rows, picks, arrays = dispatch(
         moe_all, grad_all, per_device, top_count, slots, own_first, parcels(*keys)
     )
     unpack(keys, arrays)
-    shared_res, shared_back, shared_up_grad, shared_down_grad = shared_expert(
+    keys = [(last, 1, UP)]
+    shared_res, shared_back, shared_up_grad, shared_down_grad, arrays = shared_expert(
         moe_all,
         grad_all,
         proj_in,
@@ -2836,7 +2861,9 @@
         shared_part,
         seq_devices,
         inner,
-    )
+        parcels(*keys),
+    )
+    unpack(keys, arrays)
     order = [
         (shift, expert, kind)
         for shift in range(inner)
@@ -2848,7 +2875,7 @@
         expert_res, expert_back, grads, sent = experts(
             expert_rows,
             grad_rows,
-            [early.get(key, pieces[key]) for key in order],
+            [early[key] if key in early else pieces[key] for key in order],
             hidden,
             top_count,
             own_first,
@@ -2856,7 +2883,7 @@
             [
                 (
                     order.index(key),
-                    pieces[key],
+                    parcels(key)[0] if key in late_keys else pieces[key],
                     [(place_of + key[0]) % inner for place_of in early_from[key[0]]],
                 )
                 for key in order
@@ -2942,9 +2969,15 @@
     layer_out = to_low(after_mix + out_sum)
     keys = [(1, 1, DOWN)]
     swap = [PlaneSwap(rows_from_owner([proj_out_grad, shared_down_grad]))]
+    shared_parts = shared_up_grad.reshape(shard_devices, depth_rows, -1)
+    if outer == 1:
+        swap += [
+            Parcel(shared_parts, shift, inner, lambda to: to) for shift in range(1, inner)
+        ]
     hidden_part, main_grad, rest_grad, (taken, *arrays) = project_back(
         gate_in_grad, rows_grad, hidden_in, proj_in, dt_columns, seq_devices, swap + back_parcels(*keys)
     )
+    shared_came, arrays = arrays[: len(swap) - 1], arrays[len(swap) - 1 :]
     unpack_back(keys, arrays)
     experts_grad, experts_down_grad = collect(
         place[None], [returned[key] for key in order], per_device
@@ -2970,16 +3003,21 @@
             expert_total,
             heads,
         )
-        tokens_grad, main_all, rows_all, shared_all, small_all = settle(
+        tokens_grad, main_all, rows_all, small_all, shared_all = settle(
             hidden_part[None],
             small,
             tokens[0],
             mix_grad,
             gain_row,
+            to_low(
+                sum(
+                    map(to_full, shared_came),
+                    to_full(lax.dynamic_index_in_dim(shared_parts, place, 0, keepdims=False)),
+                )
+            ),
             [
                 main_grad.reshape(inner, depth_rows, -1),
                 taken.reshape(inner, -1, width),
-                shared_up_grad.reshape(inner, depth_rows, -1),
             ],
             inner,
         )

time: 966 us -> 945 us (0.978)
  Pallas kernels: 921 us -> 899 us
    pallas_call x15, Pallas kernels: 886 us -> 865 us  [run(): pl.pallas_call(wrapped, grid=grid, in_specs=list(in_specs) + [anywhere] *...]
where the time goes in v6:
time: 945 us; the launch traced here: 934 us
  Pallas kernels  899 us (95%)
  local copies, waits for them, and re-layouts  21.5 us (2%)
  other arithmetic  12.2 us (1%)
    pallas_call x15, Pallas kernels, run(): pl.pallas_call(wrapped, grid=grid, in_specs=list(in_specs) + [anywhere] *...  865 us

profile of v6, /device:TPU:0, one launch (start us, length us, event | category | flops | bytes accessed | tf_op | source)
XLA Modules:
  0.0 934.1 jit_solution(1844783290490086603)
XLA Ops:
  8.8 140.8 %begin.1 = (bf16[8,192,1536]{2,1,0:T(8,128)(2,1)}, bf16[4,8,192,1536]{3,2,1,0:T(8,128)(2,1)}, bf16[1536,1280]{1,0:T(8,128)(2,1)}, bf16[4,32,896]{2,1,0:T(8,128)(...) custom-call(bf16[192,1536]{1,0:T(8,128)(2,1)} %bitcast.72, ...), custom_call_target="tpu_custom_call" | custom-call | bytes 468000000 | tf_op jit(solution)/shard_map/begin/pallas_call | solution.py:718
  151.0 1.3 fusion.9
  153.3 11.5 %project.1 = (bf16[1536,1536]{1,0:T(8,128)(2,1)}, f32[1536,384]{1,0:T(8,128)}, bf16[1536,768]{1,0:T(8,128)(2,1)}) custom-call(bf16[1536,1536]{1,0:T(8,128)(2,1)} %bitcast.77, f32[1,1536]{1,0:T(1,128)} %convert.8.refs_1_.refs_4_, bf16[1536,1280]{1,0:T(8,128)(2,1)} %get-tuple-element.126.refs_2_.refs_3_, bf16[1536,128]{1,0:T(8,128)(2,1)} %maximum_select_fusion.refs_3_.refs_4_), custom_call_target="tpu_custom_call" | custom-call | bytes 39600000 | tf_op jit(solution)/shard_map/project/pallas_call | solution.py:718
  169.3 36.3 %scan_forward.1 = (bf16[1536,384]{1,0:T(8,128)(2,1)}, bf16[1536,768]{1,0:T(8,128)(2,1)}, f32[6,384,128]{2,1,0:T(8,128)}, bf16[8,64,1536]{2,1,0:T(8,128)(2,1)}, b...) custom-call(s32[4]{0:T(128)} %bitcast.92, s32[1,1536]{1,0:T(1,128)} %refs_1_.5, ...), custom_call_target="tpu_custom_call" | custom-call | bytes 90000000 | tf_op jit(solution)/shard_map/scan_forward/pallas_call | solution.py:718
  207.1 32.7 %mix_out.1 = (f32[192,1664]{1,0:T(8,128)}, bf16[128,1536]{1,0:T(8,128)(2,1)}, bf16[128,1536]{1,0:T(8,128)(2,1)}, bf16[128,1536]{1,0:T(8,128)(2,1)}) custom-call(bf16[1536,384]{1,0:T(8,128)(2,1)} %get-tuple-element.130.refs_0_.refs_1_, f32[1536,384]{1,0:T(8,128)} %get-tuple-element.131.refs_1_.refs_2_, f32[1,384]{1,0:T(1,128)} %reshape.146.refs_2_.refs_3_, ...), custom_call_target="tpu_custom_call" | custom-call | bytes 126000000 | tf_op jit(solution)/shard_map/mix_out/pallas_call | solution.py:718
  242.0 3.6 token_forward.1
  245.6 113.7 %gather_rows.2 = (bf16[4,8,192,1664]{3,2,1,0:T(8,128)(2,1)}, bf16[384,1024]{1,0:T(8,128)(2,1)}, bf16[384,1024]{1,0:T(8,128)(2,1)}, bf16[384,1024]{1,0:T(8,128)(2,1)}) custom-call(bf16[192,1664]{1,0:T(8,128)(2,1)} %get-tuple-element.137.refs_0_.wide_ref, bf16[8,384,1024]{2,1,0:T(8,128)(2,1)} %refs_25_.1, bf16[8,384,1024]{2,1,0:T(8,128)(2,1)} %refs_25_.1, ...), custom_call_target="tpu_custom_call" | custom-call | bytes 360000000 | tf_op jit(solution)/shard_map/gather_rows/pallas_call | solution.py:718
  359.3 41.7 %dispatch.1 = (bf16[2,1024,1664]{2,1,0:T(8,128)(2,1)}, bf16[2,1024,1536]{2,1,0:T(8,128)(2,1)}, bf16[32,192,128]{2,1,0:T(8,128)(2,1)}, bf16[384,1024]{1,0:T(8,128)(2,1)}) custom-call(bf16[32,192,1664]{2,1,0:T(8,128)(2,1)} %bitcast.62, bf16[32,192,1536]{2,1,0:T(8,128)(2,1)} %bitcast.64, bf16[8,384,1024]{2,1,0:T(8,128)(2,1)} %refs_25_.1), custom_call_target="tpu_custom_call" | custom-call | bytes 108000000 | tf_op jit(solution)/shard_map/dispatch/pallas_call | solution.py:718
  401.0 23.1 %shared_expert.1 = (bf16[8,192,1536]{2,1,0:T(8,128)(2,1)}, bf16[8,192,1536]{2,1,0:T(8,128)(2,1)}, bf16[1536,256]{1,0:T(8,128)(2,1)}, bf16[128,1536]{1,0:T(8,128)(2,1)}, bf16[384,1024]{1,0:T(8,128)(2,1)}) custom-call(bf16[32,192,1664]{2,1,0:T(8,128)(2,1)} %bitcast.63, bf16[32,192,1536]{2,1,0:T(8,128)(2,1)} %bitcast.65, ...), custom_call_target="tpu_custom_call" | custom-call | bytes 64800000 | tf_op jit(solution)/shard_map/shared_expert/pallas_call | solution.py:718
  424.1 54.6 %experts.1 = (bf16[2,1024,1536]{2,1,0:T(8,128)(2,1)}, bf16[2,1024,1664]{2,1,0:T(8,128)(2,1)}, bf16[384,1024]{1,0:T(8,128)(2,1)}, bf16[128,1536]{1,0:T(8,128)(2,1...) custom-call(bf16[2,1024,1664]{2,1,0:T(8,128)(2,1)} %get-tuple-elemen, ...), custom_call_target="tpu_custom_call" | custom-call | bytes 162000000 | tf_op jit(solution)/shard_map/experts/pallas_call | solution.py:718
  478.8 34.0 %combine.1 = (bf16[32,192,1536]{2,1,0:T(8,128)(2,1)}, bf16[32,192,1664]{2,1,0:T(8,128)(2,1)}, bf16[384,1024]{1,0:T(8,128)(2,1)}, bf16[128,1536]{1,0:T(8,128)(2,1)}) custom-call(bf16[32,192,128]{2,1,0:T(8,128)(2,1)} %get-tuple-element.140.refs_0_, bf16[2,1024,1536]{2,1,0:T(8,128)(2,1)} %get-tuple-element.162.refs_1_, ...), custom_call_target="tpu_custom_call" | custom-call | bytes 108000000 | tf_op jit(solution)/shard_map/combine/pallas_call | solution.py:718
  512.7 107.0 %reduce_rows.1 = (f32[192,1664]{1,0:T(8,128)}, bf16[384,1024]{1,0:T(8,128)(2,1)}, bf16[128,1536]{1,0:T(8,128)(2,1)}, bf16[384,1024]{1,0:T(8,128)(2,1)}) custom-call(bf16[4,8,192,1664]{3,2,1,0:T(8,128)(2,1)} %bitcast.66, bf16[384,1024]{1,0:T(8,128)(2,1)} %get-tuple-element.169.refs_1_, bf16[128,1536]{1,0:T(8,128)(2,1)} %get-tuple-element.170.refs_2_, ...), custom_call_target="tpu_custom_call" | custom-call | bytes 360000000 | tf_op jit(solution)/shard_map/reduce_rows/pallas_call | solution.py:718
  619.7 6.2 token_back.1
  625.9 29.6 %gather_rows.3 = (bf16[1,8,192,1664]{3,2,1,0:T(8,128)(2,1)}, bf16[128,1536]{1,0:T(8,128)(2,1)}, bf16[128,1536]{1,0:T(8,128)(2,1)}) custom-call(bf16[192,1664]{1,0:T(8,128)(2,1)} %get-tuple-element.174.refs_0_, bf16[128,1536]{1,0:T(8,128)(2,1)} %get-tuple-element.175.refs_1_, bf16[128,1536]{1,0:T(8,128)(2,1)} %get-tuple-element.176.refs_2_), custom_call_target="tpu_custom_call" | custom-call | bytes 90000000 | tf_op jit(solution)/shard_map/gather_rows/pallas_call | solution.py:718
  655.5 12.4 %mix_back.1 = (bf16[1536,384]{1,0:T(8,128)(2,1)}, bf16[1536,384]{1,0:T(8,128)(2,1)}, bf16[384,1536]{1,0:T(8,128)(2,1)}, f32[8,384]{1,0:T(8,128)}) custom-call(bf16[8,192,1664]{2,1,0:T(8,128)(2,1)} %bitcast.75, bf16[1536,384]{1,0:T(8,128)(2,1)} %get-tuple-element.130.refs_0_.refs_1_, f32[1536,384]{1,0:T(8,128)} %get-tuple-element.131.refs_1_.refs_2_, ...), custom_call_target="tpu_custom_call" | custom-call | bytes 43200000 | tf_op jit(solution)/shard_map/mix_back/pallas_call | solution.py:718
  667.9 102.1 %scan_backward.1 = (bf16[1536,768]{1,0:T(8,128)(2,1)}, f32[8,640]{1,0:T(8,128)}, f32[8,128]{1,0:T(8,128)}, f32[192,1536]{1,0:T(8,128)}, bf16[384,1024]{1,0:T(8,128)(2,1)}, /*index=5*/bf16[384,1024]{1,0:T(8,128)(2,1)}) custom-call(s32[4]{0:T(128)} %bitcast.93, s32[1,1536]{1,0:T(1,128)} %refs_1_.5, bf16[1536,768]{1,0:T(8,128)(2,1)} %get-tuple-element.135.refs_2_, ...), custom_call_target="tpu_custom_call" | custom-call | bytes 144000000 | tf_op jit(solution)/shard_map/scan_backward/pallas_call | solution.py:718
  770.1 2.3 fusion
  772.4 1.3 maximum_bitcast_fusion.refs_5_
  773.7 28.7 %project_back.1 = (bf16[8,192,1536]{2,1,0:T(8,128)(2,1)}, bf16[1536,768]{1,0:T(8,128)(2,1)}, bf16[1536,384]{1,0:T(8,128)(2,1)}, bf16[8,64,1536]{2,1,0:T(8,128)(2...) custom-call(bf16[1536,384]{1,0:T(8,128)(2,1)} %get-tuple-element.183, ...), custom_call_target="tpu_custom_call" | custom-call | bytes 90000000 | tf_op jit(solution)/shard_map/project_back/pallas_call | solution.py:718
  802.4 2.9 pack.1.refs_1_
  805.3 1.7 fusion.3.refs_5_
  807.1 96.5 %settle.1 = (bf16[192,1536]{1,0:T(8,128)(2,1)}, bf16[8,384,768]{2,1,0:T(8,128)(2,1)}, bf16[8,128,1536]{2,1,0:T(8,128)(2,1)}, bf16[8,64,384]{2,1,0:T(8,128)(2,1)}, bf16[8,384,256]{2,1,0:T(8,128)(2,1)}) custom-call(bf16[1,8,192,1536]{3,2,1,0:T(8,128)(2,1)} %bitcast.76, bf16[4,8,64,384]{3,2,1,0:T(8,128)(2,1)} %pack.1.refs_1_, bf16[192,1536]{1,0:T(8,128)(2,1)} %bitcast.74, ...), custom_call_target="tpu_custom_call" | custom-call | bytes 324000000 | tf_op jit(solution)/shard_map/settle/pallas_call | solution.py:718
  905.5 11.4 %assemble.1 = (f32[384,6400]{1,0:T(8,128)}, f32[384,2048]{1,0:T(8,128)}, f32[2,8,48,1536]{3,2,1,0:T(8,128)}, f32[2,8,16,1536]{3,2,1,0:T(8,128)}) custom-call(bf16[8,384,768]{2,1,0:T(8,128)(2,1)} %get-tuple-element.205.main_ref, bf16[8,384,256]{2,1,0:T(8,128)(2,1)} %get-tuple-element.206.shared_in_ref, bf16[8,64,384]{2,1,0:T(8,128)(2,1)} %get-tuple-element.204.small_ref, ...), custom_call_target="tpu_custom_call" | custom-call | bytes 36000000 | tf_op jit(solution)/shard_map/assemble/pallas_call | solution.py:2263
  922.4 10.7 %collect.1 = (f32[8,384,1024]{2,1,0:T(8,128)}, f32[8,128,1536]{2,1,0:T(8,128)}) custom-call(s32[1]{0:T(128)} %bitcast.41.place_ref, bf16[384,1024]{1,0:T(8,128)(2,1)} %get-tuple-element.212.refs_0_, bf16[128,1536]{1,0:T(8,128)(2,1)} %get-tuple-element.213.refs_1_, bf16[384,1024]{1,0:T(8,128)(2,1)} %get-tuple-element.214.refs_2_, ...), custom_call_target="tpu_custom_call" | custom-call | bytes 43200000 | tf_op jit(solution)/shard_map/collect/pallas_call | solution.py:2309
  (94 shorter events, 27.1 us)
Async XLA Ops:
  0.7 6.2 copy-start
  207.1 33.3 %copy-start.3 = (bf16[4,384,128]{2,1,0:T(8,128)(2,1)S(1)}, bf16[4,384,128]{2,1,0:T(8,128)(2,1)}, u32[]{:S(2)}) copy-start(bf16[4,384,128]{2,1,0:T(8,128)(2,1)} %get-tuple-element.127) | copy-start | bytes 1179652
  207.1 34.1 %copy-start.10 = (s32[1,192,6]{1,0,2:T(1,128)S(1)}, s32[1,192,6]{1,0,2:T(1,128)}, u32[]{:S(2)}) copy-start(s32[1,192,6]{1,0,2:T(1,128)} %param.25) | copy-start | bytes 13828
  667.9 102.2 %copy-start.2 = (f32[192,1536]{1,0:T(8,128)S(1)}, f32[192,1536]{1,0:T(8,128)}, u32[]{:S(2)}) copy-start(f32[192,1536]{1,0:T(8,128)} %get-tuple-element.134.after_ref) | copy-start | bytes 3538948
  770.1 2.4 copy-start.4
  770.1 2.4 copy-start.6
  802.4 3.0 copy-start.7
  802.4 3.0 copy-start.8
  802.4 2.9 copy-start.9
  807.1 97.8 %copy-start.11 = (bf16[384]{0:T(512)(128)(2,1)S(1)}, bf16[384]{0:T(512)(128)(2,1)}, u32[]{:S(2)}) copy-start(bf16[384]{0:T(512)(128)(2,1)} %param.26) | copy-start | bytes 2308
  922.4 10.7 %copy-start.5 = (bf16[192,1536]{1,0:T(8,128)(2,1)S(1)}, bf16[192,1536]{1,0:T(8,128)(2,1)}, u32[]{:S(2)}) copy-start(bf16[192,1536]{1,0:T(8,128)(2,1)} %get-tuple-element.203) | copy-start | bytes 1769476
  922.4 11.5 %copy-start.1 = (bf16[384,48]{0,1:T(8,128)(2,1)S(1)}, bf16[384,48]{0,1:T(8,128)(2,1)}, u32[]{:S(2)}) copy-start(bf16[384,48]{0,1:T(8,128)(2,1)} %param.28) | copy-start | bytes 110596

commit v7 on v6

--- a/solution.py
+++ b/solution.py
@@ -1421,6 +1421,7 @@
 def settle_kernel(
     inner,
     counts,
+    depart,
     hidden_ref,
     small_ref,
     x_ref,
@@ -1527,6 +1528,7 @@
     gather_part(0)
     if counts > 1:
         push_rest(1, every[1:])
+    depart()
     for index in range(1, counts):
         planes[index - 1][1]()
         if index > 1:
@@ -1548,7 +1550,7 @@
         copy.wait()
 
 
-def settle(hidden, small, x, mix, gain, done, parts, inner):
+def settle(hidden, small, x, mix, gain, done, parts, inner, freight):
     _, _, rows, width = hidden.shape
     seq_devices = lax.axis_size("seq")
     anywhere = pl.BlockSpec(memory_space=pl.ANY)
@@ -1576,8 +1578,10 @@
         out_shape=[jax.ShapeDtypeStruct((rows, width), low)]
         + [jax.ShapeDtypeStruct((seq_devices,) + shape, low) for shape in shapes],
         scratch=scratch,
+        freight=freight,
         flips=FLIPS,
         inner=inner,
+        late=True,
         micros=90,
         name="settle",
     )
@@ -2927,7 +2931,7 @@
         picks, expert_res, expert_back, shared_res, shared_back, inner, back_parcels(*keys)
     )
     unpack_back(keys, arrays)
-    keys = [(last, 1, UP), (2, 1, DOWN), (1, 1, UP)]
+    keys = [(last, 1, UP), (2, 0, UP)]
     back, arrays = reduce_rows(
         back_part.reshape(inner, seq_devices, tok_rows, -1), back_parcels(*keys)
     )
@@ -2953,7 +2957,7 @@
     dy, gate_in_grad, proj_out_grad, gain_gate_grad = mix_back(
         mix_group[0], y, gate_in, gate_gain, own_weights
     )
-    keys = [(2, 1, UP), (2, 0, UP)]
+    keys = [(2, 1, UP), (1, 1, UP)]
     rows_grad, conv_grad, head_grad, out_sum, arrays = scan_backward(
         lengths[0],
         deal_order,
@@ -2967,7 +2971,7 @@
     )
     unpack_back(keys, arrays)
     layer_out = to_low(after_mix + out_sum)
-    keys = [(1, 1, DOWN)]
+    keys = [(1, 1, DOWN)] if outer == 1 else [(1, 1, DOWN), (2, 1, DOWN)]
     swap = [PlaneSwap(rows_from_owner([proj_out_grad, shared_down_grad]))]
     shared_parts = shared_up_grad.reshape(shard_devices, depth_rows, -1)
     if outer == 1:
@@ -2979,9 +2983,6 @@
     )
     shared_came, arrays = arrays[: len(swap) - 1], arrays[len(swap) - 1 :]
     unpack_back(keys, arrays)
-    experts_grad, experts_down_grad = collect(
-        place[None], [returned[key] for key in order], per_device
-    )
     def spread(values, length, axis=0):
         shape = values.shape[:axis] + (length,) + values.shape[axis + 1 :]
         return lax.dynamic_update_slice_in_dim(
@@ -3003,7 +3004,8 @@
             expert_total,
             heads,
         )
-        tokens_grad, main_all, rows_all, small_all, shared_all = settle(
+        keys = [(2, 1, DOWN)]
+        tokens_grad, main_all, rows_all, small_all, shared_all, arrays = settle(
             hidden_part[None],
             small,
             tokens[0],
@@ -3020,7 +3022,9 @@
                 taken.reshape(inner, -1, width),
             ],
             inner,
-        )
+            back_parcels(*keys),
+        )
+        unpack_back(keys, arrays)
         w_in_grad, w_shared_grad, w_out_grad, w_shared_down_grad = assemble(
             main_all,
             shared_all,
@@ -3111,6 +3115,9 @@
         conv_w_grad, conv_b_grad, dt_bias_grad, a_log_grad, d_skip_grad, norm_gate_grad = results
         norm_moe_grad = depth_sum[:, used - 1]
         last_lane = used - 2
+    experts_grad, experts_down_grad = collect(
+        place[None], [returned[key] for key in order], per_device
+    )
     start = state_columns
     w_router_grad = depth_sum[:, start : start + expert_total]
     start += expert_total

time: 945 us -> 952 us (level)
  no operation moved by 1% of the time
where the time goes in v7:
time: 952 us; the launch traced here: 938 us
  Pallas kernels  903 us (95%)
  local copies, waits for them, and re-layouts  21.5 us (2%)
  other arithmetic  12.2 us (1%)
    pallas_call x15, Pallas kernels, run(): pl.pallas_call(wrapped, grid=grid, in_specs=list(in_specs) + [anywhere] *...  869 us

profile of v7, /device:TPU:0, one launch (start us, length us, event | category | flops | bytes accessed | tf_op | source)
XLA Modules:
  0.0 938.3 jit_solution(6983174359031266583)
XLA Ops:
  8.8 140.8 %begin.1 = (bf16[8,192,1536]{2,1,0:T(8,128)(2,1)}, bf16[4,8,192,1536]{3,2,1,0:T(8,128)(2,1)}, bf16[1536,1280]{1,0:T(8,128)(2,1)}, bf16[4,32,896]{2,1,0:T(8,128)(...) custom-call(bf16[192,1536]{1,0:T(8,128)(2,1)} %bitcast.72, ...), custom_call_target="tpu_custom_call" | custom-call | bytes 468000000 | tf_op jit(solution)/shard_map/begin/pallas_call | solution.py:718
  151.0 1.3 fusion.9
  153.3 11.5 %project.1 = (bf16[1536,1536]{1,0:T(8,128)(2,1)}, f32[1536,384]{1,0:T(8,128)}, bf16[1536,768]{1,0:T(8,128)(2,1)}) custom-call(bf16[1536,1536]{1,0:T(8,128)(2,1)} %bitcast.77, f32[1,1536]{1,0:T(1,128)} %convert.8.refs_1_.refs_4_, bf16[1536,1280]{1,0:T(8,128)(2,1)} %get-tuple-element.126.refs_2_.refs_3_, bf16[1536,128]{1,0:T(8,128)(2,1)} %maximum_select_fusion.refs_3_.refs_4_), custom_call_target="tpu_custom_call" | custom-call | bytes 39600000 | tf_op jit(solution)/shard_map/project/pallas_call | solution.py:718
  169.3 36.3 %scan_forward.1 = (bf16[1536,384]{1,0:T(8,128)(2,1)}, bf16[1536,768]{1,0:T(8,128)(2,1)}, f32[6,384,128]{2,1,0:T(8,128)}, bf16[8,64,1536]{2,1,0:T(8,128)(2,1)}, b...) custom-call(s32[4]{0:T(128)} %bitcast.92, s32[1,1536]{1,0:T(1,128)} %refs_1_.5, ...), custom_call_target="tpu_custom_call" | custom-call | bytes 90000000 | tf_op jit(solution)/shard_map/scan_forward/pallas_call | solution.py:718
  207.1 32.7 %mix_out.1 = (f32[192,1664]{1,0:T(8,128)}, bf16[128,1536]{1,0:T(8,128)(2,1)}, bf16[128,1536]{1,0:T(8,128)(2,1)}, bf16[128,1536]{1,0:T(8,128)(2,1)}) custom-call(bf16[1536,384]{1,0:T(8,128)(2,1)} %get-tuple-element.130.refs_0_.refs_1_, f32[1536,384]{1,0:T(8,128)} %get-tuple-element.131.refs_1_.refs_2_, f32[1,384]{1,0:T(1,128)} %reshape.146.refs_2_.refs_3_, ...), custom_call_target="tpu_custom_call" | custom-call | bytes 126000000 | tf_op jit(solution)/shard_map/mix_out/pallas_call | solution.py:718
  242.0 3.6 token_forward.1
  245.6 113.8 %gather_rows.2 = (bf16[4,8,192,1664]{3,2,1,0:T(8,128)(2,1)}, bf16[384,1024]{1,0:T(8,128)(2,1)}, bf16[384,1024]{1,0:T(8,128)(2,1)}, bf16[384,1024]{1,0:T(8,128)(2,1)}) custom-call(bf16[192,1664]{1,0:T(8,128)(2,1)} %get-tuple-element.137.refs_0_.wide_ref, bf16[8,384,1024]{2,1,0:T(8,128)(2,1)} %refs_25_.1, bf16[8,384,1024]{2,1,0:T(8,128)(2,1)} %refs_25_.1, ...), custom_call_target="tpu_custom_call" | custom-call | bytes 360000000 | tf_op jit(solution)/shard_map/gather_rows/pallas_call | solution.py:718
  359.4 41.7 %dispatch.1 = (bf16[2,1024,1664]{2,1,0:T(8,128)(2,1)}, bf16[2,1024,1536]{2,1,0:T(8,128)(2,1)}, bf16[32,192,128]{2,1,0:T(8,128)(2,1)}, bf16[384,1024]{1,0:T(8,128)(2,1)}) custom-call(bf16[32,192,1664]{2,1,0:T(8,128)(2,1)} %bitcast.62, bf16[32,192,1536]{2,1,0:T(8,128)(2,1)} %bitcast.64, bf16[8,384,1024]{2,1,0:T(8,128)(2,1)} %refs_25_.1), custom_call_target="tpu_custom_call" | custom-call | bytes 108000000 | tf_op jit(solution)/shard_map/dispatch/pallas_call | solution.py:718
  401.1 23.1 %shared_expert.1 = (bf16[8,192,1536]{2,1,0:T(8,128)(2,1)}, bf16[8,192,1536]{2,1,0:T(8,128)(2,1)}, bf16[1536,256]{1,0:T(8,128)(2,1)}, bf16[128,1536]{1,0:T(8,128)(2,1)}, bf16[384,1024]{1,0:T(8,128)(2,1)}) custom-call(bf16[32,192,1664]{2,1,0:T(8,128)(2,1)} %bitcast.63, bf16[32,192,1536]{2,1,0:T(8,128)(2,1)} %bitcast.65, ...), custom_call_target="tpu_custom_call" | custom-call | bytes 64800000 | tf_op jit(solution)/shard_map/shared_expert/pallas_call | solution.py:718
  424.2 54.6 %experts.1 = (bf16[2,1024,1536]{2,1,0:T(8,128)(2,1)}, bf16[2,1024,1664]{2,1,0:T(8,128)(2,1)}, bf16[384,1024]{1,0:T(8,128)(2,1)}, bf16[128,1536]{1,0:T(8,128)(2,1...) custom-call(bf16[2,1024,1664]{2,1,0:T(8,128)(2,1)} %get-tuple-elemen, ...), custom_call_target="tpu_custom_call" | custom-call | bytes 162000000 | tf_op jit(solution)/shard_map/experts/pallas_call | solution.py:718
  478.8 34.0 %combine.1 = (bf16[32,192,1536]{2,1,0:T(8,128)(2,1)}, bf16[32,192,1664]{2,1,0:T(8,128)(2,1)}, bf16[384,1024]{1,0:T(8,128)(2,1)}, bf16[128,1536]{1,0:T(8,128)(2,1)}) custom-call(bf16[32,192,128]{2,1,0:T(8,128)(2,1)} %get-tuple-element.140.refs_0_, bf16[2,1024,1536]{2,1,0:T(8,128)(2,1)} %get-tuple-element.162.refs_1_, ...), custom_call_target="tpu_custom_call" | custom-call | bytes 108000000 | tf_op jit(solution)/shard_map/combine/pallas_call | solution.py:718
  512.8 106.8 %reduce_rows.1 = (f32[192,1664]{1,0:T(8,128)}, bf16[384,1024]{1,0:T(8,128)(2,1)}, bf16[384,1024]{1,0:T(8,128)(2,1)}) custom-call(bf16[4,8,192,1664]{3,2,1,0:T(8,128)(2,1)} %bitcast.66, bf16[384,1024]{1,0:T(8,128)(2,1)} %get-tuple-element.169.refs_1_, bf16[384,1024]{1,0:T(8,128)(2,1)} %get-tuple-element.170.refs_2_), custom_call_target="tpu_custom_call" | custom-call | bytes 360000000 | tf_op jit(solution)/shard_map/reduce_rows/pallas_call | solution.py:718
  619.6 6.2 token_back.1
  625.8 29.5 %gather_rows.3 = (bf16[1,8,192,1664]{3,2,1,0:T(8,128)(2,1)}, bf16[128,1536]{1,0:T(8,128)(2,1)}, bf16[128,1536]{1,0:T(8,128)(2,1)}) custom-call(bf16[192,1664]{1,0:T(8,128)(2,1)} %get-tuple-element.173.refs_0_, bf16[128,1536]{1,0:T(8,128)(2,1)} %get-tuple-element.174.refs_1_, bf16[128,1536]{1,0:T(8,128)(2,1)} %get-tuple-element.175.refs_2_), custom_call_target="tpu_custom_call" | custom-call | bytes 90000000 | tf_op jit(solution)/shard_map/gather_rows/pallas_call | solution.py:718
  655.3 12.4 %mix_back.1 = (bf16[1536,384]{1,0:T(8,128)(2,1)}, bf16[1536,384]{1,0:T(8,128)(2,1)}, bf16[384,1536]{1,0:T(8,128)(2,1)}, f32[8,384]{1,0:T(8,128)}) custom-call(bf16[8,192,1664]{2,1,0:T(8,128)(2,1)} %bitcast.75, bf16[1536,384]{1,0:T(8,128)(2,1)} %get-tuple-element.130.refs_0_.refs_1_, f32[1536,384]{1,0:T(8,128)} %get-tuple-element.131.refs_1_.refs_2_, ...), custom_call_target="tpu_custom_call" | custom-call | bytes 43200000 | tf_op jit(solution)/shard_map/mix_back/pallas_call | solution.py:718
  667.7 101.8 %scan_backward.1 = (bf16[1536,768]{1,0:T(8,128)(2,1)}, f32[8,640]{1,0:T(8,128)}, f32[8,128]{1,0:T(8,128)}, f32[192,1536]{1,0:T(8,128)}, bf16[384,1024]{1,0:T(8,128)(2,1)}, /*index=5*/bf16[384,1024]{1,0:T(8,128)(2,1)}) custom-call(s32[4]{0:T(128)} %bitcast.93, s32[1,1536]{1,0:T(1,128)} %refs_1_.5, bf16[1536,768]{1,0:T(8,128)(2,1)} %get-tuple-element.135.refs_2_, ...), custom_call_target="tpu_custom_call" | custom-call | bytes 144000000 | tf_op jit(solution)/shard_map/scan_backward/pallas_call | solution.py:718
  769.5 2.3 fusion
  771.8 1.3 maximum_bitcast_fusion.refs_5_
  773.1 29.6 %project_back.1 = (bf16[8,192,1536]{2,1,0:T(8,128)(2,1)}, bf16[1536,768]{1,0:T(8,128)(2,1)}, bf16[1536,384]{1,0:T(8,128)(2,1)}, bf16[8,64,1536]{2,1,0:T(8,128)(2...) custom-call(bf16[1536,384]{1,0:T(8,128)(2,1)} %get-tuple-element.182, ...), custom_call_target="tpu_custom_call" | custom-call | bytes 90000000 | tf_op jit(solution)/shard_map/project_back/pallas_call | solution.py:718
  802.8 2.9 pack.1.refs_1_
  805.7 1.7 fusion.3.refs_5_
  807.4 100.3 %settle.1 = (bf16[192,1536]{1,0:T(8,128)(2,1)}, bf16[8,384,768]{2,1,0:T(8,128)(2,1)}, bf16[8,128,1536]{2,1,0:T(8,128)(2,1)}, bf16[8,64,384]{2,1,0:T(8,128)(2,1)}...) custom-call(bf16[1,8,192,1536]{3,2,1,0:T(8,128)(2,1)} %bitcast.76, bf16[4,8,64,384]{3,2,1,0:T(8,128)(2,1)} %pack.1.refs_1_, ...), custom_call_target="tpu_custom_call" | custom-call | bytes 324000000 | tf_op jit(solution)/shard_map/settle/pallas_call | solution.py:718
  909.6 11.4 %assemble.1 = (f32[384,6400]{1,0:T(8,128)}, f32[384,2048]{1,0:T(8,128)}, f32[2,8,48,1536]{3,2,1,0:T(8,128)}, f32[2,8,16,1536]{3,2,1,0:T(8,128)}) custom-call(bf16[8,384,768]{2,1,0:T(8,128)(2,1)} %get-tuple-element.205.main_ref, bf16[8,384,256]{2,1,0:T(8,128)(2,1)} %get-tuple-element.206.shared_in_ref, bf16[8,64,384]{2,1,0:T(8,128)(2,1)} %get-tuple-element.204.small_ref, ...), custom_call_target="tpu_custom_call" | custom-call | bytes 36000000 | tf_op jit(solution)/shard_map/assemble/pallas_call | solution.py:2267
  926.6 10.7 %collect.1 = (f32[8,384,1024]{2,1,0:T(8,128)}, f32[8,128,1536]{2,1,0:T(8,128)}) custom-call(s32[1]{0:T(128)} %bitcast.41.place_ref, bf16[384,1024]{1,0:T(8,128)(2,1)} %get-tuple-element.212.refs_0_, bf16[128,1536]{1,0:T(8,128)(2,1)} %get-tuple-element.213.refs_1_, bf16[384,1024]{1,0:T(8,128)(2,1)} %get-tuple-element.214.refs_2_, ...), custom_call_target="tpu_custom_call" | custom-call | bytes 43200000 | tf_op jit(solution)/shard_map/collect/pallas_call | solution.py:2313
  (94 shorter events, 27.1 us)
Async XLA Ops:
  0.7 6.2 copy-start
  207.1 33.3 %copy-start.3 = (bf16[4,384,128]{2,1,0:T(8,128)(2,1)S(1)}, bf16[4,384,128]{2,1,0:T(8,128)(2,1)}, u32[]{:S(2)}) copy-start(bf16[4,384,128]{2,1,0:T(8,128)(2,1)} %get-tuple-element.127) | copy-start | bytes 1179652
  207.1 34.1 %copy-start.10 = (s32[1,192,6]{1,0,2:T(1,128)S(1)}, s32[1,192,6]{1,0,2:T(1,128)}, u32[]{:S(2)}) copy-start(s32[1,192,6]{1,0,2:T(1,128)} %param.25) | copy-start | bytes 13828
  667.7 101.8 %copy-start.2 = (f32[192,1536]{1,0:T(8,128)S(1)}, f32[192,1536]{1,0:T(8,128)}, u32[]{:S(2)}) copy-start(f32[192,1536]{1,0:T(8,128)} %get-tuple-element.134.after_ref) | copy-start | bytes 3538948
  769.5 2.4 copy-start.4
  769.5 2.4 copy-start.6
  802.8 3.0 copy-start.7
  802.8 3.0 copy-start.8
  802.8 2.9 copy-start.9
  807.4 101.6 %copy-start.11 = (bf16[384]{0:T(512)(128)(2,1)S(1)}, bf16[384]{0:T(512)(128)(2,1)}, u32[]{:S(2)}) copy-start(bf16[384]{0:T(512)(128)(2,1)} %param.26) | copy-start | bytes 2308
  926.6 10.7 %copy-start.5 = (bf16[192,1536]{1,0:T(8,128)(2,1)S(1)}, bf16[192,1536]{1,0:T(8,128)(2,1)}, u32[]{:S(2)}) copy-start(bf16[192,1536]{1,0:T(8,128)(2,1)} %get-tuple-element.203) | copy-start | bytes 1769476
  926.6 11.5 %copy-start.1 = (bf16[384,48]{0,1:T(8,128)(2,1)S(1)}, bf16[384,48]{0,1:T(8,128)(2,1)}, u32[]{:S(2)}) copy-start(bf16[384,48]{0,1:T(8,128)(2,1)} %param.28) | copy-start | bytes 110596
